TPU v7x, 128 devices: a whole 4x4x4 slice. The times are simulated.
128 devices in a mesh: seq: 16 (over z_lo, y, core), ch: 8 (over x, z_hi).
Axes of the slice: x: 4, y: 4, z: 4 (z_hi: 2, z_lo: 2; z = z_hi * 2 + z_lo), core: 2. Of those that a mesh axis runs over, the one named last changes fastest.
Arguments:
- inputs: bfloat16 [65536, 1536], P('seq', 'ch'), may hold values from -6 to 6
- factor_one: bfloat16 [256, 256, 256], P('seq'), may hold values from -0.375 to 0.375
- factor_two: bfloat16 [256, 256, 256], P('seq'), may hold values from -0.375 to 0.375
- w_input_gate: bfloat16 [1536, 384], P(('seq', 'ch')), may hold values from -0.3125 to 0.3125
- norm_gain: float32 [1536], replicated, may hold values from 0.25 to 1.75
- w_gate: bfloat16 [1536, 768], P(('seq', 'ch')), may hold values from -0.3125 to 0.3125
- w_up: bfloat16 [1536, 768], P(('seq', 'ch')), may hold values from -0.3125 to 0.3125
- w_down: bfloat16 [3072, 384], P(('seq', 'ch')), may hold values from -0.21875 to 0.21875
- grad_out: bfloat16 [65536, 1536], P(('seq', 'ch')), may hold values from -6 to 6
Outputs:
- mixed_out: bfloat16 [65536, 1536], P(('seq', 'ch'))
- grad_inputs: bfloat16 [65536, 1536], P('seq', 'ch')
- grad_factor_one: float32 [256, 256, 256], P('seq', 'ch')
- grad_factor_two: float32 [256, 256, 256], P('seq', 'ch')
- grad_w_input_gate: float32 [1536, 384], P(('seq', 'ch'))
- grad_norm_gain: float32 [1536], replicated
- grad_w_gate: float32 [1536, 768], P(('seq', 'ch'))
- grad_w_up: float32 [1536, 768], P(('seq', 'ch'))
- grad_w_down: float32 [3072, 384], P(('seq', 'ch'))
All inputs are finite; a program needn't handle non-finite values.
Results may differ from a plain program's by a relative error of at most 0.025.
Values may be sent and summed in bfloat16 or wider, within the bound.
No kernel may reach another device: no remote copies, remote signals or barrier semaphores. Data moves between devices by JAX's collectives and lax.ppermute only.
A program may use at most 128 MiB of HBM per device.

v0:
```python
import math

import jax
import jax.numpy as jnp
from jax import lax
from jax.sharding import PartitionSpec as P

D = 1536
H = 3072
NBLK = 4
SEQL = 65536


def silu_slope(value):
    sig = jax.nn.sigmoid(value)
    return sig * (1.0 + value * (1.0 - sig))


def per_device(
    inputs, factor_one, factor_two, w_input_gate, norm_gain, w_gate, w_up, w_down, grad_out
):
    tok_scale = 1.0 / math.sqrt(SEQL)
    chan_scale = 1.0 / math.sqrt(D)
    blocks_here = factor_one.shape[0]
    block_len = factor_one.shape[1]
    chan_here = inputs.shape[1]
    token_blocks = inputs.reshape(blocks_here, block_len, chan_here)
    first_local = jnp.einsum(
        "iaj,ijc->iac", factor_one, token_blocks, preferred_element_type=jnp.float32
    ).astype(jnp.bfloat16)
    piece = lax.all_to_all(first_local, "seq", split_axis=1, concat_axis=0, tiled=True)
    result = jnp.einsum("aki,iac->kac", factor_two, piece, preferred_element_type=jnp.float32)
    first_cols = piece
    second_cols = result.astype(jnp.bfloat16)
    second_tok = lax.all_to_all(
        second_cols, "seq", split_axis=0, concat_axis=1, tiled=True
    ).reshape(inputs.shape)
    input_mlp, second_mlp = (
        lax.all_to_all(inputs, "ch", split_axis=0, concat_axis=1, tiled=True),
        lax.all_to_all(second_tok, "ch", split_axis=0, concat_axis=1, tiled=True),
    )
    rows_mlp = input_mlp.shape[0]
    gate_all, upper_all, down_all, entry_all = (
        lax.all_gather(w_gate, ("seq", "ch"), axis=0, tiled=True),
        lax.all_gather(w_up, ("seq", "ch"), axis=0, tiled=True),
        lax.all_gather(w_down, ("seq", "ch"), axis=0, tiled=True),
        lax.all_gather(w_input_gate, ("seq", "ch"), axis=0, tiled=True),
    )
    hidden_block = gate_all.shape[1]
    width_block = down_all.shape[1]
    wg3 = gate_all.reshape(NBLK, width_block, hidden_block)
    wu3 = upper_all.reshape(NBLK, width_block, hidden_block)
    wd3 = down_all.reshape(NBLK, hidden_block, width_block)
    win3 = entry_all.reshape(NBLK, width_block, width_block)
    input3 = input_mlp.reshape(rows_mlp, NBLK, width_block)
    pgate = (
        jnp.einsum("tbd,bde->tbe", input3, win3, preferred_element_type=jnp.float32)
        .reshape(rows_mlp, D)
        .astype(jnp.bfloat16)
    )
    pgate_f = pgate.astype(jnp.float32)
    input_f = input_mlp.astype(jnp.float32)
    silu_in = jax.nn.silu(input_f)
    second_f = second_mlp.astype(jnp.float32)
    resid = (input_f + second_f * pgate_f * silu_in).astype(jnp.bfloat16)
    resid_f = resid.astype(jnp.float32)
    rstd = lax.rsqrt(jnp.mean(resid_f * resid_f, axis=1, keepdims=True) + 1e-06)
    normed = (resid_f * rstd * norm_gain).astype(jnp.bfloat16)
    normed3 = normed.reshape(rows_mlp, NBLK, width_block)
    gate = jnp.einsum("tbd,bdh->tbh", normed3, wg3, preferred_element_type=jnp.float32)
    upper = jnp.einsum("tbd,bdh->tbh", normed3, wu3, preferred_element_type=jnp.float32)
    sig = jax.nn.sigmoid(gate)
    hidden = (gate * sig * upper).astype(jnp.bfloat16)
    down_out = jnp.einsum("tbh,bhe->tbe", hidden, wd3, preferred_element_type=jnp.float32)
    mixed_out = (resid_f + down_out.reshape(rows_mlp, D)).astype(jnp.bfloat16)
    cot3 = grad_out.reshape(rows_mlp, NBLK, width_block)
    g_hidden = jnp.einsum("tbe,bhe->tbh", cot3, wd3, preferred_element_type=jnp.float32)
    term_down = (
        jnp.einsum("tbh,tbe->bhe", hidden, cot3, preferred_element_type=jnp.float32).reshape(
            H, width_block
        )
        * tok_scale
    )
    g_gate = (g_hidden * upper * sig * (1.0 + gate * (1.0 - sig))).astype(jnp.bfloat16)
    g_up = (g_hidden * gate * sig).astype(jnp.bfloat16)
    term_gate = (
        jnp.einsum("tbd,tbh->bdh", normed3, g_gate, preferred_element_type=jnp.float32).reshape(
            D, hidden_block
        )
        * tok_scale
    )
    term_up = (
        jnp.einsum("tbd,tbh->bdh", normed3, g_up, preferred_element_type=jnp.float32).reshape(
            D, hidden_block
        )
        * tok_scale
    )
    g_normed = jnp.einsum("tbh,bdh->tbd", g_gate, wg3, preferred_element_type=jnp.float32)
    g_normed = (
        g_normed + jnp.einsum("tbh,bdh->tbd", g_up, wu3, preferred_element_type=jnp.float32)
    ).reshape(rows_mlp, D)
    grad_norm_gain = lax.psum(jnp.sum(g_normed * resid_f * rstd, axis=0), ("seq", "ch")) * tok_scale
    scaled = g_normed * norm_gain
    cot_f = grad_out.astype(jnp.float32)
    g_resid = (
        cot_f
        + rstd * scaled
        - resid_f * rstd**3 * jnp.mean(scaled * resid_f, axis=1, keepdims=True)
    ).astype(jnp.bfloat16)
    resid_grad = g_resid.astype(jnp.float32)
    g_pgate = (resid_grad * second_f * silu_in).astype(jnp.bfloat16)
    g_pgate3 = g_pgate.reshape(rows_mlp, NBLK, width_block)
    term_entry = (
        jnp.einsum("tbd,tbe->bde", input3, g_pgate3, preferred_element_type=jnp.float32).reshape(
            D, width_block
        )
        * tok_scale
    )
    grad_w_gate, grad_w_up, grad_w_down, grad_w_input_gate = (
        lax.psum_scatter(term_gate, ("seq", "ch"), scatter_dimension=0, tiled=True),
        lax.psum_scatter(term_up, ("seq", "ch"), scatter_dimension=0, tiled=True),
        lax.psum_scatter(term_down, ("seq", "ch"), scatter_dimension=0, tiled=True),
        lax.psum_scatter(term_entry, ("seq", "ch"), scatter_dimension=0, tiled=True),
    )
    g_second = (resid_grad * pgate_f * silu_in).astype(jnp.bfloat16)
    through_gate = jnp.einsum(
        "tbe,bde->tbd", g_pgate3, win3, preferred_element_type=jnp.float32
    ).reshape(rows_mlp, D)
    g_direct = (
        resid_grad * (1.0 + second_f * pgate_f * silu_slope(input_f)) + through_gate
    ).astype(jnp.bfloat16)
    second_grad_tok, direct_tok = (
        lax.all_to_all(g_second, "ch", split_axis=1, concat_axis=0, tiled=True),
        lax.all_to_all(g_direct, "ch", split_axis=1, concat_axis=0, tiled=True),
    )
    piece = lax.all_to_all(
        second_grad_tok.reshape(blocks_here, block_len, chan_here),
        "seq",
        split_axis=1,
        concat_axis=0,
        tiled=True,
    )
    result = jnp.einsum("aki,kac->iac", factor_two, piece, preferred_element_type=jnp.float32)
    first_grad_cols = result.astype(jnp.bfloat16)
    term_two = (
        jnp.einsum("kac,iac->aki", piece, first_cols, preferred_element_type=jnp.float32)
        * chan_scale
    )
    g_first = lax.all_to_all(first_grad_cols, "seq", split_axis=0, concat_axis=1, tiled=True)
    term_one = (
        jnp.einsum("iac,ijc->iaj", g_first, token_blocks, preferred_element_type=jnp.float32)
        * chan_scale
    )
    grad_factor_one, grad_factor_two = (
        lax.psum_scatter(
            term_one.astype(jnp.bfloat16), "ch", scatter_dimension=1, tiled=True
        ).astype(jnp.float32),
        lax.psum_scatter(
            term_two.astype(jnp.bfloat16), "ch", scatter_dimension=1, tiled=True
        ).astype(jnp.float32),
    )
    back_in = jnp.einsum(
        "iaj,iac->ijc", factor_one, g_first, preferred_element_type=jnp.float32
    ).reshape(inputs.shape)
    grad_inputs = (direct_tok.astype(jnp.float32) + back_in).astype(jnp.bfloat16)
    return (
        mixed_out,
        grad_inputs,
        grad_factor_one,
        grad_factor_two,
        grad_w_input_gate,
        grad_norm_gain,
        grad_w_gate,
        grad_w_up,
        grad_w_down,
    )


def solution(mesh):
    return jax.shard_map(
        per_device,
        mesh=mesh,
        in_specs=(
            P("seq", "ch"),
            P("seq", None, None),
            P("seq", None, None),
            P(("seq", "ch"), None),
            P(),
            P(("seq", "ch"), None),
            P(("seq", "ch"), None),
            P(("seq", "ch"), None),
            P(("seq", "ch"), None),
        ),
        out_specs=(
            P(("seq", "ch"), None),
            P("seq", "ch"),
            P("seq", "ch", None),
            P("seq", "ch", None),
            P(("seq", "ch"), None),
            P(),
            P(("seq", "ch"), None),
            P(("seq", "ch"), None),
            P(("seq", "ch"), None),
        ),
        check_vma=False,
    )
```

profile of v0, /device:TPU:2, one launch (start us, length us, event | category | flops | bytes accessed | tf_op | source)
XLA Modules:
  0.0 2364.2 jit_solution(17390138294775311688)
XLA Ops:
  17.9 33.6 %all_to_all.127 = bf16[16,256,192]{2,0,1:T(8,128)(2,1)S(1)} all-to-all(bf16[16,256,192]{2,0,1:T(8,128)(2,1)} %copy.148), channel_id=1, replica_groups=mesh['seq'=16,'ch'=8] {'seq'}, dimensions={1} | all-to-all | bytes 3145728 | tf_op jit(solution)/shard_map/all_to_all | solution.py:31
  66.0 31.4 %all_to_all.128 = bf16[256,16,192]{2,1,0:T(8,128)(2,1)S(1)} all-to-all(bf16[256,16,192]{2,1,0:T(8,128)(2,1)} %copy.152), channel_id=1, replica_groups=mesh['seq'=16,'ch'=8] {'seq'}, dimensions={0} | all-to-all | bytes 3145728 | tf_op jit(solution)/shard_map/all_to_all | solution.py:35
  102.8 7.8 all-to-all-start.3
  113.9 17.8 all-to-all-done.3
  131.8 6.3 all-to-all-start
  141.3 184.7 %all-gather.10.cloned.1.call-done = bf16[128,12,384]{2,1,0:T(8,128)(2,1)} async-done(((bf16[1,12,384]{2,1,0:T(8,128)(2,1)}), bf16[128,12,384]{2,1,0:T(8,128)(2,1)}) %all-gather.10.cloned.1.call-update) | async-done | bytes 1179664 | tf_op jit(solution)/shard_map/all_gather | solution.py:47
  331.7 5.6 fusion.48
  341.1 289.6 %all-gather.14.cloned.1.call-done = bf16[128,12,768]{2,1,0:T(8,128)(2,1)} async-done(((bf16[1,12,768]{2,1,0:T(8,128)(2,1)}), bf16[128,12,768]{2,1,0:T(8,128)(2,1)}) %all-gather.14.cloned.1.call-update) | async-done | bytes 2359312 | tf_op jit(solution)/shard_map/all_gather | solution.py:45
  635.7 302.7 %all-gather.12.cloned.1.call-done = bf16[128,12,768]{2,1,0:T(8,128)(2,1)} async-done(((bf16[1,12,768]{2,1,0:T(8,128)(2,1)}), bf16[128,12,768]{2,1,0:T(8,128)(2,1)}) %all-gather.12.cloned.1.call-update) | async-done | bytes 2359312 | tf_op jit(solution)/shard_map/all_gather | solution.py:44
  943.3 6.9 fusion.62
  954.8 285.9 %all-gather.8.cloned.1.call-done = bf16[3072,384]{1,0:T(8,128)(2,1)} async-done(((bf16[24,384]{1,0:T(8,128)(2,1)}), bf16[3072,384]{1,0:T(8,128)(2,1)}) %all-gather.8.cloned.1.call-update) | async-done | bytes 2359312 | tf_op jit(solution)/shard_map/all_gather | solution.py:46
  1240.7 9.2 fusion.7
  1261.1 28.9 %all_to_all.129 = bf16[512,8,192]{0,2,1:T(8,128)(2,1)S(1)} all-to-all(bf16[512,8,192]{0,2,1:T(8,128)(2,1)S(1)} %bitcast.283), channel_id=1, replica_groups=mesh['seq'=16,'ch'=8] {'ch'}, dimensions={1} | all-to-all | bytes 3145728 | tf_op jit(solution)/shard_map/all_to_all | solution.py:133
  1300.3 31.9 %all_to_all.130 = bf16[16,256,192]{2,0,1:T(8,128)(2,1)S(1)} all-to-all(bf16[16,256,192]{2,0,1:T(8,128)(2,1)} %copy.166), channel_id=1, replica_groups=mesh['seq'=16,'ch'=8] {'seq'}, dimensions={1} | all-to-all | bytes 3145728 | tf_op jit(solution)/shard_map/all_to_all | solution.py:136
  1350.6 31.7 %all_to_all.131 = bf16[256,16,192]{2,1,0:T(8,128)(2,1)S(1)} all-to-all(bf16[256,16,192]{2,1,0:T(8,128)(2,1)} %copy.170), channel_id=1, replica_groups=mesh['seq'=16,'ch'=8] {'seq'}, dimensions={0} | all-to-all | bytes 3145728 | tf_op jit(solution)/shard_map/all_to_all | solution.py:149
  1386.7 6.4 broadcast_multiply_fusion
  1406.5 5.8 all-to-all-start.4
  1423.9 450.6 %fusion.66 = (f32[16,384]{1,0:T(8,128)S(1)}, f32[16,768]{1,0:T(8,128)S(1)}, f32[16,768]{1,0:T(8,128)S(1)}) fusion(f32[1536,384]{1,0:T(8,128)} %bitcast.266, f32[1536,768]{1,0:T(8,128)} %bitcast.258, f32[1536,768]{1,0:T(8,128)} %bitcast.259), kind=kCustom, calls=%all-reduce-scatter.3 | all-reduce-scatter fusion | flops 3932161 | bytes 11919360
  1874.5 5.8 collective-permute-start
  1880.3 6.3 collective-permute-start.1
  1886.7 7.5 collective-permute-start.31
  1898.0 5.3 collective-permute-start.12
  1903.3 7.6 collective-permute-start.13
  1974.9 5.5 collective-permute-start.64
  1995.9 7.8 collective-permute-start.68
  2075.8 6.6 collective-permute-start.36
  2087.2 5.5 collective-permute-start.39
  2122.3 62.8 %psum.7 = f32[1536]{0:T(1024)S(1)} all-reduce(f32[1536]{0:T(1024)S(1)} %reduce_sum.32), channel_id=1, replica_groups=mesh['seq'=16,'ch'=8] {'seq','ch'}, use_global_device_ids=true, to_apply=%region_6.7 | all-reduce | flops 1536 | bytes 12288 | tf_op jit(solution)/shard_map/psum | solution.py:102
  2191.9 8.0 collective-permute-start.55
  2208.4 25.5 %concatenate = f32[524,384]{1,0:T(8,128)S(1)} concatenate(f32[12,384]{1,0:T(8,128)} %copy-done.85, f32[16,384]{1,0:T(8,128)} %copy-done.108, f32[16,384]{1,0:T(8,128)} %copy-done.106, f32[16,384]{1,0:T(8,128)} %copy-done.105, f32[16,384]{1,0:T(8,128)} %copy-done.104, f32[16,384]{1,0:T(8,128)} %copy-done.103, f32[16,384]{1,0:T(8,128)} %copy-done.102, f32[16,384]{1,0:T(8,128)} %copy-done.101, ...), dimensions={0} | concatenate | bytes 1609728
  2248.5 47.5 %concatenate.2 = f32[524,768]{1,0:T(8,128)} concatenate(f32[12,768]{1,0:T(8,128)S(1)} %collective-permute-done.95, f32[16,768]{1,0:T(8,128)} %copy-done.49, f32[16,768]{1,0:T(8,128)} %copy-done.46, f32[16,768]{1,0:T(8,128)} %copy-done.43, f32[16,768]{1,0:T(8,128)} %copy-done.42, f32[16,768]{1,0:T(8,128)} %copy-done.41, f32[16,768]{1,0:T(8,128)} %copy-done.40, ...), dimensions={0} | concatenate | bytes 3219456
  2296.2 47.2 %concatenate.1 = f32[524,768]{1,0:T(8,128)} concatenate(f32[12,768]{1,0:T(8,128)S(1)} %collective-permute-done.63, f32[16,768]{1,0:T(8,128)} %collective-permute-done.62, f32[16,768]{1,0:T(8,128)} %collective-permute-done.61, f32[16,768]{1,0:T(8,128)} %collective-permute-done.60, f32[16,768]{1,0:T(8,128)} %collective-permute-done.59, f32[16,768]{1,0:T(8,128)} %collective-permute-done.58, ...), dimensions={0} | concatenate | bytes 3219456
  (481 shorter events, 360.7 us)
Async XLA Ops:
  7.2 318.8 %all-gather.10.cloned.1.call-start = ((), (), s32[]{:S(2)}) async-start(), calls=%async_computation.14 | async-start | bytes 1585152 | tf_op jit(solution)/shard_map/all_gather | solution.py:47
  7.9 622.8 %all-gather.14.cloned.1.call-start = ((), (), s32[]{:S(2)}) async-start(), calls=%async_computation.16 | async-start | bytes 3170304 | tf_op jit(solution)/shard_map/all_gather | solution.py:45
  8.7 929.7 %all-gather.12.cloned.1.call-start = ((), (), s32[]{:S(2)}) async-start(), calls=%async_computation.15 | async-start | bytes 3170304 | tf_op jit(solution)/shard_map/all_gather | solution.py:44
  102.8 29.0 %all-to-all-start.3 = ((bf16[8,512,192]{1,2,0:T(8,128)(2,1)}), bf16[8,512,192]{1,2,0:T(8,128)(2,1)}, u32[]{:S(2)}, u32[]{:S(2)}) async-start(bf16[8,512,192]{1,2,0:T(8,128)(2,1)} %copy.154), calls=%async_computation.3 | async-start | bytes 3145728 | tf_op jit(solution)/shard_map/all_to_all | solution.py:40
  110.6 1130.1 %all-gather.8.cloned.1.call-start = ((), (), s32[]{:S(2)}) async-start(), calls=%async_computation.11 | async-start | bytes 2377728 | tf_op jit(solution)/shard_map/all_gather | solution.py:46
  131.8 200.0 %all-to-all-start = ((bf16[8,512,192]{1,2,0:T(8,128)(2,1)}), bf16[8,512,192]{1,2,0:T(8,128)(2,1)}, u32[]{:S(2)}, u32[]{:S(2)}) async-start(bf16[8,512,192]{1,2,0:T(8,128)(2,1)} %bitcast.278), calls=%async_computation | async-start | bytes 3145728 | tf_op jit(solution)/shard_map/all_to_all | solution.py:39
  138.1 2215.1 %reduce-scatter.15.cloned.1.call-start = ((), (), s32[]{:S(2)}) async-start(), calls=%async_computation.13 | async-start | bytes 2359296 | tf_op jit(solution)/shard_map/reduce_scatter | solution.py:158
  1343.0 1012.1 %reduce-scatter.13.cloned.1.call-start = ((), (), s32[]{:S(2)}) async-start(), calls=%async_computation.12 | async-start | bytes 2359296 | tf_op jit(solution)/shard_map/reduce_scatter | solution.py:155
  1386.4 970.4 %reduce-scatter.17.cloned.1.call-start = ((), (), s32[]{:S(2)}) async-start(), calls=%async_computation.17 | async-start | bytes 4755456
  1406.5 940.0 %all-to-all-start.4 = ((bf16[512,8,192]{0,2,1:T(8,128)(2,1)}), bf16[512,8,192]{0,2,1:T(8,128)(2,1)}, u32[]{:S(2)}, u32[]{:S(2)}) async-start(bf16[512,8,192]{0,2,1:T(8,128)(2,1)} %bitcast.284), calls=%async_computation.4 | async-start | bytes 3145728 | tf_op jit(solution)/shard_map/all_to_all | solution.py:134
  1874.5 28.8 %collective-permute-start = (f32[16,384]{1,0:T(8,128)S(1)}, f32[16,384]{1,0:T(8,128)S(1)}, u32[]{:S(2)}, u32[]{:S(2)}) collective-permute-start(f32[16,384]{1,0:T(8,128)S(1)} %get-tuple-element.50), channel_id=1, source_target_pairs={{0,1},{1,2},{2,3},{3,4},{4,5},{5,6},{6,7},{7,8},{8,9},{9,10},{10,1... | collective-permute-start | bytes 73736
  1880.3 30.6 %collective-permute-start.1 = (f32[16,384]{1,0:T(8,128)S(1)}, f32[16,384]{1,0:T(8,128)S(1)}, u32[]{:S(2)}, u32[]{:S(2)}) collective-permute-start(f32[16,384]{1,0:T(8,128)S(1)} %get-tuple-element.50), channel_id=1, source_target_pairs={{0,2},{1,3},{2,4},{3,5},{4,6},{5,7},{6,8},{7,9},{8,10},{9,11},{10,... | collective-permute-start | bytes 73736
  1894.3 21.2 collective-permute-start.10
  1895.8 21.0 collective-permute-start.11
  1898.0 22.3 collective-permute-start.12
  1974.9 28.8 %collective-permute-start.64 = (f32[16,768]{1,0:T(8,128)S(1)}, f32[16,768]{1,0:T(8,128)S(1)}, u32[]{:S(2)}, u32[]{:S(2)}) collective-permute-start(f32[16,768]{1,0:T(8,128)S(1)} %get-tuple-element.52), channel_id=1, source_target_pairs={{0,1},{1,2},{2,3},{3,4},{4,5},{5,6},{6,7},{7,8},{8,9},{9,10},{10,1... | collective-permute-start | bytes 147464
  1981.1 25.5 %collective-permute-start.65 = (f32[16,768]{1,0:T(8,128)S(1)}, f32[16,768]{1,0:T(8,128)S(1)}, u32[]{:S(2)}, u32[]{:S(2)}) collective-permute-start(f32[16,768]{1,0:T(8,128)S(1)} %get-tuple-element.52), channel_id=1, source_target_pairs={{0,2},{1,3},{2,4},{3,5},{4,6},{5,7},{6,8},{7,9},{8,10},{9,11},{10,... | collective-permute-start | bytes 147464
  2111.0 74.1 %collective-permute-start.48 = (f32[16,768]{1,0:T(8,128)S(1)}, f32[16,768]{1,0:T(8,128)S(1)}, u32[]{:S(2)}, u32[]{:S(2)}) collective-permute-start(f32[16,768]{1,0:T(8,128)S(1)} %get-tuple-element.51), channel_id=1, source_target_pairs={{0,17},{1,18},{2,19},{3,20},{4,21},{5,22},{6,23},{7,24},{8,25},{9,... | collective-permute-start | bytes 147464
  2112.3 75.5 %collective-permute-start.49 = (f32[16,768]{1,0:T(8,128)S(1)}, f32[16,768]{1,0:T(8,128)S(1)}, u32[]{:S(2)}, u32[]{:S(2)}) collective-permute-start(f32[16,768]{1,0:T(8,128)S(1)} %get-tuple-element.51), channel_id=1, source_target_pairs={{0,18},{1,19},{2,20},{3,21},{4,22},{5,23},{6,24},{7,25},{8,26},{9,... | collective-permute-start | bytes 147464
  2113.7 78.1 %collective-permute-start.50 = (f32[16,768]{1,0:T(8,128)S(1)}, f32[16,768]{1,0:T(8,128)S(1)}, u32[]{:S(2)}, u32[]{:S(2)}) collective-permute-start(f32[16,768]{1,0:T(8,128)S(1)} %get-tuple-element.51), channel_id=1, source_target_pairs={{0,19},{1,20},{2,21},{3,22},{4,23},{5,24},{6,25},{7,26},{8,27},{9,... | collective-permute-start | bytes 147464
  2117.2 82.6 %collective-permute-start.51 = (f32[16,768]{1,0:T(8,128)S(1)}, f32[16,768]{1,0:T(8,128)S(1)}, u32[]{:S(2)}, u32[]{:S(2)}) collective-permute-start(f32[16,768]{1,0:T(8,128)S(1)} %get-tuple-element.51), channel_id=1, source_target_pairs={{0,20},{1,21},{2,22},{3,23},{4,24},{5,25},{6,26},{7,27},{8,28},{9,... | collective-permute-start | bytes 147464
  2118.5 83.2 %collective-permute-start.52 = (f32[16,768]{1,0:T(8,128)S(1)}, f32[16,768]{1,0:T(8,128)S(1)}, u32[]{:S(2)}, u32[]{:S(2)}) collective-permute-start(f32[16,768]{1,0:T(8,128)S(1)} %get-tuple-element.51), channel_id=1, source_target_pairs={{0,21},{1,22},{2,23},{3,24},{4,25},{5,26},{6,27},{7,28},{8,29},{9,... | collective-permute-start | bytes 147464
  2185.1 48.8 %collective-permute-start.53 = (f32[16,768]{1,0:T(8,128)S(1)}, f32[16,768]{1,0:T(8,128)}, u32[]{:S(2)}, u32[]{:S(2)}) collective-permute-start(f32[16,768]{1,0:T(8,128)S(1)} %get-tuple-element.51), channel_id=1, source_target_pairs={{0,22},{1,23},{2,24},{3,25},{4,26},{5,27},{6,28},{7,29},{8,30},{9,... | collective-permute-start | bytes 147464
  2187.8 49.7 %collective-permute-start.54 = (f32[16,768]{1,0:T(8,128)S(1)}, f32[16,768]{1,0:T(8,128)}, u32[]{:S(2)}, u32[]{:S(2)}) collective-permute-start(f32[16,768]{1,0:T(8,128)S(1)} %get-tuple-element.51), channel_id=1, source_target_pairs={{0,23},{1,24},{2,25},{3,26},{4,27},{5,28},{6,29},{7,30},{8,31},{9,... | collective-permute-start | bytes 147464
  2191.9 48.0 %collective-permute-start.55 = (f32[16,768]{1,0:T(8,128)S(1)}, f32[16,768]{1,0:T(8,128)}, u32[]{:S(2)}, u32[]{:S(2)}) collective-permute-start(f32[16,768]{1,0:T(8,128)S(1)} %get-tuple-element.51), channel_id=1, source_target_pairs={{0,24},{1,25},{2,26},{3,27},{4,28},{5,29},{6,30},{7,31},{8,32},{9,... | collective-permute-start | bytes 147464
  2199.8 42.9 %collective-permute-start.56 = (f32[16,768]{1,0:T(8,128)S(1)}, f32[16,768]{1,0:T(8,128)}, u32[]{:S(2)}, u32[]{:S(2)}) collective-permute-start(f32[16,768]{1,0:T(8,128)S(1)} %get-tuple-element.51), channel_id=1, source_target_pairs={{0,25},{1,26},{2,27},{3,28},{4,29},{5,30},{6,31},{7,32},{8,33},{9,... | collective-permute-start | bytes 147464
  2201.7 42.9 %collective-permute-start.57 = (f32[16,768]{1,0:T(8,128)S(1)}, f32[16,768]{1,0:T(8,128)}, u32[]{:S(2)}, u32[]{:S(2)}) collective-permute-start(f32[16,768]{1,0:T(8,128)S(1)} %get-tuple-element.51), channel_id=1, source_target_pairs={{0,26},{1,27},{2,28},{3,29},{4,30},{5,31},{6,32},{7,33},{8,34},{9,... | collective-permute-start | bytes 147464
  2233.9 62.1 %collective-permute-start.58 = (f32[16,768]{1,0:T(8,128)S(1)}, f32[16,768]{1,0:T(8,128)}, u32[]{:S(2)}, u32[]{:S(2)}) collective-permute-start(f32[16,768]{1,0:T(8,128)S(1)} %get-tuple-element.51), channel_id=1, source_target_pairs={{0,27},{1,28},{2,29},{3,30},{4,31},{5,32},{6,33},{7,34},{8,35},{9,... | collective-permute-start | bytes 147464
  2237.5 58.5 %collective-permute-start.59 = (f32[16,768]{1,0:T(8,128)S(1)}, f32[16,768]{1,0:T(8,128)}, u32[]{:S(2)}, u32[]{:S(2)}) collective-permute-start(f32[16,768]{1,0:T(8,128)S(1)} %get-tuple-element.51), channel_id=1, source_target_pairs={{0,28},{1,29},{2,30},{3,31},{4,32},{5,33},{6,34},{7,35},{8,36},{9,... | collective-permute-start | bytes 147464
  2239.9 56.2 %collective-permute-start.60 = (f32[16,768]{1,0:T(8,128)S(1)}, f32[16,768]{1,0:T(8,128)}, u32[]{:S(2)}, u32[]{:S(2)}) collective-permute-start(f32[16,768]{1,0:T(8,128)S(1)} %get-tuple-element.51), channel_id=1, source_target_pairs={{0,29},{1,30},{2,31},{3,32},{4,33},{5,34},{6,35},{7,36},{8,37},{9,... | collective-permute-start | bytes 147464
  2242.7 53.4 %collective-permute-start.61 = (f32[16,768]{1,0:T(8,128)S(1)}, f32[16,768]{1,0:T(8,128)}, u32[]{:S(2)}, u32[]{:S(2)}) collective-permute-start(f32[16,768]{1,0:T(8,128)S(1)} %get-tuple-element.51), channel_id=1, source_target_pairs={{0,30},{1,31},{2,32},{3,33},{4,34},{5,35},{6,36},{7,37},{8,38},{9,... | collective-permute-start | bytes 147464
  2244.6 51.5 %collective-permute-start.62 = (f32[16,768]{1,0:T(8,128)S(1)}, f32[16,768]{1,0:T(8,128)}, u32[]{:S(2)}, u32[]{:S(2)}) collective-permute-start(f32[16,768]{1,0:T(8,128)S(1)} %get-tuple-element.51), channel_id=1, source_target_pairs={{0,31},{1,32},{2,33},{3,34},{4,35},{5,36},{6,37},{7,38},{8,39},{9,... | collective-permute-start | bytes 147464
  (186 other events, 5184.8 us)
Sparse Core Ops, SparseCore 0:
  9.7 316.2 all-gather.9
  327.7 303.0 all-gather.13
  632.4 305.8 all-gather.11
  939.9 300.7 all-gather.7
  1343.1 100.7 reduce-scatter.14
  1448.0 99.1 reduce-scatter.12
  1550.2 665.2 reduce-scatter.16
where the time goes:
time: 2380 us; the launch traced here: 2360 us
  waiting for transfers between devices  1090 us (46%)
  blocking collectives  671 us (28%)
  starting transfers between devices  298 us (13%)
  local copies, waits for them, and re-layouts  198 us (8%)
  matrix products  67.5 us (3%)
  other arithmetic  27.9 us (1%)
    unnamed x1, blocking collectives  451 us
    all_gather x1, waiting for transfers between devices, per_device(): lax.all_gather(w_gate, ('seq', 'ch'), axis=0, tiled=True)  303 us
    all_gather x1, waiting for transfers between devices, per_device(): lax.all_gather(w_up, ('seq', 'ch'), axis=0, tiled=True)  290 us
    all_gather x1, waiting for transfers between devices, per_device(): lax.all_gather(w_down, ('seq', 'ch'), axis=0, tiled=True)  286 us
    unnamed x97, starting transfers between devices  277 us
    all_gather x1, waiting for transfers between devices, per_device(): lax.all_gather(w_input_gate, ('seq', 'ch'), axis=0, tiled=True)  185 us
    unnamed x235, local copies, waits for them, and re-layouts  139 us
    psum x1, blocking collectives, per_device(): lax.psum(jnp.sum(g_normed * resid_f * rstd, axis=0), ('seq', 'ch'))  62.8 us
  transfers between devices with their start and end apart: 106, of which 6 were waited for; matrix products, arithmetic and copies ran while one was open for 29% of the time, Pallas kernels for 0%

commit v1 on v0

v1 whole, which is shorter than its diff:
```python
import math

import jax
import jax.numpy as jnp
from jax import lax
from jax.sharding import Mesh
from jax.sharding import PartitionSpec as P

D = 1536
NBLK = 4
SEQL = 65536
DB = D // NBLK
BF = jnp.bfloat16
F32 = jnp.float32

SEQ = ("zl", "y", "core")
CH = ("x", "zh")
ALL = SEQ + CH
SIZES = (2, 4, 2, 4, 2)
PLANE = SEQ + ("zh",)


def index_of(zl, y, k, x, zh):
    return (((zl * 4 + y) * 2 + k) * 4 + x) * 2 + zh


def shard_moves():
    moves = []
    for zl in range(2):
        for y in range(4):
            for k in range(2):
                for x in range(4):
                    for zh in range(2):
                        there = index_of(x // 2, (x % 2) * 2 + y % 2, k, zl * 2 + y // 2, zh)
                        moves.append((index_of(zl, y, k, x, zh), there))
    return moves


SWAP = [(0, 1), (1, 0)]


def silu_slope(value):
    sig = jax.nn.sigmoid(value)
    return sig * (1.0 + value * (1.0 - sig))


def sum_over_x(value):
    total = value
    for step in (1, 3, 2):
        total = total + lax.ppermute(value, "x", [(i, (i + step) % 4) for i in range(4)])
    return total


def exchange_x(parts):
    me = lax.axis_index("x")
    got = jnp.zeros_like(parts)
    own = lax.dynamic_index_in_dim(parts, me, 0, keepdims=True)
    got = lax.dynamic_update_slice_in_dim(got, own, me, 0)
    for step in (1, 3, 2):
        to = lax.rem(me + step, 4)
        frm = lax.rem(me + 4 - step, 4)
        piece = lax.dynamic_index_in_dim(parts, to, 0, keepdims=True)
        piece = lax.ppermute(piece, "x", [(i, (i + step) % 4) for i in range(4)])
        got = lax.dynamic_update_slice_in_dim(got, piece, frm, 0)
    return got


def per_device(
    inputs, factor_one, factor_two, w_input_gate, norm_gain, w_gate, w_up, w_down, grad_out
):
    tok_scale = 1.0 / math.sqrt(SEQL)
    chan_scale = 1.0 / math.sqrt(D)
    zh = lax.axis_index("zh")
    xi = lax.axis_index("x")

    payload = jnp.concatenate([w_gate, w_up, w_input_gate, w_down[:12], w_down[12:]], axis=1)
    payload = lax.ppermute(payload, ALL, shard_moves())
    gathered = lax.all_gather(payload, PLANE, axis=0, tiled=False)
    gathered = gathered.reshape(4, 2, 2, 2, 12, 2688).transpose(1, 2, 0, 3, 4, 5)
    upper_part = gathered[..., :1920].reshape(DB, 1920)
    wg, wu, win = upper_part[:, :768], upper_part[:, 768:1536], upper_part[:, 1536:]
    wd = gathered[..., 1920:].reshape(32, 12, 2, DB).transpose(0, 2, 1, 3).reshape(768, DB)
    gain = lax.dynamic_slice_in_dim(norm_gain, xi * DB, DB, 0)

    cot = exchange_x(grad_out.reshape(512, 4, DB).transpose(1, 0, 2)).reshape(2048, DB)
    halves = inputs.reshape(4, 2, 512, 192)
    mine = lax.dynamic_index_in_dim(halves, zh, 1, keepdims=False)
    other = lax.dynamic_index_in_dim(halves, 1 - zh, 1, keepdims=False)
    other = lax.ppermute(other, "zh", SWAP)
    input_mlp = jnp.where(
        zh == 0,
        jnp.concatenate([mine, other], axis=2),
        jnp.concatenate([other, mine], axis=2),
    ).reshape(2048, DB)

    def permuted(value):
        return value.reshape((4, 2, 2) + value.shape[1:]).swapaxes(0, 1).reshape(value.shape)

    f1 = permuted(factor_one)
    f1_half = lax.dynamic_slice_in_dim(f1, zh * 8, 8, 0)
    f2 = lax.dynamic_slice_in_dim(factor_two, zh * 8, 8, 0)
    f2 = f2.reshape(8, 16, 4, 2, 2, 16, 4, 2, 2).transpose(0, 1, 3, 2, 4, 5, 7, 6, 8)
    f2 = f2.reshape(8, 256, 256)

    token_blocks = permuted(inputs.reshape(16, 256, 192))
    first_local = jnp.einsum("iaj,ijc->iac", f1, token_blocks, preferred_element_type=F32)
    first_local = first_local.astype(BF).reshape(16, 32, 8, 192)
    piece = lax.all_to_all(first_local, PLANE, split_axis=1, concat_axis=0, tiled=False)
    first_cols = piece.reshape(16, 2, 16, 8, 192).transpose(0, 2, 3, 1, 4).reshape(256, 8, DB)
    second_cols = jnp.einsum("aki,iac->kac", f2, first_cols, preferred_element_type=F32)
    second_cols = second_cols.astype(BF).reshape(32, 8, 8, DB)
    second_mlp = lax.all_to_all(second_cols, PLANE, split_axis=0, concat_axis=1, tiled=False)
    second_mlp = second_mlp.reshape(2048, DB)

    pgate = jnp.dot(input_mlp, win, preferred_element_type=F32).astype(BF)
    pgate_f = pgate.astype(F32)
    input_f = input_mlp.astype(F32)
    silu_in = jax.nn.silu(input_f)
    second_f = second_mlp.astype(F32)
    resid = (input_f + second_f * pgate_f * silu_in).astype(BF)
    resid_f = resid.astype(F32)
    square = sum_over_x(jnp.sum(resid_f * resid_f, axis=1).reshape(16, 128)).reshape(2048, 1)
    rstd = lax.rsqrt(square * (1.0 / D) + 1e-06)
    normed = (resid_f * rstd * gain).astype(BF)
    gate = jnp.dot(normed, wg, preferred_element_type=F32)
    upper = jnp.dot(normed, wu, preferred_element_type=F32)
    sig = jax.nn.sigmoid(gate)
    hidden = (gate * sig * upper).astype(BF)
    down_out = jnp.dot(hidden, wd, preferred_element_type=F32)
    mixed = (resid_f + down_out).astype(BF)
    mixed_out = exchange_x(mixed.reshape(4, 512, DB)).transpose(1, 0, 2).reshape(512, D)
    g_hidden = jnp.einsum("te,he->th", cot, wd, preferred_element_type=F32)
    g_gate = (g_hidden * upper * sig * (1.0 + gate * (1.0 - sig))).astype(BF)
    g_up = (g_hidden * gate * sig).astype(BF)
    g_normed = jnp.einsum("th,dh->td", g_gate, wg, preferred_element_type=F32)
    g_normed = g_normed + jnp.einsum("th,dh->td", g_up, wu, preferred_element_type=F32)
    gain_term = jnp.sum(g_normed * resid_f * rstd, axis=0)
    scaled = g_normed * gain
    inner = sum_over_x(jnp.sum(scaled * resid_f, axis=1).reshape(16, 128)).reshape(2048, 1)
    cot_f = cot.astype(F32)
    g_resid = (cot_f + rstd * scaled - resid_f * rstd**3 * (inner * (1.0 / D))).astype(BF)
    resid_grad = g_resid.astype(F32)
    g_pgate = (resid_grad * second_f * silu_in).astype(BF)
    g_second = (resid_grad * pgate_f * silu_in).astype(BF)
    through_gate = jnp.einsum("te,de->td", g_pgate, win, preferred_element_type=F32)
    g_direct = (
        resid_grad * (1.0 + second_f * pgate_f * silu_slope(input_f)) + through_gate
    ).astype(BF)

    term_gate = jnp.einsum("td,th->dh", normed, g_gate, preferred_element_type=F32)
    term_up = jnp.einsum("td,th->dh", normed, g_up, preferred_element_type=F32)
    term_down = jnp.einsum("th,te->he", hidden, cot, preferred_element_type=F32)
    term_entry = jnp.einsum("td,te->de", input_mlp, g_pgate, preferred_element_type=F32)
    down2 = term_down.reshape(32, 2, 12, DB).transpose(0, 2, 1, 3).reshape(DB, 2 * DB)
    terms = jnp.concatenate([term_gate, term_up, term_entry, down2], axis=1).astype(BF)
    terms = terms.reshape(2, 2, 4, 2, 12, 2688).transpose(2, 0, 1, 3, 4, 5).reshape(32, 12, 2688)
    gain_row = jnp.pad(gain_term.astype(BF), (0, 2688 - DB)).reshape(1, 1, 2688)
    terms = jnp.concatenate([terms, jnp.broadcast_to(gain_row, (32, 1, 2688))], axis=1)
    by_core = terms.reshape(8, 2, 2, 13, 2688).swapaxes(0, 1).reshape(2, 16, 13, 2688)
    me = lax.axis_index("core")
    keep = lax.dynamic_index_in_dim(by_core, me, 0, keepdims=False)
    give = lax.dynamic_index_in_dim(by_core, 1 - me, 0, keepdims=False)
    pair = (keep.astype(F32) + lax.ppermute(give, "core", SWAP).astype(F32)).astype(BF)
    pair = lax.all_to_all(pair, ("zl", "y", "zh"), split_axis=0, concat_axis=0, tiled=True)
    summed = jnp.sum(pair.astype(F32), axis=0) * tok_scale
    back = [(there, here) for here, there in shard_moves()]
    own = lax.ppermute(summed[:12], ALL, back)
    grad_w_gate, grad_w_up = own[:, :768], own[:, 768:1536]
    grad_w_input_gate = own[:, 1536:1920]
    grad_w_down = jnp.concatenate([own[:, 1920:2304], own[:, 2304:]], axis=0)
    gain_here = summed[12, :DB].reshape(1, DB)
    grad_norm_gain = exchange_x(jnp.broadcast_to(gain_here, (4, DB))).reshape(D)

    piece = g_second.reshape(8, 32, 8, DB)
    piece = lax.all_to_all(piece, PLANE, split_axis=1, concat_axis=0, tiled=False)
    second_grad = piece.reshape(256, 8, DB)
    first_grad = jnp.einsum("aki,kac->iac", f2, second_grad, preferred_element_type=F32)
    first_grad = first_grad.astype(BF).reshape(32, 8, 8, DB)
    term_two = jnp.einsum("kac,iac->aki", second_grad, first_cols, preferred_element_type=F32)
    term_two = (term_two * chan_scale).astype(BF)
    term_two = term_two.reshape(8, 16, 2, 4, 2, 16, 2, 4, 2).transpose(0, 1, 3, 2, 4, 5, 7, 6, 8)
    term_two = term_two.reshape(8, 8, 32, 256)
    term_two = lax.all_to_all(term_two, CH, split_axis=1, concat_axis=0, tiled=False)
    grad_factor_two = jnp.sum(term_two.reshape(4, 16, 32, 256).astype(F32), axis=0)

    g_first = lax.all_to_all(first_grad, PLANE, split_axis=0, concat_axis=1, tiled=False)
    g_first = g_first.reshape(8, 256, DB)
    in_blocks = input_mlp.reshape(8, 256, DB)
    term_one = jnp.einsum("iac,ijc->iaj", g_first, in_blocks, preferred_element_type=F32)
    term_one = (term_one * chan_scale).astype(BF).reshape(8, 8, 32, 256)
    term_one = lax.all_to_all(term_one, CH, split_axis=1, concat_axis=0, tiled=False)
    grad_factor_one = jnp.sum(term_one.reshape(4, 2, 8, 32, 256).astype(F32), axis=0)
    grad_factor_one = grad_factor_one.reshape(2, 4, 2, 32, 256).swapaxes(0, 1).reshape(16, 32, 256)

    back_in = jnp.einsum("iaj,iac->ijc", f1_half, g_first, preferred_element_type=F32)
    total = (g_direct.astype(F32) + back_in.reshape(2048, DB)).astype(BF)
    total = total.reshape(4, 512, 2, 192)
    mine = lax.dynamic_index_in_dim(total, zh, 2, keepdims=False)
    other = lax.dynamic_index_in_dim(total, 1 - zh, 2, keepdims=False)
    other = lax.ppermute(other, "zh", SWAP)
    grad_inputs = jnp.where(
        zh == 0, jnp.stack([mine, other], axis=1), jnp.stack([other, mine], axis=1)
    ).reshape(4096, 192)
    return (
        mixed_out,
        grad_inputs,
        grad_factor_one,
        grad_factor_two,
        grad_w_input_gate,
        grad_norm_gain,
        grad_w_gate,
        grad_w_up,
        grad_w_down,
    )


def solution(mesh):
    fine = Mesh(mesh.devices.reshape(SIZES), ALL)
    return jax.shard_map(
        per_device,
        mesh=fine,
        in_specs=(
            P(SEQ, CH),
            P(SEQ, None, None),
            P(SEQ, None, None),
            P(ALL, None),
            P(),
            P(ALL, None),
            P(ALL, None),
            P(ALL, None),
            P(ALL, None),
        ),
        out_specs=(
            P(ALL, None),
            P(SEQ, CH),
            P(SEQ, CH, None),
            P(SEQ, CH, None),
            P(ALL, None),
            P(),
            P(ALL, None),
            P(ALL, None),
            P(ALL, None),
        ),
        check_vma=False,
    )
```

time: 2380 us -> 484 us (0.20)
  waiting for transfers between devices: 1090 us -> 43.1 us
  blocking collectives: 671 us -> 0 us
  starting transfers between devices: 298 us -> 87.2 us
  local copies, waits for them, and re-layouts: 198 us -> 229 us
    all_gather x4 -> x1, waiting for transfers between devices: 1060 us -> 0.01 us  [per_device(): gathered = lax.all_gather(payload, PLANE, axis=0, tiled=False)]
    unnamed x1 -> x0, blocking collectives: 451 us -> none
    unnamed x97 -> x0, starting transfers between devices: 277 us -> none
    all_to_all x5 -> x0, blocking collectives: 158 us -> none  [the longest x1 33.6 us: per_device(): lax.all_to_all(first_local, 'seq', split_axis=1, concat_axis=0, tiled=True)]
    unnamed x235 -> x47, local copies, waits for them, and re-layouts: 139 us -> 15.1 us
    psum x1 -> x0, blocking collectives: 62.8 us -> none  [per_device(): lax.psum(jnp.sum(g_normed * resid_f * rstd, axis=0), ('seq', 'ch'))]
    ppermute x0 -> x20, starting transfers between devices: none -> 43.2 us  [the longest x9 17.6 us: exchange_x(): piece = lax.ppermute(piece, 'x', [(i, (i + step) % 4) for i in range(4)])]
    another operation x0 -> x15, local copies, waits for them, and re-layouts: none -> 39.1 us  [the longest x1 14.4 us: per_device(): lax.all_to_all(term_two, CH, split_axis=1, concat_axis=0, tiled=False)]
  transfers between devices with their start and end apart: 106 -> 28, of which waited for: 6 -> 6; matrix products, arithmetic and copies ran while one was open for 29% -> 56% of each run, Pallas kernels for 0% -> 0%
where the time goes in v1:
time: 484 us; the launch traced here: 474 us
  local copies, waits for them, and re-layouts  229 us (47%)
  starting transfers between devices  87.2 us (18%)
  matrix products  69.3 us (14%)
  waiting for transfers between devices  43.1 us (9%)
  other arithmetic  30.4 us (6%)
  between operations  14.8 us (3%)
    ppermute x9, starting transfers between devices, exchange_x(): piece = lax.ppermute(piece, 'x', [(i, (i + step) % 4) for i in range(4)])  17.6 us
    reshape x1, local copies, waits for them, and re-layouts, per_device(): f2 = f2.reshape(8, 256, 256)  15.9 us
    ppermute x2, waiting for transfers between devices, per_device(): other = lax.ppermute(other, 'zh', SWAP)  15.9 us
    unnamed x47, local copies, waits for them, and re-layouts  15.1 us
    transpose x1, local copies, waits for them, and re-layouts, per_device(): term_two.reshape(8, 16, 2, 4, 2, 16, 2, 4, 2)  14.5 us
    transpose x1, local copies, waits for them, and re-layouts, per_device(): f2.reshape(8, 16, 4, 2, 2, 16, 4, 2, 2).transpose(0, 1, 3, 2, 4, 5, 7, 6, 8)  14.5 us
    another operation x1, local copies, waits for them, and re-layouts, per_device(): lax.all_to_all(term_two, CH, split_axis=1, concat_axis=0, tiled=False)  14.4 us
    all_to_all x1, waiting for transfers between devices, per_device(): lax.all_to_all(piece, PLANE, split_axis=1, concat_axis=0, tiled=False)  13.5 us
  transfers between devices with their start and end apart: 28, of which 6 were waited for; matrix products, arithmetic and copies ran while one was open for 56% of the time, Pallas kernels for 0%

profile of v1, /device:TPU:2, one launch (start us, length us, event | category | flops | bytes accessed | tf_op | source)
XLA Modules:
  0.0 474.1 jit_solution(17947802271868277475)
XLA Ops:
  11.0 5.1 %collective-permute-start.1 = (bf16[12,2688]{1,0:T(8,128)(2,1)S(1)}, bf16[12,2688]{1,0:T(8,128)(2,1)S(1)}, u32[]{:S(2)}, u32[]{:S(2)}) collective-permute-start(bf16[12,2688]{1,0:T(8,128)(2,1)S(1)} %slice_dynamic-update-slice_fusion), channel_id=1, source_target_pairs={{0,0},{1,1},{2,32},{3,33},{4,64},{5,65},{6,96},{7,97},{8,8},{9,9},... | collective-permute-start | bytes 193544 | tf_op jit(solution)/shard_map/ppermute | solution.py:77
  16.1 4.4 collective-permute-done.1
  28.0 4.1 copy.209
  42.8 8.7 %all-to-all-start = ((bf16[1,16,32,8,192]{4,3,1,0,2:T(8,128)(2,1)}), bf16[1,16,32,8,192]{4,3,1,0,2:T(8,128)(2,1)}, u32[]{:S(2)}, u32[]{:S(2)}) async-start(bf16[1,16,32,8,192]{4,3,1,0,2:T(8,128)(2,1)} %copy.213), calls=%async_computation | async-start | bytes 4194304 | tf_op jit(solution)/shard_map/all_to_all | solution.py:108
  51.6 11.4 %copy.215 = bf16[8,256,256]{0,2,1:T(8,128)(2,1)} copy(bf16[8,256,256]{2,1,0:T(8,128)(2,1)S(1)} %constant_dynamic-slice_fusion.11) | data formatting | bytes 2097152 | tf_op jit(solution)/shard_map/dynamic_slice | solution.py:101
  63.0 14.5 %copy.216 = bf16[8,16,2,4,2,16,2,4,2]{0,8,7,6,5,4,3,2,1:T(2,128)(2,1)} copy(bf16[8,16,2,4,2,16,2,4,2]{0,8,6,7,5,4,2,3,1:T(2,128)(2,1)} %bitcast.195) | data formatting | bytes 2097152 | tf_op jit(solution)/shard_map/transpose | solution.py:102
  77.5 15.9 %copy.233 = bf16[8,256,256]{1,2,0:T(8,128)(2,1)S(1)} copy(bf16[8,256,256]{0,2,1:T(8,128)(2,1)} %bitcast.196) | data formatting | bytes 2097152 | tf_op jit(solution)/shard_map/reshape | solution.py:103
  102.8 7.6 %all-to-all-start.1 = ((bf16[32,8,1,8,384]{4,1,3,2,0:T(8,128)(2,1)}), bf16[32,8,1,8,384]{4,1,3,2,0:T(8,128)(2,1)}, u32[]{:S(2)}, u32[]{:S(2)}) async-start(bf16[32,8,1,8,384]{4,1,3,2,0:T(8,128)(2,1)} %copy.218), calls=%async_computation.1 | async-start | bytes 3145728 | tf_op jit(solution)/shard_map/all_to_all | solution.py:112
  113.3 4.4 constant_dynamic-slice_fusion.13
  135.2 4.4 copy.267
  142.5 4.8 %collective-permute-done.8 = bf16[1,512,384]{2,1,0:T(8,128)(2,1)} collective-permute-done((bf16[1,512,384]{2,1,0:T(8,128)(2,1)}, bf16[1,512,384]{2,1,0:T(8,128)(2,1)}, u32[]{:S(2)}, u32[]{:S(2)}) %collective-permute-start.8) | collective-permute-done | bytes 393248 | tf_op jit(solution)/shard_map/ppermute | solution.py:63
  169.7 6.7 %fusion.18 = (f32[2048]{0:T(1024)S(1)}, bf16[2048,384]{1,0:T(8,128)(2,1)}, f32[2048,384]{1,0:T(8,128)}, bf16[2048,384]{1,0:T(8,128)(2,1)}) fusion(f32[1,8,32,1,8,384]{5,4,2,1,3,0:T(8,128)} %copy.219, bf16[2048,192]{1,0:T(8,128)(2,1)S(1)} %bitcast.200, bf16[2048,192]{1,0:T(8,128)(2,1)S(1)} %bitcast.208, pred[]{:T(512)S(6)} %eq.4, bf16[384,1920]{1,0:T(8,128)(2,1)} %reshape.206), kind=kOutput, calls=%fused_computation.39 | convolution fusion | flops 629143552 | bytes 13935616 | tf_op jit(solution)/shard_map/dot_general | solution.py:115
  196.9 5.6 %fusion = (bf16[768,2048]{1,0:T(8,128)(2,1)}, f32[2048,768]{0,1:T(8,128)}) fusion(f32[2048,768]{0,1:T(8,128)S(1)} %fusion.59, bf16[384,1920]{1,0:T(8,128)(2,1)S(1)} %copy-done.12, bf16[2048,384]{1,0:T(8,128)(2,1)S(1)} %copy-done.3, f32[384]{0:T(512)S(1)} %dynamic_slice.63, f32[2048]{0:T(1024)S(1)} %get-tuple-element.14), kind=kOutput, calls=%fused_computation.7 | convolution fusion | flops 1220542464 | bytes 17901568 | tf_op jit(solution)/shard_map/dot_general | solution.py:126
  202.5 6.2 %multiply_convert_fusion = (bf16[2048,768]{0,1:T(8,128)(2,1)S(1)}, bf16[2048,768]{0,1:T(8,128)(2,1)S(1)}) fusion(f32[2048,768]{0,1:T(8,128)S(1)} %fusion.59, f32[2048,768]{0,1:T(8,128)} %get-tuple-element.42, bf16[2048,384]{1,0:T(8,128)(2,1)} %bitcast.34, bf16[768,384]{1,0:T(8,128)(2,1)S(1)} %copy-done.16), kind=kOutput, calls=%fused_computation.13 | convolution fusion | flops 1228406784 | bytes 21037056 | tf_op jit(solution)/shard_map/te,he->th/dot_general | solution.py:132
  213.3 4.2 fusion.27
  221.4 6.1 %dot_general.79 = bf16[32,2,12,2048]{3,2,1,0:T(8,128)(2,1)} reshape(bf16[768,2048]{1,0:T(8,128)(2,1)} %get-tuple-element.41) | data formatting | bytes 6291456 | tf_op jit(solution)/shard_map/th,te->he/dot_general | solution.py:152
  227.5 4.7 fusion.50
  243.3 6.8 %fusion.7 = (bf16[2048,384]{1,0:T(8,128)(2,1)S(1)}, bf16[2048,384]{1,0:T(8,128)(2,1)}) fusion(f32[1,8,32,1,8,384]{5,4,2,1,3,0:T(8,128)} %copy.219, bf16[2048,192]{1,0:T(8,128)(2,1)S(1)} %bitcast.201, bf16[2048,192]{1,0:T(8,128)(2,1)S(1)} %bitcast.209, pred[]{:T(512)S(6)} %eq.4, f32[2048]{0:T(1024)S(1)} %multiply_bitcast_fusion, ...), kind=kLoop, calls=%fused_computation.28 | loop fusion | flops 21233664 | bytes 14181889 | tf_op jit(solution)/shard_map/convert_element_type | solution.py:143
  263.0 5.9 %constant_dynamic-slice_fusion.1 = (bf16[1,16,13,2688]{3,0,2,1:T(2,128)(2,1)}, bf16[1,16,13,2688]{3,0,2,1:T(2,128)(2,1)S(1)}) fusion(bf16[2,16,13,2688]{3,0,2,1:T(2,128)(2,1)S(1)} %bitcast.199, s32[]{:T(128)S(6)} %select_n.99, s32[]{:T(128)S(6)} %select_n.100), kind=kLoop, calls=%fused_computation.119 | loop fusion | bytes 4472840 | tf_op jit(solution)/shard_map/jit(dynamic_index_in_dim)/dynamic_slice | solution.py:161
  275.5 5.4 %all-to-all-start.2 = ((bf16[1,8,32,8,384]{4,3,1,0,2:T(8,128)(2,1)}), bf16[1,8,32,8,384]{4,3,1,0,2:T(8,128)(2,1)}, u32[]{:S(2)}, u32[]{:S(2)}) async-start(bf16[1,8,32,8,384]{4,3,1,0,2:T(8,128)(2,1)} %copy.231), calls=%async_computation.2 | async-start | bytes 3145728 | tf_op jit(solution)/shard_map/all_to_all | solution.py:175
  290.7 13.5 %all-to-all-done.2 = bf16[1,8,32,8,384]{4,3,1,0,2:T(8,128)(2,1)} async-done(((bf16[1,8,32,8,384]{4,3,1,0,2:T(8,128)(2,1)}), bf16[1,8,32,8,384]{4,3,1,0,2:T(8,128)(2,1)}, u32[]{:S(2)}, u32[]{:S(2)}) %all-to-all-start.2) | async-done | bytes 1572896 | tf_op jit(solution)/shard_map/all_to_all | solution.py:175
  304.2 4.4 all-to-all-start.6
  308.6 7.5 %fusion.21 = bf16[2048,384]{1,0:T(8,128)(2,1)S(1)} fusion(bf16[2048,384]{1,0:T(8,128)(2,1)} %get-tuple-element.16, bf16[768,384]{1,0:T(8,128)(2,1)} %reshape.209, f32[2048,768]{0,1:T(8,128)} %get-tuple-element.42, f32[2048,768]{0,1:T(8,128)} %copy-done.2), kind=kOutput, calls=%fused_computation.42 | convolution fusion | flops 1219756032 | bytes 16318464 | tf_op jit(solution)/shard_map/dot_general | solution.py:129
  331.4 5.5 %all-to-all-start.3 = ((bf16[32,8,1,8,384]{4,1,3,2,0:T(8,128)(2,1)}), bf16[32,8,1,8,384]{4,1,3,2,0:T(8,128)(2,1)}, u32[]{:S(2)}, u32[]{:S(2)}) async-start(bf16[32,8,1,8,384]{4,1,3,2,0:T(8,128)(2,1)} %copy.234), calls=%async_computation.3 | async-start | bytes 3145728 | tf_op jit(solution)/shard_map/all_to_all | solution.py:186
  355.0 11.6 %copy.247 = bf16[8,256,256]{0,2,1:T(8,128)(2,1)} copy(bf16[8,256,256]{2,1,0:T(8,128)(2,1)S(1)} %multiply_convert_fusion.6) | data formatting | bytes 2097152 | tf_op jit(solution)/shard_map/convert_element_type | solution.py:180
  366.7 14.5 %copy.248 = bf16[8,16,4,2,2,16,4,2,2]{0,8,7,6,5,4,3,2,1:T(2,128)(2,1)} copy(bf16[8,16,4,2,2,16,4,2,2]{0,8,6,7,5,4,2,3,1:T(2,128)(2,1)} %bitcast.197) | data formatting | bytes 2097152 | tf_op jit(solution)/shard_map/transpose | solution.py:181
  381.2 14.4 %copy.249 = bf16[1,8,8,32,256]{4,3,1,0,2:T(8,128)(2,1)} copy(bf16[1,8,8,32,256]{1,4,3,2,0:T(8,128)(2,1)} %bitcast.198) | data formatting | bytes 2097152 | tf_op jit(solution)/shard_map/broadcast_in_dim;reshape | solution.py:183
  395.6 5.0 %collective-permute-start.16 = (f32[12,2688]{1,0:T(8,128)S(1)}, f32[12,2688]{1,0:T(8,128)S(1)}, u32[]{:S(2)}, u32[]{:S(2)}) collective-permute-start(f32[12,2688]{1,0:T(8,128)S(1)} %bitcast.233), channel_id=1, source_target_pairs={{0,0},{1,1},{32,2},{33,3},{64,4},{65,5},{96,6},{97,7},{8,8},{9,9},... | collective-permute-start | bytes 387080 | tf_op jit(solution)/shard_map/ppermute | solution.py:167
  401.4 7.6 %all-to-all-start.5 = ((bf16[1,8,8,32,256]{4,3,1,0,2:T(8,128)(2,1)}), bf16[1,8,8,32,256]{4,3,1,0,2:T(8,128)(2,1)S(1)}, u32[]{:S(2)}, u32[]{:S(2)}) async-start(bf16[1,8,8,32,256]{4,3,1,0,2:T(8,128)(2,1)} %copy.249), calls=%async_computation.5 | async-start | bytes 2097152 | tf_op jit(solution)/shard_map/all_to_all | solution.py:183
  411.6 5.5 %fusion.28 = bf16[2048,384]{1,0:T(8,128)(2,1)} fusion(f32[8,256,384]{2,1,0:T(8,128)S(1)} %fusion.34, bf16[2048,384]{1,0:T(8,128)(2,1)S(1)} %copy-done.14, f32[2048,384]{1,0:T(8,128)} %get-tuple-element.19, bf16[2048,384]{1,0:T(8,128)(2,1)S(1)} %copy-done.8, bf16[384,1920]{1,0:T(8,128)(2,1)} %reshape.206, bf16[2048,192]{1,0:T(8,128)(2,1)S(1)} %bitcast.205, ...), kind=kOutput, calls=%fused_computation.51 | convolution fusion | flops 624427008 | bytes 12877825 | tf_op jit(solution)/shard_map/te,de->td/dot_general | solution.py:145
  431.7 4.8 %all-to-all-start.4 = ((bf16[1,8,8,32,256]{4,3,1,0,2:T(8,128)(2,1)}), bf16[1,8,8,32,256]{4,3,1,0,2:T(8,128)(2,1)}, u32[]{:S(2)}, u32[]{:S(2)}) async-start(bf16[1,8,8,32,256]{4,3,1,0,2:T(8,128)(2,1)} %copy.243), calls=%async_computation.4 | async-start | bytes 2097152 | tf_op jit(solution)/shard_map/all_to_all | solution.py:191
  439.9 15.9 %collective-permute-done.14 = bf16[4,512,192]{1,2,0:T(8,128)(2,1)} collective-permute-done((bf16[4,512,192]{1,2,0:T(8,128)(2,1)}, bf16[4,512,192]{1,2,0:T(8,128)(2,1)}, u32[]{:S(2)}, u32[]{:S(2)}) %collective-permute-start.14) | collective-permute-done | bytes 786464 | tf_op jit(solution)/shard_map/ppermute | solution.py:200
  (188 shorter events, 212.1 us)
Async XLA Ops:
  7.2 44.3 %copy-start = (bf16[16,256,256]{2,1,0:T(8,128)(2,1)S(1)}, bf16[16,256,256]{2,1,0:T(8,128)(2,1)}, u32[]{:S(2)}) copy-start(bf16[16,256,256]{2,1,0:T(8,128)(2,1)} %param.11) | copy-start | bytes 6291460
  7.2 151.4 %all-gather.4.cloned.1.call-start = ((), (), s32[]{:S(2)}) async-start(), calls=%async_computation.7 | async-start | bytes 2838528 | tf_op jit(solution)/shard_map/all_gather | solution.py:78
  11.0 9.5 %collective-permute-start.1 = (bf16[12,2688]{1,0:T(8,128)(2,1)S(1)}, bf16[12,2688]{1,0:T(8,128)(2,1)S(1)}, u32[]{:S(2)}, u32[]{:S(2)}) collective-permute-start(bf16[12,2688]{1,0:T(8,128)(2,1)S(1)} %slice_dynamic-update-slice_fusion), channel_id=1, source_target_pairs={{0,0},{1,1},{2,32},{3,33},{4,64},{5,65},{6,96},{7,97},{8,8},{9,9},... | collective-permute-start | bytes 193544 | tf_op jit(solution)/shard_map/ppermute | solution.py:77
  42.8 50.7 %all-to-all-start = ((bf16[1,16,32,8,192]{4,3,1,0,2:T(8,128)(2,1)}), bf16[1,16,32,8,192]{4,3,1,0,2:T(8,128)(2,1)}, u32[]{:S(2)}, u32[]{:S(2)}) async-start(bf16[1,16,32,8,192]{4,3,1,0,2:T(8,128)(2,1)} %copy.213), calls=%async_computation | async-start | bytes 4194304 | tf_op jit(solution)/shard_map/all_to_all | solution.py:108
  102.8 51.8 %all-to-all-start.1 = ((bf16[32,8,1,8,384]{4,1,3,2,0:T(8,128)(2,1)}), bf16[32,8,1,8,384]{4,1,3,2,0:T(8,128)(2,1)}, u32[]{:S(2)}, u32[]{:S(2)}) async-start(bf16[32,8,1,8,384]{4,1,3,2,0:T(8,128)(2,1)} %copy.218), calls=%async_computation.1 | async-start | bytes 3145728 | tf_op jit(solution)/shard_map/all_to_all | solution.py:112
  119.0 34.2 %collective-permute-start = (bf16[4,512,192]{1,2,0:T(8,128)(2,1)}, bf16[4,512,192]{1,2,0:T(8,128)(2,1)}, u32[]{:S(2)}, u32[]{:S(2)}) collective-permute-start(bf16[4,512,192]{1,2,0:T(8,128)(2,1)} %bitcast.191), channel_id=1, source_target_pairs={{0,1},{1,0},{2,3},{3,2},{4,5},{5,4},{6,7},{7,6},{8,9},{9,8},{10,11... | collective-permute-start | bytes 2359304 | tf_op jit(solution)/shard_map/ppermute | solution.py:89
  127.1 20.2 %collective-permute-start.8 = (bf16[1,512,384]{2,1,0:T(8,128)(2,1)}, bf16[1,512,384]{2,1,0:T(8,128)(2,1)}, u32[]{:S(2)}, u32[]{:S(2)}) collective-permute-start(bf16[1,512,384]{2,1,0:T(8,128)(2,1)} %bitcast.31), channel_id=1, source_target_pairs={{0,2},{2,4},{4,6},{6,0},{1,3},{3,5},{5,7},{7,1},{8,10},{10,12},{12... | collective-permute-start | bytes 1179656 | tf_op jit(solution)/shard_map/ppermute | solution.py:63
  132.1 19.3 %collective-permute-start.9 = (bf16[1,512,384]{2,1,0:T(8,128)(2,1)}, bf16[1,512,384]{2,1,0:T(8,128)(2,1)}, u32[]{:S(2)}, u32[]{:S(2)}) collective-permute-start(bf16[1,512,384]{2,1,0:T(8,128)(2,1)} %bitcast.32), channel_id=1, source_target_pairs={{0,6},{2,0},{4,2},{6,4},{1,7},{3,1},{5,3},{7,5},{8,14},{10,8},{12,... | collective-permute-start | bytes 1179656 | tf_op jit(solution)/shard_map/ppermute | solution.py:63
  133.0 48.6 %collective-permute-start.10 = (bf16[1,512,384]{2,1,0:T(8,128)(2,1)}, bf16[1,512,384]{2,1,0:T(8,128)(2,1)S(1)}, u32[]{:S(2)}, u32[]{:S(2)}) collective-permute-start(bf16[1,512,384]{2,1,0:T(8,128)(2,1)} %bitcast.33), channel_id=1, source_target_pairs={{0,4},{2,6},{4,0},{6,2},{1,5},{3,7},{5,1},{7,3},{8,12},{10,14},{12... | collective-permute-start | bytes 1179656 | tf_op jit(solution)/shard_map/ppermute | solution.py:63
  176.4 16.0 %collective-permute-start.3 = (f32[16,128]{1,0:T(8,128)S(1)}, f32[16,128]{1,0:T(8,128)}, u32[]{:S(2)}, u32[]{:S(2)}) collective-permute-start(f32[16,128]{1,0:T(8,128)S(1)} %bitcast.238), channel_id=1, source_target_pairs={{0,6},{2,0},{4,2},{6,4},{1,7},{3,1},{5,3},{7,5},{8,14},{10,8},{12,... | collective-permute-start | bytes 24584 | tf_op jit(solution)/shard_map/ppermute | solution.py:50
  176.4 16.0 %collective-permute-start.4 = (f32[16,128]{1,0:T(8,128)S(1)}, f32[16,128]{1,0:T(8,128)}, u32[]{:S(2)}, u32[]{:S(2)}) collective-permute-start(f32[16,128]{1,0:T(8,128)S(1)} %bitcast.239), channel_id=1, source_target_pairs={{0,4},{2,6},{4,0},{6,2},{1,5},{3,7},{5,1},{7,3},{8,12},{10,14},{12... | collective-permute-start | bytes 24584 | tf_op jit(solution)/shard_map/ppermute | solution.py:50
  178.6 13.8 %collective-permute-start.2 = (f32[16,128]{1,0:T(8,128)S(1)}, f32[16,128]{1,0:T(8,128)}, u32[]{:S(2)}, u32[]{:S(2)}) collective-permute-start(f32[16,128]{1,0:T(8,128)S(1)} %bitcast.240), channel_id=1, source_target_pairs={{0,2},{2,4},{4,6},{6,0},{1,3},{3,5},{5,7},{7,1},{8,10},{10,12},{12... | collective-permute-start | bytes 24584 | tf_op jit(solution)/shard_map/ppermute | solution.py:50
  196.9 5.6 %copy-start.2 = (f32[2048,768]{0,1:T(8,128)}, f32[2048,768]{0,1:T(8,128)S(1)}, u32[]{:S(2)}) copy-start(f32[2048,768]{0,1:T(8,128)S(1)} %fusion.59) | copy-start | bytes 18874372
  217.5 25.7 %collective-permute-start.12 = (f32[16,128]{1,0:T(8,128)S(1)}, f32[16,128]{1,0:T(8,128)S(1)}, u32[]{:S(2)}, u32[]{:S(2)}) collective-permute-start(f32[16,128]{1,0:T(8,128)S(1)} %bitcast.235), channel_id=1, source_target_pairs={{0,6},{2,0},{4,2},{6,4},{1,7},{3,1},{5,3},{7,5},{8,14},{10,8},{12,... | collective-permute-start | bytes 24584 | tf_op jit(solution)/shard_map/ppermute | solution.py:50
  217.5 25.7 %collective-permute-start.13 = (f32[16,128]{1,0:T(8,128)S(1)}, f32[16,128]{1,0:T(8,128)S(1)}, u32[]{:S(2)}, u32[]{:S(2)}) collective-permute-start(f32[16,128]{1,0:T(8,128)S(1)} %bitcast.236), channel_id=1, source_target_pairs={{0,4},{2,6},{4,0},{6,2},{1,5},{3,7},{5,1},{7,3},{8,12},{10,14},{12... | collective-permute-start | bytes 24584 | tf_op jit(solution)/shard_map/ppermute | solution.py:50
  219.0 24.3 %collective-permute-start.11 = (f32[16,128]{1,0:T(8,128)S(1)}, f32[16,128]{1,0:T(8,128)S(1)}, u32[]{:S(2)}, u32[]{:S(2)}) collective-permute-start(f32[16,128]{1,0:T(8,128)S(1)} %bitcast.237), channel_id=1, source_target_pairs={{0,2},{2,4},{4,6},{6,0},{1,3},{3,5},{5,7},{7,1},{8,10},{10,12},{12... | collective-permute-start | bytes 24584 | tf_op jit(solution)/shard_map/ppermute | solution.py:50
  270.1 17.1 %collective-permute-start.15 = (bf16[16,13,2688]{2,0,1:T(8,128)(2,1)}, bf16[16,13,2688]{2,0,1:T(8,128)(2,1)}, u32[]{:S(2)}, u32[]{:S(2)}) collective-permute-start(bf16[16,13,2688]{2,0,1:T(8,128)(2,1)} %bitcast.190), channel_id=1, source_target_pairs={{0,8},{8,0},{1,9},{9,1},{2,10},{10,2},{3,11},{11,3},{4,12},{12,4},... | collective-permute-start | bytes 3354632 | tf_op jit(solution)/shard_map/ppermute | solution.py:163
  275.5 28.7 %all-to-all-start.2 = ((bf16[1,8,32,8,384]{4,3,1,0,2:T(8,128)(2,1)}), bf16[1,8,32,8,384]{4,3,1,0,2:T(8,128)(2,1)}, u32[]{:S(2)}, u32[]{:S(2)}) async-start(bf16[1,8,32,8,384]{4,3,1,0,2:T(8,128)(2,1)} %copy.231), calls=%async_computation.2 | async-start | bytes 3145728 | tf_op jit(solution)/shard_map/all_to_all | solution.py:175
  304.2 27.2 %all-to-all-start.6 = ((bf16[16,13,2688]{2,1,0:T(8,128)(2,1)}), bf16[16,13,2688]{2,1,0:T(8,128)(2,1)}, u32[]{:S(2)}, u32[]{:S(2)}) async-start(bf16[16,13,2688]{2,1,0:T(8,128)(2,1)} %copy.258), calls=%async_computation.6 | async-start | bytes 2752512 | tf_op jit(solution)/shard_map/all_to_all | solution.py:164
  318.7 20.1 %collective-permute-start.6 = (bf16[1,512,384]{2,1,0:T(8,128)(2,1)}, bf16[1,512,384]{2,1,0:T(8,128)(2,1)S(1)}, u32[]{:S(2)}, u32[]{:S(2)}) collective-permute-start(bf16[1,512,384]{2,1,0:T(8,128)(2,1)} %get-tuple-element.29), channel_id=1, source_target_pairs={{0,6},{2,0},{4,2},{6,4},{1,7},{3,1},{5,3},{7,5},{8,14},{10,8},{12,... | collective-permute-start | bytes 1179656 | tf_op jit(solution)/shard_map/ppermute | solution.py:63
  318.8 18.1 %collective-permute-start.5 = (bf16[1,512,384]{2,1,0:T(8,128)(2,1)}, bf16[1,512,384]{2,1,0:T(8,128)(2,1)}, u32[]{:S(2)}, u32[]{:S(2)}) collective-permute-start(bf16[1,512,384]{2,1,0:T(8,128)(2,1)} %get-tuple-element.30), channel_id=1, source_target_pairs={{0,2},{2,4},{4,6},{6,0},{1,3},{3,5},{5,7},{7,1},{8,10},{10,12},{12... | collective-permute-start | bytes 1179656 | tf_op jit(solution)/shard_map/ppermute | solution.py:63
  322.2 17.4 %collective-permute-start.7 = (bf16[1,512,384]{2,1,0:T(8,128)(2,1)}, bf16[1,512,384]{2,1,0:T(8,128)(2,1)}, u32[]{:S(2)}, u32[]{:S(2)}) collective-permute-start(bf16[1,512,384]{2,1,0:T(8,128)(2,1)} %get-tuple-element.28), channel_id=1, source_target_pairs={{0,4},{2,6},{4,0},{6,2},{1,5},{3,7},{5,1},{7,3},{8,12},{10,14},{12... | collective-permute-start | bytes 1179656 | tf_op jit(solution)/shard_map/ppermute | solution.py:63
  331.4 70.0 %all-to-all-start.3 = ((bf16[32,8,1,8,384]{4,1,3,2,0:T(8,128)(2,1)}), bf16[32,8,1,8,384]{4,1,3,2,0:T(8,128)(2,1)}, u32[]{:S(2)}, u32[]{:S(2)}) async-start(bf16[32,8,1,8,384]{4,1,3,2,0:T(8,128)(2,1)} %copy.234), calls=%async_computation.3 | async-start | bytes 3145728 | tf_op jit(solution)/shard_map/all_to_all | solution.py:186
  341.3 11.5 %copy-start.6 = (bf16[256,8,384]{2,0,1:T(8,128)(2,1)S(1)}, bf16[256,8,384]{2,0,1:T(8,128)(2,1)}, u32[]{:S(2)}) copy-start(bf16[256,8,384]{2,0,1:T(8,128)(2,1)} %reshape.202) | copy-start | bytes 4718596
  345.8 54.9 %collective-permute-start.19 = (f32[1,384]{1,0:T(1,128)S(1)}, f32[1,384]{1,0:T(1,128)S(1)}, u32[]{:S(2)}, u32[]{:S(2)}) collective-permute-start(f32[1,384]{1,0:T(1,128)S(1)} %slice.63), channel_id=1, source_target_pairs={{0,4},{2,6},{4,0},{6,2},{1,5},{3,7},{5,1},{7,3},{8,12},{10,14},{12... | collective-permute-start | bytes 4616 | tf_op jit(solution)/shard_map/ppermute | solution.py:63
  349.8 50.9 %collective-permute-start.18 = (f32[1,384]{1,0:T(1,128)S(1)}, f32[1,384]{1,0:T(1,128)S(1)}, u32[]{:S(2)}, u32[]{:S(2)}) collective-permute-start(f32[1,384]{1,0:T(1,128)S(1)} %slice.63), channel_id=1, source_target_pairs={{0,6},{2,0},{4,2},{6,4},{1,7},{3,1},{5,3},{7,5},{8,14},{10,8},{12,... | collective-permute-start | bytes 4616 | tf_op jit(solution)/shard_map/ppermute | solution.py:63
  351.5 49.1 %collective-permute-start.17 = (f32[1,384]{1,0:T(1,128)S(1)}, f32[1,384]{1,0:T(1,128)S(1)}, u32[]{:S(2)}, u32[]{:S(2)}) collective-permute-start(f32[1,384]{1,0:T(1,128)S(1)} %slice.63), channel_id=1, source_target_pairs={{0,2},{2,4},{4,6},{6,0},{1,3},{3,5},{5,7},{7,1},{8,10},{10,12},{12... | collective-permute-start | bytes 4616 | tf_op jit(solution)/shard_map/ppermute | solution.py:63
  395.6 40.9 %collective-permute-start.16 = (f32[12,2688]{1,0:T(8,128)S(1)}, f32[12,2688]{1,0:T(8,128)S(1)}, u32[]{:S(2)}, u32[]{:S(2)}) collective-permute-start(f32[12,2688]{1,0:T(8,128)S(1)} %bitcast.233), channel_id=1, source_target_pairs={{0,0},{1,1},{32,2},{33,3},{64,4},{65,5},{96,6},{97,7},{8,8},{9,9},... | collective-permute-start | bytes 387080 | tf_op jit(solution)/shard_map/ppermute | solution.py:167
  401.4 30.3 %all-to-all-start.5 = ((bf16[1,8,8,32,256]{4,3,1,0,2:T(8,128)(2,1)}), bf16[1,8,8,32,256]{4,3,1,0,2:T(8,128)(2,1)S(1)}, u32[]{:S(2)}, u32[]{:S(2)}) async-start(bf16[1,8,8,32,256]{4,3,1,0,2:T(8,128)(2,1)} %copy.249), calls=%async_computation.5 | async-start | bytes 2097152 | tf_op jit(solution)/shard_map/all_to_all | solution.py:183
  428.7 27.1 %collective-permute-start.14 = (bf16[4,512,192]{1,2,0:T(8,128)(2,1)}, bf16[4,512,192]{1,2,0:T(8,128)(2,1)}, u32[]{:S(2)}, u32[]{:S(2)}) collective-permute-start(bf16[4,512,192]{1,2,0:T(8,128)(2,1)} %bitcast.192), channel_id=1, source_target_pairs={{0,1},{1,0},{2,3},{3,2},{4,5},{5,4},{6,7},{7,6},{8,9},{9,8},{10,11... | collective-permute-start | bytes 2359304 | tf_op jit(solution)/shard_map/ppermute | solution.py:200
  431.7 29.8 %all-to-all-start.4 = ((bf16[1,8,8,32,256]{4,3,1,0,2:T(8,128)(2,1)}), bf16[1,8,8,32,256]{4,3,1,0,2:T(8,128)(2,1)}, u32[]{:S(2)}, u32[]{:S(2)}) async-start(bf16[1,8,8,32,256]{4,3,1,0,2:T(8,128)(2,1)} %copy.243), calls=%async_computation.4 | async-start | bytes 2097152 | tf_op jit(solution)/shard_map/all_to_all | solution.py:191
  461.4 5.6 %copy-start.1 = (bf16[16,256,256]{2,1,0:T(8,128)(2,1)S(1)}, bf16[16,256,256]{2,1,0:T(8,128)(2,1)}, u32[]{:S(2)}) copy-start(bf16[16,256,256]{2,1,0:T(8,128)(2,1)} %param.11) | copy-start | bytes 6291460
  (16 other events, 48.2 us)
Sparse Core Ops, SparseCore 0:
  21.3 114.6 all-gather.3

commit v2 on v1

v2 whole, which is shorter than its diff:
```python
import math

import jax
import jax.numpy as jnp
from jax import lax
from jax.experimental import pallas as pl
from jax.experimental.pallas import tpu as pltpu
from jax.sharding import Mesh
from jax.sharding import PartitionSpec as P

D = 1536
NBLK = 4
SEQL = 65536
DB = D // NBLK
BF = jnp.bfloat16
F32 = jnp.float32

SEQ = ("zl", "y", "core")
CH = ("x", "zh")
ALL = SEQ + CH
SIZES = (2, 4, 2, 4, 2)
PLANE = SEQ + ("zh",)


def index_of(zl, y, k, x, zh):
    return (((zl * 4 + y) * 2 + k) * 4 + x) * 2 + zh


def shard_moves():
    moves = []
    for zl in range(2):
        for y in range(4):
            for k in range(2):
                for x in range(4):
                    for zh in range(2):
                        there = index_of(k, x, y % 2, zl * 2 + y // 2, zh)
                        moves.append((index_of(zl, y, k, x, zh), there))
    return moves


SWAP = [(0, 1), (1, 0)]


def call(body, grid, ins, outs, shapes, cost, scratch=()):
    return pl.pallas_call(
        body,
        grid_spec=pltpu.PrefetchScalarGridSpec(
            num_scalar_prefetch=1,
            grid=grid,
            in_specs=ins,
            out_specs=outs,
            scratch_shapes=list(scratch),
        ),
        out_shape=shapes,
        compiler_params=pltpu.CompilerParams(
            dimension_semantics=("arbitrary",) * len(grid), vmem_limit_bytes=56 * 1024 * 1024
        ),
        cost_estimate=pl.CostEstimate(flops=cost[0], bytes_accessed=cost[1], transcendentals=0),
    )


def whole(*shape):
    return pl.BlockSpec(shape, lambda t, s: (0,) * len(shape))


def rows(width, height=512):
    return pl.BlockSpec((height, width), lambda t, s: (t, 0))


def lead(*shape):
    return pl.BlockSpec((1,) + shape, lambda t, s: (t,) + (0,) * len(shape))


PIECES = pl.BlockSpec((32, 2, 8, DB), lambda t, s: (0, t, 0, 0))


def read_pieces(ref):
    return jnp.concatenate(
        [ref[:, r].astype(F32).reshape(256, DB) for r in range(2)], axis=0
    )


def row_sums(value):
    ones = jnp.ones((8, DB), BF)
    total = jnp.zeros((8, value.shape[0]), F32)
    for _ in range(3):
        part = value.astype(BF)
        total = total + lax.dot_general(
            ones, part, (((1,), (1,)), ((), ())), preferred_element_type=F32
        )
        value = value - part.astype(F32)
    return total


def as_column(row):
    turned = jnp.transpose(jnp.broadcast_to(row, (128, row.shape[1])))
    return jnp.concatenate([turned] * (DB // 128), axis=1)


def dot(a, b):
    return jnp.dot(a, b, preferred_element_type=F32)


def dot_t(a, b):
    return lax.dot_general(a, b, (((1,), (1,)), ((), ())), preferred_element_type=F32)


def first_kernel(_, f1_ref, in_ref, out_ref):
    results = [
        dot(f1_ref[r], in_ref[r * 256 : (r + 1) * 256]).reshape(32, 8, 192) for r in range(2)
    ]
    out_ref[:, 0] = jnp.concatenate(results, axis=2).astype(BF)


def give_kernel(_, in_ref, out_ref):
    value = in_ref[0]
    out_ref[...] = jnp.concatenate([value[:256], value[256:]], axis=1)


def put_rows(refs, row, value):
    for j, ref in enumerate(refs):
        ref[row : row + value.shape[0], :] = value[:, j * 128 : (j + 1) * 128]


def put_position(refs, a, value):
    for j, ref in enumerate(refs):
        ref[pl.ds(a, 256, stride=8), :] = value[:, j * 128 : (j + 1) * 128]


def take_position(refs, a):
    parts = [ref[pl.ds(a, 256, stride=8), :] for ref in refs]
    return jnp.concatenate(parts, axis=1).astype(BF)


def second_kernel(_, piece_ref, f2_ref, out_ref, first_ref, *scratch):
    cols, result = scratch[:3], scratch[3:]
    for s in range(16):
        for pair in range(8):
            low, high = (piece_ref[2 * s + h, pair].astype(F32) for h in range(2))
            row = (s * 16 + pair * 2) * 8
            put_rows(cols, row, jnp.concatenate([low[:, :192], high[:, :192]], axis=1))
            put_rows(cols, row + 8, jnp.concatenate([low[:, 192:], high[:, 192:]], axis=1))
    for a in range(8):
        first = take_position(cols, a)
        first_ref[a] = first
        put_position(result, a, dot(f2_ref[a], first))
    write_blocks(result, out_ref)


def first_grad_kernel(_, piece_ref, f2_ref, out_ref, grad_ref, *scratch):
    cols, result = scratch[:3], scratch[3:]
    for dev in range(32):
        s, h = dev // 2, dev % 2
        for x in range(4):
            row = (s * 16 + x * 4 + h * 2) * 8
            put_rows(cols, row, piece_ref[dev, 2 * x : 2 * x + 2].astype(F32).reshape(16, DB))
    for a in range(8):
        grad = take_position(cols, a)
        grad_ref[a] = grad
        put_position(result, a, lax.dot_general(
            f2_ref[a], grad, (((0,), (0,)), ((), ())), preferred_element_type=F32
        ))
    write_blocks(result, out_ref)


def write_blocks(result, out_ref):
    for dev in range(32):
        s, h = dev // 2, dev % 2
        for x in range(4):
            row = (s * 16 + x * 4 + h * 2) * 8
            value = jnp.concatenate([ref[row : row + 16, :] for ref in result], axis=1)
            out_ref[dev, 2 * x : 2 * x + 2] = value.reshape(2, 8, DB).astype(BF)


def gating_kernel(zh_ref, own_ref, got_ref, second_ref, win_ref, in_ref, resid_ref, pgate_ref, sum_ref):
    zh = zh_ref[0]
    own = own_ref[0]
    got = jnp.concatenate([got_ref[:, :192], got_ref[:, 192:]], axis=0)
    first_half = jnp.where(zh == 0, own, got)
    second_half = jnp.where(zh == 0, got, own)
    value = jnp.concatenate([first_half, second_half], axis=1)
    in_ref[...] = value
    pgate = dot(value, win_ref[...]).astype(BF)
    pgate_ref[...] = pgate
    value_f = value.astype(F32)
    silu_in = value_f * jax.nn.sigmoid(value_f)
    resid = (value_f + read_pieces(second_ref) * pgate.astype(F32) * silu_in).astype(BF)
    resid_ref[...] = resid
    resid_f = resid.astype(F32)
    sum_ref[0] = row_sums(resid_f * resid_f)


def mlp_kernel(
    _, resid_ref, cot_ref, square_ref, gain_ref, wg_ref, wu_ref, wd_ref,
    mixed_ref, normed_ref, hidden_ref, grads_ref, gnormed_ref, inner_ref, gain_out_ref,
):
    resid_f = resid_ref[...].astype(F32)
    rstd = as_column(lax.rsqrt(square_ref[0] * (1.0 / D) + 1e-06))
    gain = gain_ref[...]
    scaled_resid = resid_f * rstd
    normed = (scaled_resid * gain).astype(BF)
    normed_ref[...] = normed
    gate = dot(normed, wg_ref[...])
    upper = dot(normed, wu_ref[...])
    g_hidden = dot_t(cot_ref[0], wd_ref[...])
    sig = jax.nn.sigmoid(gate)
    act = gate * sig
    hidden = (act * upper).astype(BF)
    hidden_ref[...] = hidden
    g_gate = (g_hidden * upper * sig * (1.0 + gate * (1.0 - sig))).astype(BF)
    g_up = (g_hidden * act).astype(BF)
    grads_ref[:, :768] = g_gate
    grads_ref[:, 768:] = g_up
    mixed_ref[0] = (resid_f + dot(hidden, wd_ref[...])).astype(BF)
    g_normed = dot_t(g_gate, wg_ref[...]) + dot_t(g_up, wu_ref[...])
    gnormed_ref[...] = g_normed
    inner_ref[0] = row_sums(g_normed * gain * resid_f)
    term = jnp.sum((g_normed * scaled_resid).reshape(64, 8, DB), axis=0)

    @pl.when(pl.program_id(0) == 0)
    def _():
        gain_out_ref[...] = jnp.zeros_like(gain_out_ref)

    gain_out_ref[...] += term


def resid_grad_kernel(
    _, resid_ref, cot_ref, square_ref, inner_ref, gain_ref, gnormed_ref, in_ref, pgate_ref,
    g_resid_ref, g_second_ref,
):
    rstd_row = lax.rsqrt(square_ref[0] * (1.0 / D) + 1e-06)
    rstd = as_column(rstd_row)
    factor = as_column(rstd_row * rstd_row * rstd_row * (inner_ref[0] * (1.0 / D)))
    scaled = gnormed_ref[...] * gain_ref[...]
    g_resid = (
        cot_ref[0].astype(F32) + rstd * scaled - resid_ref[...].astype(F32) * factor
    ).astype(BF)
    g_resid_ref[...] = g_resid
    value = in_ref[...].astype(F32)
    silu_in = value * jax.nn.sigmoid(value)
    g_second = (g_resid.astype(F32) * pgate_ref[...].astype(F32) * silu_in).astype(BF)
    for r in range(2):
        g_second_ref[:, r] = g_second[r * 256 : (r + 1) * 256].reshape(32, 8, DB)


def direct_kernel(_, g_resid_ref, in_ref, second_ref, pgate_ref, win_ref, g_direct_ref, term_ref):
    resid_grad = g_resid_ref[...].astype(F32)
    value = in_ref[...].astype(F32)
    sig = jax.nn.sigmoid(value)
    second = read_pieces(second_ref)
    g_pgate = (resid_grad * second * (value * sig)).astype(BF)
    slope = sig * (1.0 + value * (1.0 - sig))
    through = dot_t(g_pgate, win_ref[...])
    g_direct_ref[...] = (
        resid_grad * (1.0 + second * pgate_ref[...].astype(F32) * slope) + through
    ).astype(BF)
    term = lax.dot_general(
        in_ref[...], g_pgate, (((0,), (0,)), ((), ())), preferred_element_type=F32
    )

    @pl.when(pl.program_id(0) == 0)
    def _():
        term_ref[...] = jnp.zeros_like(term_ref)

    term_ref[...] += term


def back_kernel(zh_ref, g_first_ref, in_ref, f1_ref, direct_ref, term_ref, own_ref, give_ref):
    zh = zh_ref[0]
    gives = []
    for r in range(2):
        here = slice(r * 256, (r + 1) * 256)
        g_first = g_first_ref[:, r].reshape(256, DB)
        term = dot_t(g_first, in_ref[here]) * (1.0 / math.sqrt(D))
        term_ref[:, r] = term.astype(BF).reshape(8, 32, 256)
        back = lax.dot_general(
            f1_ref[0, r], g_first, (((0,), (0,)), ((), ())), preferred_element_type=F32
        )
        total = direct_ref[here].astype(F32) + back
        low, high = total[:, :192], total[:, 192:]
        own_ref[here] = jnp.where(zh == 0, low, high).astype(BF)
        gives.append(jnp.where(zh == 0, high, low))
    give_ref[...] = jnp.concatenate(gives, axis=1).astype(BF)


def join_kernel(zh_ref, own_ref, got_ref, out_ref):
    zh = zh_ref[0]
    own = own_ref[...]
    got = jnp.concatenate([got_ref[:, :192], got_ref[:, 192:]], axis=0)
    out_ref[:512] = jnp.where(zh == 0, own, got)
    out_ref[512:] = jnp.where(zh == 0, got, own)


def factor_sum_kernel(_, term_ref, out_ref):
    for h in range(2):
        total = term_ref[h].astype(F32)
        for x in range(1, 4):
            total = total + term_ref[2 * x + h].astype(F32)
        out_ref[0, h] = total


def factor_sum_two_kernel(_, term_ref, out_ref):
    for h in range(2):
        total = term_ref[h].astype(F32)
        for x in range(1, 4):
            total = total + term_ref[2 * x + h].astype(F32)
        out_ref[h] = total


def around_x(value):
    steps = [lax.ppermute(value, "x", [(i, (i + step) % 4) for i in range(4)]) for step in (1, 3, 2)]
    return [value, steps[0], steps[2], steps[1]]


def per_device(
    inputs, factor_one, factor_two, w_input_gate, norm_gain, w_gate, w_up, w_down, grad_out
):
    tok_scale = 1.0 / math.sqrt(SEQL)
    chan_scale = 1.0 / math.sqrt(D)
    zh = lax.axis_index("zh")
    xi = lax.axis_index("x")
    core = lax.axis_index("core")
    zh_arg = zh.reshape(1).astype(jnp.int32)
    bf = lambda *shape: jax.ShapeDtypeStruct(shape, BF)
    f32 = lambda *shape: jax.ShapeDtypeStruct(shape, F32)

    first_local = call(
        first_kernel, (8,),
        [pl.BlockSpec((2, 256, 256), lambda t, s: (t, 0, 0)), rows(192)],
        pl.BlockSpec((32, 1, 8, DB), lambda t, s: (0, t, 0, 0)),
        bf(32, 8, 8, DB),
        (400_000_000, 6_000_000),
    )(zh_arg, factor_one, inputs)
    piece = lax.all_to_all(first_local, PLANE, split_axis=0, concat_axis=0, tiled=True)

    payload = jnp.concatenate([w_gate, w_up, w_input_gate, w_down[:12], w_down[12:]], axis=1)
    payload = lax.ppermute(payload, ALL, shard_moves())
    payload = jnp.broadcast_to(payload, (16, 12, 2688))
    payload = lax.all_to_all(payload, ("zl", "y", "zh"), split_axis=0, concat_axis=0, tiled=True)
    across = lax.ppermute(payload, "core", SWAP)
    gathered = jnp.concatenate(
        [jnp.where(core == 0, payload, across), jnp.where(core == 0, across, payload)], axis=0
    )
    upper_part = gathered[..., :1920].reshape(DB, 1920)
    wg, wu, win = upper_part[:, :768], upper_part[:, 768:1536], upper_part[:, 1536:]
    wd = gathered[..., 1920:].reshape(32, 12, 2, DB).transpose(0, 2, 1, 3).reshape(768, DB)
    gain = lax.dynamic_slice_in_dim(norm_gain, xi * DB, DB, 0).reshape(1, DB)

    cot = lax.all_to_all(
        grad_out.reshape(512, 4, DB).transpose(1, 0, 2), "x", split_axis=0, concat_axis=0, tiled=True
    )
    packed = rows(DB, 256)
    give = call(
        give_kernel, (4,),
        [pl.BlockSpec((1, 512, 192), lambda t, s: (2 * t + 1 - s[0], 0, 0))],
        packed, bf(1024, DB), (1, 2_000_000),
    )(zh_arg, inputs.reshape(8, 512, 192))
    other = lax.ppermute(give, "zh", SWAP)
    f2 = lax.dynamic_slice_in_dim(factor_two, zh * 8, 8, 0)

    wide = [pltpu.VMEM((2048, 128), F32)] * 6
    all_pieces = whole(32, 8, 8, DB)
    second_cols, first_cols = call(
        second_kernel, (1,),
        [all_pieces, whole(8, 256, 256)],
        [all_pieces, whole(8, 256, DB)],
        [bf(32, 8, 8, DB), bf(8, 256, DB)],
        (400_000_000, 6_000_000), wide,
    )(zh_arg, piece, f2)
    second = lax.all_to_all(second_cols, PLANE, split_axis=0, concat_axis=0, tiled=True)

    chunk = pl.BlockSpec((1, 512, 192), lambda t, s: (2 * t + s[0], 0, 0))
    input_mlp, resid, pgate, square = call(
        gating_kernel, (4,),
        [chunk, packed, PIECES, whole(DB, DB)],
        [rows(DB), rows(DB), rows(DB), lead(8, 512)],
        [bf(2048, DB), bf(2048, DB), bf(2048, DB), f32(4, 8, 512)],
        (600_000_000, 10_000_000),
    )(zh_arg, inputs.reshape(8, 512, 192), other, second, win)
    square = sum(around_x(square[:, 0])).reshape(4, 1, 512)
    mixed, normed, hidden, grads, g_normed, inner, gain_term = call(
        mlp_kernel, (4,),
        [rows(DB), lead(512, DB), lead(1, 512), whole(1, DB), whole(DB, 768), whole(DB, 768), whole(768, DB)],
        [lead(512, DB), rows(DB), rows(768), rows(1536), rows(DB), lead(8, 512), whole(8, DB)],
        [bf(4, 512, DB), bf(2048, DB), bf(2048, 768), bf(2048, 1536), f32(2048, DB), f32(4, 8, 512), f32(8, DB)],
        (7_300_000_000, 24_000_000),
    )(zh_arg, resid, cot, square, gain, wg, wu, wd)
    gain_here = jnp.pad(jnp.sum(gain_term, axis=0), (0, 128)).reshape(1, 512)
    sums = around_x(jnp.concatenate([inner[:, 0], gain_here], axis=0))
    inner = sum(v[:4] for v in sums).reshape(4, 1, 512)
    gain_terms = jnp.concatenate([v[4:, :DB] for v in sums[::-1]] * 2, axis=0)
    gain_terms = lax.dynamic_slice_in_dim(gain_terms, lax.rem(7 - xi, 4), 4, 0).reshape(D)
    g_resid, g_second = call(
        resid_grad_kernel, (4,),
        [rows(DB), lead(512, DB), lead(1, 512), lead(1, 512), whole(1, DB), rows(DB), rows(DB), rows(DB)],
        [rows(DB), PIECES],
        [bf(2048, DB), bf(32, 8, 8, DB)],
        (50_000_000, 12_000_000),
    )(zh_arg, resid, cot, square, inner, gain, g_normed, input_mlp, pgate)
    piece = lax.all_to_all(g_second, PLANE, split_axis=0, concat_axis=0, tiled=True)
    mixed, g_resid = lax.optimization_barrier((mixed, g_resid))
    mixed_out = lax.all_to_all(mixed, "x", split_axis=0, concat_axis=0, tiled=True)
    mixed_out = mixed_out.transpose(1, 0, 2).reshape(512, D)
    g_direct, term_entry = call(
        direct_kernel, (4,),
        [rows(DB), rows(DB), PIECES, rows(DB), whole(DB, DB)],
        [rows(DB), whole(DB, DB)],
        [bf(2048, DB), f32(DB, DB)],
        (1_200_000_000, 10_000_000),
    )(zh_arg, g_resid, input_mlp, second, pgate, win)

    term_gu = jnp.einsum("td,th->dh", normed, grads, preferred_element_type=F32)
    term_down = jnp.einsum("th,te->he", hidden, cot.reshape(2048, DB), preferred_element_type=F32)
    down2 = term_down.astype(BF).reshape(32, 2, 12, DB).transpose(0, 2, 1, 3).reshape(32, 12, 2 * DB)
    terms = jnp.concatenate([term_gu, term_entry], axis=1).astype(BF).reshape(32, 12, 1920)
    terms = jnp.concatenate([terms, down2], axis=2)
    gain_row = jnp.pad(gain_terms.astype(BF), (0, 2688 - D)).reshape(1, 1, 2688)
    terms = jnp.concatenate([terms, jnp.broadcast_to(gain_row, (32, 1, 2688))], axis=1)
    keep = lax.dynamic_slice_in_dim(terms, core * 16, 16, 0)
    give = lax.dynamic_slice_in_dim(terms, (1 - core) * 16, 16, 0)
    pair = (keep.astype(F32) + lax.ppermute(give, "core", SWAP).astype(F32)).astype(BF)
    pair, piece = lax.optimization_barrier((pair, piece))
    pair = lax.all_to_all(pair, ("zl", "y", "zh"), split_axis=0, concat_axis=0, tiled=True)
    summed = jnp.sum(pair.astype(F32), axis=0) * tok_scale
    back = [(there, here) for here, there in shard_moves()]
    own = lax.ppermute(summed[:12], ALL, back)
    grad_w_gate, grad_w_up = own[:, :768], own[:, 768:1536]
    grad_w_input_gate = own[:, 1536:1920]
    grad_w_down = jnp.concatenate([own[:, 1920:2304], own[:, 2304:]], axis=0)
    grad_norm_gain = summed[12, :D]

    first_grad, second_grad = call(
        first_grad_kernel, (1,),
        [all_pieces, whole(8, 256, 256)],
        [all_pieces, whole(8, 256, DB)],
        [bf(32, 8, 8, DB), bf(8, 256, DB)],
        (400_000_000, 6_000_000), wide,
    )(zh_arg, piece, f2)
    g_first = lax.all_to_all(first_grad, PLANE, split_axis=0, concat_axis=0, tiled=True)
    term_two = jnp.einsum("akc,aic->aki", second_grad, first_cols, preferred_element_type=F32)
    term_two = (term_two * chan_scale).astype(BF).reshape(8, 8, 32, 256)
    term_two = lax.all_to_all(term_two.swapaxes(0, 1), CH, split_axis=0, concat_axis=0, tiled=True)
    term_in = pl.BlockSpec((8, 2, 32, 256), lambda t, s: (0, t, 0, 0))
    grad_factor_two = call(
        factor_sum_two_kernel, (4,), [term_in],
        pl.BlockSpec((2, 2, 32, 256), lambda t, s: (0, t, 0, 0)),
        f32(2, 8, 32, 256), (1, 3_000_000),
    )(zh_arg, term_two).reshape(16, 32, 256)

    term_one, own_grad, give_grad = call(
        back_kernel, (4,),
        [PIECES, rows(DB), pl.BlockSpec((1, 2, 256, 256), lambda t, s: (2 * t + s[0], 0, 0, 0)), rows(DB)],
        [term_in, rows(192), packed],
        [bf(8, 8, 32, 256), bf(2048, 192), bf(1024, DB)],
        (800_000_000, 9_000_000),
    )(zh_arg, g_first, input_mlp, factor_one.reshape(8, 2, 256, 256), g_direct)
    got_grad = lax.ppermute(give_grad, "zh", SWAP)
    term_one = lax.all_to_all(term_one, CH, split_axis=0, concat_axis=0, tiled=True)
    grad_factor_one = call(
        factor_sum_kernel, (4,), [term_in],
        pl.BlockSpec((1, 2, 2, 32, 256), lambda t, s: (t, 0, 0, 0, 0)),
        f32(4, 2, 2, 32, 256), (1, 3_000_000),
    )(zh_arg, term_one).reshape(16, 32, 256)
    grad_inputs = call(
        join_kernel, (4,), [rows(192), packed], rows(192, 1024), bf(4096, 192), (1, 4_000_000)
    )(zh_arg, own_grad, got_grad)
    return (
        mixed_out,
        grad_inputs,
        grad_factor_one,
        grad_factor_two,
        grad_w_input_gate,
        grad_norm_gain,
        grad_w_gate,
        grad_w_up,
        grad_w_down,
    )


def solution(mesh):
    fine = Mesh(mesh.devices.reshape(SIZES), ALL)
    return jax.shard_map(
        per_device,
        mesh=fine,
        in_specs=(
            P(SEQ, CH),
            P(SEQ, None, None),
            P(SEQ, None, None),
            P(ALL, None),
            P(),
            P(ALL, None),
            P(ALL, None),
            P(ALL, None),
            P(ALL, None),
        ),
        out_specs=(
            P(ALL, None),
            P(SEQ, CH),
            P(SEQ, CH, None),
            P(SEQ, CH, None),
            P(ALL, None),
            P(),
            P(ALL, None),
            P(ALL, None),
            P(ALL, None),
        ),
        check_vma=False,
    )
```

time: 484 us -> 357 us (0.74)
  local copies, waits for them, and re-layouts: 229 us -> 47.2 us
  waiting for transfers between devices: 43.1 us -> 123 us
  Pallas kernels: 0 us -> 76.9 us
  matrix products: 69.3 us -> 10.5 us
  other arithmetic: 30.4 us -> 14.7 us
  between operations: 14.8 us -> 0.99 us
  starting transfers between devices: 87.2 us -> 77.1 us
    pallas_call x0 -> x12, Pallas kernels: none -> 76.9 us  [the longest x1 17.8 us: per_device(): call(mlp_kernel, (4,), [rows(DB), lead(512, DB), lead(1, 512), whole(1, D...]
    all_to_all x6 -> x9, waiting for transfers between devices: 13.5 us -> 88.5 us  [the longest x1 20.9 us: per_device(): lax.all_to_all(first_local, PLANE, split_axis=0, concat_axis=0, tiled=True)]
    dot_general x18 -> x3, matrix products: 69.3 us -> 10.5 us  [the longest x1 6.04 us: per_device(): term_gu = jnp.einsum('td,th->dh', normed, grads, preferred_element_type=F32)]
    another operation x15 -> x0, local copies, waits for them, and re-layouts: 39.1 us -> none  [the longest x1 14.4 us: per_device(): lax.all_to_all(term_two, CH, split_axis=1, concat_axis=0, tiled=False)]
    transpose x6 -> x1, local copies, waits for them, and re-layouts: 36.2 us -> 1.72 us  [per_device(): mixed_out = mixed_out.transpose(1, 0, 2).reshape(512, D)]
    reshape x8, local copies, waits for them, and re-layouts: 34.6 us -> 6.38 us  [the longest x1 2.59 us: per_device(): grad_out.reshape(512, 4, DB).transpose(1, 0, 2)]
    convert_element_type x5 -> x2, local copies, waits for them, and re-layouts: 21.4 us -> 0.02 us  [per_device(): gain_row = jnp.pad(gain_terms.astype(BF), (0, 2688 - D)).reshape(1, 1, 2688)]
    ppermute x17 -> x9, waiting for transfers between devices: 23 us -> 6.03 us  [the longest x1 4.52 us: per_device(): got_grad = lax.ppermute(give_grad, 'zh', SWAP)]
  transfers between devices with their start and end apart: 28 -> 22, of which waited for: 6 -> 12; matrix products, arithmetic and copies ran while one was open for 56% -> 17% of each run, Pallas kernels for 0% -> 14%
where the time goes in v2:
time: 357 us; the launch traced here: 351 us
  waiting for transfers between devices  123 us (34%)
  starting transfers between devices  77.1 us (22%)
  Pallas kernels  76.9 us (22%)
  local copies, waits for them, and re-layouts  47.2 us (13%)
  other arithmetic  14.7 us (4%)
  matrix products  10.5 us (3%)
    all_to_all x1, waiting for transfers between devices, per_device(): lax.all_to_all(first_local, PLANE, split_axis=0, concat_axis=0, tiled=True)  20.9 us
    all_to_all x1, waiting for transfers between devices, per_device(): lax.all_to_all(first_grad, PLANE, split_axis=0, concat_axis=0, tiled=True)  19.6 us
    unnamed x30, local copies, waits for them, and re-layouts  19.1 us
    pallas_call x1, Pallas kernels, per_device(): call(mlp_kernel, (4,), [rows(DB), lead(512, DB), lead(1, 512), whole(1, D...  17.8 us
    all_to_all x1, waiting for transfers between devices, per_device(): lax.all_to_all(pair, ('zl', 'y', 'zh'), split_axis=0, concat_axis=0, tile...  17 us
    all_to_all x1, waiting for transfers between devices, per_device(): lax.all_to_all(mixed, 'x', split_axis=0, concat_axis=0, tiled=True)  16.7 us
    all_to_all x1, waiting for transfers between devices, per_device(): lax.all_to_all(payload, ('zl', 'y', 'zh'), split_axis=0, concat_axis=0, t...  12 us
    ppermute x6, starting transfers between devices, around_x(): lax.ppermute(value, 'x', [(i, (i + step) % 4) for i in range(4)])  11.1 us
  transfers between devices with their start and end apart: 22, of which 12 were waited for; matrix products, arithmetic and copies ran while one was open for 17% of the time, Pallas kernels for 14%

profile of v2, /device:TPU:2, one launch (start us, length us, event | category | flops | bytes accessed | tf_op | source)
XLA Modules:
  0.0 350.6 jit_solution(15057691735616016677)
XLA Ops:
  7.9 6.5 %collective-permute-done.1 = bf16[12,2688]{1,0:T(8,128)(2,1)S(1)} collective-permute-done((bf16[12,2688]{1,0:T(8,128)(2,1)S(1)}, bf16[12,2688]{1,0:T(8,128)(2,1)S(1)}, u32[]{:S(2)}, u32[]{:S(2)}) %collective-permute-start.1) | collective-permute-done | bytes 64544 | tf_op jit(solution)/shard_map/ppermute | solution.py:337
  15.5 7.6 %all-to-all-start.2 = ((bf16[16,12,2688]{2,1,0:T(8,128)(2,1)}), bf16[16,12,2688]{2,1,0:T(8,128)(2,1)S(1)}, u32[]{:S(2)}, u32[]{:S(2)}) async-start(bf16[16,12,2688]{2,1,0:T(8,128)(2,1)} %broadcast_in_dim.8), calls=%async_computation.2 | async-start | bytes 2752512 | tf_op jit(solution)/shard_map/all_to_all | solution.py:339
  23.1 3.9 %copy.55.in_ref = bf16[4096,192]{1,0:T(8,128)(2,1)} copy(bf16[4096,192]{0,1:T(8,128)(2,1)} %param.9) | data formatting | bytes 3145728 | tf_op args[0]
  27.0 7.0 %shard_map.161 = bf16[32,8,8,384]{3,2,1,0:T(8,128)(2,1)} custom-call(s32[1]{0:T(128)} %bitcast._.zh_ref, bf16[16,256,256]{2,1,0:T(8,128)(2,1)} %f1_ref.1, bf16[4096,192]{1,0:T(8,128)(2,1)} %copy.55.in_ref), custom_call_target="tpu_custom_call" | custom-call | flops 400000000 | bytes 6000000 | tf_op jit(solution)/shard_map/pallas_call | solution.py:327
  33.9 12.0 %all-to-all-done.2 = bf16[16,12,2688]{2,1,0:T(8,128)(2,1)S(1)} async-done(((bf16[16,12,2688]{2,1,0:T(8,128)(2,1)}), bf16[16,12,2688]{2,1,0:T(8,128)(2,1)S(1)}, u32[]{:S(2)}, u32[]{:S(2)}) %all-to-all-start.2) | async-done | bytes 1032224 | tf_op jit(solution)/shard_map/all_to_all | solution.py:339
  46.0 4.9 %all-to-all-start = ((bf16[32,8,8,384]{3,2,1,0:T(8,128)(2,1)}), bf16[32,8,8,384]{3,2,1,0:T(8,128)(2,1)}, u32[]{:S(2)}, u32[]{:S(2)}) async-start(bf16[32,8,8,384]{3,2,1,0:T(8,128)(2,1)} %shard_map.161), calls=%async_computation | async-start | bytes 3145728 | tf_op jit(solution)/shard_map/all_to_all | solution.py:334
  53.2 20.9 %all-to-all-done.piece_ref = bf16[32,8,8,384]{3,2,1,0:T(8,128)(2,1)} async-done(((bf16[32,8,8,384]{3,2,1,0:T(8,128)(2,1)}), bf16[32,8,8,384]{3,2,1,0:T(8,128)(2,1)}, u32[]{:S(2)}, u32[]{:S(2)}) %all-to-all-start) | async-done | bytes 1572896 | tf_op jit(solution)/shard_map/all_to_all | solution.py:334
  74.1 4.7 %shard_map.162 = (bf16[32,8,8,384]{3,2,1,0:T(8,128)(2,1)}, bf16[8,256,384]{2,1,0:T(8,128)(2,1)}) custom-call(s32[1]{0:T(128)} %bitcast._.zh_ref, bf16[32,8,8,384]{3,2,1,0:T(8,128)(2,1)} %all-to-all-done.piece_ref, bf16[8,256,256]{2,1,0:T(8,128)(2,1)} %constant_dynamic-slice_fusion.1.f2_ref), custom_call_target="tpu_custom_call" | custom-call | flops 400000000 | bytes 6000000 | tf_op jit(solution)/shard_map/pallas_call | solution.py:363
  78.8 4.1 %all-to-all-start.1 = ((bf16[32,8,8,384]{3,2,1,0:T(8,128)(2,1)}), bf16[32,8,8,384]{3,2,1,0:T(8,128)(2,1)S(1)}, u32[]{:S(2)}, u32[]{:S(2)}) async-start(bf16[32,8,8,384]{3,2,1,0:T(8,128)(2,1)} %get-tuple-element.35), calls=%async_computation.1 | async-start | bytes 3145728 | tf_op jit(solution)/shard_map/all_to_all | solution.py:370
  99.4 7.5 %all-to-all-done.1.second_ref = bf16[32,8,8,384]{3,2,1,0:T(8,128)(2,1)S(1)} async-done(((bf16[32,8,8,384]{3,2,1,0:T(8,128)(2,1)}), bf16[32,8,8,384]{3,2,1,0:T(8,128)(2,1)S(1)}, u32[]{:S(2)}, u32[]{:S(2)}) %all-to-all-start.1) | async-done | bytes 1572896 | tf_op jit(solution)/shard_map/all_to_all | solution.py:370
  108.1 7.5 %all-to-all-start.3 = ((bf16[4,512,384]{2,1,0:T(8,128)(2,1)}), bf16[4,512,384]{2,1,0:T(8,128)(2,1)S(1)}, u32[]{:S(2)}, u32[]{:S(2)}) async-start(bf16[4,512,384]{2,1,0:T(8,128)(2,1)} %bitcast.37), calls=%async_computation.3 | async-start | bytes 3145728 | tf_op jit(solution)/shard_map/all_to_all | solution.py:349
  122.9 6.5 %shard_map.163 = (bf16[2048,384]{1,0:T(8,128)(2,1)}, bf16[2048,384]{1,0:T(8,128)(2,1)}, bf16[2048,384]{1,0:T(8,128)(2,1)}, f32[4,8,512]{2,1,0:T(8,128)}) custom-call(s32[1]{0:T(128)} %bitcast._.zh_ref, bf16[8,512,192]{2,1,0:T(8,128)(2,1)} %bitcast.34, bf16[1024,384]{1,0:T(8,128)(2,1)} %collective-permute-done.got_ref, bf16[32,8,8,384]{3,2,1,0:T(8,128)(2,1)} %copy-done.2, ...), custom_call_target="tpu_custom_call" | custom-call | flops 600000000 | bytes 10000000 | tf_op jit(solution)/shard_map/pallas_call | solution.py:373
  140.3 17.8 %shard_map.164 = (bf16[4,512,384]{2,1,0:T(8,128)(2,1)}, bf16[2048,384]{1,0:T(8,128)(2,1)}, bf16[2048,768]{1,0:T(8,128)(2,1)}, bf16[2048,1536]{1,0:T(8,128)(2,1)}...) custom-call(s32[1]{0:T(128)} %bitcast._.zh_ref, bf16[2048,384]{1,0:T(8,128)(2,1)} %get-tuple-element.36.resid_ref, ...), custom_call_target="tpu_custom_call" | custom-call | flops 7299999744 | bytes 24000000 | tf_op jit(solution)/shard_map/pallas_call | solution.py:381
  166.3 6.0 %convolution_convert_fusion = bf16[384,1536]{1,0:T(8,128)(2,1)S(1)} fusion(bf16[2048,384]{1,0:T(8,128)(2,1)} %get-tuple-element.46, bf16[2048,1536]{1,0:T(8,128)(2,1)} %get-tuple-element.47), kind=kOutput, calls=%fused_computation | convolution fusion | flops 2416508928 | bytes 9043968 | tf_op jit(solution)/shard_map/td,th->dh/dot_general | solution.py:412
  177.9 6.8 %shard_map.165 = (bf16[2048,384]{1,0:T(8,128)(2,1)}, bf16[32,8,8,384]{3,2,1,0:T(8,128)(2,1)}) custom-call(s32[1]{0:T(128)} %bitcast._.zh_ref, bf16[2048,384]{1,0:T(8,128)(2,1)} %get-tuple-element.36.resid_ref, bf16[4,512,384]{2,1,0:T(8,128)(2,1)} %copy-done.3, f32[4,1,512]{2,1,0:T(1,128)} %reshape.88.square_ref, f32[4,1,512]{2,1,0:T(1,128)} %reshape.93.inner_ref, ...), custom_call_target="tpu_custom_call" | custom-call | flops 50000000 | bytes 12000000 | tf_op jit(solution)/shard_map/pallas_call | solution.py:393
  184.7 5.1 %all-to-all-start.5 = ((bf16[32,8,8,384]{3,2,1,0:T(8,128)(2,1)}), bf16[32,8,8,384]{3,2,1,0:T(8,128)(2,1)}, u32[]{:S(2)}, u32[]{:S(2)}) async-start(bf16[32,8,8,384]{3,2,1,0:T(8,128)(2,1)} %get-tuple-element.51), calls=%async_computation.5 | async-start | bytes 3145728 | tf_op jit(solution)/shard_map/all_to_all | solution.py:400
  192.1 6.6 %shard_map.166 = (bf16[2048,384]{1,0:T(8,128)(2,1)}, f32[384,384]{1,0:T(8,128)}) custom-call(s32[1]{0:T(128)} %bitcast._.zh_ref, bf16[2048,384]{1,0:T(8,128)(2,1)} %get-tuple-element.48.g_resid_ref, bf16[2048,384]{1,0:T(8,128)(2,1)} %get-tuple-element.42.in_ref, bf16[32,8,8,384]{3,2,1,0:T(8,128)(2,1)} %copy-done.2, ...), custom_call_target="tpu_custom_call" | custom-call | flops 1200000000 | bytes 10000000 | tf_op jit(solution)/shard_map/pallas_call | solution.py:404
  204.3 8.6 %all-to-all-done.5.piece_ref = bf16[32,8,8,384]{3,2,1,0:T(8,128)(2,1)} async-done(((bf16[32,8,8,384]{3,2,1,0:T(8,128)(2,1)}), bf16[32,8,8,384]{3,2,1,0:T(8,128)(2,1)}, u32[]{:S(2)}, u32[]{:S(2)}) %all-to-all-start.5) | async-done | bytes 1572896 | tf_op jit(solution)/shard_map/all_to_all | solution.py:400
  212.9 4.4 %all-to-all-start.4 = ((bf16[4,512,384]{2,1,0:T(8,128)(2,1)}), bf16[4,512,384]{2,1,0:T(8,128)(2,1)}, u32[]{:S(2)}, u32[]{:S(2)}) async-start(bf16[4,512,384]{2,1,0:T(8,128)(2,1)} %get-tuple-element.45), calls=%async_computation.4 | async-start | bytes 3145728 | tf_op jit(solution)/shard_map/all_to_all | solution.py:402
  220.0 16.7 %all-to-all-done.4 = bf16[4,512,384]{2,1,0:T(8,128)(2,1)} async-done(((bf16[4,512,384]{2,1,0:T(8,128)(2,1)}), bf16[4,512,384]{2,1,0:T(8,128)(2,1)}, u32[]{:S(2)}, u32[]{:S(2)}) %all-to-all-start.4) | async-done | bytes 1572896 | tf_op jit(solution)/shard_map/all_to_all | solution.py:402
  236.7 4.2 %all-to-all-start.9 = ((bf16[16,13,2688]{2,1,0:T(8,128)(2,1)}), bf16[16,13,2688]{2,1,0:T(8,128)(2,1)S(1)}, u32[]{:S(2)}, u32[]{:S(2)}) async-start(bf16[16,13,2688]{2,1,0:T(8,128)(2,1)} %add_convert_fusion), calls=%async_computation.9 | async-start | bytes 2752512 | tf_op jit(solution)/shard_map/all_to_all | solution.py:423
  240.9 4.7 %shard_map.167 = (bf16[32,8,8,384]{3,2,1,0:T(8,128)(2,1)}, bf16[8,256,384]{2,1,0:T(8,128)(2,1)}) custom-call(s32[1]{0:T(128)} %bitcast._.zh_ref, bf16[32,8,8,384]{3,2,1,0:T(8,128)(2,1)} %all-to-all-done.5.piece_ref, bf16[8,256,256]{2,1,0:T(8,128)(2,1)} %constant_dynamic-slice_fusion.1.f2_ref), custom_call_target="tpu_custom_call" | custom-call | flops 400000000 | bytes 6000000 | tf_op jit(solution)/shard_map/pallas_call | solution.py:432
  245.6 17.0 %all-to-all-done.9 = bf16[16,13,2688]{2,1,0:T(8,128)(2,1)S(1)} async-done(((bf16[16,13,2688]{2,1,0:T(8,128)(2,1)}), bf16[16,13,2688]{2,1,0:T(8,128)(2,1)S(1)}, u32[]{:S(2)}, u32[]{:S(2)}) %all-to-all-start.9) | async-done | bytes 1118240 | tf_op jit(solution)/shard_map/all_to_all | solution.py:423
  262.6 4.4 %all-to-all-start.6 = ((bf16[32,8,8,384]{3,2,1,0:T(8,128)(2,1)}), bf16[32,8,8,384]{3,2,1,0:T(8,128)(2,1)S(1)}, u32[]{:S(2)}, u32[]{:S(2)}) async-start(bf16[32,8,8,384]{3,2,1,0:T(8,128)(2,1)} %get-tuple-element.53), calls=%async_computation.6 | async-start | bytes 3145728 | tf_op jit(solution)/shard_map/all_to_all | solution.py:439
  270.8 19.6 %all-to-all-done.6.g_first_ref = bf16[32,8,8,384]{3,2,1,0:T(8,128)(2,1)S(1)} async-done(((bf16[32,8,8,384]{3,2,1,0:T(8,128)(2,1)}), bf16[32,8,8,384]{3,2,1,0:T(8,128)(2,1)S(1)}, u32[]{:S(2)}, u32[]{:S(2)}) %all-to-all-start.6) | async-done | bytes 1572896 | tf_op jit(solution)/shard_map/all_to_all | solution.py:439
  290.4 5.6 %all-to-all-start.8 = ((bf16[8,8,32,256]{3,2,1,0:T(8,128)(2,1)}), bf16[8,8,32,256]{3,2,1,0:T(8,128)(2,1)}, u32[]{:S(2)}, u32[]{:S(2)}) async-start(bf16[8,8,32,256]{3,2,1,0:T(8,128)(2,1)} %bitcast.40), calls=%async_computation.8 | async-start | bytes 2097152 | tf_op jit(solution)/shard_map/all_to_all | solution.py:442
  296.2 8.9 %shard_map.168 = (bf16[8,8,32,256]{3,2,1,0:T(8,128)(2,1)}, bf16[2048,192]{1,0:T(8,128)(2,1)}, bf16[1024,384]{1,0:T(8,128)(2,1)}) custom-call(s32[1]{0:T(128)} %bitcast._.zh_ref, bf16[32,8,8,384]{3,2,1,0:T(8,128)(2,1)} %copy-done.7, bf16[2048,384]{1,0:T(8,128)(2,1)} %get-tuple-element.42.in_ref, bf16[8,2,256,256]{3,2,1,0:T(8,128)(2,1)} %bitcast.36, ...), custom_call_target="tpu_custom_call" | custom-call | flops 800000000 | bytes 9000000 | tf_op jit(solution)/shard_map/pallas_call | solution.py:450
  311.2 4.9 %all-to-all-start.7 = ((bf16[8,8,32,256]{3,2,1,0:T(8,128)(2,1)}), bf16[8,8,32,256]{3,2,1,0:T(8,128)(2,1)S(1)}, u32[]{:S(2)}, u32[]{:S(2)}) async-start(bf16[8,8,32,256]{3,2,1,0:T(8,128)(2,1)} %get-tuple-element.57), calls=%async_computation.7 | async-start | bytes 2097152 | tf_op jit(solution)/shard_map/all_to_all | solution.py:458
  326.7 5.2 %collective-permute-done.11 = f32[12,2688]{1,0:T(8,128)S(1)} collective-permute-done((f32[12,2688]{1,0:T(8,128)S(1)}, f32[12,2688]{1,0:T(8,128)S(1)}, u32[]{:S(2)}, u32[]{:S(2)}) %collective-permute-start.11) | collective-permute-done | bytes 129056 | tf_op jit(solution)/shard_map/ppermute | solution.py:426
  333.8 4.5 %collective-permute-done.10.got_ref = bf16[1024,384]{1,0:T(8,128)(2,1)} collective-permute-done((bf16[1024,384]{1,0:T(8,128)(2,1)}, bf16[1024,384]{1,0:T(8,128)(2,1)}, u32[]{:S(2)}, u32[]{:S(2)}) %collective-permute-start.10) | collective-permute-done | bytes 786464 | tf_op jit(solution)/shard_map/ppermute | solution.py:457
  338.4 3.8 %shard_map.169 = bf16[4096,192]{1,0:T(8,128)(2,1)} custom-call(s32[1]{0:T(128)} %bitcast._.zh_ref, bf16[2048,192]{1,0:T(8,128)(2,1)} %get-tuple-element.55.own_ref, bf16[1024,384]{1,0:T(8,128)(2,1)} %collective-permute-done.10.got_ref), custom_call_target="tpu_custom_call" | custom-call | flops 1 | bytes 4000000 | tf_op jit(solution)/shard_map/pallas_call | solution.py:464
  342.2 4.0 %copy.73 = bf16[4096,192]{0,1:T(8,128)(2,1)} copy(bf16[4096,192]{1,0:T(8,128)(2,1)} %shard_map.169) | data formatting | bytes 3145728
  (111 shorter events, 97.6 us)
Async XLA Ops:
  0.6 51.5 %copy-start = (bf16[16,256,256]{2,1,0:T(8,128)(2,1)S(1)}, bf16[16,256,256]{2,1,0:T(8,128)(2,1)}, u32[]{:S(2)}) copy-start(bf16[16,256,256]{2,1,0:T(8,128)(2,1)} %param.11) | copy-start | bytes 6291460
  4.4 9.9 %collective-permute-start.1 = (bf16[12,2688]{1,0:T(8,128)(2,1)S(1)}, bf16[12,2688]{1,0:T(8,128)(2,1)S(1)}, u32[]{:S(2)}, u32[]{:S(2)}) collective-permute-start(bf16[12,2688]{1,0:T(8,128)(2,1)S(1)} %slice_dynamic-update-slice_fusion), channel_id=1, source_target_pairs={{0,0},{1,1},{2,16},{3,17},{4,32},{5,33},{6,48},{7,49},{8,64},{9,65... | collective-permute-start | bytes 193544 | tf_op jit(solution)/shard_map/ppermute | solution.py:337
  15.5 30.4 %all-to-all-start.2 = ((bf16[16,12,2688]{2,1,0:T(8,128)(2,1)}), bf16[16,12,2688]{2,1,0:T(8,128)(2,1)S(1)}, u32[]{:S(2)}, u32[]{:S(2)}) async-start(bf16[16,12,2688]{2,1,0:T(8,128)(2,1)} %broadcast_in_dim.8), calls=%async_computation.2 | async-start | bytes 2752512 | tf_op jit(solution)/shard_map/all_to_all | solution.py:339
  46.0 28.1 %all-to-all-start = ((bf16[32,8,8,384]{3,2,1,0:T(8,128)(2,1)}), bf16[32,8,8,384]{3,2,1,0:T(8,128)(2,1)}, u32[]{:S(2)}, u32[]{:S(2)}) async-start(bf16[32,8,8,384]{3,2,1,0:T(8,128)(2,1)} %shard_map.161), calls=%async_computation | async-start | bytes 3145728 | tf_op jit(solution)/shard_map/all_to_all | solution.py:334
  52.0 44.2 %collective-permute-start.2 = (bf16[16,12,2688]{2,0,1:T(8,128)(2,1)}, bf16[16,12,2688]{2,0,1:T(8,128)(2,1)}, u32[]{:S(2)}, u32[]{:S(2)}) collective-permute-start(bf16[16,12,2688]{2,0,1:T(8,128)(2,1)} %copy.57), channel_id=1, source_target_pairs={{0,8},{8,0},{1,9},{9,1},{2,10},{10,2},{3,11},{11,3},{4,12},{12,4},... | collective-permute-start | bytes 3096584 | tf_op jit(solution)/shard_map/ppermute | solution.py:340
  78.8 28.1 %all-to-all-start.1 = ((bf16[32,8,8,384]{3,2,1,0:T(8,128)(2,1)}), bf16[32,8,8,384]{3,2,1,0:T(8,128)(2,1)S(1)}, u32[]{:S(2)}, u32[]{:S(2)}) async-start(bf16[32,8,8,384]{3,2,1,0:T(8,128)(2,1)} %get-tuple-element.35), calls=%async_computation.1 | async-start | bytes 3145728 | tf_op jit(solution)/shard_map/all_to_all | solution.py:370
  86.4 36.5 %collective-permute-start = (bf16[1024,384]{1,0:T(8,128)(2,1)}, bf16[1024,384]{1,0:T(8,128)(2,1)}, u32[]{:S(2)}, u32[]{:S(2)}) collective-permute-start(bf16[1024,384]{1,0:T(8,128)(2,1)} %shard_map.160), channel_id=1, source_target_pairs={{0,1},{1,0},{2,3},{3,2},{4,5},{5,4},{6,7},{7,6},{8,9},{9,8},{10,11... | collective-permute-start | bytes 2359304 | tf_op jit(solution)/shard_map/ppermute | solution.py:358
  106.9 1.1 copy-start.2
  108.1 31.1 %all-to-all-start.3 = ((bf16[4,512,384]{2,1,0:T(8,128)(2,1)}), bf16[4,512,384]{2,1,0:T(8,128)(2,1)S(1)}, u32[]{:S(2)}, u32[]{:S(2)}) async-start(bf16[4,512,384]{2,1,0:T(8,128)(2,1)} %bitcast.37), calls=%async_computation.3 | async-start | bytes 3145728 | tf_op jit(solution)/shard_map/all_to_all | solution.py:349
  122.9 12.6 %copy-start.5 = (bf16[16,12,2688]{2,1,0:T(8,128)(2,1)S(1)}, bf16[16,12,2688]{2,1,0:T(8,128)(2,1)}, u32[]{:S(2)}) copy-start(bf16[16,12,2688]{2,1,0:T(8,128)(2,1)} %get-tuple-element.97) | copy-start | bytes 3096580
  122.9 12.6 %copy-start.6 = (bf16[16,12,2688]{2,1,0:T(8,128)(2,1)S(1)}, bf16[16,12,2688]{2,1,0:T(8,128)(2,1)}, u32[]{:S(2)}) copy-start(bf16[16,12,2688]{2,1,0:T(8,128)(2,1)} %get-tuple-element.98) | copy-start | bytes 3096580
  130.3 6.7 %collective-permute-start.3 = (f32[4,512]{1,0:T(4,128)S(1)}, f32[4,512]{1,0:T(4,128)S(1)}, u32[]{:S(2)}, u32[]{:S(2)}) collective-permute-start(f32[4,512]{1,0:T(4,128)S(1)} %slice_bitcast_fusion.1), channel_id=1, source_target_pairs={{0,2},{2,4},{4,6},{6,0},{1,3},{3,5},{5,7},{7,1},{8,10},{10,12},{12... | collective-permute-start | bytes 24584 | tf_op jit(solution)/shard_map/ppermute | solution.py:311
  133.4 5.2 %collective-permute-start.4 = (f32[4,512]{1,0:T(4,128)S(1)}, f32[4,512]{1,0:T(4,128)S(1)}, u32[]{:S(2)}, u32[]{:S(2)}) collective-permute-start(f32[4,512]{1,0:T(4,128)S(1)} %slice_bitcast_fusion.1), channel_id=1, source_target_pairs={{0,4},{2,6},{4,0},{6,2},{1,5},{3,7},{5,1},{7,3},{8,12},{10,14},{12... | collective-permute-start | bytes 24584 | tf_op jit(solution)/shard_map/ppermute | solution.py:311
  133.5 5.0 %collective-permute-start.5 = (f32[4,512]{1,0:T(4,128)S(1)}, f32[4,512]{1,0:T(4,128)S(1)}, u32[]{:S(2)}, u32[]{:S(2)}) collective-permute-start(f32[4,512]{1,0:T(4,128)S(1)} %slice_bitcast_fusion.1), channel_id=1, source_target_pairs={{0,6},{2,0},{4,2},{6,4},{1,7},{3,1},{5,3},{7,5},{8,14},{10,8},{12,... | collective-permute-start | bytes 24584 | tf_op jit(solution)/shard_map/ppermute | solution.py:311
  139.1 1.2 copy-start.3
  160.4 16.2 %collective-permute-start.6 = (f32[5,512]{1,0:T(8,128)S(1)}, f32[5,512]{1,0:T(8,128)}, u32[]{:S(2)}, u32[]{:S(2)}) collective-permute-start(f32[5,512]{1,0:T(8,128)S(1)} %pad_maximum_fusion.3), channel_id=1, source_target_pairs={{0,2},{2,4},{4,6},{6,0},{1,3},{3,5},{5,7},{7,1},{8,10},{10,12},{12... | collective-permute-start | bytes 30728 | tf_op jit(solution)/shard_map/ppermute | solution.py:311
  161.1 15.5 %collective-permute-start.7 = (f32[5,512]{1,0:T(8,128)S(1)}, f32[5,512]{1,0:T(8,128)}, u32[]{:S(2)}, u32[]{:S(2)}) collective-permute-start(f32[5,512]{1,0:T(8,128)S(1)} %pad_maximum_fusion.3), channel_id=1, source_target_pairs={{0,4},{2,6},{4,0},{6,2},{1,5},{3,7},{5,1},{7,3},{8,12},{10,14},{12... | collective-permute-start | bytes 30728 | tf_op jit(solution)/shard_map/ppermute | solution.py:311
  163.8 12.8 %collective-permute-start.8 = (f32[5,512]{1,0:T(8,128)S(1)}, f32[5,512]{1,0:T(8,128)}, u32[]{:S(2)}, u32[]{:S(2)}) collective-permute-start(f32[5,512]{1,0:T(8,128)S(1)} %pad_maximum_fusion.3), channel_id=1, source_target_pairs={{0,6},{2,0},{4,2},{6,4},{1,7},{3,1},{5,3},{7,5},{8,14},{10,8},{12,... | collective-permute-start | bytes 30728 | tf_op jit(solution)/shard_map/ppermute | solution.py:311
  166.3 6.0 %copy-start.4 = (bf16[4,512,384]{2,1,0:T(8,128)(2,1)S(1)}, bf16[4,512,384]{2,1,0:T(8,128)(2,1)}, u32[]{:S(2)}) copy-start(bf16[4,512,384]{2,1,0:T(8,128)(2,1)} %copy-done.3) | copy-start | bytes 4718596
  166.3 6.1 %copy-start.9 = (bf16[2048,768]{1,0:T(8,128)(2,1)S(1)}, bf16[2048,768]{1,0:T(8,128)(2,1)}, u32[]{:S(2)}) copy-start(bf16[2048,768]{1,0:T(8,128)(2,1)} %get-tuple-element.50) | copy-start | bytes 9437188
  184.7 28.2 %all-to-all-start.5 = ((bf16[32,8,8,384]{3,2,1,0:T(8,128)(2,1)}), bf16[32,8,8,384]{3,2,1,0:T(8,128)(2,1)}, u32[]{:S(2)}, u32[]{:S(2)}) async-start(bf16[32,8,8,384]{3,2,1,0:T(8,128)(2,1)} %get-tuple-element.51), calls=%async_computation.5 | async-start | bytes 3145728 | tf_op jit(solution)/shard_map/all_to_all | solution.py:400
  204.3 13.0 %collective-permute-start.9 = (bf16[16,13,2688]{2,0,1:T(8,128)(2,1)}, bf16[16,13,2688]{2,0,1:T(8,128)(2,1)}, u32[]{:S(2)}, u32[]{:S(2)}) collective-permute-start(bf16[16,13,2688]{2,0,1:T(8,128)(2,1)} %copy.69), channel_id=1, source_target_pairs={{0,8},{8,0},{1,9},{9,1},{2,10},{10,2},{3,11},{11,3},{4,12},{12,4},... | collective-permute-start | bytes 3354632 | tf_op jit(solution)/shard_map/ppermute | solution.py:421
  212.9 23.8 %all-to-all-start.4 = ((bf16[4,512,384]{2,1,0:T(8,128)(2,1)}), bf16[4,512,384]{2,1,0:T(8,128)(2,1)}, u32[]{:S(2)}, u32[]{:S(2)}) async-start(bf16[4,512,384]{2,1,0:T(8,128)(2,1)} %get-tuple-element.45), calls=%async_computation.4 | async-start | bytes 3145728 | tf_op jit(solution)/shard_map/all_to_all | solution.py:402
  236.7 25.9 %all-to-all-start.9 = ((bf16[16,13,2688]{2,1,0:T(8,128)(2,1)}), bf16[16,13,2688]{2,1,0:T(8,128)(2,1)S(1)}, u32[]{:S(2)}, u32[]{:S(2)}) async-start(bf16[16,13,2688]{2,1,0:T(8,128)(2,1)} %add_convert_fusion), calls=%async_computation.9 | async-start | bytes 2752512 | tf_op jit(solution)/shard_map/all_to_all | solution.py:423
  262.6 27.7 %all-to-all-start.6 = ((bf16[32,8,8,384]{3,2,1,0:T(8,128)(2,1)}), bf16[32,8,8,384]{3,2,1,0:T(8,128)(2,1)S(1)}, u32[]{:S(2)}, u32[]{:S(2)}) async-start(bf16[32,8,8,384]{3,2,1,0:T(8,128)(2,1)} %get-tuple-element.53), calls=%async_computation.6 | async-start | bytes 3145728 | tf_op jit(solution)/shard_map/all_to_all | solution.py:439
  290.4 5.8 %copy-start.7 = (bf16[32,8,8,384]{3,2,1,0:T(8,128)(2,1)}, bf16[32,8,8,384]{3,2,1,0:T(8,128)(2,1)S(1)}, u32[]{:S(2)}) copy-start(bf16[32,8,8,384]{3,2,1,0:T(8,128)(2,1)S(1)} %all-to-all-done.6.g_first_ref) | copy-start | bytes 4718596
  290.4 20.9 %all-to-all-start.8 = ((bf16[8,8,32,256]{3,2,1,0:T(8,128)(2,1)}), bf16[8,8,32,256]{3,2,1,0:T(8,128)(2,1)}, u32[]{:S(2)}, u32[]{:S(2)}) async-start(bf16[8,8,32,256]{3,2,1,0:T(8,128)(2,1)} %bitcast.40), calls=%async_computation.8 | async-start | bytes 2097152 | tf_op jit(solution)/shard_map/all_to_all | solution.py:442
  305.1 33.2 %collective-permute-start.10 = (bf16[1024,384]{1,0:T(8,128)(2,1)}, bf16[1024,384]{1,0:T(8,128)(2,1)}, u32[]{:S(2)}, u32[]{:S(2)}) collective-permute-start(bf16[1024,384]{1,0:T(8,128)(2,1)} %get-tuple-element.56), channel_id=1, source_target_pairs={{0,1},{1,0},{2,3},{3,2},{4,5},{5,4},{6,7},{7,6},{8,9},{9,8},{10,11... | collective-permute-start | bytes 2359304 | tf_op jit(solution)/shard_map/ppermute | solution.py:457
  311.2 35.0 %all-to-all-start.7 = ((bf16[8,8,32,256]{3,2,1,0:T(8,128)(2,1)}), bf16[8,8,32,256]{3,2,1,0:T(8,128)(2,1)S(1)}, u32[]{:S(2)}, u32[]{:S(2)}) async-start(bf16[8,8,32,256]{3,2,1,0:T(8,128)(2,1)} %get-tuple-element.57), calls=%async_computation.7 | async-start | bytes 2097152 | tf_op jit(solution)/shard_map/all_to_all | solution.py:458
  316.2 15.8 %collective-permute-start.11 = (f32[12,2688]{1,0:T(8,128)S(1)}, f32[12,2688]{1,0:T(8,128)S(1)}, u32[]{:S(2)}, u32[]{:S(2)}) collective-permute-start(f32[12,2688]{1,0:T(8,128)S(1)} %bitcast.46), channel_id=1, source_target_pairs={{0,0},{1,1},{16,2},{17,3},{32,4},{33,5},{48,6},{49,7},{64,8},{65,9... | collective-permute-start | bytes 387080 | tf_op jit(solution)/shard_map/ppermute | solution.py:426
  342.2 8.3 %copy-start.1 = (bf16[16,256,256]{2,1,0:T(8,128)(2,1)S(1)}, bf16[16,256,256]{2,1,0:T(8,128)(2,1)}, u32[]{:S(2)}) copy-start(bf16[16,256,256]{2,1,0:T(8,128)(2,1)} %param.11) | copy-start | bytes 6291460
  346.3 1.0 copy-start.8
  (1 other events, 0.6 us)

commit v3 on v2

v3 whole, which is shorter than its diff:
```python
import math

import jax
import jax.numpy as jnp
from jax import lax
from jax.experimental import pallas as pl
from jax.experimental.pallas import tpu as pltpu
from jax.sharding import Mesh
from jax.sharding import PartitionSpec as P

D = 1536
NBLK = 4
SEQL = 65536
DB = D // NBLK
BF = jnp.bfloat16
F32 = jnp.float32

SEQ = ("zl", "y", "core")
CH = ("x", "zh")
ALL = SEQ + CH
SIZES = (2, 4, 2, 4, 2)
PLANE = SEQ + ("zh",)


def index_of(zl, y, k, x, zh):
    return (((zl * 4 + y) * 2 + k) * 4 + x) * 2 + zh


def shard_moves():
    moves = []
    for zl in range(2):
        for y in range(4):
            for k in range(2):
                for x in range(4):
                    for zh in range(2):
                        there = index_of(k, x, y % 2, zl * 2 + y // 2, zh)
                        moves.append((index_of(zl, y, k, x, zh), there))
    return moves


SWAP = [(0, 1), (1, 0)]


def call(body, grid, ins, outs, shapes, cost, scratch=()):
    return pl.pallas_call(
        body,
        grid_spec=pltpu.PrefetchScalarGridSpec(
            num_scalar_prefetch=1,
            grid=grid,
            in_specs=ins,
            out_specs=outs,
            scratch_shapes=list(scratch),
        ),
        out_shape=shapes,
        name=body.__name__,
        compiler_params=pltpu.CompilerParams(
            dimension_semantics=("arbitrary",) * len(grid), vmem_limit_bytes=56 * 1024 * 1024
        ),
        cost_estimate=pl.CostEstimate(flops=cost[0], bytes_accessed=cost[1], transcendentals=0),
    )


def whole(*shape):
    return pl.BlockSpec(shape, lambda t, s: (0,) * len(shape))


def rows(width, height=512):
    return pl.BlockSpec((height, width), lambda t, s: (t, 0))


def turned_rows(width, height=512):
    return pl.BlockSpec((height, width), lambda t, s: (lax.rem(s[1] + t, 4), 0))


def columns(height, width=512):
    return pl.BlockSpec((height, width), lambda t, s: (0, t))


PIECES = pl.BlockSpec((32, 2, 8, DB), lambda t, s: (0, t, 0, 0))
SUMS = [whole(8, 512)] * 4


def read_pieces(ref):
    return jnp.concatenate(
        [ref[:, r].astype(F32).reshape(256, DB) for r in range(2)], axis=0
    )


def row_sums(value):
    ones = jnp.ones((8, DB), BF)
    high = value.astype(BF)
    low = (value - high.astype(F32)).astype(BF)
    return dot_t(ones, high) + dot_t(ones, low)


def row_of(refs, at):
    total = refs[0][...] + refs[1][...] + refs[2][...] + refs[3][...]
    here = lax.broadcasted_iota(jnp.int32, (8, 512), 0) == at
    return jnp.sum(jnp.where(here, total, 0.0), axis=0, keepdims=True)


def put_row(ref, at, value):
    here = lax.broadcasted_iota(jnp.int32, (8, 512), 0) == at
    ref[...] = jnp.where(here, value, ref[...])


def as_column(row):
    turned = jnp.transpose(jnp.broadcast_to(row, (128, row.shape[1])))
    return jnp.concatenate([turned] * (DB // 128), axis=1)


def dot(a, b):
    return jnp.dot(a, b, preferred_element_type=F32)


def dot_t(a, b):
    return lax.dot_general(a, b, (((1,), (1,)), ((), ())), preferred_element_type=F32)


def t_dot(a, b):
    return lax.dot_general(a, b, (((0,), (0,)), ((), ())), preferred_element_type=F32)


def first_kernel(_, f1_ref, in_ref, out_ref):
    results = [
        dot_t(f1_ref[r], in_ref[:, r * 256 : (r + 1) * 256]).reshape(32, 8, 192) for r in range(2)
    ]
    out_ref[:, 0] = jnp.concatenate(results, axis=2).astype(BF)


def copy_kernel(_, in_ref, out_ref):
    out_ref[...] = in_ref[...]


def copy_three_kernel(_, *refs):
    for j in range(3):
        refs[3 + j][...] = refs[j][...]


def put_rows(refs, row, value):
    for j, ref in enumerate(refs):
        ref[row : row + value.shape[0], :] = value[:, j * 128 : (j + 1) * 128]


def put_position(refs, a, value):
    for j, ref in enumerate(refs):
        ref[pl.ds(a, 256, stride=8), :] = value[:, j * 128 : (j + 1) * 128]


def take_position(refs, a):
    parts = [ref[pl.ds(a, 256, stride=8), :] for ref in refs]
    return jnp.concatenate(parts, axis=1).astype(BF)


def second_kernel(_, piece_ref, f2_ref, out_ref, first_ref, *scratch):
    cols, result = scratch[:3], scratch[3:]
    for s in range(16):
        for pair in range(8):
            low, high = (piece_ref[2 * s + h, pair].astype(F32) for h in range(2))
            row = (s * 16 + pair * 2) * 8
            put_rows(cols, row, jnp.concatenate([low[:, :192], high[:, :192]], axis=1))
            put_rows(cols, row + 8, jnp.concatenate([low[:, 192:], high[:, 192:]], axis=1))
    for a in range(8):
        first = take_position(cols, a)
        first_ref[a] = first
        put_position(result, a, dot(f2_ref[a], first))
    write_blocks(result, out_ref)


def first_grad_kernel(_, piece_ref, f2_ref, out_ref, grad_ref, *scratch):
    cols, result = scratch[:3], scratch[3:]
    for dev in range(32):
        s, h = dev // 2, dev % 2
        for x in range(4):
            row = (s * 16 + x * 4 + h * 2) * 8
            put_rows(cols, row, piece_ref[dev, 2 * x : 2 * x + 2].astype(F32).reshape(16, DB))
    for a in range(8):
        grad = take_position(cols, a)
        grad_ref[a] = grad
        put_position(result, a, t_dot(f2_ref[a], grad))
    write_blocks(result, out_ref)


def write_blocks(result, out_ref):
    for dev in range(32):
        s, h = dev // 2, dev % 2
        for x in range(4):
            row = (s * 16 + x * 4 + h * 2) * 8
            value = jnp.concatenate([ref[row : row + 16, :] for ref in result], axis=1)
            out_ref[dev, 2 * x : 2 * x + 2] = value.reshape(2, 8, DB).astype(BF)


def gating_kernel(s_ref, own_ref, got_ref, second_ref, win_ref, in_ref, resid_ref, pgate_ref, sum_ref):
    zh = s_ref[0]
    own, got = own_ref[...], got_ref[...]
    first_half = jnp.where(zh == 0, own, got)
    second_half = jnp.where(zh == 0, got, own)
    value = jnp.transpose(jnp.concatenate([first_half, second_half], axis=0))
    in_ref[...] = value
    pgate = dot(value, win_ref[...]).astype(BF)
    pgate_ref[...] = pgate
    value_f = value.astype(F32)
    silu_in = value_f * jax.nn.sigmoid(value_f)
    resid = (value_f + read_pieces(second_ref) * pgate.astype(F32) * silu_in).astype(BF)
    resid_ref[...] = resid
    resid_f = resid.astype(F32)

    @pl.when(pl.program_id(0) == 0)
    def _():
        sum_ref[...] = jnp.zeros_like(sum_ref)

    put_row(sum_ref, pl.program_id(0), row_sums(resid_f * resid_f))


def mlp_kernel(s_ref, resid_ref, gain_ref, wg_ref, wu_ref, wd_ref, *refs):
    squares, cots = refs[:4], refs[4:8]
    cot_ref, normed_ref, hidden_ref, grads_ref, gnormed_ref, inner_ref = refs[8:14]
    mixed_refs = refs[14:18]
    step = pl.program_id(0)
    chunk = lax.rem(s_ref[1] + step, 4)
    for j in range(4):

        @pl.when(step == j)
        def _(j=j):
            cot_ref[...] = cots[j][...]

    cot = cot_ref[...]
    resid_f = resid_ref[...].astype(F32)
    rstd = as_column(lax.rsqrt(row_of(squares, chunk) * (1.0 / D) + 1e-06))
    gain = gain_ref[...]
    scaled_resid = resid_f * rstd
    normed = (scaled_resid * gain).astype(BF)
    normed_ref[...] = normed
    gate = dot(normed, wg_ref[...])
    upper = dot(normed, wu_ref[...])
    g_hidden = dot_t(cot, wd_ref[...])
    sig = jax.nn.sigmoid(gate)
    act = gate * sig
    hidden = (act * upper).astype(BF)
    hidden_ref[...] = hidden
    g_gate = (g_hidden * upper * sig * (1.0 + gate * (1.0 - sig))).astype(BF)
    g_up = (g_hidden * act).astype(BF)
    grads_ref[:, :768] = g_gate
    grads_ref[:, 768:] = g_up
    mixed = (resid_f + dot(hidden, wd_ref[...])).astype(BF)
    for j in range(4):

        @pl.when(step == j)
        def _(j=j):
            mixed_refs[j][...] = mixed

    g_normed = dot_t(g_gate, wg_ref[...]) + dot_t(g_up, wu_ref[...])
    gnormed_ref[...] = g_normed

    @pl.when(step == 0)
    def _():
        inner_ref[...] = jnp.zeros_like(inner_ref)

    put_row(inner_ref, chunk, row_sums(g_normed * gain * resid_f))
    inner_ref[4:5, :DB] += jnp.sum(g_normed * scaled_resid, axis=0, keepdims=True)


def resid_grad_kernel(
    _, resid_ref, cot_ref, gain_ref, gnormed_ref, in_ref, pgate_ref, *refs
):
    squares, inners, (g_resid_ref, g_second_ref) = refs[:4], refs[4:8], refs[8:]
    step = pl.program_id(0)
    rstd_row = lax.rsqrt(row_of(squares, step) * (1.0 / D) + 1e-06)
    rstd = as_column(rstd_row)
    factor = as_column(rstd_row * rstd_row * rstd_row * (row_of(inners, step) * (1.0 / D)))
    scaled = gnormed_ref[...] * gain_ref[...]
    g_resid = (
        cot_ref[...].astype(F32) + rstd * scaled - resid_ref[...].astype(F32) * factor
    ).astype(BF)
    g_resid_ref[...] = g_resid
    value = in_ref[...].astype(F32)
    silu_in = value * jax.nn.sigmoid(value)
    g_second = (g_resid.astype(F32) * pgate_ref[...].astype(F32) * silu_in).astype(BF)
    for r in range(2):
        g_second_ref[:, r] = g_second[r * 256 : (r + 1) * 256].reshape(32, 8, DB)


def direct_kernel(_, g_resid_ref, in_ref, second_ref, pgate_ref, win_ref, g_direct_ref, term_ref):
    resid_grad = g_resid_ref[...].astype(F32)
    value = in_ref[...].astype(F32)
    sig = jax.nn.sigmoid(value)
    second = read_pieces(second_ref)
    g_pgate = (resid_grad * second * (value * sig)).astype(BF)
    slope = sig * (1.0 + value * (1.0 - sig))
    through = dot_t(g_pgate, win_ref[...])
    g_direct_ref[...] = jnp.transpose(
        (resid_grad * (1.0 + second * pgate_ref[...].astype(F32) * slope) + through).astype(BF)
    )
    term = t_dot(in_ref[...], g_pgate)

    @pl.when(pl.program_id(0) == 0)
    def _():
        term_ref[...] = jnp.zeros_like(term_ref)

    term_ref[...] += term


def put_terms(s_ref, term, scratch, refs, slot):
    scratch[...] = term * (1.0 / math.sqrt(D))
    for j in range(4):
        start = pl.multiple_of(lax.rem(s_ref[1] + j, 4) * 64, 64)
        refs[j][slot] = scratch[pl.ds(start, 64), :].astype(BF)


def term_two_kernel(s_ref, grad_ref, first_ref, *refs):
    for a in range(2):
        put_terms(s_ref, dot_t(grad_ref[a], first_ref[a]), refs[4], refs[:4], a)


def term_one_kernel(s_ref, g_first_ref, in_ref, *refs):
    for r in range(2):
        g_first = g_first_ref[:, r].reshape(256, DB)
        term = dot_t(g_first, in_ref[r * 256 : (r + 1) * 256])
        put_terms(s_ref, term, refs[4], refs[:4], r)


def factor_sum_kernel(s_ref, a_ref, b_ref, c_ref, d_ref, own_ref, give_ref):
    zh = s_ref[0]
    total = (
        a_ref[...].astype(F32) + b_ref[...].astype(F32)
        + c_ref[...].astype(F32) + d_ref[...].astype(F32)
    )
    low, high = total[:, :32], total[:, 32:]
    own_ref[...] = jnp.where(zh == 0, low, high)
    give_ref[...] = jnp.where(zh == 0, high, low).astype(BF)


def factor_join_kernel(s_ref, own_ref, got_ref, out_ref):
    zh = s_ref[0]
    own, got = own_ref[...], got_ref[...].astype(F32)
    out_ref[:, 0] = jnp.where(zh == 0, own, got)
    out_ref[:, 1] = jnp.where(zh == 0, got, own)


def back_kernel(s_ref, g_first_ref, f1_ref, direct_ref, own_ref, give_ref):
    zh = s_ref[0]
    for r in range(2):
        here = slice(r * 256, (r + 1) * 256)
        back = t_dot(g_first_ref[:, r].reshape(256, DB), f1_ref[0, r])
        total = direct_ref[:, here].astype(F32) + back
        low, high = total[:192], total[192:]
        own_ref[:, here] = jnp.where(zh == 0, low, high).astype(BF)
        give_ref[:, here] = jnp.where(zh == 0, high, low).astype(BF)


def join_kernel(s_ref, own_ref, got_ref, out_ref):
    zh = s_ref[0]
    own, got = own_ref[...], got_ref[...]
    out_ref[:, :512] = jnp.where(zh == 0, own, got)
    out_ref[:, 512:] = jnp.where(zh == 0, got, own)


def mixed_join_kernel(s_ref, *refs):
    for j in range(4):
        start = pl.multiple_of(lax.rem(s_ref[1] + 4 - j, 4) * DB, DB)
        refs[4][:, pl.ds(start, DB)] = refs[j][...]


def payload_kernel(_, wg_ref, wu_ref, win_ref, wd_ref, out_ref):
    down = wd_ref[...].astype(F32)
    out_ref[:, :768] = wg_ref[...]
    out_ref[:, 768:1536] = wu_ref[...]
    out_ref[:, 1536:1920] = win_ref[...]
    out_ref[:, 1920:2304] = down[:12].astype(BF)
    out_ref[:, 2304:] = down[12:].astype(BF)


def gather_kernel(_, *refs):
    for j in range(4):
        refs[4][:, j * 512 : (j + 1) * 512] = refs[j][...]


def stack_kernel(_, *refs):
    for j in range(4):

        @pl.when(pl.program_id(0) == j)
        def _(j=j):
            refs[4][...] = refs[j][...]


def weights_kernel(s_ref, own_ref, across_ref, wg_ref, wu_ref, win_ref, wd_ref, half, down):
    mine = pl.program_id(0) == s_ref[4]
    for shard in range(16):
        value = jnp.where(mine, own_ref[shard], across_ref[shard]).astype(F32)
        half[shard * 12 : shard * 12 + 12, :] = value[:, :1920]
        down[shard * 24 : shard * 24 + 12, :] = value[:, 1920:2304]
        down[shard * 24 + 12 : shard * 24 + 24, :] = value[:, 2304:]
    wg_ref[...] = half[:, :768].astype(BF)
    wu_ref[...] = half[:, 768:1536].astype(BF)
    win_ref[...] = half[:, 1536:].astype(BF)
    wd_ref[...] = down[...].astype(BF)


def weight_grad_kernel(
    s_ref, normed_ref, grads_ref, hidden_ref, cot_ref, entry_ref, gain_ref, keep_ref, give_ref,
    across, down,
):
    step = pl.program_id(0)

    @pl.when(step == 0)
    def _():
        across[...] = jnp.zeros_like(across)
        down[...] = jnp.zeros_like(down)

    across[...] += t_dot(normed_ref[...], grads_ref[...])
    down[...] += t_dot(hidden_ref[...], cot_ref[...])

    @pl.when(step == pl.num_programs(0) - 1)
    def _():
        for ref, core in ((keep_ref, s_ref[4]), (give_ref, 1 - s_ref[4])):
            start = pl.multiple_of(core * 192, 192)
            start_down = pl.multiple_of(core * 384, 384)
            gates = across[pl.ds(start, 192), :]
            entries = entry_ref[pl.ds(start, 192), :]
            downs = down[pl.ds(start_down, 384), :]
            for shard in range(16):
                here = slice(shard * 12, shard * 12 + 12)
                at = shard * 24
                block = jnp.concatenate(
                    [gates[here], entries[here], downs[at : at + 12], downs[at + 12 : at + 24]],
                    axis=1,
                )
                ref[shard] = jnp.concatenate([block, gain_ref[...]], axis=0).astype(BF)


def pair_kernel(_, a_ref, b_ref, out_ref):
    out_ref[...] = (a_ref[...].astype(F32) + b_ref[...].astype(F32)).astype(BF)


def turn(axis, size, step):
    return [(i, (i + step) % size) for i in range(size)]


def around(value, axis):
    return [value] + [lax.ppermute(value, axis, turn(axis, 4, -j)) for j in (1, 2, 3)]


def in_order(parts, me):
    size = parts[0].shape[0]
    return lax.dynamic_slice_in_dim(
        jnp.concatenate(parts + parts, axis=0), lax.rem(4 - me, 4) * size, 4 * size, 0
    )


def send_each(parts, axis):
    return [parts[0]] + [lax.ppermute(parts[j], axis, turn(axis, 4, j)) for j in (1, 2, 3)]


Z_RING = ("zl", "zh")


def per_device(
    inputs, factor_one, factor_two, w_input_gate, norm_gain, w_gate, w_up, w_down, grad_out
):
    tok_scale = 1.0 / math.sqrt(SEQL)
    zh = lax.axis_index("zh")
    xi = lax.axis_index("x")
    yi = lax.axis_index("y")
    core = lax.axis_index("core")
    zi = lax.axis_index("zl") * 2 + zh
    at = jnp.stack([zh, xi, yi, zi, core]).astype(jnp.int32)
    bf = lambda *shape: jax.ShapeDtypeStruct(shape, BF)
    f32 = lambda *shape: jax.ShapeDtypeStruct(shape, F32)
    turned_in = inputs.T

    give = call(
        gather_kernel, (1,),
        [pl.BlockSpec((192, 512), lambda t, s, q=q: (0, 2 * q + 1 - s[0])) for q in range(4)],
        whole(192, 2048), bf(192, 2048), (1, 1),
    )(at, *[turned_in] * 4)
    other = lax.ppermute(give, "zh", SWAP)

    payload = call(
        payload_kernel, (1,),
        [whole(12, 768), whole(12, 768), whole(12, DB), whole(24, DB)],
        whole(12, 2688), bf(12, 2688), (1, 1),
    )(at, w_gate, w_up, w_input_gate, w_down)
    payload = lax.ppermute(payload, ALL, shard_moves())
    payload = jnp.broadcast_to(payload, (16, 12, 2688))
    payload, turned_in = lax.optimization_barrier((payload, turned_in))
    payload = lax.all_to_all(payload, ("zl", "y", "zh"), split_axis=0, concat_axis=0, tiled=True)

    first_local = call(
        first_kernel, (8,),
        [pl.BlockSpec((2, 256, 256), lambda t, s: (t, 0, 0)), columns(192)],
        pl.BlockSpec((32, 1, 8, DB), lambda t, s: (0, t, 0, 0)),
        bf(32, 8, 8, DB),
        (12_000_000_000, 6_000_000),
    )(at, factor_one, turned_in)
    first_local, other, payload, turned_in, grad_out, factor_two = lax.optimization_barrier(
        (first_local, other, payload, turned_in, grad_out, factor_two)
    )
    piece = lax.all_to_all(first_local, PLANE, split_axis=0, concat_axis=0, tiled=True)
    across = lax.ppermute(payload, "core", SWAP)
    wg, wu, win, wd = call(
        weights_kernel, (2,), [whole(16, 12, 2688)] * 2,
        [rows(768, 192), rows(768, 192), rows(DB, 192), rows(DB, 384)],
        [bf(DB, 768), bf(DB, 768), bf(DB, DB), bf(768, DB)], (1, 1),
        [pltpu.VMEM((192, 1920), F32), pltpu.VMEM((384, DB), F32)],
    )(at, payload, across)
    gain = lax.dynamic_slice_in_dim(norm_gain, xi * DB, DB, 0).reshape(1, DB)

    to_send = call(
        copy_three_kernel, (1,),
        [pl.BlockSpec((512, DB), lambda t, s, j=j: (0, lax.rem(s[1] + 4 - j, 4))) for j in (1, 2, 3)],
        [whole(512, DB)] * 3, [bf(512, DB)] * 3, (1, 1),
    )(at, grad_out, grad_out, grad_out)
    cots = [lax.ppermute(to_send[j - 1], "x", turn("x", 4, -j)) for j in (1, 2, 3)]
    f2 = lax.dynamic_slice_in_dim(factor_two, zh * 8, 8, 0)

    wide = [pltpu.VMEM((2048, 128), F32)] * 6
    all_pieces = whole(32, 8, 8, DB)
    second_cols, first_cols = call(
        second_kernel, (1,),
        [all_pieces, whole(8, 256, 256)],
        [all_pieces, whole(8, 256, DB)],
        [bf(32, 8, 8, DB), bf(8, 256, DB)],
        (400_000_000, 6_000_000), wide,
    )(at, piece, f2)
    second = lax.all_to_all(second_cols, PLANE, split_axis=0, concat_axis=0, tiled=True)

    input_mlp, resid, pgate, square = call(
        gating_kernel, (4,),
        [pl.BlockSpec((192, 512), lambda t, s: (0, 2 * t + s[0])), columns(192), PIECES, whole(DB, DB)],
        [rows(DB), rows(DB), rows(DB), whole(8, 512)],
        [bf(2048, DB), bf(2048, DB), bf(2048, DB), f32(8, 512)],
        (600_000_000, 10_000_000),
    )(at, turned_in, other, second, win)
    squares = around(square, "x")
    own_cot = pl.BlockSpec((512, DB), lambda t, s: (0, s[1]))
    cot, normed, hidden, grads, g_normed, inner, *mixed = call(
        mlp_kernel, (4,),
        [turned_rows(DB), whole(1, DB), whole(DB, 768), whole(DB, 768), whole(768, DB)]
        + SUMS + [own_cot] + [whole(512, DB)] * 3,
        [turned_rows(DB), turned_rows(DB), turned_rows(768), turned_rows(1536), turned_rows(DB), whole(8, 512)]
        + [whole(512, DB)] * 4,
        [bf(2048, DB), bf(2048, DB), bf(2048, 768), bf(2048, 1536), f32(2048, DB), f32(8, 512)]
        + [bf(512, DB)] * 4,
        (7_300_000_000, 24_000_000),
    )(at, resid, gain, wg, wu, wd, *squares, grad_out, *cots)
    inners = around(inner, "x")
    g_resid, g_second = call(
        resid_grad_kernel, (4,),
        [rows(DB), rows(DB), whole(1, DB), rows(DB), rows(DB), rows(DB)] + SUMS + SUMS,
        [rows(DB), PIECES],
        [bf(2048, DB), bf(32, 8, 8, DB)],
        (50_000_000, 12_000_000),
    )(at, resid, cot, gain, g_normed, input_mlp, pgate, *squares, *inners)
    g_second, normed, hidden, grads, cot, mixed, inners = lax.optimization_barrier(
        (g_second, normed, hidden, grads, cot, mixed, inners)
    )
    piece = lax.all_to_all(g_second, PLANE, split_axis=0, concat_axis=0, tiled=True)

    mixed = send_each(mixed, "x")
    mixed_out = call(
        mixed_join_kernel, (1,), [whole(512, DB)] * 4, whole(512, D),
        bf(512, D), (1, 1),
    )(at, *mixed)
    g_direct, term_entry = call(
        direct_kernel, (4,),
        [rows(DB), rows(DB), PIECES, rows(DB), whole(DB, DB)],
        [columns(DB), whole(DB, DB)],
        [bf(DB, 2048), f32(DB, DB)],
        (1, 1),
    )(at, g_resid, input_mlp, second, pgate, win)

    gain_terms = in_order([v[4:5, :DB] for v in inners], xi).reshape(1, D)
    gain_rows = jnp.pad(gain_terms, ((0, 3), (0, 2688 - D)))
    shards = whole(16, 16, 2688)
    keep, give = call(
        weight_grad_kernel, (4,),
        [rows(DB), rows(1536), rows(768), rows(DB), whole(DB, DB), whole(4, 2688)],
        [shards] * 2, [bf(16, 16, 2688)] * 2, (1, 1),
        [pltpu.VMEM((DB, 1536), F32), pltpu.VMEM((768, DB), F32)],
    )(at, normed, grads, hidden, cot, term_entry, gain_rows)
    got = lax.ppermute(give, "core", SWAP)
    quarter = pl.BlockSpec((8, 16, 2688), lambda t, s: (t, 0, 0))
    pair = call(pair_kernel, (2,), [quarter] * 2, quarter, bf(16, 16, 2688), (1, 1))(at, keep, got)

    piece, pair = lax.optimization_barrier((piece, pair))
    pair = lax.all_to_all(pair, ("zl", "y", "zh"), split_axis=0, concat_axis=0, tiled=True)

    first_grad, second_grad = call(
        first_grad_kernel, (1,),
        [all_pieces, whole(8, 256, 256)],
        [all_pieces, whole(8, 256, DB)],
        [bf(32, 8, 8, DB), bf(8, 256, DB)],
        (400_000_000, 6_000_000), wide,
    )(at, piece, f2)
    square_scratch = [pltpu.VMEM((256, 256), F32)]
    term_out = pl.BlockSpec((2, 64, 256), lambda t, s: (t, 0, 0))

    terms_two = call(
        term_two_kernel, (4,),
        [pl.BlockSpec((2, 256, DB), lambda t, s: (t, 0, 0))] * 2,
        [term_out] * 4, [bf(8, 64, 256)] * 4, (1, 1), square_scratch,
    )(at, second_grad, first_cols)
    first_grad, terms_two, pair, mixed_out = lax.optimization_barrier(
        (first_grad, terms_two, pair, mixed_out)
    )
    g_first = lax.all_to_all(first_grad, PLANE, split_axis=0, concat_axis=0, tiled=True)

    def factor_sums(terms):
        return call(
            factor_sum_kernel, (1,), [whole(8, 64, 256)] * 4, [whole(8, 32, 256)] * 2,
            [f32(8, 32, 256), bf(8, 32, 256)], (1, 1),
        )(at, *send_each(terms, "x"))

    def factor_gradient(sums, slots):
        own, give = sums
        got = lax.ppermute(give, "zh", SWAP)
        shape = (slots, 8 // slots, 32, 256)
        joined = call(
            factor_join_kernel, (1,), [whole(*shape)] * 2, whole(slots, 2, 8 // slots, 32, 256),
            f32(slots, 2, 8 // slots, 32, 256), (1, 1),
        )(at, own.reshape(shape), got.reshape(shape))
        return joined.reshape(16, 32, 256)

    sums_two = factor_sums(terms_two)

    summed = jnp.sum(pair.astype(F32), axis=0) * tok_scale
    back = [(there, here) for here, there in shard_moves()]
    own = lax.ppermute(summed[:12], ALL, back)
    g_first, own, sums_two = lax.optimization_barrier((g_first, own, sums_two))
    grad_w_gate, grad_w_up = own[:, :768], own[:, 768:1536]
    grad_w_input_gate = own[:, 1536:1920]
    grad_w_down = jnp.concatenate([own[:, 1920:2304], own[:, 2304:]], axis=0)
    grad_norm_gain = summed[12, :D]
    grad_factor_two = factor_gradient(sums_two, 1)

    own_grad, give_grad = call(
        back_kernel, (4,),
        [PIECES, pl.BlockSpec((1, 2, 256, 256), lambda t, s: (2 * t + s[0], 0, 0, 0)), columns(DB)],
        [columns(192), columns(192)],
        [bf(192, 2048), bf(192, 2048)],
        (400_000_000, 6_000_000),
    )(at, g_first, factor_one.reshape(8, 2, 256, 256), g_direct)
    g_first, give_grad = lax.optimization_barrier((g_first, give_grad))
    terms_one = call(
        term_one_kernel, (4,), [PIECES, rows(DB)],
        [term_out] * 4, [bf(8, 64, 256)] * 4, (1, 1), square_scratch,
    )(at, g_first, input_mlp)
    grad_factor_one = factor_gradient(factor_sums(terms_one), 4)

    got_grad = lax.ppermute(give_grad, "zh", SWAP)
    grad_inputs = call(
        join_kernel, (4,), [columns(192), columns(192)], columns(192, 1024), bf(192, 4096), (1, 1)
    )(at, own_grad, got_grad).T
    return (
        mixed_out,
        grad_inputs,
        grad_factor_one,
        grad_factor_two,
        grad_w_input_gate,
        grad_norm_gain,
        grad_w_gate,
        grad_w_up,
        grad_w_down,
    )


def solution(mesh):
    fine = Mesh(mesh.devices.reshape(SIZES), ALL)
    return jax.shard_map(
        per_device,
        mesh=fine,
        in_specs=(
            P(SEQ, CH),
            P(SEQ, None, None),
            P(SEQ, None, None),
            P(ALL, None),
            P(),
            P(ALL, None),
            P(ALL, None),
            P(ALL, None),
            P(ALL, None),
        ),
        out_specs=(
            P(ALL, None),
            P(SEQ, CH),
            P(SEQ, CH, None),
            P(SEQ, CH, None),
            P(ALL, None),
            P(),
            P(ALL, None),
            P(ALL, None),
            P(ALL, None),
        ),
        check_vma=False,
    )
```

time: 357 us -> 330 us (0.924)
  Pallas kernels: 76.9 us -> 119 us
  local copies, waits for them, and re-layouts: 47.2 us -> 20.2 us
  waiting for transfers between devices: 123 us -> 97.1 us
  other arithmetic: 14.7 us -> 0.82 us
  starting transfers between devices: 77.1 us -> 87.7 us
  matrix products: 10.5 us -> 0 us
    pallas_call x8 -> x18, Pallas kernels: 53.9 us -> 93.9 us  [the longest x1 19.9 us: per_device(): call(mlp_kernel, (4,), [turned_rows(DB), whole(1, DB), whole(DB, 768), wh...]
    ppermute x7 -> x21, waiting for transfers between devices: 1.51 us -> 38.7 us  [the longest x9 31 us: send_each(): lax.ppermute(parts[j], axis, turn(axis, 4, j))]
    ppermute x7 -> x21, starting transfers between devices: 11.2 us -> 37.4 us  [the longest x9 18.8 us: send_each(): lax.ppermute(parts[j], axis, turn(axis, 4, j))]
    all_to_all x4 -> x0, starting transfers between devices: 22.3 us -> none  [the longest x1 7.45 us: per_device(): lax.all_to_all(grad_out.reshape(512, 4, DB).transpose(1, 0, 2), 'x', spli...]
    ppermute x1, waiting for transfers between devices: 0.01 us -> 19.9 us  [per_device(): other = lax.ppermute(give, 'zh', SWAP)]
    all_to_all x4 -> x0, waiting for transfers between devices: 19.8 us -> none  [the longest x1 16.7 us: per_device(): lax.all_to_all(mixed, 'x', split_axis=0, concat_axis=0, tiled=True)]
    all_to_all x1, waiting for transfers between devices: 17 us -> 0.01 us  [per_device(): lax.all_to_all(pair, ('zl', 'y', 'zh'), split_axis=0, concat_axis=0, tile...]
    all_to_all x1, waiting for transfers between devices: 19.6 us -> 3.74 us  [per_device(): lax.all_to_all(first_grad, PLANE, split_axis=0, concat_axis=0, tiled=True)]
  transfers between devices with their start and end apart: 22 -> 32, of which waited for: 12 -> 18; matrix products, arithmetic and copies ran while one was open for 17% -> 3% of each run, Pallas kernels for 14% -> 23%
where the time goes in v3:
time: 330 us; the launch traced here: 326 us
  Pallas kernels  119 us (36%)
  waiting for transfers between devices  97.1 us (29%)
  starting transfers between devices  87.7 us (27%)
  local copies, waits for them, and re-layouts  20.2 us (6%)
    ppermute x9, waiting for transfers between devices, send_each(): lax.ppermute(parts[j], axis, turn(axis, 4, j))  31 us
    all_to_all x1, waiting for transfers between devices, per_device(): lax.all_to_all(first_local, PLANE, split_axis=0, concat_axis=0, tiled=True)  22.1 us
    ppermute x1, waiting for transfers between devices, per_device(): other = lax.ppermute(give, 'zh', SWAP)  19.9 us
    pallas_call x1, Pallas kernels, per_device(): call(mlp_kernel, (4,), [turned_rows(DB), whole(1, DB), whole(DB, 768), wh...  19.9 us
    ppermute x9, starting transfers between devices, send_each(): lax.ppermute(parts[j], axis, turn(axis, 4, j))  18.8 us
    ppermute x6, starting transfers between devices, around(): lax.ppermute(value, axis, turn(axis, 4, -j))  11.5 us
    pallas_call x1, Pallas kernels, per_device(): call(weight_grad_kernel, (4,), [rows(DB), rows(1536), rows(768), rows(DB)...  11 us
    unnamed x60, local copies, waits for them, and re-layouts  9.05 us
  transfers between devices with their start and end apart: 32, of which 18 were waited for; matrix products, arithmetic and copies ran while one was open for 3% of the time, Pallas kernels for 23%

profile of v3, /device:TPU:2, one launch (start us, length us, event | category | flops | bytes accessed | tf_op | source)
XLA Modules:
  0.0 326.1 jit_solution(10106602380851718975)
XLA Ops:
  9.7 3.9 %collective-permute-start.1 = (bf16[192,2048]{1,0:T(8,128)(2,1)}, bf16[192,2048]{1,0:T(8,128)(2,1)}, u32[]{:S(2)}, u32[]{:S(2)}) collective-permute-start(bf16[192,2048]{1,0:T(8,128)(2,1)} %gather_kernel.1), channel_id=1, source_target_pairs={{0,1},{1,0},{2,3},{3,2},{4,5},{5,4},{6,7},{7,6},{8,9},{9,8},{10,11... | collective-permute-start | bytes 2359304 | tf_op jit(solution)/shard_map/ppermute | solution.py:476
  14.8 7.5 %all-to-all-start = ((bf16[16,12,2688]{2,1,0:T(8,128)(2,1)}), bf16[16,12,2688]{2,1,0:T(8,128)(2,1)S(1)}, u32[]{:S(2)}, u32[]{:S(2)}) async-start(bf16[16,12,2688]{2,1,0:T(8,128)(2,1)} %broadcast_in_dim.3), calls=%async_computation | async-start | bytes 2752512 | tf_op jit(solution)/shard_map/all_to_all | solution.py:486
  22.3 7.6 %first_kernel.1 = bf16[32,8,8,384]{3,2,1,0:T(8,128)(2,1)} custom-call(s32[5]{0:T(128)} %stack.23._.s_ref, bf16[16,256,256]{2,1,0:T(8,128)(2,1)} %f1_ref.1, bf16[192,4096]{1,0:T(8,128)(2,1)} %bitcast.23), custom_call_target="tpu_custom_call" | custom-call | flops 12000000000 | bytes 6000000 | tf_op jit(solution)/shard_map/first_kernel/pallas_call | solution.py:488
  29.9 19.9 %collective-permute-done.1.got_ref = bf16[192,2048]{1,0:T(8,128)(2,1)} collective-permute-done((bf16[192,2048]{1,0:T(8,128)(2,1)}, bf16[192,2048]{1,0:T(8,128)(2,1)}, u32[]{:S(2)}, u32[]{:S(2)}) %collective-permute-start.1) | collective-permute-done | bytes 786464 | tf_op jit(solution)/shard_map/ppermute | solution.py:476
  49.8 3.6 %all-to-all-done.own_ref = bf16[16,12,2688]{2,1,0:T(8,128)(2,1)S(1)} async-done(((bf16[16,12,2688]{2,1,0:T(8,128)(2,1)}), bf16[16,12,2688]{2,1,0:T(8,128)(2,1)S(1)}, u32[]{:S(2)}, u32[]{:S(2)}) %all-to-all-start) | async-done | bytes 1032224 | tf_op jit(solution)/shard_map/all_to_all | solution.py:486
  53.4 5.7 %all-to-all-start.1 = ((bf16[32,8,8,384]{3,2,1,0:T(8,128)(2,1)}), bf16[32,8,8,384]{3,2,1,0:T(8,128)(2,1)}, u32[]{:S(2)}, u32[]{:S(2)}) async-start(bf16[32,8,8,384]{3,2,1,0:T(8,128)(2,1)} %first_kernel.1), calls=%async_computation.1 | async-start | bytes 3145728 | tf_op jit(solution)/shard_map/all_to_all | solution.py:498
  60.2 22.1 %all-to-all-done.1.piece_ref = bf16[32,8,8,384]{3,2,1,0:T(8,128)(2,1)} async-done(((bf16[32,8,8,384]{3,2,1,0:T(8,128)(2,1)}), bf16[32,8,8,384]{3,2,1,0:T(8,128)(2,1)}, u32[]{:S(2)}, u32[]{:S(2)}) %all-to-all-start.1) | async-done | bytes 1572896 | tf_op jit(solution)/shard_map/all_to_all | solution.py:498
  82.4 5.4 %second_kernel.1 = (bf16[32,8,8,384]{3,2,1,0:T(8,128)(2,1)}, bf16[8,256,384]{2,1,0:T(8,128)(2,1)}) custom-call(s32[5]{0:T(128)} %stack.23._.s_ref, bf16[32,8,8,384]{3,2,1,0:T(8,128)(2,1)} %all-to-all-done.1.piece_ref, bf16[8,256,256]{2,1,0:T(8,128)(2,1)} %constant_dynamic-slice_fusion.f2_ref), custom_call_target="tpu_custom_call" | custom-call | flops 400000000 | bytes 6000000 | tf_op jit(solution)/shard_map/second_kernel/pallas_call | solution.py:518
  87.8 4.1 %all-to-all-start.2 = ((bf16[32,8,8,384]{3,2,1,0:T(8,128)(2,1)}), bf16[32,8,8,384]{3,2,1,0:T(8,128)(2,1)S(1)}, u32[]{:S(2)}, u32[]{:S(2)}) async-start(bf16[32,8,8,384]{3,2,1,0:T(8,128)(2,1)} %get-tuple-element.96), calls=%async_computation.2 | async-start | bytes 3145728 | tf_op jit(solution)/shard_map/all_to_all | solution.py:525
  102.2 4.0 %weights_kernel.1 = (bf16[384,768]{1,0:T(8,128)(2,1)}, bf16[384,768]{1,0:T(8,128)(2,1)}, bf16[384,384]{1,0:T(8,128)(2,1)}, bf16[768,384]{1,0:T(8,128)(2,1)}) custom-call(s32[5]{0:T(128)} %stack.23._.s_ref, bf16[16,12,2688]{2,1,0:T(8,128)(2,1)} %copy-done.4, bf16[16,12,2688]{2,1,0:T(8,128)(2,1)} %copy.19.across_ref), custom_call_target="tpu_custom_call" | custom-call | flops 1 | bytes 1 | tf_op jit(solution)/shard_map/weights_kernel/pallas_call | solution.py:500
  106.1 9.0 %all-to-all-done.2.second_ref = bf16[32,8,8,384]{3,2,1,0:T(8,128)(2,1)S(1)} async-done(((bf16[32,8,8,384]{3,2,1,0:T(8,128)(2,1)}), bf16[32,8,8,384]{3,2,1,0:T(8,128)(2,1)S(1)}, u32[]{:S(2)}, u32[]{:S(2)}) %all-to-all-start.2) | async-done | bytes 1572896 | tf_op jit(solution)/shard_map/all_to_all | solution.py:525
  116.3 6.7 %gating_kernel.1 = (bf16[2048,384]{1,0:T(8,128)(2,1)}, bf16[2048,384]{1,0:T(8,128)(2,1)}, bf16[2048,384]{1,0:T(8,128)(2,1)}, f32[8,512]{1,0:T(8,128)}) custom-call(s32[5]{0:T(128)} %stack.23._.s_ref, bf16[192,4096]{1,0:T(8,128)(2,1)} %bitcast.24, bf16[192,2048]{1,0:T(8,128)(2,1)} %collective-permute-done.1.got_ref, bf16[32,8,8,384]{3,2,1,0:T(8,128)(2,1)} %copy-done.2, ...), custom_call_target="tpu_custom_call" | custom-call | flops 600000000 | bytes 10000000 | tf_op jit(solution)/shard_map/gating_kernel/pallas_call | solution.py:527
  130.7 19.9 %mlp_kernel.1 = (bf16[2048,384]{1,0:T(8,128)(2,1)}, bf16[2048,384]{1,0:T(8,128)(2,1)}, bf16[2048,768]{1,0:T(8,128)(2,1)}, bf16[2048,1536]{1,0:T(8,128)(2,1)}, f3...) custom-call(s32[5]{0:T(128)} %stack.23._.s_ref, ...), custom_call_target="tpu_custom_call" | custom-call | flops 7299999744 | bytes 24000000 | tf_op jit(solution)/shard_map/mlp_kernel/pallas_call | solution.py:536
  159.6 7.3 %resid_grad_kernel.1 = (bf16[2048,384]{1,0:T(8,128)(2,1)}, bf16[32,8,8,384]{3,2,1,0:T(8,128)(2,1)}) custom-call(s32[5]{0:T(128)} %stack.23._.s_ref, bf16[2048,384]{1,0:T(8,128)(2,1)} %get-tuple-element.99.resid_ref, bf16[2048,384]{1,0:T(8,128)(2,1)} %get-tuple-element.125.cot_ref, f32[1,384]{1,0:T(1,128)} %reshape.45.gain_ref, ...), custom_call_target="tpu_custom_call" | custom-call | flops 50000000 | bytes 12000000 | tf_op jit(solution)/shard_map/resid_grad_kernel/pallas_call | solution.py:547
  167.0 4.1 %all-to-all-start.3 = ((bf16[32,8,8,384]{3,2,1,0:T(8,128)(2,1)}), bf16[32,8,8,384]{3,2,1,0:T(8,128)(2,1)S(1)}, u32[]{:S(2)}, u32[]{:S(2)}) async-start(bf16[32,8,8,384]{3,2,1,0:T(8,128)(2,1)} %get-tuple-element.121), calls=%async_computation.3 | async-start | bytes 3145728 | tf_op jit(solution)/shard_map/all_to_all | solution.py:557
  171.1 7.1 %direct_kernel.1 = (bf16[384,2048]{1,0:T(8,128)(2,1)}, f32[384,384]{1,0:T(8,128)}) custom-call(s32[5]{0:T(128)} %stack.23._.s_ref, bf16[2048,384]{1,0:T(8,128)(2,1)} %get-tuple-element.126.g_resid_ref, bf16[2048,384]{1,0:T(8,128)(2,1)} %get-tuple-element.110.in_ref, bf16[32,8,8,384]{3,2,1,0:T(8,128)(2,1)} %copy-done.2, ...), custom_call_target="tpu_custom_call" | custom-call | flops 1 | bytes 1 | tf_op jit(solution)/shard_map/direct_kernel/pallas_call | solution.py:564
  181.7 11.0 %weight_grad_kernel.1 = (bf16[16,16,2688]{2,1,0:T(8,128)(2,1)}, bf16[16,16,2688]{2,1,0:T(8,128)(2,1)}) custom-call(s32[5]{0:T(128)} %stack.23._.s_ref, bf16[2048,384]{1,0:T(8,128)(2,1)} %get-tuple-element.122.normed_ref, bf16[2048,1536]{1,0:T(8,128)(2,1)} %get-tuple-element.123.grads_ref, bf16[2048,768]{1,0:T(8,128)(2,1)} %get-tuple-element.124.hidden_ref, ...), custom_call_target="tpu_custom_call" | custom-call | flops 1 | bytes 1 | tf_op jit(solution)/shard_map/weight_grad_kernel/pallas_call | solution.py:575
  200.5 7.1 %all-to-all-start.4 = ((bf16[16,16,2688]{2,1,0:T(8,128)(2,1)}), bf16[16,16,2688]{2,1,0:T(8,128)(2,1)S(1)}, u32[]{:S(2)}, u32[]{:S(2)}) async-start(bf16[16,16,2688]{2,1,0:T(8,128)(2,1)} %pair_kernel.1), calls=%async_computation.4 | async-start | bytes 2752512 | tf_op jit(solution)/shard_map/all_to_all | solution.py:586
  212.5 7.4 %collective-permute-done.13.refs_1_ = bf16[512,384]{1,0:T(8,128)(2,1)S(1)} collective-permute-done((bf16[512,384]{1,0:T(8,128)(2,1)}, bf16[512,384]{1,0:T(8,128)(2,1)S(1)}, u32[]{:S(2)}, u32[]{:S(2)}) %collective-permute-start.13) | collective-permute-done | bytes 393248 | tf_op jit(solution)/shard_map/ppermute | solution.py:451
  222.5 7.0 %collective-permute-done.15.refs_3_ = bf16[512,384]{1,0:T(8,128)(2,1)S(1)} collective-permute-done((bf16[512,384]{1,0:T(8,128)(2,1)}, bf16[512,384]{1,0:T(8,128)(2,1)S(1)}, u32[]{:S(2)}, u32[]{:S(2)}) %collective-permute-start.15) | collective-permute-done | bytes 393248 | tf_op jit(solution)/shard_map/ppermute | solution.py:451
  233.5 5.4 %first_grad_kernel.1 = (bf16[32,8,8,384]{3,2,1,0:T(8,128)(2,1)}, bf16[8,256,384]{2,1,0:T(8,128)(2,1)}) custom-call(s32[5]{0:T(128)} %stack.23._.s_ref, bf16[32,8,8,384]{3,2,1,0:T(8,128)(2,1)} %copy-done.5, bf16[8,256,256]{2,1,0:T(8,128)(2,1)} %constant_dynamic-slice_fusion.f2_ref), custom_call_target="tpu_custom_call" | custom-call | flops 400000000 | bytes 6000000 | tf_op jit(solution)/shard_map/first_grad_kernel/pallas_call | solution.py:588
  238.9 5.1 %term_two_kernel.1 = (bf16[8,64,256]{2,1,0:T(8,128)(2,1)}, bf16[8,64,256]{2,1,0:T(8,128)(2,1)}, bf16[8,64,256]{2,1,0:T(8,128)(2,1)}, bf16[8,64,256]{2,1,0:T(8,128)(2,1)}) custom-call(s32[5]{0:T(128)} %stack.23._.s_ref, bf16[8,256,384]{2,1,0:T(8,128)(2,1)} %get-tuple-element.136.grad_ref, bf16[8,256,384]{2,1,0:T(8,128)(2,1)} %get-tuple-element.137.first_ref), custom_call_target="tpu_custom_call" | custom-call | flops 1 | bytes 1 | tf_op jit(solution)/shard_map/term_two_kernel/pallas_call | solution.py:598
  244.0 7.2 %all-to-all-start.5 = ((bf16[32,8,8,384]{3,2,1,0:T(8,128)(2,1)}), bf16[32,8,8,384]{3,2,1,0:T(8,128)(2,1)S(1)}, u32[]{:S(2)}, u32[]{:S(2)}) async-start(bf16[32,8,8,384]{3,2,1,0:T(8,128)(2,1)} %get-tuple-element.148), calls=%async_computation.5 | async-start | bytes 3145728 | tf_op jit(solution)/shard_map/all_to_all | solution.py:606
  256.7 4.7 %collective-permute-start.16 = (f32[12,2688]{1,0:T(8,128)S(1)}, f32[12,2688]{1,0:T(8,128)S(1)}, u32[]{:S(2)}, u32[]{:S(2)}) collective-permute-start(f32[12,2688]{1,0:T(8,128)S(1)} %bitcast.31), channel_id=1, source_target_pairs={{0,0},{1,1},{16,2},{17,3},{32,4},{33,5},{48,6},{49,7},{64,8},{65,9... | collective-permute-start | bytes 387080 | tf_op jit(solution)/shard_map/ppermute | solution.py:628
  262.8 4.6 %collective-permute-done.19.d_ref = bf16[8,64,256]{2,1,0:T(8,128)(2,1)S(1)} collective-permute-done((bf16[8,64,256]{2,1,0:T(8,128)(2,1)}, bf16[8,64,256]{2,1,0:T(8,128)(2,1)S(1)}, u32[]{:S(2)}, u32[]{:S(2)}) %collective-permute-start.19) | collective-permute-done | bytes 262176 | tf_op jit(solution)/shard_map/ppermute | solution.py:451
  270.9 3.7 %all-to-all-done.5.g_first_ref = bf16[32,8,8,384]{3,2,1,0:T(8,128)(2,1)S(1)} async-done(((bf16[32,8,8,384]{3,2,1,0:T(8,128)(2,1)}), bf16[32,8,8,384]{3,2,1,0:T(8,128)(2,1)S(1)}, u32[]{:S(2)}, u32[]{:S(2)}) %all-to-all-start.5) | async-done | bytes 1572896 | tf_op jit(solution)/shard_map/all_to_all | solution.py:606
  275.7 5.4 %back_kernel.1 = (bf16[192,2048]{1,0:T(8,128)(2,1)}, bf16[192,2048]{1,0:T(8,128)(2,1)}) custom-call(s32[5]{0:T(128)} %stack.23._.s_ref, bf16[32,8,8,384]{3,2,1,0:T(8,128)(2,1)} %copy-done.3, bf16[8,2,256,256]{3,2,1,0:T(8,128)(2,1)} %bitcast.25, bf16[384,2048]{1,0:T(8,128)(2,1)} %get-tuple-element.157.direct_ref), custom_call_target="tpu_custom_call" | custom-call | flops 400000000 | bytes 6000000 | tf_op jit(solution)/shard_map/back_kernel/pallas_call | solution.py:636
  283.4 5.1 %term_one_kernel.1 = (bf16[8,64,256]{2,1,0:T(8,128)(2,1)}, bf16[8,64,256]{2,1,0:T(8,128)(2,1)}, bf16[8,64,256]{2,1,0:T(8,128)(2,1)}, bf16[8,64,256]{2,1,0:T(8,128)(2,1)}) custom-call(s32[5]{0:T(128)} %stack.23._.s_ref, bf16[32,8,8,384]{3,2,1,0:T(8,128)(2,1)} %copy-done.3, bf16[2048,384]{1,0:T(8,128)(2,1)} %get-tuple-element.110.in_ref), custom_call_target="tpu_custom_call" | custom-call | flops 1 | bytes 1 | tf_op jit(solution)/shard_map/term_one_kernel/pallas_call | solution.py:644
  288.6 3.9 %collective-permute-start.21 = (bf16[8,64,256]{2,1,0:T(8,128)(2,1)}, bf16[8,64,256]{2,1,0:T(8,128)(2,1)S(1)}, u32[]{:S(2)}, u32[]{:S(2)}) collective-permute-start(bf16[8,64,256]{2,1,0:T(8,128)(2,1)} %get-tuple-element.163), channel_id=1, source_target_pairs={{0,2},{2,4},{4,6},{6,0},{1,3},{3,5},{5,7},{7,1},{8,10},{10,12},{12... | collective-permute-start | bytes 786440 | tf_op jit(solution)/shard_map/ppermute | solution.py:451
  299.0 4.4 %collective-permute-done.22.c_ref = bf16[8,64,256]{2,1,0:T(8,128)(2,1)S(1)} collective-permute-done((bf16[8,64,256]{2,1,0:T(8,128)(2,1)}, bf16[8,64,256]{2,1,0:T(8,128)(2,1)S(1)}, u32[]{:S(2)}, u32[]{:S(2)}) %collective-permute-start.22) | collective-permute-done | bytes 262176 | tf_op jit(solution)/shard_map/ppermute | solution.py:451
  303.5 3.7 %collective-permute-done.23.d_ref = bf16[8,64,256]{2,1,0:T(8,128)(2,1)S(1)} collective-permute-done((bf16[8,64,256]{2,1,0:T(8,128)(2,1)}, bf16[8,64,256]{2,1,0:T(8,128)(2,1)S(1)}, u32[]{:S(2)}, u32[]{:S(2)}) %collective-permute-start.23) | collective-permute-done | bytes 262176 | tf_op jit(solution)/shard_map/ppermute | solution.py:451
  321.8 4.3 %join_kernel.1 = bf16[192,4096]{1,0:T(8,128)(2,1)} custom-call(s32[5]{0:T(128)} %stack.23._.s_ref, bf16[192,2048]{1,0:T(8,128)(2,1)} %get-tuple-element.158.own_ref, bf16[192,2048]{1,0:T(8,128)(2,1)} %copy-done.7), custom_call_target="tpu_custom_call" | custom-call | flops 1 | bytes 1 | tf_op jit(solution)/shard_map/join_kernel/pallas_call | solution.py:651
  (133 shorter events, 97.3 us)
Async XLA Ops:
  3.4 10.2 %collective-permute-start = (bf16[12,2688]{1,0:T(8,128)(2,1)}, bf16[12,2688]{1,0:T(8,128)(2,1)S(1)}, u32[]{:S(2)}, u32[]{:S(2)}) collective-permute-start(bf16[12,2688]{1,0:T(8,128)(2,1)} %payload_kernel.1), channel_id=1, source_target_pairs={{0,0},{1,1},{2,16},{3,17},{4,32},{5,33},{6,48},{7,49},{8,64},{9,65... | collective-permute-start | bytes 193544 | tf_op jit(solution)/shard_map/ppermute | solution.py:483
  9.7 40.1 %collective-permute-start.1 = (bf16[192,2048]{1,0:T(8,128)(2,1)}, bf16[192,2048]{1,0:T(8,128)(2,1)}, u32[]{:S(2)}, u32[]{:S(2)}) collective-permute-start(bf16[192,2048]{1,0:T(8,128)(2,1)} %gather_kernel.1), channel_id=1, source_target_pairs={{0,1},{1,0},{2,3},{3,2},{4,5},{5,4},{6,7},{7,6},{8,9},{9,8},{10,11... | collective-permute-start | bytes 2359304 | tf_op jit(solution)/shard_map/ppermute | solution.py:476
  14.8 38.6 %all-to-all-start = ((bf16[16,12,2688]{2,1,0:T(8,128)(2,1)}), bf16[16,12,2688]{2,1,0:T(8,128)(2,1)S(1)}, u32[]{:S(2)}, u32[]{:S(2)}) async-start(bf16[16,12,2688]{2,1,0:T(8,128)(2,1)} %broadcast_in_dim.3), calls=%async_computation | async-start | bytes 2752512 | tf_op jit(solution)/shard_map/all_to_all | solution.py:486
  53.4 29.0 %all-to-all-start.1 = ((bf16[32,8,8,384]{3,2,1,0:T(8,128)(2,1)}), bf16[32,8,8,384]{3,2,1,0:T(8,128)(2,1)}, u32[]{:S(2)}, u32[]{:S(2)}) async-start(bf16[32,8,8,384]{3,2,1,0:T(8,128)(2,1)} %first_kernel.1), calls=%async_computation.1 | async-start | bytes 3145728 | tf_op jit(solution)/shard_map/all_to_all | solution.py:498
  87.8 27.4 %all-to-all-start.2 = ((bf16[32,8,8,384]{3,2,1,0:T(8,128)(2,1)}), bf16[32,8,8,384]{3,2,1,0:T(8,128)(2,1)S(1)}, u32[]{:S(2)}, u32[]{:S(2)}) async-start(bf16[32,8,8,384]{3,2,1,0:T(8,128)(2,1)} %get-tuple-element.96), calls=%async_computation.2 | async-start | bytes 3145728 | tf_op jit(solution)/shard_map/all_to_all | solution.py:525
  92.1 8.8 %collective-permute-start.2 = (bf16[16,12,2688]{2,0,1:T(8,128)(2,1)S(1)}, bf16[16,12,2688]{2,0,1:T(8,128)(2,1)S(1)}, u32[]{:S(2)}, u32[]{:S(2)}) collective-permute-start(bf16[16,12,2688]{2,0,1:T(8,128)(2,1)S(1)} %copy.18), channel_id=1, source_target_pairs={{0,8},{8,0},{1,9},{9,1},{2,10},{10,2},{3,11},{11,3},{4,12},{12,4},... | collective-permute-start | bytes 3096584 | tf_op jit(solution)/shard_map/ppermute | solution.py:499
  95.4 30.6 %collective-permute-start.6 = (bf16[512,384]{1,0:T(8,128)(2,1)}, bf16[512,384]{1,0:T(8,128)(2,1)S(1)}, u32[]{:S(2)}, u32[]{:S(2)}) collective-permute-start(bf16[512,384]{1,0:T(8,128)(2,1)} %get-tuple-element.105), channel_id=1, source_target_pairs={{0,6},{2,0},{4,2},{6,4},{1,7},{3,1},{5,3},{7,5},{8,14},{10,8},{12,... | collective-permute-start | bytes 1179656 | tf_op jit(solution)/shard_map/ppermute | solution.py:513
  95.8 34.0 %collective-permute-start.7 = (bf16[512,384]{1,0:T(8,128)(2,1)}, bf16[512,384]{1,0:T(8,128)(2,1)S(1)}, u32[]{:S(2)}, u32[]{:S(2)}) collective-permute-start(bf16[512,384]{1,0:T(8,128)(2,1)} %get-tuple-element.106), channel_id=1, source_target_pairs={{0,4},{2,6},{4,0},{6,2},{1,5},{3,7},{5,1},{7,3},{8,12},{10,14},{12... | collective-permute-start | bytes 1179656 | tf_op jit(solution)/shard_map/ppermute | solution.py:513
  98.4 31.4 %collective-permute-start.8 = (bf16[512,384]{1,0:T(8,128)(2,1)}, bf16[512,384]{1,0:T(8,128)(2,1)S(1)}, u32[]{:S(2)}, u32[]{:S(2)}) collective-permute-start(bf16[512,384]{1,0:T(8,128)(2,1)} %get-tuple-element.107), channel_id=1, source_target_pairs={{0,2},{2,4},{4,6},{6,0},{1,3},{3,5},{5,7},{7,1},{8,10},{10,12},{12... | collective-permute-start | bytes 1179656 | tf_op jit(solution)/shard_map/ppermute | solution.py:513
  123.0 6.9 %collective-permute-start.5 = (f32[8,512]{1,0:T(8,128)}, f32[8,512]{1,0:T(8,128)S(1)}, u32[]{:S(2)}, u32[]{:S(2)}) collective-permute-start(f32[8,512]{1,0:T(8,128)} %get-tuple-element.103.refs_0_), channel_id=1, source_target_pairs={{0,2},{2,4},{4,6},{6,0},{1,3},{3,5},{5,7},{7,1},{8,10},{10,12},{12... | collective-permute-start | bytes 49160 | tf_op jit(solution)/shard_map/ppermute | solution.py:440
  124.6 5.5 %collective-permute-start.4 = (f32[8,512]{1,0:T(8,128)}, f32[8,512]{1,0:T(8,128)S(1)}, u32[]{:S(2)}, u32[]{:S(2)}) collective-permute-start(f32[8,512]{1,0:T(8,128)} %get-tuple-element.103.refs_0_), channel_id=1, source_target_pairs={{0,4},{2,6},{4,0},{6,2},{1,5},{3,7},{5,1},{7,3},{8,12},{10,14},{12... | collective-permute-start | bytes 49160 | tf_op jit(solution)/shard_map/ppermute | solution.py:440
  125.9 4.2 %collective-permute-start.3 = (f32[8,512]{1,0:T(8,128)}, f32[8,512]{1,0:T(8,128)S(1)}, u32[]{:S(2)}, u32[]{:S(2)}) collective-permute-start(f32[8,512]{1,0:T(8,128)} %get-tuple-element.103.refs_0_), channel_id=1, source_target_pairs={{0,6},{2,0},{4,2},{6,4},{1,7},{3,1},{5,3},{7,5},{8,14},{10,8},{12,... | collective-permute-start | bytes 49160 | tf_op jit(solution)/shard_map/ppermute | solution.py:440
  150.6 6.0 %collective-permute-start.11 = (f32[8,512]{1,0:T(8,128)}, f32[8,512]{1,0:T(8,128)S(1)}, u32[]{:S(2)}, u32[]{:S(2)}) collective-permute-start(f32[8,512]{1,0:T(8,128)} %get-tuple-element.128.refs_4_), channel_id=1, source_target_pairs={{0,2},{2,4},{4,6},{6,0},{1,3},{3,5},{5,7},{7,1},{8,10},{10,12},{12... | collective-permute-start | bytes 49160 | tf_op jit(solution)/shard_map/ppermute | solution.py:440
  152.5 5.5 %collective-permute-start.10 = (f32[8,512]{1,0:T(8,128)}, f32[8,512]{1,0:T(8,128)S(1)}, u32[]{:S(2)}, u32[]{:S(2)}) collective-permute-start(f32[8,512]{1,0:T(8,128)} %get-tuple-element.128.refs_4_), channel_id=1, source_target_pairs={{0,4},{2,6},{4,0},{6,2},{1,5},{3,7},{5,1},{7,3},{8,12},{10,14},{12... | collective-permute-start | bytes 49160 | tf_op jit(solution)/shard_map/ppermute | solution.py:440
  155.1 3.9 %collective-permute-start.9 = (f32[8,512]{1,0:T(8,128)}, f32[8,512]{1,0:T(8,128)S(1)}, u32[]{:S(2)}, u32[]{:S(2)}) collective-permute-start(f32[8,512]{1,0:T(8,128)} %get-tuple-element.128.refs_4_), channel_id=1, source_target_pairs={{0,6},{2,0},{4,2},{6,4},{1,7},{3,1},{5,3},{7,5},{8,14},{10,8},{12,... | collective-permute-start | bytes 49160 | tf_op jit(solution)/shard_map/ppermute | solution.py:440
  167.0 33.6 %all-to-all-start.3 = ((bf16[32,8,8,384]{3,2,1,0:T(8,128)(2,1)}), bf16[32,8,8,384]{3,2,1,0:T(8,128)(2,1)S(1)}, u32[]{:S(2)}, u32[]{:S(2)}) async-start(bf16[32,8,8,384]{3,2,1,0:T(8,128)(2,1)} %get-tuple-element.121), calls=%async_computation.3 | async-start | bytes 3145728 | tf_op jit(solution)/shard_map/all_to_all | solution.py:557
  192.7 3.3 %collective-permute-start.12 = (bf16[16,16,2688]{2,1,0:T(8,128)(2,1)}, bf16[16,16,2688]{2,1,0:T(8,128)(2,1)S(1)}, u32[]{:S(2)}, u32[]{:S(2)}) collective-permute-start(bf16[16,16,2688]{2,1,0:T(8,128)(2,1)} %get-tuple-element.133), channel_id=1, source_target_pairs={{0,8},{8,0},{1,9},{9,1},{2,10},{10,2},{3,11},{11,3},{4,12},{12,4},... | collective-permute-start | bytes 4128776 | tf_op jit(solution)/shard_map/ppermute | solution.py:581
  200.5 43.5 %all-to-all-start.4 = ((bf16[16,16,2688]{2,1,0:T(8,128)(2,1)}), bf16[16,16,2688]{2,1,0:T(8,128)(2,1)S(1)}, u32[]{:S(2)}, u32[]{:S(2)}) async-start(bf16[16,16,2688]{2,1,0:T(8,128)(2,1)} %pair_kernel.1), calls=%async_computation.4 | async-start | bytes 2752512 | tf_op jit(solution)/shard_map/all_to_all | solution.py:586
  207.6 12.3 %collective-permute-start.13 = (bf16[512,384]{1,0:T(8,128)(2,1)}, bf16[512,384]{1,0:T(8,128)(2,1)S(1)}, u32[]{:S(2)}, u32[]{:S(2)}) collective-permute-start(bf16[512,384]{1,0:T(8,128)(2,1)} %get-tuple-element.144), channel_id=1, source_target_pairs={{0,2},{2,4},{4,6},{6,0},{1,3},{3,5},{5,7},{7,1},{8,10},{10,12},{12... | collective-permute-start | bytes 1179656 | tf_op jit(solution)/shard_map/ppermute | solution.py:451
  208.7 13.8 %collective-permute-start.14 = (bf16[512,384]{1,0:T(8,128)(2,1)}, bf16[512,384]{1,0:T(8,128)(2,1)S(1)}, u32[]{:S(2)}, u32[]{:S(2)}) collective-permute-start(bf16[512,384]{1,0:T(8,128)(2,1)} %get-tuple-element.145), channel_id=1, source_target_pairs={{0,4},{2,6},{4,0},{6,2},{1,5},{3,7},{5,1},{7,3},{8,12},{10,14},{12... | collective-permute-start | bytes 1179656 | tf_op jit(solution)/shard_map/ppermute | solution.py:451
  211.3 18.1 %collective-permute-start.15 = (bf16[512,384]{1,0:T(8,128)(2,1)}, bf16[512,384]{1,0:T(8,128)(2,1)S(1)}, u32[]{:S(2)}, u32[]{:S(2)}) collective-permute-start(bf16[512,384]{1,0:T(8,128)(2,1)} %get-tuple-element.146), channel_id=1, source_target_pairs={{0,6},{2,0},{4,2},{6,4},{1,7},{3,1},{5,3},{7,5},{8,14},{10,8},{12,... | collective-permute-start | bytes 1179656 | tf_op jit(solution)/shard_map/ppermute | solution.py:451
  244.0 30.6 %all-to-all-start.5 = ((bf16[32,8,8,384]{3,2,1,0:T(8,128)(2,1)}), bf16[32,8,8,384]{3,2,1,0:T(8,128)(2,1)S(1)}, u32[]{:S(2)}, u32[]{:S(2)}) async-start(bf16[32,8,8,384]{3,2,1,0:T(8,128)(2,1)} %get-tuple-element.148), calls=%async_computation.5 | async-start | bytes 3145728 | tf_op jit(solution)/shard_map/all_to_all | solution.py:606
  251.2 10.2 %collective-permute-start.17 = (bf16[8,64,256]{2,1,0:T(8,128)(2,1)}, bf16[8,64,256]{2,1,0:T(8,128)(2,1)S(1)}, u32[]{:S(2)}, u32[]{:S(2)}) collective-permute-start(bf16[8,64,256]{2,1,0:T(8,128)(2,1)} %get-tuple-element.151), channel_id=1, source_target_pairs={{0,2},{2,4},{4,6},{6,0},{1,3},{3,5},{5,7},{7,1},{8,10},{10,12},{12... | collective-permute-start | bytes 786440 | tf_op jit(solution)/shard_map/ppermute | solution.py:451
  251.9 10.9 %collective-permute-start.18 = (bf16[8,64,256]{2,1,0:T(8,128)(2,1)}, bf16[8,64,256]{2,1,0:T(8,128)(2,1)S(1)}, u32[]{:S(2)}, u32[]{:S(2)}) collective-permute-start(bf16[8,64,256]{2,1,0:T(8,128)(2,1)} %get-tuple-element.152), channel_id=1, source_target_pairs={{0,4},{2,6},{4,0},{6,2},{1,5},{3,7},{5,1},{7,3},{8,12},{10,14},{12... | collective-permute-start | bytes 786440 | tf_op jit(solution)/shard_map/ppermute | solution.py:451
  254.6 12.8 %collective-permute-start.19 = (bf16[8,64,256]{2,1,0:T(8,128)(2,1)}, bf16[8,64,256]{2,1,0:T(8,128)(2,1)S(1)}, u32[]{:S(2)}, u32[]{:S(2)}) collective-permute-start(bf16[8,64,256]{2,1,0:T(8,128)(2,1)} %get-tuple-element.153), channel_id=1, source_target_pairs={{0,6},{2,0},{4,2},{6,4},{1,7},{3,1},{5,3},{7,5},{8,14},{10,8},{12,... | collective-permute-start | bytes 786440 | tf_op jit(solution)/shard_map/ppermute | solution.py:451
  256.7 14.1 %collective-permute-start.16 = (f32[12,2688]{1,0:T(8,128)S(1)}, f32[12,2688]{1,0:T(8,128)S(1)}, u32[]{:S(2)}, u32[]{:S(2)}) collective-permute-start(f32[12,2688]{1,0:T(8,128)S(1)} %bitcast.31), channel_id=1, source_target_pairs={{0,0},{1,1},{16,2},{17,3},{32,4},{33,5},{48,6},{49,7},{64,8},{65,9... | collective-permute-start | bytes 387080 | tf_op jit(solution)/shard_map/ppermute | solution.py:628
  281.2 39.7 %collective-permute-start.20 = (bf16[192,2048]{1,0:T(8,128)(2,1)}, bf16[192,2048]{1,0:T(8,128)(2,1)S(1)}, u32[]{:S(2)}, u32[]{:S(2)}) collective-permute-start(bf16[192,2048]{1,0:T(8,128)(2,1)} %get-tuple-element.160), channel_id=1, source_target_pairs={{0,1},{1,0},{2,3},{3,2},{4,5},{5,4},{6,7},{7,6},{8,9},{9,8},{10,11... | collective-permute-start | bytes 2359304 | tf_op jit(solution)/shard_map/ppermute | solution.py:650
  288.6 10.4 %collective-permute-start.21 = (bf16[8,64,256]{2,1,0:T(8,128)(2,1)}, bf16[8,64,256]{2,1,0:T(8,128)(2,1)S(1)}, u32[]{:S(2)}, u32[]{:S(2)}) collective-permute-start(bf16[8,64,256]{2,1,0:T(8,128)(2,1)} %get-tuple-element.163), channel_id=1, source_target_pairs={{0,2},{2,4},{4,6},{6,0},{1,3},{3,5},{5,7},{7,1},{8,10},{10,12},{12... | collective-permute-start | bytes 786440 | tf_op jit(solution)/shard_map/ppermute | solution.py:451
  292.5 11.0 %collective-permute-start.22 = (bf16[8,64,256]{2,1,0:T(8,128)(2,1)}, bf16[8,64,256]{2,1,0:T(8,128)(2,1)S(1)}, u32[]{:S(2)}, u32[]{:S(2)}) collective-permute-start(bf16[8,64,256]{2,1,0:T(8,128)(2,1)} %get-tuple-element.164), channel_id=1, source_target_pairs={{0,4},{2,6},{4,0},{6,2},{1,5},{3,7},{5,1},{7,3},{8,12},{10,14},{12... | collective-permute-start | bytes 786440 | tf_op jit(solution)/shard_map/ppermute | solution.py:451
  294.7 12.5 %collective-permute-start.23 = (bf16[8,64,256]{2,1,0:T(8,128)(2,1)}, bf16[8,64,256]{2,1,0:T(8,128)(2,1)S(1)}, u32[]{:S(2)}, u32[]{:S(2)}) collective-permute-start(bf16[8,64,256]{2,1,0:T(8,128)(2,1)} %get-tuple-element.165), channel_id=1, source_target_pairs={{0,6},{2,0},{4,2},{6,4},{1,7},{3,1},{5,3},{7,5},{8,14},{10,8},{12,... | collective-permute-start | bytes 786440 | tf_op jit(solution)/shard_map/ppermute | solution.py:451
  297.8 14.9 %collective-permute-start.25 = (bf16[8,32,256]{2,1,0:T(8,128)(2,1)S(1)}, bf16[8,32,256]{2,1,0:T(8,128)(2,1)S(1)}, u32[]{:S(2)}, u32[]{:S(2)}) collective-permute-start(bf16[8,32,256]{2,1,0:T(8,128)(2,1)S(1)} %copy-done.28), channel_id=1, source_target_pairs={{0,1},{1,0},{2,3},{3,2},{4,5},{5,4},{6,7},{7,6},{8,9},{9,8},{10,11... | collective-permute-start | bytes 393224 | tf_op jit(solution)/shard_map/ppermute | solution.py:616
  310.6 7.1 %collective-permute-start.24 = (bf16[8,32,256]{2,1,0:T(8,128)(2,1)}, bf16[8,32,256]{2,1,0:T(8,128)(2,1)S(1)}, u32[]{:S(2)}, u32[]{:S(2)}) collective-permute-start(bf16[8,32,256]{2,1,0:T(8,128)(2,1)} %get-tuple-element.167), channel_id=1, source_target_pairs={{0,1},{1,0},{2,3},{3,2},{4,5},{5,4},{6,7},{7,6},{8,9},{9,8},{10,11... | collective-permute-start | bytes 393224 | tf_op jit(solution)/shard_map/ppermute | solution.py:616
  (29 other events, 210.6 us)

commit v4 on v3

--- a/solution.py
+++ b/solution.py
@@ -33,7 +33,7 @@
             for k in range(2):
                 for x in range(4):
                     for zh in range(2):
-                        there = index_of(k, x, y % 2, zl * 2 + y // 2, zh)
+                        there = index_of(y % 2, k * 2 + x // 2, x % 2, zl * 2 + y // 2, zh)
                         moves.append((index_of(zl, y, k, x, zh), there))
     return moves
 
@@ -121,11 +121,22 @@
     return lax.dot_general(a, b, (((0,), (0,)), ((), ())), preferred_element_type=F32)
 
 
-def first_kernel(_, f1_ref, in_ref, out_ref):
-    results = [
-        dot_t(f1_ref[r], in_ref[:, r * 256 : (r + 1) * 256]).reshape(32, 8, 192) for r in range(2)
-    ]
-    out_ref[:, 0] = jnp.concatenate(results, axis=2).astype(BF)
+def first_kernel(_, f1_ref, in_ref, payload_ref, out_ref):
+    step = pl.program_id(0)
+
+    @pl.when(step < 8)
+    def _():
+        results = [
+            dot_t(f1_ref[r], in_ref[:, r * 256 : (r + 1) * 256]).reshape(32, 8, 192)
+            for r in range(2)
+        ]
+        out_ref[:, 0] = jnp.concatenate(results, axis=2).astype(BF)
+
+    @pl.when(step >= 8)
+    def _():
+        halves = [payload_ref[core, lax.max(step - 8, 0)] for core in range(2)]
+        for dev in range(32):
+            out_ref[dev, 0] = halves[dev // 2 % 2]
 
 
 def copy_kernel(_, in_ref, out_ref):
@@ -167,7 +178,7 @@
     write_blocks(result, out_ref)
 
 
-def first_grad_kernel(_, piece_ref, f2_ref, out_ref, grad_ref, *scratch):
+def first_grad_kernel(_, piece_ref, f2_ref, keep_ref, got_ref, out_ref, grad_ref, *scratch):
     cols, result = scratch[:3], scratch[3:]
     for dev in range(32):
         s, h = dev // 2, dev % 2
@@ -179,6 +190,9 @@
         grad_ref[a] = grad
         put_position(result, a, t_dot(f2_ref[a], grad))
     write_blocks(result, out_ref)
+    for dev in range(32):
+        total = keep_ref[dev].astype(F32) + got_ref[dev].astype(F32)
+        out_ref[dev, 8:] = total.astype(BF)
 
 
 def write_blocks(result, out_ref):
@@ -350,9 +364,11 @@
 
 def join_kernel(s_ref, own_ref, got_ref, out_ref):
     zh = s_ref[0]
-    own, got = own_ref[...], got_ref[...]
-    out_ref[:, :512] = jnp.where(zh == 0, own, got)
-    out_ref[:, 512:] = jnp.where(zh == 0, got, own)
+    for q in range(2):
+        here = slice(q * 512, (q + 1) * 512)
+        own, got = own_ref[:, here], got_ref[:, here]
+        out_ref[:, q * 1024 : q * 1024 + 512] = jnp.where(zh == 0, own, got)
+        out_ref[:, q * 1024 + 512 : (q + 1) * 1024] = jnp.where(zh == 0, got, own)
 
 
 def mixed_join_kernel(s_ref, *refs):
@@ -362,12 +378,14 @@
 
 
 def payload_kernel(_, wg_ref, wu_ref, win_ref, wd_ref, out_ref):
-    down = wd_ref[...].astype(F32)
-    out_ref[:, :768] = wg_ref[...]
-    out_ref[:, 768:1536] = wu_ref[...]
-    out_ref[:, 1536:1920] = win_ref[...]
-    out_ref[:, 1920:2304] = down[:12].astype(BF)
-    out_ref[:, 2304:] = down[12:].astype(BF)
+    wg, wu = wg_ref[...].astype(F32), wu_ref[...].astype(F32)
+    win, down = win_ref[...].astype(F32), wd_ref[...].astype(F32)
+    put_half(out_ref, 0, [wg[:, :DB], wg[:, DB:], win, jnp.zeros_like(win)])
+    put_half(out_ref, 1, [wu[:, :DB], wu[:, DB:], down])
+
+
+def put_half(ref, at, parts):
+    ref[at] = jnp.concatenate(parts, axis=0).reshape(6, 8, DB).astype(BF)
 
 
 def gather_kernel(_, *refs):
@@ -375,25 +393,19 @@
         refs[4][:, j * 512 : (j + 1) * 512] = refs[j][...]
 
 
-def stack_kernel(_, *refs):
-    for j in range(4):
-
-        @pl.when(pl.program_id(0) == j)
-        def _(j=j):
-            refs[4][...] = refs[j][...]
-
-
-def weights_kernel(s_ref, own_ref, across_ref, wg_ref, wu_ref, win_ref, wd_ref, half, down):
-    mine = pl.program_id(0) == s_ref[4]
-    for shard in range(16):
-        value = jnp.where(mine, own_ref[shard], across_ref[shard]).astype(F32)
-        half[shard * 12 : shard * 12 + 12, :] = value[:, :1920]
-        down[shard * 24 : shard * 24 + 12, :] = value[:, 1920:2304]
-        down[shard * 24 + 12 : shard * 24 + 24, :] = value[:, 2304:]
-    wg_ref[...] = half[:, :768].astype(BF)
-    wu_ref[...] = half[:, 768:1536].astype(BF)
-    win_ref[...] = half[:, 1536:].astype(BF)
-    wd_ref[...] = down[...].astype(BF)
+def weights_kernel(s_ref, own_ref, across_ref, wg_ref, wu_ref, win_ref, wd_ref):
+    first = s_ref[4] == 0
+    gates, ups, entries, downs = [], [], [], []
+    for shard in range(8):
+        own = own_ref[shard].astype(F32).reshape(48, DB)
+        across = across_ref[shard].astype(F32).reshape(48, DB)
+        low, high = jnp.where(first, own, across), jnp.where(first, across, own)
+        gates.append(jnp.concatenate([low[:12], low[12:24]], axis=1))
+        entries.append(low[24:36])
+        ups.append(jnp.concatenate([high[:12], high[12:24]], axis=1))
+        downs.append(high[24:])
+    for ref, parts in ((wg_ref, gates), (wu_ref, ups), (win_ref, entries), (wd_ref, downs)):
+        ref[...] = jnp.concatenate(parts, axis=0).astype(BF)
 
 
 def weight_grad_kernel(
@@ -412,24 +424,27 @@
 
     @pl.when(step == pl.num_programs(0) - 1)
     def _():
-        for ref, core in ((keep_ref, s_ref[4]), (give_ref, 1 - s_ref[4])):
-            start = pl.multiple_of(core * 192, 192)
-            start_down = pl.multiple_of(core * 384, 384)
-            gates = across[pl.ds(start, 192), :]
-            entries = entry_ref[pl.ds(start, 192), :]
-            downs = down[pl.ds(start_down, 384), :]
-            for shard in range(16):
-                here = slice(shard * 12, shard * 12 + 12)
-                at = shard * 24
-                block = jnp.concatenate(
-                    [gates[here], entries[here], downs[at : at + 12], downs[at + 12 : at + 24]],
-                    axis=1,
-                )
-                ref[shard] = jnp.concatenate([block, gain_ref[...]], axis=0).astype(BF)
-
-
-def pair_kernel(_, a_ref, b_ref, out_ref):
-    out_ref[...] = (a_ref[...].astype(F32) + b_ref[...].astype(F32)).astype(BF)
+        first = s_ref[4] == 0
+        fill = jnp.zeros((8, DB), F32)
+        for shard in range(32):
+            here = slice(shard * 12, shard * 12 + 12)
+            gates, entries = across[here, :], entry_ref[here, :]
+            low = [gates[:, :DB], gates[:, DB : 2 * DB], entries, gain_ref[...], fill]
+            high = [gates[:, 2 * DB : 3 * DB], gates[:, 3 * DB :]]
+            high.append(down[shard * 24 : shard * 24 + 24, :])
+            low = jnp.concatenate(low, axis=0)
+            high = jnp.concatenate(high, axis=0)
+            put_half(keep_ref, shard, [jnp.where(first, low, high)])
+            put_half(give_ref, shard, [jnp.where(first, high, low)])
+
+
+def weight_sum_kernel(_, in_ref, out_ref):
+    for core in range(2):
+        total = jnp.zeros((2, 8, DB), F32)
+        for pair in range(8):
+            for zh in range(2):
+                total = total + in_ref[pair * 4 + core * 2 + zh].astype(F32)
+        out_ref[core] = total * (1.0 / math.sqrt(SEQL))
 
 
 def turn(axis, size, step):
@@ -474,35 +489,26 @@
         whole(192, 2048), bf(192, 2048), (1, 1),
     )(at, *[turned_in] * 4)
     other = lax.ppermute(give, "zh", SWAP)
+    give, turned_in, w_gate = lax.optimization_barrier((give, turned_in, w_gate))
 
     payload = call(
         payload_kernel, (1,),
         [whole(12, 768), whole(12, 768), whole(12, DB), whole(24, DB)],
-        whole(12, 2688), bf(12, 2688), (1, 1),
+        whole(2, 6, 8, DB), bf(2, 6, 8, DB), (1, 1),
     )(at, w_gate, w_up, w_input_gate, w_down)
     payload = lax.ppermute(payload, ALL, shard_moves())
-    payload = jnp.broadcast_to(payload, (16, 12, 2688))
-    payload, turned_in = lax.optimization_barrier((payload, turned_in))
-    payload = lax.all_to_all(payload, ("zl", "y", "zh"), split_axis=0, concat_axis=0, tiled=True)
-
     first_local = call(
-        first_kernel, (8,),
-        [pl.BlockSpec((2, 256, 256), lambda t, s: (t, 0, 0)), columns(192)],
+        first_kernel, (14,),
+        [pl.BlockSpec((2, 256, 256), lambda t, s: (lax.min(t, 7), 0, 0)),
+         pl.BlockSpec((192, 512), lambda t, s: (0, lax.min(t, 7))), whole(2, 6, 8, DB)],
         pl.BlockSpec((32, 1, 8, DB), lambda t, s: (0, t, 0, 0)),
-        bf(32, 8, 8, DB),
+        bf(32, 14, 8, DB),
         (12_000_000_000, 6_000_000),
-    )(at, factor_one, turned_in)
-    first_local, other, payload, turned_in, grad_out, factor_two = lax.optimization_barrier(
-        (first_local, other, payload, turned_in, grad_out, factor_two)
+    )(at, factor_one, turned_in, payload)
+    first_local, other, turned_in, grad_out, factor_two = lax.optimization_barrier(
+        (first_local, other, turned_in, grad_out, factor_two)
     )
     piece = lax.all_to_all(first_local, PLANE, split_axis=0, concat_axis=0, tiled=True)
-    across = lax.ppermute(payload, "core", SWAP)
-    wg, wu, win, wd = call(
-        weights_kernel, (2,), [whole(16, 12, 2688)] * 2,
-        [rows(768, 192), rows(768, 192), rows(DB, 192), rows(DB, 384)],
-        [bf(DB, 768), bf(DB, 768), bf(DB, DB), bf(768, DB)], (1, 1),
-        [pltpu.VMEM((192, 1920), F32), pltpu.VMEM((384, DB), F32)],
-    )(at, payload, across)
     gain = lax.dynamic_slice_in_dim(norm_gain, xi * DB, DB, 0).reshape(1, DB)
 
     to_send = call(
@@ -517,16 +523,27 @@
     all_pieces = whole(32, 8, 8, DB)
     second_cols, first_cols = call(
         second_kernel, (1,),
-        [all_pieces, whole(8, 256, 256)],
+        [whole(32, 14, 8, DB), whole(8, 256, 256)],
         [all_pieces, whole(8, 256, DB)],
         [bf(32, 8, 8, DB), bf(8, 256, DB)],
         (400_000_000, 6_000_000), wide,
     )(at, piece, f2)
+    second_cols, piece = lax.optimization_barrier((second_cols, piece))
     second = lax.all_to_all(second_cols, PLANE, split_axis=0, concat_axis=0, tiled=True)
+
+    half = piece[:, 8:]
+    across = lax.ppermute(half, "core", SWAP)
+    shards = pl.BlockSpec((8, 6, 8, DB), lambda t, s: (t, 0, 0, 0))
+    wg, wu, win, wd = call(
+        weights_kernel, (4,), [shards] * 2,
+        [rows(768, 96), rows(768, 96), rows(DB, 96), rows(DB, 192)],
+        [bf(DB, 768), bf(DB, 768), bf(DB, DB), bf(768, DB)], (1, 1),
+    )(at, half, across)
 
     input_mlp, resid, pgate, square = call(
         gating_kernel, (4,),
-        [pl.BlockSpec((192, 512), lambda t, s: (0, 2 * t + s[0])), columns(192), PIECES, whole(DB, DB)],
+        [pl.BlockSpec((192, 512), lambda t, s: (0, 2 * t + s[0])),
+         columns(192), PIECES, whole(DB, DB)],
         [rows(DB), rows(DB), rows(DB), whole(8, 512)],
         [bf(2048, DB), bf(2048, DB), bf(2048, DB), f32(8, 512)],
         (600_000_000, 10_000_000),
@@ -570,50 +587,36 @@
     )(at, g_resid, input_mlp, second, pgate, win)
 
     gain_terms = in_order([v[4:5, :DB] for v in inners], xi).reshape(1, D)
-    gain_rows = jnp.pad(gain_terms, ((0, 3), (0, 2688 - D)))
-    shards = whole(16, 16, 2688)
+    gain_rows = gain_terms.reshape(4, DB)
+    halves = whole(32, 6, 8, DB)
     keep, give = call(
-        weight_grad_kernel, (4,),
-        [rows(DB), rows(1536), rows(768), rows(DB), whole(DB, DB), whole(4, 2688)],
-        [shards] * 2, [bf(16, 16, 2688)] * 2, (1, 1),
+        weight_grad_kernel, (2,),
+        [rows(DB, 1024), rows(1536, 1024), rows(768, 1024), rows(DB, 1024), whole(DB, DB), whole(4, DB)],
+        [halves] * 2, [bf(32, 6, 8, DB)] * 2, (1, 1),
         [pltpu.VMEM((DB, 1536), F32), pltpu.VMEM((768, DB), F32)],
     )(at, normed, grads, hidden, cot, term_entry, gain_rows)
     got = lax.ppermute(give, "core", SWAP)
-    quarter = pl.BlockSpec((8, 16, 2688), lambda t, s: (t, 0, 0))
-    pair = call(pair_kernel, (2,), [quarter] * 2, quarter, bf(16, 16, 2688), (1, 1))(at, keep, got)
-
-    piece, pair = lax.optimization_barrier((piece, pair))
-    pair = lax.all_to_all(pair, ("zl", "y", "zh"), split_axis=0, concat_axis=0, tiled=True)
 
     first_grad, second_grad = call(
         first_grad_kernel, (1,),
-        [all_pieces, whole(8, 256, 256)],
-        [all_pieces, whole(8, 256, DB)],
-        [bf(32, 8, 8, DB), bf(8, 256, DB)],
+        [all_pieces, whole(8, 256, 256), halves, halves],
+        [whole(32, 14, 8, DB), whole(8, 256, DB)],
+        [bf(32, 14, 8, DB), bf(8, 256, DB)],
         (400_000_000, 6_000_000), wide,
-    )(at, piece, f2)
+    )(at, piece, f2, keep, got)
     square_scratch = [pltpu.VMEM((256, 256), F32)]
     term_out = pl.BlockSpec((2, 64, 256), lambda t, s: (t, 0, 0))
 
-    terms_two = call(
-        term_two_kernel, (4,),
-        [pl.BlockSpec((2, 256, DB), lambda t, s: (t, 0, 0))] * 2,
-        [term_out] * 4, [bf(8, 64, 256)] * 4, (1, 1), square_scratch,
-    )(at, second_grad, first_cols)
-    first_grad, terms_two, pair, mixed_out = lax.optimization_barrier(
-        (first_grad, terms_two, pair, mixed_out)
-    )
+    first_grad, second_grad = lax.optimization_barrier((first_grad, second_grad))
     g_first = lax.all_to_all(first_grad, PLANE, split_axis=0, concat_axis=0, tiled=True)
 
     def factor_sums(terms):
         return call(
             factor_sum_kernel, (1,), [whole(8, 64, 256)] * 4, [whole(8, 32, 256)] * 2,
             [f32(8, 32, 256), bf(8, 32, 256)], (1, 1),
-        )(at, *send_each(terms, "x"))
-
-    def factor_gradient(sums, slots):
-        own, give = sums
-        got = lax.ppermute(give, "zh", SWAP)
+        )(at, *terms)
+
+    def factor_gradient(own, got, slots):
         shape = (slots, 8 // slots, 32, 256)
         joined = call(
             factor_join_kernel, (1,), [whole(*shape)] * 2, whole(slots, 2, 8 // slots, 32, 256),
@@ -621,35 +624,52 @@
         )(at, own.reshape(shape), got.reshape(shape))
         return joined.reshape(16, 32, 256)
 
-    sums_two = factor_sums(terms_two)
-
-    summed = jnp.sum(pair.astype(F32), axis=0) * tok_scale
-    back = [(there, here) for here, there in shard_moves()]
-    own = lax.ppermute(summed[:12], ALL, back)
-    g_first, own, sums_two = lax.optimization_barrier((g_first, own, sums_two))
-    grad_w_gate, grad_w_up = own[:, :768], own[:, 768:1536]
-    grad_w_input_gate = own[:, 1536:1920]
-    grad_w_down = jnp.concatenate([own[:, 1920:2304], own[:, 2304:]], axis=0)
-    grad_norm_gain = summed[12, :D]
-    grad_factor_two = factor_gradient(sums_two, 1)
-
+    terms_two = call(
+        term_two_kernel, (4,),
+        [pl.BlockSpec((2, 256, DB), lambda t, s: (t, 0, 0))] * 2,
+        [term_out] * 4, [bf(8, 64, 256)] * 4, (1, 1), square_scratch,
+    )(at, second_grad, first_cols)
+    sums_two = factor_sums(send_each(terms_two, "x"))
+
+    g_first, sums_two, mixed_out = lax.optimization_barrier((g_first, sums_two, mixed_out))
     own_grad, give_grad = call(
         back_kernel, (4,),
         [PIECES, pl.BlockSpec((1, 2, 256, 256), lambda t, s: (2 * t + s[0], 0, 0, 0)), columns(DB)],
         [columns(192), columns(192)],
         [bf(192, 2048), bf(192, 2048)],
-        (400_000_000, 6_000_000),
+        (12_000_000_000, 6_000_000),
     )(at, g_first, factor_one.reshape(8, 2, 256, 256), g_direct)
     g_first, give_grad = lax.optimization_barrier((g_first, give_grad))
     terms_one = call(
         term_one_kernel, (4,), [PIECES, rows(DB)],
         [term_out] * 4, [bf(8, 64, 256)] * 4, (1, 1), square_scratch,
     )(at, g_first, input_mlp)
-    grad_factor_one = factor_gradient(factor_sums(terms_one), 4)
-
+
+    terms_one, sums_two = lax.optimization_barrier((terms_one, sums_two))
+    got_two = lax.ppermute(sums_two[1], "zh", SWAP)
+    for_sums, got_two = lax.optimization_barrier((g_first, got_two))
     got_grad = lax.ppermute(give_grad, "zh", SWAP)
+    summed = call(
+        weight_sum_kernel, (3,),
+        [pl.BlockSpec((32, 2, 8, DB), lambda t, s: (0, t + 4, 0, 0))],
+        pl.BlockSpec((2, 2, 8, DB), lambda t, s: (0, t, 0, 0)), f32(2, 6, 8, DB), (1, 1),
+    )(at, for_sums)
+    back = [(there, here) for here, there in shard_moves()]
+    own = lax.ppermute(summed, ALL, back).reshape(2, 48, DB)
+    low, high = own[0], own[1]
+    grad_w_gate = jnp.concatenate([low[:12], low[12:24]], axis=1)
+    grad_w_up = jnp.concatenate([high[:12], high[12:24]], axis=1)
+    grad_w_input_gate = low[24:36]
+    grad_w_down = high[24:]
+    grad_norm_gain = summed[0].reshape(48, DB)[36:40].reshape(D)
+
+    grad_factor_two = factor_gradient(sums_two[0], got_two, 1)
+    terms_one, got_grad = lax.optimization_barrier((send_each(terms_one, "x"), got_grad))
+    sums_one = factor_sums(terms_one)
+    got_one = lax.ppermute(sums_one[1], "zh", SWAP)
+    grad_factor_one = factor_gradient(sums_one[0], got_one, 4)
     grad_inputs = call(
-        join_kernel, (4,), [columns(192), columns(192)], columns(192, 1024), bf(192, 4096), (1, 1)
+        join_kernel, (2,), [columns(192, 1024)] * 2, columns(192, 2048), bf(192, 4096), (1, 1)
     )(at, own_grad, got_grad).T
     return (
         mixed_out,

time: 330 us -> 304 us (0.921)
  waiting for transfers between devices: 97.1 us -> 74.5 us
  starting transfers between devices: 87.7 us -> 80.9 us
  Pallas kernels: 119 us -> 123 us
    ppermute x9, waiting for transfers between devices: 31 us -> 5.23 us  [send_each(): lax.ppermute(parts[j], axis, turn(axis, 4, j))]
    ppermute x1, waiting for transfers between devices: 19.9 us -> 4.17 us  [per_device(): other = lax.ppermute(give, 'zh', SWAP)]
    all_to_all x2 -> x0, starting transfers between devices: 14.6 us -> none  [the longest x1 7.51 us: per_device(): lax.all_to_all(payload, ('zl', 'y', 'zh'), split_axis=0, concat_axis=0, t...]
    all_to_all x1, waiting for transfers between devices: 22.1 us -> 34.8 us  [per_device(): lax.all_to_all(first_local, PLANE, split_axis=0, concat_axis=0, tiled=True)]
    ppermute x1, waiting for transfers between devices: 0.01 us -> 9.75 us  [per_device(): got_grad = lax.ppermute(give_grad, 'zh', SWAP)]
    ppermute x9, starting transfers between devices: 18.8 us -> 24 us  [send_each(): lax.ppermute(parts[j], axis, turn(axis, 4, j))]
    all_to_all x1, waiting for transfers between devices: 3.74 us -> 0.01 us  [per_device(): lax.all_to_all(first_grad, PLANE, split_axis=0, concat_axis=0, tiled=True)]
    all_to_all x2 -> x0, waiting for transfers between devices: 3.58 us -> none  [the longest x1 3.58 us: per_device(): lax.all_to_all(payload, ('zl', 'y', 'zh'), split_axis=0, concat_axis=0, t...]
  transfers between devices with their start and end apart: 32 -> 30, of which waited for: 18 -> 13; matrix products, arithmetic and copies ran while one was open for 3% -> 4% of each run, Pallas kernels for 23% -> 21%
where the time goes in v4:
time: 304 us; the launch traced here: 302 us
  Pallas kernels  123 us (40%)
  starting transfers between devices  80.9 us (27%)
  waiting for transfers between devices  74.5 us (25%)
  local copies, waits for them, and re-layouts  21.6 us (7%)
    all_to_all x1, waiting for transfers between devices, per_device(): lax.all_to_all(first_local, PLANE, split_axis=0, concat_axis=0, tiled=True)  34.8 us
    ppermute x9, starting transfers between devices, send_each(): lax.ppermute(parts[j], axis, turn(axis, 4, j))  24 us
    pallas_call x1, Pallas kernels, per_device(): call(mlp_kernel, (4,), [turned_rows(DB), whole(1, DB), whole(DB, 768), wh...  20 us
    pallas_call x1, Pallas kernels, per_device(): call(weight_grad_kernel, (2,), [rows(DB, 1024), rows(1536, 1024), rows(76...  11 us
    unnamed x70, local copies, waits for them, and re-layouts  10.8 us
    ppermute x6, starting transfers between devices, around(): lax.ppermute(value, axis, turn(axis, 4, -j))  9.99 us
    pallas_call x1, Pallas kernels, per_device(): call(first_kernel, (14,), [pl.BlockSpec((2, 256, 256), lambda t, s: (lax....  9.85 us
    ppermute x1, waiting for transfers between devices, per_device(): got_grad = lax.ppermute(give_grad, 'zh', SWAP)  9.75 us
  transfers between devices with their start and end apart: 30, of which 13 were waited for; matrix products, arithmetic and copies ran while one was open for 4% of the time, Pallas kernels for 21%

profile of v4, /device:TPU:2, one launch (start us, length us, event | category | flops | bytes accessed | tf_op | source)
XLA Modules:
  0.0 301.7 jit_solution(9842950023342698535)
XLA Ops:
  1.3 2.9 gather_kernel.1
  8.2 4.0 %collective-permute-start.1 = (bf16[192,2048]{1,0:T(8,128)(2,1)}, bf16[192,2048]{1,0:T(8,128)(2,1)S(1)}, u32[]{:S(2)}, u32[]{:S(2)}) collective-permute-start(bf16[192,2048]{1,0:T(8,128)(2,1)} %gather_kernel.1), channel_id=1, source_target_pairs={{0,1},{1,0},{2,3},{3,2},{4,5},{5,4},{6,7},{7,6},{8,9},{9,8},{10,11... | collective-permute-start | bytes 2359304 | tf_op jit(solution)/shard_map/ppermute | solution.py:491
  12.2 3.6 %collective-permute-done.payload_ref = bf16[2,6,8,384]{3,2,1,0:T(8,128)(2,1)S(1)} collective-permute-done((bf16[2,6,8,384]{3,2,1,0:T(8,128)(2,1)}, bf16[2,6,8,384]{3,2,1,0:T(8,128)(2,1)S(1)}, u32[]{:S(2)}, u32[]{:S(2)}) %collective-permute-start) | collective-permute-done | bytes 73760 | tf_op jit(solution)/shard_map/ppermute | solution.py:499
  16.4 9.8 %first_kernel.1 = bf16[32,14,8,384]{3,2,1,0:T(8,128)(2,1)} custom-call(s32[5]{0:T(128)} %stack.23._.s_ref, bf16[16,256,256]{2,1,0:T(8,128)(2,1)} %f1_ref.1, bf16[192,4096]{1,0:T(8,128)(2,1)} %bitcast.26, bf16[2,6,8,384]{3,2,1,0:T(8,128)(2,1)} %copy-done.34), custom_call_target="tpu_custom_call" | custom-call | flops 12000000000 | bytes 6000000 | tf_op jit(solution)/shard_map/first_kernel/pallas_call | solution.py:500
  26.2 4.2 %collective-permute-done.1.got_ref = bf16[192,2048]{1,0:T(8,128)(2,1)S(1)} collective-permute-done((bf16[192,2048]{1,0:T(8,128)(2,1)}, bf16[192,2048]{1,0:T(8,128)(2,1)S(1)}, u32[]{:S(2)}, u32[]{:S(2)}) %collective-permute-start.1) | collective-permute-done | bytes 786464 | tf_op jit(solution)/shard_map/ppermute | solution.py:491
  31.3 9.2 %all-to-all-start = ((bf16[32,14,8,384]{3,2,1,0:T(8,128)(2,1)}), bf16[32,14,8,384]{3,2,1,0:T(8,128)(2,1)}, u32[]{:S(2)}, u32[]{:S(2)}) async-start(bf16[32,14,8,384]{3,2,1,0:T(8,128)(2,1)} %first_kernel.1), calls=%async_computation | async-start | bytes 5505024 | tf_op jit(solution)/shard_map/all_to_all | solution.py:511
  41.6 34.8 %all-to-all-done.piece_ref = bf16[32,14,8,384]{3,2,1,0:T(8,128)(2,1)} async-done(((bf16[32,14,8,384]{3,2,1,0:T(8,128)(2,1)}), bf16[32,14,8,384]{3,2,1,0:T(8,128)(2,1)}, u32[]{:S(2)}, u32[]{:S(2)}) %all-to-all-start) | async-done | bytes 2752544 | tf_op jit(solution)/shard_map/all_to_all | solution.py:511
  76.4 5.7 %second_kernel.1 = (bf16[32,8,8,384]{3,2,1,0:T(8,128)(2,1)}, bf16[8,256,384]{2,1,0:T(8,128)(2,1)}) custom-call(s32[5]{0:T(128)} %stack.23._.s_ref, bf16[32,14,8,384]{3,2,1,0:T(8,128)(2,1)} %all-to-all-done.piece_ref, bf16[8,256,256]{2,1,0:T(8,128)(2,1)} %constant_dynamic-slice_fusion.1.f2_ref), custom_call_target="tpu_custom_call" | custom-call | flops 400000000 | bytes 6000000 | tf_op jit(solution)/shard_map/second_kernel/pallas_call | solution.py:524
  82.1 6.3 %all-to-all-start.1 = ((bf16[32,8,8,384]{3,2,1,0:T(8,128)(2,1)}), bf16[32,8,8,384]{3,2,1,0:T(8,128)(2,1)S(1)}, u32[]{:S(2)}, u32[]{:S(2)}) async-start(bf16[32,8,8,384]{3,2,1,0:T(8,128)(2,1)} %get-tuple-element.102), calls=%async_computation.1 | async-start | bytes 3145728 | tf_op jit(solution)/shard_map/all_to_all | solution.py:532
  90.2 3.0 copy_three_kernel.1
  93.1 2.9 collective-permute-start.6
  98.9 4.6 %weights_kernel.1 = (bf16[384,768]{1,0:T(8,128)(2,1)}, bf16[384,768]{1,0:T(8,128)(2,1)}, bf16[384,384]{1,0:T(8,128)(2,1)}, bf16[768,384]{1,0:T(8,128)(2,1)}) custom-call(s32[5]{0:T(128)} %stack.23._.s_ref, bf16[32,6,8,384]{3,2,1,0:T(8,128)(2,1)} %copy-done.5, bf16[32,6,8,384]{3,2,1,0:T(8,128)(2,1)} %copy-done.7), custom_call_target="tpu_custom_call" | custom-call | flops 1 | bytes 1 | tf_op jit(solution)/shard_map/weights_kernel/pallas_call | solution.py:537
  103.5 8.2 %all-to-all-done.1.second_ref = bf16[32,8,8,384]{3,2,1,0:T(8,128)(2,1)S(1)} async-done(((bf16[32,8,8,384]{3,2,1,0:T(8,128)(2,1)}), bf16[32,8,8,384]{3,2,1,0:T(8,128)(2,1)S(1)}, u32[]{:S(2)}, u32[]{:S(2)}) %all-to-all-start.1) | async-done | bytes 1572896 | tf_op jit(solution)/shard_map/all_to_all | solution.py:532
  112.8 6.7 %gating_kernel.1 = (bf16[2048,384]{1,0:T(8,128)(2,1)}, bf16[2048,384]{1,0:T(8,128)(2,1)}, bf16[2048,384]{1,0:T(8,128)(2,1)}, f32[8,512]{1,0:T(8,128)}) custom-call(s32[5]{0:T(128)} %stack.23._.s_ref, bf16[192,4096]{1,0:T(8,128)(2,1)} %bitcast.27, bf16[192,2048]{1,0:T(8,128)(2,1)} %copy-done.8, bf16[32,8,8,384]{3,2,1,0:T(8,128)(2,1)} %copy-done.3, ...), custom_call_target="tpu_custom_call" | custom-call | flops 600000000 | bytes 10000000 | tf_op jit(solution)/shard_map/gating_kernel/pallas_call | solution.py:543
  129.1 20.0 %mlp_kernel.1 = (bf16[2048,384]{1,0:T(8,128)(2,1)}, bf16[2048,384]{1,0:T(8,128)(2,1)}, bf16[2048,768]{1,0:T(8,128)(2,1)}, bf16[2048,1536]{1,0:T(8,128)(2,1)}, f3...) custom-call(s32[5]{0:T(128)} %stack.23._.s_ref, ...), custom_call_target="tpu_custom_call" | custom-call | flops 7299999744 | bytes 24000000 | tf_op jit(solution)/shard_map/mlp_kernel/pallas_call | solution.py:553
  156.3 7.4 %resid_grad_kernel.1 = (bf16[2048,384]{1,0:T(8,128)(2,1)}, bf16[32,8,8,384]{3,2,1,0:T(8,128)(2,1)}) custom-call(s32[5]{0:T(128)} %stack.23._.s_ref, bf16[2048,384]{1,0:T(8,128)(2,1)} %get-tuple-element.105.resid_ref, bf16[2048,384]{1,0:T(8,128)(2,1)} %get-tuple-element.131.cot_ref, f32[1,384]{1,0:T(1,128)} %reshape.51.gain_ref, ...), custom_call_target="tpu_custom_call" | custom-call | flops 50000000 | bytes 12000000 | tf_op jit(solution)/shard_map/resid_grad_kernel/pallas_call | solution.py:564
  163.7 4.1 %all-to-all-start.2 = ((bf16[32,8,8,384]{3,2,1,0:T(8,128)(2,1)}), bf16[32,8,8,384]{3,2,1,0:T(8,128)(2,1)S(1)}, u32[]{:S(2)}, u32[]{:S(2)}) async-start(bf16[32,8,8,384]{3,2,1,0:T(8,128)(2,1)} %get-tuple-element.127), calls=%async_computation.2 | async-start | bytes 3145728 | tf_op jit(solution)/shard_map/all_to_all | solution.py:574
  167.8 7.2 %direct_kernel.1 = (bf16[384,2048]{1,0:T(8,128)(2,1)}, f32[384,384]{1,0:T(8,128)}) custom-call(s32[5]{0:T(128)} %stack.23._.s_ref, bf16[2048,384]{1,0:T(8,128)(2,1)} %get-tuple-element.132.g_resid_ref, bf16[2048,384]{1,0:T(8,128)(2,1)} %get-tuple-element.116.in_ref, bf16[32,8,8,384]{3,2,1,0:T(8,128)(2,1)} %copy-done.3, ...), custom_call_target="tpu_custom_call" | custom-call | flops 1 | bytes 1 | tf_op jit(solution)/shard_map/direct_kernel/pallas_call | solution.py:581
  178.4 11.0 %weight_grad_kernel.1 = (bf16[32,6,8,384]{3,2,1,0:T(8,128)(2,1)}, bf16[32,6,8,384]{3,2,1,0:T(8,128)(2,1)}) custom-call(s32[5]{0:T(128)} %stack.23._.s_ref, bf16[2048,384]{1,0:T(8,128)(2,1)} %get-tuple-element.128.normed_ref, bf16[2048,1536]{1,0:T(8,128)(2,1)} %get-tuple-element.129.grads_ref, bf16[2048,768]{1,0:T(8,128)(2,1)} %get-tuple-element.130.hidden_ref, ...), custom_call_target="tpu_custom_call" | custom-call | flops 1 | bytes 1 | tf_op jit(solution)/shard_map/weight_grad_kernel/pallas_call | solution.py:592
  194.1 6.6 %first_grad_kernel.1 = (bf16[32,14,8,384]{3,2,1,0:T(8,128)(2,1)}, bf16[8,256,384]{2,1,0:T(8,128)(2,1)}) custom-call(s32[5]{0:T(128)} %stack.23._.s_ref, bf16[32,8,8,384]{3,2,1,0:T(8,128)(2,1)} %copy-done.4, bf16[8,256,256]{2,1,0:T(8,128)(2,1)} %constant_dynamic-slice_fusion.1.f2_ref, bf16[32,6,8,384]{3,2,1,0:T(8,128)(2,1)} %get-tuple-element.138.keep_ref, ...), custom_call_target="tpu_custom_call" | custom-call | flops 400000000 | bytes 6000000 | tf_op jit(solution)/shard_map/first_grad_kernel/pallas_call | solution.py:600
  200.6 7.5 %all-to-all-start.3 = ((bf16[32,14,8,384]{3,2,1,0:T(8,128)(2,1)}), bf16[32,14,8,384]{3,2,1,0:T(8,128)(2,1)S(1)}, u32[]{:S(2)}, u32[]{:S(2)}) async-start(bf16[32,14,8,384]{3,2,1,0:T(8,128)(2,1)} %get-tuple-element.140), calls=%async_computation.3 | async-start | bytes 5505024 | tf_op jit(solution)/shard_map/all_to_all | solution.py:611
  213.2 5.2 %term_two_kernel.1 = (bf16[8,64,256]{2,1,0:T(8,128)(2,1)}, bf16[8,64,256]{2,1,0:T(8,128)(2,1)}, bf16[8,64,256]{2,1,0:T(8,128)(2,1)}, bf16[8,64,256]{2,1,0:T(8,128)(2,1)}) custom-call(s32[5]{0:T(128)} %stack.23._.s_ref, bf16[8,256,384]{2,1,0:T(8,128)(2,1)} %get-tuple-element.141.grad_ref, bf16[8,256,384]{2,1,0:T(8,128)(2,1)} %get-tuple-element.142.first_ref), custom_call_target="tpu_custom_call" | custom-call | flops 1 | bytes 1 | tf_op jit(solution)/shard_map/term_two_kernel/pallas_call | solution.py:627
  221.9 10.2 %collective-permute-start.15 = (bf16[8,64,256]{2,1,0:T(8,128)(2,1)}, bf16[8,64,256]{2,1,0:T(8,128)(2,1)S(1)}, u32[]{:S(2)}, u32[]{:S(2)}) collective-permute-start(bf16[8,64,256]{2,1,0:T(8,128)(2,1)} %get-tuple-element.146), channel_id=1, source_target_pairs={{0,6},{2,0},{4,2},{6,4},{1,7},{3,1},{5,3},{7,5},{8,14},{10,8},{12,... | collective-permute-start | bytes 786440 | tf_op jit(solution)/shard_map/ppermute | solution.py:466
  233.6 3.3 %mixed_join_kernel.1 = bf16[512,1536]{1,0:T(8,128)(2,1)} custom-call(s32[5]{0:T(128)} %stack.23._.s_ref, bf16[512,384]{1,0:T(8,128)(2,1)} %get-tuple-element.149.refs_0_, bf16[512,384]{1,0:T(8,128)(2,1)} %copy-done.10, bf16[512,384]{1,0:T(8,128)(2,1)} %copy-done.11, bf16[512,384]{1,0:T(8,128)(2,1)} %copy-done.12), custom_call_target="tpu_custom_call" | custom-call | flops 1 | bytes 1 | tf_op jit(solution)/shard_map/mixed_join_kernel/pallas_call | solution.py:577
  237.6 4.6 %collective-permute-done.15.d_ref = bf16[8,64,256]{2,1,0:T(8,128)(2,1)S(1)} collective-permute-done((bf16[8,64,256]{2,1,0:T(8,128)(2,1)}, bf16[8,64,256]{2,1,0:T(8,128)(2,1)S(1)}, u32[]{:S(2)}, u32[]{:S(2)}) %collective-permute-start.15) | collective-permute-done | bytes 262176 | tf_op jit(solution)/shard_map/ppermute | solution.py:466
  247.1 5.3 %back_kernel.1 = (bf16[192,2048]{1,0:T(8,128)(2,1)}, bf16[192,2048]{1,0:T(8,128)(2,1)}) custom-call(s32[5]{0:T(128)} %stack.23._.s_ref, bf16[32,14,8,384]{3,2,1,0:T(8,128)(2,1)} %copy-done.2, bf16[8,2,256,256]{3,2,1,0:T(8,128)(2,1)} %bitcast.35, bf16[384,2048]{1,0:T(8,128)(2,1)} %get-tuple-element.155.direct_ref), custom_call_target="tpu_custom_call" | custom-call | flops 12000000000 | bytes 6000000 | tf_op jit(solution)/shard_map/back_kernel/pallas_call | solution.py:635
  252.4 5.3 %term_one_kernel.1 = (bf16[8,64,256]{2,1,0:T(8,128)(2,1)}, bf16[8,64,256]{2,1,0:T(8,128)(2,1)}, bf16[8,64,256]{2,1,0:T(8,128)(2,1)}, bf16[8,64,256]{2,1,0:T(8,128)(2,1)}) custom-call(s32[5]{0:T(128)} %stack.23._.s_ref, bf16[32,14,8,384]{3,2,1,0:T(8,128)(2,1)} %copy-done.2, bf16[2048,384]{1,0:T(8,128)(2,1)} %get-tuple-element.116.in_ref), custom_call_target="tpu_custom_call" | custom-call | flops 1 | bytes 1 | tf_op jit(solution)/shard_map/term_one_kernel/pallas_call | solution.py:643
  257.7 3.2 %collective-permute-start.24 = (bf16[8,32,256]{2,1,0:T(8,128)(2,1)S(1)}, bf16[8,32,256]{2,1,0:T(8,128)(2,1)S(1)}, u32[]{:S(2)}, u32[]{:S(2)}) collective-permute-start(bf16[8,32,256]{2,1,0:T(8,128)(2,1)S(1)} %copy-done.33), channel_id=1, source_target_pairs={{0,1},{1,0},{2,3},{3,2},{4,5},{5,4},{6,7},{7,6},{8,9},{9,8},{10,11... | collective-permute-start | bytes 393224 | tf_op jit(solution)/shard_map/ppermute | solution.py:649
  266.6 3.5 %weight_sum_kernel.1 = f32[2,6,8,384]{3,2,1,0:T(8,128)} custom-call(s32[5]{0:T(128)} %stack.23._.s_ref, bf16[32,14,8,384]{3,2,1,0:T(8,128)(2,1)} %copy-done.2), custom_call_target="tpu_custom_call" | custom-call | flops 1 | bytes 1 | tf_op jit(solution)/shard_map/weight_sum_kernel/pallas_call | solution.py:652
  270.0 4.6 %collective-permute-start.25 = (f32[2,6,8,384]{3,2,1,0:T(8,128)}, f32[2,6,8,384]{3,2,1,0:T(8,128)S(1)}, u32[]{:S(2)}, u32[]{:S(2)}) collective-permute-start(f32[2,6,8,384]{3,2,1,0:T(8,128)} %weight_sum_kernel.1), channel_id=1, source_target_pairs={{0,0},{1,1},{8,2},{9,3},{16,4},{17,5},{24,6},{25,7},{32,8},{33,9},... | collective-permute-start | bytes 442376 | tf_op jit(solution)/shard_map/ppermute | solution.py:658
  279.3 9.8 %collective-permute-done.22.got_ref = bf16[192,2048]{1,0:T(8,128)(2,1)S(1)} collective-permute-done((bf16[192,2048]{1,0:T(8,128)(2,1)S(1)}, bf16[192,2048]{1,0:T(8,128)(2,1)S(1)}, u32[]{:S(2)}, u32[]{:S(2)}) %collective-permute-start.22) | collective-permute-done | bytes 786464 | tf_op jit(solution)/shard_map/ppermute | solution.py:651
  293.5 3.1 %join_kernel.1 = bf16[192,4096]{1,0:T(8,128)(2,1)} custom-call(s32[5]{0:T(128)} %stack.23._.s_ref, bf16[192,2048]{1,0:T(8,128)(2,1)} %get-tuple-element.156.own_ref, bf16[192,2048]{1,0:T(8,128)(2,1)} %copy-done.9), custom_call_target="tpu_custom_call" | custom-call | flops 1 | bytes 1 | tf_op jit(solution)/shard_map/join_kernel/pallas_call | solution.py:671
  (139 shorter events, 73.3 us)
Async XLA Ops:
  0.6 39.8 %copy-start = (bf16[16,256,256]{2,1,0:T(8,128)(2,1)S(1)}, bf16[16,256,256]{2,1,0:T(8,128)(2,1)}, u32[]{:S(2)}) copy-start(bf16[16,256,256]{2,1,0:T(8,128)(2,1)} %param.11) | copy-start | bytes 6291460
  6.3 9.4 %collective-permute-start = (bf16[2,6,8,384]{3,2,1,0:T(8,128)(2,1)}, bf16[2,6,8,384]{3,2,1,0:T(8,128)(2,1)S(1)}, u32[]{:S(2)}, u32[]{:S(2)}) collective-permute-start(bf16[2,6,8,384]{3,2,1,0:T(8,128)(2,1)} %payload_kernel.1), channel_id=1, source_target_pairs={{0,0},{1,1},{2,8},{3,9},{4,16},{5,17},{6,24},{7,25},{8,32},{9,33},... | collective-permute-start | bytes 221192 | tf_op jit(solution)/shard_map/ppermute | solution.py:499
  8.2 22.2 %collective-permute-start.1 = (bf16[192,2048]{1,0:T(8,128)(2,1)}, bf16[192,2048]{1,0:T(8,128)(2,1)S(1)}, u32[]{:S(2)}, u32[]{:S(2)}) collective-permute-start(bf16[192,2048]{1,0:T(8,128)(2,1)} %gather_kernel.1), channel_id=1, source_target_pairs={{0,1},{1,0},{2,3},{3,2},{4,5},{5,4},{6,7},{7,6},{8,9},{9,8},{10,11... | collective-permute-start | bytes 2359304 | tf_op jit(solution)/shard_map/ppermute | solution.py:491
  31.3 45.1 %all-to-all-start = ((bf16[32,14,8,384]{3,2,1,0:T(8,128)(2,1)}), bf16[32,14,8,384]{3,2,1,0:T(8,128)(2,1)}, u32[]{:S(2)}, u32[]{:S(2)}) async-start(bf16[32,14,8,384]{3,2,1,0:T(8,128)(2,1)} %first_kernel.1), calls=%async_computation | async-start | bytes 5505024 | tf_op jit(solution)/shard_map/all_to_all | solution.py:511
  82.1 29.6 %all-to-all-start.1 = ((bf16[32,8,8,384]{3,2,1,0:T(8,128)(2,1)}), bf16[32,8,8,384]{3,2,1,0:T(8,128)(2,1)S(1)}, u32[]{:S(2)}, u32[]{:S(2)}) async-start(bf16[32,8,8,384]{3,2,1,0:T(8,128)(2,1)} %get-tuple-element.102), calls=%async_computation.1 | async-start | bytes 3145728 | tf_op jit(solution)/shard_map/all_to_all | solution.py:532
  89.8 8.1 %collective-permute-start.2 = (bf16[32,6,8,384]{3,2,1,0:T(8,128)(2,1)S(1)}, bf16[32,6,8,384]{3,2,1,0:T(8,128)(2,1)S(1)}, u32[]{:S(2)}, u32[]{:S(2)}) collective-permute-start(bf16[32,6,8,384]{3,2,1,0:T(8,128)(2,1)S(1)} %slice.51.own_ref), channel_id=1, source_target_pairs={{0,8},{8,0},{1,9},{9,1},{2,10},{10,2},{3,11},{11,3},{4,12},{12,4},... | collective-permute-start | bytes 3538952 | tf_op jit(solution)/shard_map/ppermute | solution.py:535
  93.1 31.4 %collective-permute-start.6 = (bf16[512,384]{1,0:T(8,128)(2,1)}, bf16[512,384]{1,0:T(8,128)(2,1)S(1)}, u32[]{:S(2)}, u32[]{:S(2)}) collective-permute-start(bf16[512,384]{1,0:T(8,128)(2,1)} %get-tuple-element.111), channel_id=1, source_target_pairs={{0,6},{2,0},{4,2},{6,4},{1,7},{3,1},{5,3},{7,5},{8,14},{10,8},{12,... | collective-permute-start | bytes 1179656 | tf_op jit(solution)/shard_map/ppermute | solution.py:519
  96.0 29.9 %collective-permute-start.7 = (bf16[512,384]{1,0:T(8,128)(2,1)}, bf16[512,384]{1,0:T(8,128)(2,1)S(1)}, u32[]{:S(2)}, u32[]{:S(2)}) collective-permute-start(bf16[512,384]{1,0:T(8,128)(2,1)} %get-tuple-element.112), channel_id=1, source_target_pairs={{0,4},{2,6},{4,0},{6,2},{1,5},{3,7},{5,1},{7,3},{8,12},{10,14},{12... | collective-permute-start | bytes 1179656 | tf_op jit(solution)/shard_map/ppermute | solution.py:519
  97.2 28.7 %collective-permute-start.8 = (bf16[512,384]{1,0:T(8,128)(2,1)}, bf16[512,384]{1,0:T(8,128)(2,1)S(1)}, u32[]{:S(2)}, u32[]{:S(2)}) collective-permute-start(bf16[512,384]{1,0:T(8,128)(2,1)} %get-tuple-element.113), channel_id=1, source_target_pairs={{0,2},{2,4},{4,6},{6,0},{1,3},{3,5},{5,7},{7,1},{8,10},{10,12},{12... | collective-permute-start | bytes 1179656 | tf_op jit(solution)/shard_map/ppermute | solution.py:519
  119.5 6.4 %collective-permute-start.5 = (f32[8,512]{1,0:T(8,128)}, f32[8,512]{1,0:T(8,128)S(1)}, u32[]{:S(2)}, u32[]{:S(2)}) collective-permute-start(f32[8,512]{1,0:T(8,128)} %get-tuple-element.109.refs_0_), channel_id=1, source_target_pairs={{0,2},{2,4},{4,6},{6,0},{1,3},{3,5},{5,7},{7,1},{8,10},{10,12},{12... | collective-permute-start | bytes 49160 | tf_op jit(solution)/shard_map/ppermute | solution.py:455
  122.1 5.5 %collective-permute-start.4 = (f32[8,512]{1,0:T(8,128)}, f32[8,512]{1,0:T(8,128)S(1)}, u32[]{:S(2)}, u32[]{:S(2)}) collective-permute-start(f32[8,512]{1,0:T(8,128)} %get-tuple-element.109.refs_0_), channel_id=1, source_target_pairs={{0,4},{2,6},{4,0},{6,2},{1,5},{3,7},{5,1},{7,3},{8,12},{10,14},{12... | collective-permute-start | bytes 49160 | tf_op jit(solution)/shard_map/ppermute | solution.py:455
  124.5 4.0 %collective-permute-start.3 = (f32[8,512]{1,0:T(8,128)}, f32[8,512]{1,0:T(8,128)S(1)}, u32[]{:S(2)}, u32[]{:S(2)}) collective-permute-start(f32[8,512]{1,0:T(8,128)} %get-tuple-element.109.refs_0_), channel_id=1, source_target_pairs={{0,6},{2,0},{4,2},{6,4},{1,7},{3,1},{5,3},{7,5},{8,14},{10,8},{12,... | collective-permute-start | bytes 49160 | tf_op jit(solution)/shard_map/ppermute | solution.py:455
  149.0 5.0 %collective-permute-start.11 = (f32[8,512]{1,0:T(8,128)}, f32[8,512]{1,0:T(8,128)S(1)}, u32[]{:S(2)}, u32[]{:S(2)}) collective-permute-start(f32[8,512]{1,0:T(8,128)} %get-tuple-element.134.refs_4_), channel_id=1, source_target_pairs={{0,2},{2,4},{4,6},{6,0},{1,3},{3,5},{5,7},{7,1},{8,10},{10,12},{12... | collective-permute-start | bytes 49160 | tf_op jit(solution)/shard_map/ppermute | solution.py:455
  149.1 5.5 %collective-permute-start.10 = (f32[8,512]{1,0:T(8,128)}, f32[8,512]{1,0:T(8,128)S(1)}, u32[]{:S(2)}, u32[]{:S(2)}) collective-permute-start(f32[8,512]{1,0:T(8,128)} %get-tuple-element.134.refs_4_), channel_id=1, source_target_pairs={{0,4},{2,6},{4,0},{6,2},{1,5},{3,7},{5,1},{7,3},{8,12},{10,14},{12... | collective-permute-start | bytes 49160 | tf_op jit(solution)/shard_map/ppermute | solution.py:455
  151.5 4.2 %collective-permute-start.9 = (f32[8,512]{1,0:T(8,128)}, f32[8,512]{1,0:T(8,128)S(1)}, u32[]{:S(2)}, u32[]{:S(2)}) collective-permute-start(f32[8,512]{1,0:T(8,128)} %get-tuple-element.134.refs_4_), channel_id=1, source_target_pairs={{0,6},{2,0},{4,2},{6,4},{1,7},{3,1},{5,3},{7,5},{8,14},{10,8},{12,... | collective-permute-start | bytes 49160 | tf_op jit(solution)/shard_map/ppermute | solution.py:455
  163.7 28.9 %all-to-all-start.2 = ((bf16[32,8,8,384]{3,2,1,0:T(8,128)(2,1)}), bf16[32,8,8,384]{3,2,1,0:T(8,128)(2,1)S(1)}, u32[]{:S(2)}, u32[]{:S(2)}) async-start(bf16[32,8,8,384]{3,2,1,0:T(8,128)(2,1)} %get-tuple-element.127), calls=%async_computation.2 | async-start | bytes 3145728 | tf_op jit(solution)/shard_map/all_to_all | solution.py:574
  189.5 3.1 %collective-permute-start.12 = (bf16[32,6,8,384]{3,2,1,0:T(8,128)(2,1)}, bf16[32,6,8,384]{3,2,1,0:T(8,128)(2,1)S(1)}, u32[]{:S(2)}, u32[]{:S(2)}) collective-permute-start(bf16[32,6,8,384]{3,2,1,0:T(8,128)(2,1)} %get-tuple-element.139), channel_id=1, source_target_pairs={{0,8},{8,0},{1,9},{9,1},{2,10},{10,2},{3,11},{11,3},{4,12},{12,4},... | collective-permute-start | bytes 3538952 | tf_op jit(solution)/shard_map/ppermute | solution.py:598
  200.6 45.0 %all-to-all-start.3 = ((bf16[32,14,8,384]{3,2,1,0:T(8,128)(2,1)}), bf16[32,14,8,384]{3,2,1,0:T(8,128)(2,1)S(1)}, u32[]{:S(2)}, u32[]{:S(2)}) async-start(bf16[32,14,8,384]{3,2,1,0:T(8,128)(2,1)} %get-tuple-element.140), calls=%async_computation.3 | async-start | bytes 5505024 | tf_op jit(solution)/shard_map/all_to_all | solution.py:611
  208.2 13.8 %collective-permute-start.16 = (bf16[512,384]{1,0:T(8,128)(2,1)}, bf16[512,384]{1,0:T(8,128)(2,1)S(1)}, u32[]{:S(2)}, u32[]{:S(2)}) collective-permute-start(bf16[512,384]{1,0:T(8,128)(2,1)} %get-tuple-element.150), channel_id=1, source_target_pairs={{0,2},{2,4},{4,6},{6,0},{1,3},{3,5},{5,7},{7,1},{8,10},{10,12},{12... | collective-permute-start | bytes 1179656 | tf_op jit(solution)/shard_map/ppermute | solution.py:466
  210.0 22.2 %collective-permute-start.17 = (bf16[512,384]{1,0:T(8,128)(2,1)S(1)}, bf16[512,384]{1,0:T(8,128)(2,1)S(1)}, u32[]{:S(2)}, u32[]{:S(2)}) collective-permute-start(bf16[512,384]{1,0:T(8,128)(2,1)S(1)} %copy-done.29), channel_id=1, source_target_pairs={{0,4},{2,6},{4,0},{6,2},{1,5},{3,7},{5,1},{7,3},{8,12},{10,14},{12... | collective-permute-start | bytes 1179656 | tf_op jit(solution)/shard_map/ppermute | solution.py:466
  212.6 19.5 %collective-permute-start.18 = (bf16[512,384]{1,0:T(8,128)(2,1)S(1)}, bf16[512,384]{1,0:T(8,128)(2,1)S(1)}, u32[]{:S(2)}, u32[]{:S(2)}) collective-permute-start(bf16[512,384]{1,0:T(8,128)(2,1)S(1)} %copy-done.28), channel_id=1, source_target_pairs={{0,6},{2,0},{4,2},{6,4},{1,7},{3,1},{5,3},{7,5},{8,14},{10,8},{12,... | collective-permute-start | bytes 1179656 | tf_op jit(solution)/shard_map/ppermute | solution.py:466
  218.4 18.5 %collective-permute-start.13 = (bf16[8,64,256]{2,1,0:T(8,128)(2,1)}, bf16[8,64,256]{2,1,0:T(8,128)(2,1)S(1)}, u32[]{:S(2)}, u32[]{:S(2)}) collective-permute-start(bf16[8,64,256]{2,1,0:T(8,128)(2,1)} %get-tuple-element.144), channel_id=1, source_target_pairs={{0,2},{2,4},{4,6},{6,0},{1,3},{3,5},{5,7},{7,1},{8,10},{10,12},{12... | collective-permute-start | bytes 786440 | tf_op jit(solution)/shard_map/ppermute | solution.py:466
  219.8 17.7 %collective-permute-start.14 = (bf16[8,64,256]{2,1,0:T(8,128)(2,1)}, bf16[8,64,256]{2,1,0:T(8,128)(2,1)S(1)}, u32[]{:S(2)}, u32[]{:S(2)}) collective-permute-start(bf16[8,64,256]{2,1,0:T(8,128)(2,1)} %get-tuple-element.145), channel_id=1, source_target_pairs={{0,4},{2,6},{4,0},{6,2},{1,5},{3,7},{5,1},{7,3},{8,12},{10,14},{12... | collective-permute-start | bytes 786440 | tf_op jit(solution)/shard_map/ppermute | solution.py:466
  221.9 20.2 %collective-permute-start.15 = (bf16[8,64,256]{2,1,0:T(8,128)(2,1)}, bf16[8,64,256]{2,1,0:T(8,128)(2,1)S(1)}, u32[]{:S(2)}, u32[]{:S(2)}) collective-permute-start(bf16[8,64,256]{2,1,0:T(8,128)(2,1)} %get-tuple-element.146), channel_id=1, source_target_pairs={{0,6},{2,0},{4,2},{6,4},{1,7},{3,1},{5,3},{7,5},{8,14},{10,8},{12,... | collective-permute-start | bytes 786440 | tf_op jit(solution)/shard_map/ppermute | solution.py:466
  252.4 13.8 %copy-start.27 = (bf16[192,2048]{1,0:T(8,128)(2,1)S(1)}, bf16[192,2048]{1,0:T(8,128)(2,1)}, u32[]{:S(2)}) copy-start(bf16[192,2048]{1,0:T(8,128)(2,1)} %get-tuple-element.169) | copy-start | bytes 2359300
  257.7 8.9 %collective-permute-start.24 = (bf16[8,32,256]{2,1,0:T(8,128)(2,1)S(1)}, bf16[8,32,256]{2,1,0:T(8,128)(2,1)S(1)}, u32[]{:S(2)}, u32[]{:S(2)}) collective-permute-start(bf16[8,32,256]{2,1,0:T(8,128)(2,1)S(1)} %copy-done.33), channel_id=1, source_target_pairs={{0,1},{1,0},{2,3},{3,2},{4,5},{5,4},{6,7},{7,6},{8,9},{9,8},{10,11... | collective-permute-start | bytes 393224 | tf_op jit(solution)/shard_map/ppermute | solution.py:649
  260.9 18.4 %collective-permute-start.19 = (bf16[8,64,256]{2,1,0:T(8,128)(2,1)}, bf16[8,64,256]{2,1,0:T(8,128)(2,1)S(1)}, u32[]{:S(2)}, u32[]{:S(2)}) collective-permute-start(bf16[8,64,256]{2,1,0:T(8,128)(2,1)} %get-tuple-element.166), channel_id=1, source_target_pairs={{0,2},{2,4},{4,6},{6,0},{1,3},{3,5},{5,7},{7,1},{8,10},{10,12},{12... | collective-permute-start | bytes 786440 | tf_op jit(solution)/shard_map/ppermute | solution.py:466
  261.6 17.7 %collective-permute-start.20 = (bf16[8,64,256]{2,1,0:T(8,128)(2,1)}, bf16[8,64,256]{2,1,0:T(8,128)(2,1)S(1)}, u32[]{:S(2)}, u32[]{:S(2)}) collective-permute-start(bf16[8,64,256]{2,1,0:T(8,128)(2,1)} %get-tuple-element.167), channel_id=1, source_target_pairs={{0,4},{2,6},{4,0},{6,2},{1,5},{3,7},{5,1},{7,3},{8,12},{10,14},{12... | collective-permute-start | bytes 786440 | tf_op jit(solution)/shard_map/ppermute | solution.py:466
  264.2 15.1 %collective-permute-start.21 = (bf16[8,64,256]{2,1,0:T(8,128)(2,1)}, bf16[8,64,256]{2,1,0:T(8,128)(2,1)S(1)}, u32[]{:S(2)}, u32[]{:S(2)}) collective-permute-start(bf16[8,64,256]{2,1,0:T(8,128)(2,1)} %get-tuple-element.168), channel_id=1, source_target_pairs={{0,6},{2,0},{4,2},{6,4},{1,7},{3,1},{5,3},{7,5},{8,14},{10,8},{12,... | collective-permute-start | bytes 786440 | tf_op jit(solution)/shard_map/ppermute | solution.py:466
  266.2 22.9 %collective-permute-start.22 = (bf16[192,2048]{1,0:T(8,128)(2,1)S(1)}, bf16[192,2048]{1,0:T(8,128)(2,1)S(1)}, u32[]{:S(2)}, u32[]{:S(2)}) collective-permute-start(bf16[192,2048]{1,0:T(8,128)(2,1)S(1)} %copy-done.27), channel_id=1, source_target_pairs={{0,1},{1,0},{2,3},{3,2},{4,5},{5,4},{6,7},{7,6},{8,9},{9,8},{10,11... | collective-permute-start | bytes 2359304 | tf_op jit(solution)/shard_map/ppermute | solution.py:651
  270.0 8.6 %collective-permute-start.25 = (f32[2,6,8,384]{3,2,1,0:T(8,128)}, f32[2,6,8,384]{3,2,1,0:T(8,128)S(1)}, u32[]{:S(2)}, u32[]{:S(2)}) collective-permute-start(f32[2,6,8,384]{3,2,1,0:T(8,128)} %weight_sum_kernel.1), channel_id=1, source_target_pairs={{0,0},{1,1},{8,2},{9,3},{16,4},{17,5},{24,6},{25,7},{32,8},{33,9},... | collective-permute-start | bytes 442376 | tf_op jit(solution)/shard_map/ppermute | solution.py:658
  291.8 6.7 %collective-permute-start.23 = (bf16[8,32,256]{2,1,0:T(8,128)(2,1)}, bf16[8,32,256]{2,1,0:T(8,128)(2,1)S(1)}, u32[]{:S(2)}, u32[]{:S(2)}) collective-permute-start(bf16[8,32,256]{2,1,0:T(8,128)(2,1)} %get-tuple-element.176), channel_id=1, source_target_pairs={{0,1},{1,0},{2,3},{3,2},{4,5},{5,4},{6,7},{7,6},{8,9},{9,8},{10,11... | collective-permute-start | bytes 393224 | tf_op jit(solution)/shard_map/ppermute | solution.py:669
  (33 other events, 127.8 us)

commit v5 on v4

--- a/solution.py
+++ b/solution.py
@@ -121,6 +121,10 @@
     return lax.dot_general(a, b, (((0,), (0,)), ((), ())), preferred_element_type=F32)
 
 
+def sigmoid(value):
+    return 0.5 * jnp.tanh(0.5 * value) + 0.5
+
+
 def first_kernel(_, f1_ref, in_ref, payload_ref, out_ref):
     step = pl.program_id(0)
 
@@ -214,7 +218,7 @@
     pgate = dot(value, win_ref[...]).astype(BF)
     pgate_ref[...] = pgate
     value_f = value.astype(F32)
-    silu_in = value_f * jax.nn.sigmoid(value_f)
+    silu_in = value_f * sigmoid(value_f)
     resid = (value_f + read_pieces(second_ref) * pgate.astype(F32) * silu_in).astype(BF)
     resid_ref[...] = resid
     resid_f = resid.astype(F32)
@@ -248,11 +252,11 @@
     gate = dot(normed, wg_ref[...])
     upper = dot(normed, wu_ref[...])
     g_hidden = dot_t(cot, wd_ref[...])
-    sig = jax.nn.sigmoid(gate)
+    sig = sigmoid(gate)
     act = gate * sig
     hidden = (act * upper).astype(BF)
     hidden_ref[...] = hidden
-    g_gate = (g_hidden * upper * sig * (1.0 + gate * (1.0 - sig))).astype(BF)
+    g_gate = (g_hidden * upper * (sig + act * (1.0 - sig))).astype(BF)
     g_up = (g_hidden * act).astype(BF)
     grads_ref[:, :768] = g_gate
     grads_ref[:, 768:] = g_up
@@ -288,7 +292,7 @@
     ).astype(BF)
     g_resid_ref[...] = g_resid
     value = in_ref[...].astype(F32)
-    silu_in = value * jax.nn.sigmoid(value)
+    silu_in = value * sigmoid(value)
     g_second = (g_resid.astype(F32) * pgate_ref[...].astype(F32) * silu_in).astype(BF)
     for r in range(2):
         g_second_ref[:, r] = g_second[r * 256 : (r + 1) * 256].reshape(32, 8, DB)
@@ -297,7 +301,7 @@
 def direct_kernel(_, g_resid_ref, in_ref, second_ref, pgate_ref, win_ref, g_direct_ref, term_ref):
     resid_grad = g_resid_ref[...].astype(F32)
     value = in_ref[...].astype(F32)
-    sig = jax.nn.sigmoid(value)
+    sig = sigmoid(value)
     second = read_pieces(second_ref)
     g_pgate = (resid_grad * second * (value * sig)).astype(BF)
     slope = sig * (1.0 + value * (1.0 - sig))
@@ -409,9 +413,9 @@
 
 
 def weight_grad_kernel(
-    s_ref, normed_ref, grads_ref, hidden_ref, cot_ref, entry_ref, gain_ref, keep_ref, give_ref,
-    across, down,
+    s_ref, normed_ref, grads_ref, hidden_ref, cot_ref, entry_ref, *refs,
 ):
+    inners, (keep_ref, give_ref, across, down) = refs[:4], refs[4:]
     step = pl.program_id(0)
 
     @pl.when(step == 0)
@@ -426,10 +430,15 @@
     def _():
         first = s_ref[4] == 0
         fill = jnp.zeros((8, DB), F32)
+        block = lax.broadcasted_iota(jnp.int32, (4, DB), 0)
+        gains = jnp.zeros((4, DB), F32)
+        for j in range(4):
+            mine = jnp.broadcast_to(inners[j][4:5, :DB], (4, DB))
+            gains = gains + jnp.where(block == lax.rem(s_ref[1] + j, 4), mine, 0.0)
         for shard in range(32):
             here = slice(shard * 12, shard * 12 + 12)
             gates, entries = across[here, :], entry_ref[here, :]
-            low = [gates[:, :DB], gates[:, DB : 2 * DB], entries, gain_ref[...], fill]
+            low = [gates[:, :DB], gates[:, DB : 2 * DB], entries, gains, fill]
             high = [gates[:, 2 * DB : 3 * DB], gates[:, 3 * DB :]]
             high.append(down[shard * 24 : shard * 24 + 24, :])
             low = jnp.concatenate(low, axis=0)
@@ -453,13 +462,6 @@
 
 def around(value, axis):
     return [value] + [lax.ppermute(value, axis, turn(axis, 4, -j)) for j in (1, 2, 3)]
-
-
-def in_order(parts, me):
-    size = parts[0].shape[0]
-    return lax.dynamic_slice_in_dim(
-        jnp.concatenate(parts + parts, axis=0), lax.rem(4 - me, 4) * size, 4 * size, 0
-    )
 
 
 def send_each(parts, axis):
@@ -503,7 +505,7 @@
          pl.BlockSpec((192, 512), lambda t, s: (0, lax.min(t, 7))), whole(2, 6, 8, DB)],
         pl.BlockSpec((32, 1, 8, DB), lambda t, s: (0, t, 0, 0)),
         bf(32, 14, 8, DB),
-        (12_000_000_000, 6_000_000),
+        (1, 1),
     )(at, factor_one, turned_in, payload)
     first_local, other, turned_in, grad_out, factor_two = lax.optimization_barrier(
         (first_local, other, turned_in, grad_out, factor_two)
@@ -586,15 +588,13 @@
         (1, 1),
     )(at, g_resid, input_mlp, second, pgate, win)
 
-    gain_terms = in_order([v[4:5, :DB] for v in inners], xi).reshape(1, D)
-    gain_rows = gain_terms.reshape(4, DB)
     halves = whole(32, 6, 8, DB)
     keep, give = call(
         weight_grad_kernel, (2,),
-        [rows(DB, 1024), rows(1536, 1024), rows(768, 1024), rows(DB, 1024), whole(DB, DB), whole(4, DB)],
+        [rows(DB, 1024), rows(1536, 1024), rows(768, 1024), rows(DB, 1024), whole(DB, DB)] + SUMS,
         [halves] * 2, [bf(32, 6, 8, DB)] * 2, (1, 1),
         [pltpu.VMEM((DB, 1536), F32), pltpu.VMEM((768, DB), F32)],
-    )(at, normed, grads, hidden, cot, term_entry, gain_rows)
+    )(at, normed, grads, hidden, cot, term_entry, *inners)
     got = lax.ppermute(give, "core", SWAP)
 
     first_grad, second_grad = call(
@@ -639,15 +639,16 @@
         [bf(192, 2048), bf(192, 2048)],
         (12_000_000_000, 6_000_000),
     )(at, g_first, factor_one.reshape(8, 2, 256, 256), g_direct)
-    g_first, give_grad = lax.optimization_barrier((g_first, give_grad))
+    got_two = lax.ppermute(sums_two[1], "zh", SWAP)
+    g_first, give_grad, got_two = lax.optimization_barrier((g_first, give_grad, got_two))
     terms_one = call(
         term_one_kernel, (4,), [PIECES, rows(DB)],
         [term_out] * 4, [bf(8, 64, 256)] * 4, (1, 1), square_scratch,
     )(at, g_first, input_mlp)
 
-    terms_one, sums_two = lax.optimization_barrier((terms_one, sums_two))
-    got_two = lax.ppermute(sums_two[1], "zh", SWAP)
-    for_sums, got_two = lax.optimization_barrier((g_first, got_two))
+    got_two, terms_one = lax.optimization_barrier((got_two, terms_one))
+    terms_one = send_each(terms_one, "x")
+    for_sums, terms_one = lax.optimization_barrier((g_first, terms_one))
     got_grad = lax.ppermute(give_grad, "zh", SWAP)
     summed = call(
         weight_sum_kernel, (3,),
@@ -664,7 +665,6 @@
     grad_norm_gain = summed[0].reshape(48, DB)[36:40].reshape(D)
 
     grad_factor_two = factor_gradient(sums_two[0], got_two, 1)
-    terms_one, got_grad = lax.optimization_barrier((send_each(terms_one, "x"), got_grad))
     sums_one = factor_sums(terms_one)
     got_one = lax.ppermute(sums_one[1], "zh", SWAP)
     grad_factor_one = factor_gradient(sums_one[0], got_one, 4)

time: 304 us -> 295 us (0.970)
  starting transfers between devices: 80.9 us -> 73.8 us
  local copies, waits for them, and re-layouts: 21.6 us -> 17.1 us
  waiting for transfers between devices: 74.5 us -> 77.7 us
    ppermute x9, waiting for transfers between devices: 5.23 us -> 21.2 us  [send_each(): lax.ppermute(parts[j], axis, turn(axis, 4, j))]
    ppermute x9, starting transfers between devices: 24 us -> 13.3 us  [send_each(): lax.ppermute(parts[j], axis, turn(axis, 4, j))]
    ppermute x1, waiting for transfers between devices: 9.75 us -> 0.01 us  [per_device(): got_grad = lax.ppermute(give_grad, 'zh', SWAP)]
    ppermute x1, waiting for transfers between devices: 4.17 us -> 0.01 us  [per_device(): other = lax.ppermute(give, 'zh', SWAP)]
    ppermute x1, waiting for transfers between devices: 3.56 us -> 7.53 us  [per_device(): payload = lax.ppermute(payload, ALL, shard_moves())]
    all_to_all x1, starting transfers between devices: 9.19 us -> 5.51 us  [per_device(): lax.all_to_all(first_local, PLANE, split_axis=0, concat_axis=0, tiled=True)]
    unnamed x70 -> x68, local copies, waits for them, and re-layouts: 10.8 us -> 9.82 us
  transfers between devices with their start and end apart: 30 -> 30, of which waited for: 13 -> 17; matrix products, arithmetic and copies ran while one was open for 4% -> 2% of each run, Pallas kernels for 21% -> 25%
where the time goes in v5:
time: 295 us; the launch traced here: 293 us
  Pallas kernels  122 us (41%)
  waiting for transfers between devices  77.7 us (26%)
  starting transfers between devices  73.8 us (25%)
  local copies, waits for them, and re-layouts  17.1 us (6%)
    all_to_all x1, waiting for transfers between devices, per_device(): lax.all_to_all(first_local, PLANE, split_axis=0, concat_axis=0, tiled=True)  34.8 us
    ppermute x9, waiting for transfers between devices, send_each(): lax.ppermute(parts[j], axis, turn(axis, 4, j))  21.2 us
    pallas_call x1, Pallas kernels, per_device(): call(mlp_kernel, (4,), [turned_rows(DB), whole(1, DB), whole(DB, 768), wh...  19.4 us
    ppermute x9, starting transfers between devices, send_each(): lax.ppermute(parts[j], axis, turn(axis, 4, j))  13.3 us
    ppermute x6, starting transfers between devices, around(): lax.ppermute(value, axis, turn(axis, 4, -j))  12.2 us
    pallas_call x1, Pallas kernels, per_device(): call(weight_grad_kernel, (2,), [rows(DB, 1024), rows(1536, 1024), rows(76...  11.1 us
    pallas_call x1, Pallas kernels, per_device(): call(first_kernel, (14,), [pl.BlockSpec((2, 256, 256), lambda t, s: (lax....  9.89 us
    unnamed x68, local copies, waits for them, and re-layouts  9.82 us
  transfers between devices with their start and end apart: 30, of which 17 were waited for; matrix products, arithmetic and copies ran while one was open for 2% of the time, Pallas kernels for 25%

profile of v5, /device:TPU:2, one launch (start us, length us, event | category | flops | bytes accessed | tf_op | source)
XLA Modules:
  0.0 292.5 jit_solution(15881836762212216602)
XLA Ops:
  1.3 2.8 gather_kernel.1
  4.1 3.9 %collective-permute-start.1 = (bf16[192,2048]{1,0:T(8,128)(2,1)}, bf16[192,2048]{1,0:T(8,128)(2,1)S(1)}, u32[]{:S(2)}, u32[]{:S(2)}) collective-permute-start(bf16[192,2048]{1,0:T(8,128)(2,1)} %gather_kernel.1), channel_id=1, source_target_pairs={{0,1},{1,0},{2,3},{3,2},{4,5},{5,4},{6,7},{7,6},{8,9},{9,8},{10,11... | collective-permute-start | bytes 2359304 | tf_op jit(solution)/shard_map/ppermute | solution.py:493
  12.0 7.5 %collective-permute-done.payload_ref = bf16[2,6,8,384]{3,2,1,0:T(8,128)(2,1)S(1)} collective-permute-done((bf16[2,6,8,384]{3,2,1,0:T(8,128)(2,1)}, bf16[2,6,8,384]{3,2,1,0:T(8,128)(2,1)S(1)}, u32[]{:S(2)}, u32[]{:S(2)}) %collective-permute-start) | collective-permute-done | bytes 73760 | tf_op jit(solution)/shard_map/ppermute | solution.py:501
  20.1 9.9 %first_kernel.1 = bf16[32,14,8,384]{3,2,1,0:T(8,128)(2,1)} custom-call(s32[5]{0:T(128)} %stack.23._.s_ref, bf16[16,256,256]{2,1,0:T(8,128)(2,1)} %f1_ref.1, bf16[192,4096]{1,0:T(8,128)(2,1)} %bitcast.26, bf16[2,6,8,384]{3,2,1,0:T(8,128)(2,1)} %copy-done.21), custom_call_target="tpu_custom_call" | custom-call | flops 1 | bytes 1 | tf_op jit(solution)/shard_map/first_kernel/pallas_call | solution.py:502
  30.9 5.5 %all-to-all-start = ((bf16[32,14,8,384]{3,2,1,0:T(8,128)(2,1)}), bf16[32,14,8,384]{3,2,1,0:T(8,128)(2,1)}, u32[]{:S(2)}, u32[]{:S(2)}) async-start(bf16[32,14,8,384]{3,2,1,0:T(8,128)(2,1)} %first_kernel.1), calls=%async_computation | async-start | bytes 5505024 | tf_op jit(solution)/shard_map/all_to_all | solution.py:513
  37.6 34.8 %all-to-all-done.piece_ref = bf16[32,14,8,384]{3,2,1,0:T(8,128)(2,1)} async-done(((bf16[32,14,8,384]{3,2,1,0:T(8,128)(2,1)}), bf16[32,14,8,384]{3,2,1,0:T(8,128)(2,1)}, u32[]{:S(2)}, u32[]{:S(2)}) %all-to-all-start) | async-done | bytes 2752544 | tf_op jit(solution)/shard_map/all_to_all | solution.py:513
  72.3 5.7 %second_kernel.1 = (bf16[32,8,8,384]{3,2,1,0:T(8,128)(2,1)}, bf16[8,256,384]{2,1,0:T(8,128)(2,1)}) custom-call(s32[5]{0:T(128)} %stack.23._.s_ref, bf16[32,14,8,384]{3,2,1,0:T(8,128)(2,1)} %all-to-all-done.piece_ref, bf16[8,256,256]{2,1,0:T(8,128)(2,1)} %constant_dynamic-slice_fusion.f2_ref), custom_call_target="tpu_custom_call" | custom-call | flops 400000000 | bytes 6000000 | tf_op jit(solution)/shard_map/second_kernel/pallas_call | solution.py:526
  78.1 6.3 %all-to-all-start.1 = ((bf16[32,8,8,384]{3,2,1,0:T(8,128)(2,1)}), bf16[32,8,8,384]{3,2,1,0:T(8,128)(2,1)S(1)}, u32[]{:S(2)}, u32[]{:S(2)}) async-start(bf16[32,8,8,384]{3,2,1,0:T(8,128)(2,1)} %get-tuple-element.100), calls=%async_computation.1 | async-start | bytes 3145728 | tf_op jit(solution)/shard_map/all_to_all | solution.py:534
  86.1 3.0 %copy_three_kernel.1 = (bf16[512,384]{1,0:T(8,128)(2,1)}, bf16[512,384]{1,0:T(8,128)(2,1)}, bf16[512,384]{1,0:T(8,128)(2,1)}) custom-call(s32[5]{0:T(128)} %stack.23._.s_ref, bf16[512,1536]{1,0:T(8,128)(2,1)} %refs_4_, bf16[512,1536]{1,0:T(8,128)(2,1)} %refs_4_, bf16[512,1536]{1,0:T(8,128)(2,1)} %refs_4_), custom_call_target="tpu_custom_call" | custom-call | flops 1 | bytes 1 | tf_op jit(solution)/shard_map/copy_three_kernel/pallas_call | solution.py:516
  97.2 4.6 %weights_kernel.1 = (bf16[384,768]{1,0:T(8,128)(2,1)}, bf16[384,768]{1,0:T(8,128)(2,1)}, bf16[384,384]{1,0:T(8,128)(2,1)}, bf16[768,384]{1,0:T(8,128)(2,1)}) custom-call(s32[5]{0:T(128)} %stack.23._.s_ref, bf16[32,6,8,384]{3,2,1,0:T(8,128)(2,1)} %copy-done.5, bf16[32,6,8,384]{3,2,1,0:T(8,128)(2,1)} %copy-done.7), custom_call_target="tpu_custom_call" | custom-call | flops 1 | bytes 1 | tf_op jit(solution)/shard_map/weights_kernel/pallas_call | solution.py:539
  101.8 5.9 %all-to-all-done.1.second_ref = bf16[32,8,8,384]{3,2,1,0:T(8,128)(2,1)S(1)} async-done(((bf16[32,8,8,384]{3,2,1,0:T(8,128)(2,1)}), bf16[32,8,8,384]{3,2,1,0:T(8,128)(2,1)S(1)}, u32[]{:S(2)}, u32[]{:S(2)}) %all-to-all-start.1) | async-done | bytes 1572896 | tf_op jit(solution)/shard_map/all_to_all | solution.py:534
  108.8 6.6 %gating_kernel.1 = (bf16[2048,384]{1,0:T(8,128)(2,1)}, bf16[2048,384]{1,0:T(8,128)(2,1)}, bf16[2048,384]{1,0:T(8,128)(2,1)}, f32[8,512]{1,0:T(8,128)}) custom-call(s32[5]{0:T(128)} %stack.23._.s_ref, bf16[192,4096]{1,0:T(8,128)(2,1)} %bitcast.27, bf16[192,2048]{1,0:T(8,128)(2,1)} %copy-done.8, bf16[32,8,8,384]{3,2,1,0:T(8,128)(2,1)} %copy-done.3, ...), custom_call_target="tpu_custom_call" | custom-call | flops 600000000 | bytes 10000000 | tf_op jit(solution)/shard_map/gating_kernel/pallas_call | solution.py:545
  124.7 19.4 %mlp_kernel.1 = (bf16[2048,384]{1,0:T(8,128)(2,1)}, bf16[2048,384]{1,0:T(8,128)(2,1)}, bf16[2048,768]{1,0:T(8,128)(2,1)}, bf16[2048,1536]{1,0:T(8,128)(2,1)}, f3...) custom-call(s32[5]{0:T(128)} %stack.23._.s_ref, ...), custom_call_target="tpu_custom_call" | custom-call | flops 7299999744 | bytes 24000000 | tf_op jit(solution)/shard_map/mlp_kernel/pallas_call | solution.py:555
  153.1 7.5 %resid_grad_kernel.1 = (bf16[2048,384]{1,0:T(8,128)(2,1)}, bf16[32,8,8,384]{3,2,1,0:T(8,128)(2,1)}) custom-call(s32[5]{0:T(128)} %stack.23._.s_ref, bf16[2048,384]{1,0:T(8,128)(2,1)} %get-tuple-element.103.resid_ref, bf16[2048,384]{1,0:T(8,128)(2,1)} %get-tuple-element.129.cot_ref, f32[1,384]{1,0:T(1,128)} %reshape.51.gain_ref, ...), custom_call_target="tpu_custom_call" | custom-call | flops 50000000 | bytes 12000000 | tf_op jit(solution)/shard_map/resid_grad_kernel/pallas_call | solution.py:566
  160.6 4.1 %all-to-all-start.2 = ((bf16[32,8,8,384]{3,2,1,0:T(8,128)(2,1)}), bf16[32,8,8,384]{3,2,1,0:T(8,128)(2,1)S(1)}, u32[]{:S(2)}, u32[]{:S(2)}) async-start(bf16[32,8,8,384]{3,2,1,0:T(8,128)(2,1)} %get-tuple-element.125), calls=%async_computation.2 | async-start | bytes 3145728 | tf_op jit(solution)/shard_map/all_to_all | solution.py:576
  164.7 7.1 %direct_kernel.1 = (bf16[384,2048]{1,0:T(8,128)(2,1)}, f32[384,384]{1,0:T(8,128)}) custom-call(s32[5]{0:T(128)} %stack.23._.s_ref, bf16[2048,384]{1,0:T(8,128)(2,1)} %get-tuple-element.130.g_resid_ref, bf16[2048,384]{1,0:T(8,128)(2,1)} %get-tuple-element.114.in_ref, bf16[32,8,8,384]{3,2,1,0:T(8,128)(2,1)} %copy-done.3, ...), custom_call_target="tpu_custom_call" | custom-call | flops 1 | bytes 1 | tf_op jit(solution)/shard_map/direct_kernel/pallas_call | solution.py:583
  171.7 11.1 %weight_grad_kernel.1 = (bf16[32,6,8,384]{3,2,1,0:T(8,128)(2,1)}, bf16[32,6,8,384]{3,2,1,0:T(8,128)(2,1)}) custom-call(s32[5]{0:T(128)} %stack.23._.s_ref, bf16[2048,384]{1,0:T(8,128)(2,1)} %get-tuple-element.126.normed_ref, bf16[2048,1536]{1,0:T(8,128)(2,1)} %get-tuple-element.127.grads_ref, bf16[2048,768]{1,0:T(8,128)(2,1)} %get-tuple-element.128.hidden_ref, ...), custom_call_target="tpu_custom_call" | custom-call | flops 1 | bytes 1 | tf_op jit(solution)/shard_map/weight_grad_kernel/pallas_call | solution.py:592
  183.1 2.8 collective-permute-done.12.got_ref
  189.1 6.6 %first_grad_kernel.1 = (bf16[32,14,8,384]{3,2,1,0:T(8,128)(2,1)}, bf16[8,256,384]{2,1,0:T(8,128)(2,1)}) custom-call(s32[5]{0:T(128)} %stack.23._.s_ref, bf16[32,8,8,384]{3,2,1,0:T(8,128)(2,1)} %copy-done.4, bf16[8,256,256]{2,1,0:T(8,128)(2,1)} %constant_dynamic-slice_fusion.f2_ref, bf16[32,6,8,384]{3,2,1,0:T(8,128)(2,1)} %get-tuple-element.136.keep_ref, ...), custom_call_target="tpu_custom_call" | custom-call | flops 400000000 | bytes 6000000 | tf_op jit(solution)/shard_map/first_grad_kernel/pallas_call | solution.py:600
  195.7 5.8 %all-to-all-start.3 = ((bf16[32,14,8,384]{3,2,1,0:T(8,128)(2,1)}), bf16[32,14,8,384]{3,2,1,0:T(8,128)(2,1)S(1)}, u32[]{:S(2)}, u32[]{:S(2)}) async-start(bf16[32,14,8,384]{3,2,1,0:T(8,128)(2,1)} %get-tuple-element.138), calls=%async_computation.3 | async-start | bytes 5505024 | tf_op jit(solution)/shard_map/all_to_all | solution.py:611
  206.3 5.2 %term_two_kernel.1 = (bf16[8,64,256]{2,1,0:T(8,128)(2,1)}, bf16[8,64,256]{2,1,0:T(8,128)(2,1)}, bf16[8,64,256]{2,1,0:T(8,128)(2,1)}, bf16[8,64,256]{2,1,0:T(8,128)(2,1)}) custom-call(s32[5]{0:T(128)} %stack.23._.s_ref, bf16[8,256,384]{2,1,0:T(8,128)(2,1)} %get-tuple-element.139.grad_ref, bf16[8,256,384]{2,1,0:T(8,128)(2,1)} %get-tuple-element.140.first_ref), custom_call_target="tpu_custom_call" | custom-call | flops 1 | bytes 1 | tf_op jit(solution)/shard_map/term_two_kernel/pallas_call | solution.py:627
  215.2 8.5 %collective-permute-done.18.refs_3_ = bf16[512,384]{1,0:T(8,128)(2,1)S(1)} collective-permute-done((bf16[512,384]{1,0:T(8,128)(2,1)S(1)}, bf16[512,384]{1,0:T(8,128)(2,1)S(1)}, u32[]{:S(2)}, u32[]{:S(2)}) %collective-permute-start.18) | collective-permute-done | bytes 393248 | tf_op jit(solution)/shard_map/ppermute | solution.py:468
  224.5 3.3 %mixed_join_kernel.1 = bf16[512,1536]{1,0:T(8,128)(2,1)} custom-call(s32[5]{0:T(128)} %stack.23._.s_ref, bf16[512,384]{1,0:T(8,128)(2,1)} %get-tuple-element.147.refs_0_, bf16[512,384]{1,0:T(8,128)(2,1)} %copy-done.10, bf16[512,384]{1,0:T(8,128)(2,1)} %copy-done.11, bf16[512,384]{1,0:T(8,128)(2,1)} %copy-done.12), custom_call_target="tpu_custom_call" | custom-call | flops 1 | bytes 1 | tf_op jit(solution)/shard_map/mixed_join_kernel/pallas_call | solution.py:579
  229.3 4.8 %collective-permute-done.15.d_ref = bf16[8,64,256]{2,1,0:T(8,128)(2,1)S(1)} collective-permute-done((bf16[8,64,256]{2,1,0:T(8,128)(2,1)}, bf16[8,64,256]{2,1,0:T(8,128)(2,1)S(1)}, u32[]{:S(2)}, u32[]{:S(2)}) %collective-permute-start.15) | collective-permute-done | bytes 262176 | tf_op jit(solution)/shard_map/ppermute | solution.py:468
  237.6 3.2 %collective-permute-start.19 = (bf16[8,32,256]{2,1,0:T(8,128)(2,1)}, bf16[8,32,256]{2,1,0:T(8,128)(2,1)S(1)}, u32[]{:S(2)}, u32[]{:S(2)}) collective-permute-start(bf16[8,32,256]{2,1,0:T(8,128)(2,1)} %get-tuple-element.156), channel_id=1, source_target_pairs={{0,1},{1,0},{2,3},{3,2},{4,5},{5,4},{6,7},{7,6},{8,9},{9,8},{10,11... | collective-permute-start | bytes 393224 | tf_op jit(solution)/shard_map/ppermute | solution.py:642
  240.8 5.3 %back_kernel.1 = (bf16[192,2048]{1,0:T(8,128)(2,1)}, bf16[192,2048]{1,0:T(8,128)(2,1)}) custom-call(s32[5]{0:T(128)} %stack.23._.s_ref, bf16[32,14,8,384]{3,2,1,0:T(8,128)(2,1)} %copy-done.2, bf16[8,2,256,256]{3,2,1,0:T(8,128)(2,1)} %bitcast.28, bf16[384,2048]{1,0:T(8,128)(2,1)} %get-tuple-element.153.direct_ref), custom_call_target="tpu_custom_call" | custom-call | flops 12000000000 | bytes 6000000 | tf_op jit(solution)/shard_map/back_kernel/pallas_call | solution.py:635
  246.2 5.3 %term_one_kernel.1 = (bf16[8,64,256]{2,1,0:T(8,128)(2,1)}, bf16[8,64,256]{2,1,0:T(8,128)(2,1)}, bf16[8,64,256]{2,1,0:T(8,128)(2,1)}, bf16[8,64,256]{2,1,0:T(8,128)(2,1)}) custom-call(s32[5]{0:T(128)} %stack.23._.s_ref, bf16[32,14,8,384]{3,2,1,0:T(8,128)(2,1)} %copy-done.2, bf16[2048,384]{1,0:T(8,128)(2,1)} %get-tuple-element.114.in_ref), custom_call_target="tpu_custom_call" | custom-call | flops 1 | bytes 1 | tf_op jit(solution)/shard_map/term_one_kernel/pallas_call | solution.py:644
  252.1 2.9 collective-permute-start.22
  263.1 3.7 %collective-permute-done.23.d_ref = bf16[8,64,256]{2,1,0:T(8,128)(2,1)S(1)} collective-permute-done((bf16[8,64,256]{2,1,0:T(8,128)(2,1)}, bf16[8,64,256]{2,1,0:T(8,128)(2,1)S(1)}, u32[]{:S(2)}, u32[]{:S(2)}) %collective-permute-start.23) | collective-permute-done | bytes 262176 | tf_op jit(solution)/shard_map/ppermute | solution.py:468
  272.0 3.5 %weight_sum_kernel.1 = f32[2,6,8,384]{3,2,1,0:T(8,128)} custom-call(s32[5]{0:T(128)} %stack.23._.s_ref, bf16[32,14,8,384]{3,2,1,0:T(8,128)(2,1)} %copy-done.2), custom_call_target="tpu_custom_call" | custom-call | flops 1 | bytes 1 | tf_op jit(solution)/shard_map/weight_sum_kernel/pallas_call | solution.py:653
  275.5 6.4 %collective-permute-start.25 = (f32[2,6,8,384]{3,2,1,0:T(8,128)}, f32[2,6,8,384]{3,2,1,0:T(8,128)S(1)}, u32[]{:S(2)}, u32[]{:S(2)}) collective-permute-start(f32[2,6,8,384]{3,2,1,0:T(8,128)} %weight_sum_kernel.1), channel_id=1, source_target_pairs={{0,0},{1,1},{8,2},{9,3},{16,4},{17,5},{24,6},{25,7},{32,8},{33,9},... | collective-permute-start | bytes 442376 | tf_op jit(solution)/shard_map/ppermute | solution.py:659
  289.4 3.1 %join_kernel.1 = bf16[192,4096]{1,0:T(8,128)(2,1)} custom-call(s32[5]{0:T(128)} %stack.23._.s_ref, bf16[192,2048]{1,0:T(8,128)(2,1)} %get-tuple-element.154.own_ref, bf16[192,2048]{1,0:T(8,128)(2,1)} %copy-done.9), custom_call_target="tpu_custom_call" | custom-call | flops 1 | bytes 1 | tf_op jit(solution)/shard_map/join_kernel/pallas_call | solution.py:671
  (131 shorter events, 75.8 us)
Async XLA Ops:
  0.6 35.8 %copy-start = (bf16[16,256,256]{2,1,0:T(8,128)(2,1)S(1)}, bf16[16,256,256]{2,1,0:T(8,128)(2,1)}, u32[]{:S(2)}) copy-start(bf16[16,256,256]{2,1,0:T(8,128)(2,1)} %param.11) | copy-start | bytes 6291460
  4.1 25.9 %collective-permute-start.1 = (bf16[192,2048]{1,0:T(8,128)(2,1)}, bf16[192,2048]{1,0:T(8,128)(2,1)S(1)}, u32[]{:S(2)}, u32[]{:S(2)}) collective-permute-start(bf16[192,2048]{1,0:T(8,128)(2,1)} %gather_kernel.1), channel_id=1, source_target_pairs={{0,1},{1,0},{2,3},{3,2},{4,5},{5,4},{6,7},{7,6},{8,9},{9,8},{10,11... | collective-permute-start | bytes 2359304 | tf_op jit(solution)/shard_map/ppermute | solution.py:493
  10.1 9.4 %collective-permute-start = (bf16[2,6,8,384]{3,2,1,0:T(8,128)(2,1)}, bf16[2,6,8,384]{3,2,1,0:T(8,128)(2,1)S(1)}, u32[]{:S(2)}, u32[]{:S(2)}) collective-permute-start(bf16[2,6,8,384]{3,2,1,0:T(8,128)(2,1)} %payload_kernel.1), channel_id=1, source_target_pairs={{0,0},{1,1},{2,8},{3,9},{4,16},{5,17},{6,24},{7,25},{8,32},{9,33},... | collective-permute-start | bytes 221192 | tf_op jit(solution)/shard_map/ppermute | solution.py:501
  30.9 41.4 %all-to-all-start = ((bf16[32,14,8,384]{3,2,1,0:T(8,128)(2,1)}), bf16[32,14,8,384]{3,2,1,0:T(8,128)(2,1)}, u32[]{:S(2)}, u32[]{:S(2)}) async-start(bf16[32,14,8,384]{3,2,1,0:T(8,128)(2,1)} %first_kernel.1), calls=%async_computation | async-start | bytes 5505024 | tf_op jit(solution)/shard_map/all_to_all | solution.py:513
  78.1 29.5 %all-to-all-start.1 = ((bf16[32,8,8,384]{3,2,1,0:T(8,128)(2,1)}), bf16[32,8,8,384]{3,2,1,0:T(8,128)(2,1)S(1)}, u32[]{:S(2)}, u32[]{:S(2)}) async-start(bf16[32,8,8,384]{3,2,1,0:T(8,128)(2,1)} %get-tuple-element.100), calls=%async_computation.1 | async-start | bytes 3145728 | tf_op jit(solution)/shard_map/all_to_all | solution.py:534
  85.8 10.4 %collective-permute-start.2 = (bf16[32,6,8,384]{3,2,1,0:T(8,128)(2,1)S(1)}, bf16[32,6,8,384]{3,2,1,0:T(8,128)(2,1)S(1)}, u32[]{:S(2)}, u32[]{:S(2)}) collective-permute-start(bf16[32,6,8,384]{3,2,1,0:T(8,128)(2,1)S(1)} %slice.39.own_ref), channel_id=1, source_target_pairs={{0,8},{8,0},{1,9},{9,1},{2,10},{10,2},{3,11},{11,3},{4,12},{12,4},... | collective-permute-start | bytes 3538952 | tf_op jit(solution)/shard_map/ppermute | solution.py:537
  89.1 30.8 %collective-permute-start.6 = (bf16[512,384]{1,0:T(8,128)(2,1)}, bf16[512,384]{1,0:T(8,128)(2,1)S(1)}, u32[]{:S(2)}, u32[]{:S(2)}) collective-permute-start(bf16[512,384]{1,0:T(8,128)(2,1)} %get-tuple-element.109), channel_id=1, source_target_pairs={{0,6},{2,0},{4,2},{6,4},{1,7},{3,1},{5,3},{7,5},{8,14},{10,8},{12,... | collective-permute-start | bytes 1179656 | tf_op jit(solution)/shard_map/ppermute | solution.py:521
  91.4 32.4 %collective-permute-start.7 = (bf16[512,384]{1,0:T(8,128)(2,1)}, bf16[512,384]{1,0:T(8,128)(2,1)S(1)}, u32[]{:S(2)}, u32[]{:S(2)}) collective-permute-start(bf16[512,384]{1,0:T(8,128)(2,1)} %get-tuple-element.110), channel_id=1, source_target_pairs={{0,4},{2,6},{4,0},{6,2},{1,5},{3,7},{5,1},{7,3},{8,12},{10,14},{12... | collective-permute-start | bytes 1179656 | tf_op jit(solution)/shard_map/ppermute | solution.py:521
  93.5 30.3 %collective-permute-start.8 = (bf16[512,384]{1,0:T(8,128)(2,1)}, bf16[512,384]{1,0:T(8,128)(2,1)S(1)}, u32[]{:S(2)}, u32[]{:S(2)}) collective-permute-start(bf16[512,384]{1,0:T(8,128)(2,1)} %get-tuple-element.111), channel_id=1, source_target_pairs={{0,2},{2,4},{4,6},{6,0},{1,3},{3,5},{5,7},{7,1},{8,10},{10,12},{12... | collective-permute-start | bytes 1179656 | tf_op jit(solution)/shard_map/ppermute | solution.py:521
  115.4 8.4 %collective-permute-start.5 = (f32[8,512]{1,0:T(8,128)}, f32[8,512]{1,0:T(8,128)S(1)}, u32[]{:S(2)}, u32[]{:S(2)}) collective-permute-start(f32[8,512]{1,0:T(8,128)} %get-tuple-element.107.refs_0_), channel_id=1, source_target_pairs={{0,2},{2,4},{4,6},{6,0},{1,3},{3,5},{5,7},{7,1},{8,10},{10,12},{12... | collective-permute-start | bytes 49160 | tf_op jit(solution)/shard_map/ppermute | solution.py:464
  117.6 6.2 %collective-permute-start.4 = (f32[8,512]{1,0:T(8,128)}, f32[8,512]{1,0:T(8,128)S(1)}, u32[]{:S(2)}, u32[]{:S(2)}) collective-permute-start(f32[8,512]{1,0:T(8,128)} %get-tuple-element.107.refs_0_), channel_id=1, source_target_pairs={{0,4},{2,6},{4,0},{6,2},{1,5},{3,7},{5,1},{7,3},{8,12},{10,14},{12... | collective-permute-start | bytes 49160 | tf_op jit(solution)/shard_map/ppermute | solution.py:464
  119.9 4.2 %collective-permute-start.3 = (f32[8,512]{1,0:T(8,128)}, f32[8,512]{1,0:T(8,128)S(1)}, u32[]{:S(2)}, u32[]{:S(2)}) collective-permute-start(f32[8,512]{1,0:T(8,128)} %get-tuple-element.107.refs_0_), channel_id=1, source_target_pairs={{0,6},{2,0},{4,2},{6,4},{1,7},{3,1},{5,3},{7,5},{8,14},{10,8},{12,... | collective-permute-start | bytes 49160 | tf_op jit(solution)/shard_map/ppermute | solution.py:464
  144.1 5.1 %collective-permute-start.11 = (f32[8,512]{1,0:T(8,128)}, f32[8,512]{1,0:T(8,128)S(1)}, u32[]{:S(2)}, u32[]{:S(2)}) collective-permute-start(f32[8,512]{1,0:T(8,128)} %get-tuple-element.132.refs_4_.refs_0_), channel_id=1, source_target_pairs={{0,2},{2,4},{4,6},{6,0},{1,3},{3,5},{5,7},{7,1},{8,10},{10,12},{12... | collective-permute-start | bytes 49160 | tf_op jit(solution)/shard_map/ppermute | solution.py:464
  145.9 5.5 %collective-permute-start.10 = (f32[8,512]{1,0:T(8,128)}, f32[8,512]{1,0:T(8,128)S(1)}, u32[]{:S(2)}, u32[]{:S(2)}) collective-permute-start(f32[8,512]{1,0:T(8,128)} %get-tuple-element.132.refs_4_.refs_0_), channel_id=1, source_target_pairs={{0,4},{2,6},{4,0},{6,2},{1,5},{3,7},{5,1},{7,3},{8,12},{10,14},{12... | collective-permute-start | bytes 49160 | tf_op jit(solution)/shard_map/ppermute | solution.py:464
  148.6 4.0 %collective-permute-start.9 = (f32[8,512]{1,0:T(8,128)}, f32[8,512]{1,0:T(8,128)S(1)}, u32[]{:S(2)}, u32[]{:S(2)}) collective-permute-start(f32[8,512]{1,0:T(8,128)} %get-tuple-element.132.refs_4_.refs_0_), channel_id=1, source_target_pairs={{0,6},{2,0},{4,2},{6,4},{1,7},{3,1},{5,3},{7,5},{8,14},{10,8},{12,... | collective-permute-start | bytes 49160 | tf_op jit(solution)/shard_map/ppermute | solution.py:464
  160.6 27.4 %all-to-all-start.2 = ((bf16[32,8,8,384]{3,2,1,0:T(8,128)(2,1)}), bf16[32,8,8,384]{3,2,1,0:T(8,128)(2,1)S(1)}, u32[]{:S(2)}, u32[]{:S(2)}) async-start(bf16[32,8,8,384]{3,2,1,0:T(8,128)(2,1)} %get-tuple-element.125), calls=%async_computation.2 | async-start | bytes 3145728 | tf_op jit(solution)/shard_map/all_to_all | solution.py:576
  182.8 3.1 %collective-permute-start.12 = (bf16[32,6,8,384]{3,2,1,0:T(8,128)(2,1)}, bf16[32,6,8,384]{3,2,1,0:T(8,128)(2,1)S(1)}, u32[]{:S(2)}, u32[]{:S(2)}) collective-permute-start(bf16[32,6,8,384]{3,2,1,0:T(8,128)(2,1)} %get-tuple-element.137), channel_id=1, source_target_pairs={{0,8},{8,0},{1,9},{9,1},{2,10},{10,2},{3,11},{11,3},{4,12},{12,4},... | collective-permute-start | bytes 3538952 | tf_op jit(solution)/shard_map/ppermute | solution.py:598
  195.7 41.9 %all-to-all-start.3 = ((bf16[32,14,8,384]{3,2,1,0:T(8,128)(2,1)}), bf16[32,14,8,384]{3,2,1,0:T(8,128)(2,1)S(1)}, u32[]{:S(2)}, u32[]{:S(2)}) async-start(bf16[32,14,8,384]{3,2,1,0:T(8,128)(2,1)} %get-tuple-element.138), calls=%async_computation.3 | async-start | bytes 5505024 | tf_op jit(solution)/shard_map/all_to_all | solution.py:611
  201.5 12.2 %collective-permute-start.16 = (bf16[512,384]{1,0:T(8,128)(2,1)}, bf16[512,384]{1,0:T(8,128)(2,1)S(1)}, u32[]{:S(2)}, u32[]{:S(2)}) collective-permute-start(bf16[512,384]{1,0:T(8,128)(2,1)} %get-tuple-element.148), channel_id=1, source_target_pairs={{0,2},{2,4},{4,6},{6,0},{1,3},{3,5},{5,7},{7,1},{8,10},{10,12},{12... | collective-permute-start | bytes 1179656 | tf_op jit(solution)/shard_map/ppermute | solution.py:468
  201.7 13.5 %collective-permute-start.17 = (bf16[512,384]{1,0:T(8,128)(2,1)S(1)}, bf16[512,384]{1,0:T(8,128)(2,1)S(1)}, u32[]{:S(2)}, u32[]{:S(2)}) collective-permute-start(bf16[512,384]{1,0:T(8,128)(2,1)S(1)} %copy-done.30), channel_id=1, source_target_pairs={{0,4},{2,6},{4,0},{6,2},{1,5},{3,7},{5,1},{7,3},{8,12},{10,14},{12... | collective-permute-start | bytes 1179656 | tf_op jit(solution)/shard_map/ppermute | solution.py:468
  204.3 19.4 %collective-permute-start.18 = (bf16[512,384]{1,0:T(8,128)(2,1)S(1)}, bf16[512,384]{1,0:T(8,128)(2,1)S(1)}, u32[]{:S(2)}, u32[]{:S(2)}) collective-permute-start(bf16[512,384]{1,0:T(8,128)(2,1)S(1)} %copy-done.29), channel_id=1, source_target_pairs={{0,6},{2,0},{4,2},{6,4},{1,7},{3,1},{5,3},{7,5},{8,14},{10,8},{12,... | collective-permute-start | bytes 1179656 | tf_op jit(solution)/shard_map/ppermute | solution.py:468
  211.5 16.3 %collective-permute-start.13 = (bf16[8,64,256]{2,1,0:T(8,128)(2,1)}, bf16[8,64,256]{2,1,0:T(8,128)(2,1)S(1)}, u32[]{:S(2)}, u32[]{:S(2)}) collective-permute-start(bf16[8,64,256]{2,1,0:T(8,128)(2,1)} %get-tuple-element.142), channel_id=1, source_target_pairs={{0,2},{2,4},{4,6},{6,0},{1,3},{3,5},{5,7},{7,1},{8,10},{10,12},{12... | collective-permute-start | bytes 786440 | tf_op jit(solution)/shard_map/ppermute | solution.py:468
  211.6 17.8 %collective-permute-start.14 = (bf16[8,64,256]{2,1,0:T(8,128)(2,1)}, bf16[8,64,256]{2,1,0:T(8,128)(2,1)S(1)}, u32[]{:S(2)}, u32[]{:S(2)}) collective-permute-start(bf16[8,64,256]{2,1,0:T(8,128)(2,1)} %get-tuple-element.143), channel_id=1, source_target_pairs={{0,4},{2,6},{4,0},{6,2},{1,5},{3,7},{5,1},{7,3},{8,12},{10,14},{12... | collective-permute-start | bytes 786440 | tf_op jit(solution)/shard_map/ppermute | solution.py:468
  213.7 20.4 %collective-permute-start.15 = (bf16[8,64,256]{2,1,0:T(8,128)(2,1)}, bf16[8,64,256]{2,1,0:T(8,128)(2,1)S(1)}, u32[]{:S(2)}, u32[]{:S(2)}) collective-permute-start(bf16[8,64,256]{2,1,0:T(8,128)(2,1)} %get-tuple-element.144), channel_id=1, source_target_pairs={{0,6},{2,0},{4,2},{6,4},{1,7},{3,1},{5,3},{7,5},{8,14},{10,8},{12,... | collective-permute-start | bytes 786440 | tf_op jit(solution)/shard_map/ppermute | solution.py:468
  237.6 8.5 %collective-permute-start.19 = (bf16[8,32,256]{2,1,0:T(8,128)(2,1)}, bf16[8,32,256]{2,1,0:T(8,128)(2,1)S(1)}, u32[]{:S(2)}, u32[]{:S(2)}) collective-permute-start(bf16[8,32,256]{2,1,0:T(8,128)(2,1)} %get-tuple-element.156), channel_id=1, source_target_pairs={{0,1},{1,0},{2,3},{3,2},{4,5},{5,4},{6,7},{7,6},{8,9},{9,8},{10,11... | collective-permute-start | bytes 393224 | tf_op jit(solution)/shard_map/ppermute | solution.py:642
  246.2 10.4 %copy-start.28 = (bf16[192,2048]{1,0:T(8,128)(2,1)S(1)}, bf16[192,2048]{1,0:T(8,128)(2,1)}, u32[]{:S(2)}) copy-start(bf16[192,2048]{1,0:T(8,128)(2,1)} %get-tuple-element.157) | copy-start | bytes 2359300
  251.4 9.5 %collective-permute-start.21 = (bf16[8,64,256]{2,1,0:T(8,128)(2,1)}, bf16[8,64,256]{2,1,0:T(8,128)(2,1)S(1)}, u32[]{:S(2)}, u32[]{:S(2)}) collective-permute-start(bf16[8,64,256]{2,1,0:T(8,128)(2,1)} %get-tuple-element.165), channel_id=1, source_target_pairs={{0,2},{2,4},{4,6},{6,0},{1,3},{3,5},{5,7},{7,1},{8,10},{10,12},{12... | collective-permute-start | bytes 786440 | tf_op jit(solution)/shard_map/ppermute | solution.py:468
  252.1 11.0 %collective-permute-start.22 = (bf16[8,64,256]{2,1,0:T(8,128)(2,1)}, bf16[8,64,256]{2,1,0:T(8,128)(2,1)S(1)}, u32[]{:S(2)}, u32[]{:S(2)}) collective-permute-start(bf16[8,64,256]{2,1,0:T(8,128)(2,1)} %get-tuple-element.166), channel_id=1, source_target_pairs={{0,4},{2,6},{4,0},{6,2},{1,5},{3,7},{5,1},{7,3},{8,12},{10,14},{12... | collective-permute-start | bytes 786440 | tf_op jit(solution)/shard_map/ppermute | solution.py:468
  255.0 11.8 %collective-permute-start.23 = (bf16[8,64,256]{2,1,0:T(8,128)(2,1)}, bf16[8,64,256]{2,1,0:T(8,128)(2,1)S(1)}, u32[]{:S(2)}, u32[]{:S(2)}) collective-permute-start(bf16[8,64,256]{2,1,0:T(8,128)(2,1)} %get-tuple-element.167), channel_id=1, source_target_pairs={{0,6},{2,0},{4,2},{6,4},{1,7},{3,1},{5,3},{7,5},{8,14},{10,8},{12,... | collective-permute-start | bytes 786440 | tf_op jit(solution)/shard_map/ppermute | solution.py:468
  256.5 32.0 %collective-permute-start.20 = (bf16[192,2048]{1,0:T(8,128)(2,1)S(1)}, bf16[192,2048]{1,0:T(8,128)(2,1)S(1)}, u32[]{:S(2)}, u32[]{:S(2)}) collective-permute-start(bf16[192,2048]{1,0:T(8,128)(2,1)S(1)} %copy-done.28), channel_id=1, source_target_pairs={{0,1},{1,0},{2,3},{3,2},{4,5},{5,4},{6,7},{7,6},{8,9},{9,8},{10,11... | collective-permute-start | bytes 2359304 | tf_op jit(solution)/shard_map/ppermute | solution.py:652
  270.3 13.1 %collective-permute-start.24 = (bf16[8,32,256]{2,1,0:T(8,128)(2,1)}, bf16[8,32,256]{2,1,0:T(8,128)(2,1)S(1)}, u32[]{:S(2)}, u32[]{:S(2)}) collective-permute-start(bf16[8,32,256]{2,1,0:T(8,128)(2,1)} %get-tuple-element.173), channel_id=1, source_target_pairs={{0,1},{1,0},{2,3},{3,2},{4,5},{5,4},{6,7},{7,6},{8,9},{9,8},{10,11... | collective-permute-start | bytes 393224 | tf_op jit(solution)/shard_map/ppermute | solution.py:669
  275.5 11.1 %collective-permute-start.25 = (f32[2,6,8,384]{3,2,1,0:T(8,128)}, f32[2,6,8,384]{3,2,1,0:T(8,128)S(1)}, u32[]{:S(2)}, u32[]{:S(2)}) collective-permute-start(f32[2,6,8,384]{3,2,1,0:T(8,128)} %weight_sum_kernel.1), channel_id=1, source_target_pairs={{0,0},{1,1},{8,2},{9,3},{16,4},{17,5},{24,6},{25,7},{32,8},{33,9},... | collective-permute-start | bytes 442376 | tf_op jit(solution)/shard_map/ppermute | solution.py:659
  (32 other events, 93.7 us)

commit v6 on v5

--- a/solution.py
+++ b/solution.py
@@ -128,19 +128,22 @@
 def first_kernel(_, f1_ref, in_ref, payload_ref, out_ref):
     step = pl.program_id(0)
 
-    @pl.when(step < 8)
+    @pl.when(step < 4)
     def _():
-        results = [
-            dot_t(f1_ref[r], in_ref[:, r * 256 : (r + 1) * 256]).reshape(32, 8, 192)
-            for r in range(2)
-        ]
-        out_ref[:, 0] = jnp.concatenate(results, axis=2).astype(BF)
-
-    @pl.when(step >= 8)
+        for q in range(2):
+            results = []
+            for r in range(2 * q, 2 * q + 2):
+                value = dot_t(f1_ref[r], in_ref[:, r * 256 : (r + 1) * 256])
+                results.append(value.reshape(32, 8, 192))
+            out_ref[:, q] = jnp.concatenate(results, axis=2).astype(BF)
+
+    @pl.when(step >= 4)
     def _():
-        halves = [payload_ref[core, lax.max(step - 8, 0)] for core in range(2)]
-        for dev in range(32):
-            out_ref[dev, 0] = halves[dev // 2 % 2]
+        for q in range(2):
+            slot = lax.max(2 * step - 8, 0) + q
+            halves = [payload_ref[core, slot] for core in range(2)]
+            for dev in range(32):
+                out_ref[dev, q] = halves[dev // 2 % 2]
 
 
 def copy_kernel(_, in_ref, out_ref):
@@ -500,10 +503,10 @@
     )(at, w_gate, w_up, w_input_gate, w_down)
     payload = lax.ppermute(payload, ALL, shard_moves())
     first_local = call(
-        first_kernel, (14,),
-        [pl.BlockSpec((2, 256, 256), lambda t, s: (lax.min(t, 7), 0, 0)),
-         pl.BlockSpec((192, 512), lambda t, s: (0, lax.min(t, 7))), whole(2, 6, 8, DB)],
-        pl.BlockSpec((32, 1, 8, DB), lambda t, s: (0, t, 0, 0)),
+        first_kernel, (7,),
+        [pl.BlockSpec((4, 256, 256), lambda t, s: (lax.min(t, 3), 0, 0)),
+         pl.BlockSpec((192, 1024), lambda t, s: (0, lax.min(t, 3))), whole(2, 6, 8, DB)],
+        pl.BlockSpec((32, 2, 8, DB), lambda t, s: (0, t, 0, 0)),
         bf(32, 14, 8, DB),
         (1, 1),
     )(at, factor_one, turned_in, payload)
@@ -647,8 +650,8 @@
     )(at, g_first, input_mlp)
 
     got_two, terms_one = lax.optimization_barrier((got_two, terms_one))
+    for_sums, terms_one = lax.optimization_barrier((g_first, terms_one))
     terms_one = send_each(terms_one, "x")
-    for_sums, terms_one = lax.optimization_barrier((g_first, terms_one))
     got_grad = lax.ppermute(give_grad, "zh", SWAP)
     summed = call(
         weight_sum_kernel, (3,),
@@ -656,17 +659,20 @@
         pl.BlockSpec((2, 2, 8, DB), lambda t, s: (0, t, 0, 0)), f32(2, 6, 8, DB), (1, 1),
     )(at, for_sums)
     back = [(there, here) for here, there in shard_moves()]
-    own = lax.ppermute(summed, ALL, back).reshape(2, 48, DB)
+    own = lax.ppermute(summed, ALL, back)
+    grad_norm_gain = summed[0].reshape(48, DB)[36:40].reshape(D)
+
+    grad_factor_two = factor_gradient(sums_two[0], got_two, 1)
+    sums_one = factor_sums(terms_one)
+    give_one, got_grad = lax.optimization_barrier((sums_one[1], got_grad))
+    got_one = lax.ppermute(give_one, "zh", SWAP)
+    own, got_one = lax.optimization_barrier((own, got_one))
+    own = own.reshape(2, 48, DB)
     low, high = own[0], own[1]
     grad_w_gate = jnp.concatenate([low[:12], low[12:24]], axis=1)
     grad_w_up = jnp.concatenate([high[:12], high[12:24]], axis=1)
     grad_w_input_gate = low[24:36]
     grad_w_down = high[24:]
-    grad_norm_gain = summed[0].reshape(48, DB)[36:40].reshape(D)
-
-    grad_factor_two = factor_gradient(sums_two[0], got_two, 1)
-    sums_one = factor_sums(terms_one)
-    got_one = lax.ppermute(sums_one[1], "zh", SWAP)
     grad_factor_one = factor_gradient(sums_one[0], got_one, 4)
     grad_inputs = call(
         join_kernel, (2,), [columns(192, 1024)] * 2, columns(192, 2048), bf(192, 4096), (1, 1)

time: 295 us -> 287 us (0.973)
  waiting for transfers between devices: 77.7 us -> 65.9 us
  starting transfers between devices: 73.8 us -> 81.6 us
  Pallas kernels: 122 us -> 119 us
    ppermute x9, waiting for transfers between devices: 21.2 us -> 5.21 us  [send_each(): lax.ppermute(parts[j], axis, turn(axis, 4, j))]
    ppermute x9, starting transfers between devices: 13.3 us -> 23.9 us  [send_each(): lax.ppermute(parts[j], axis, turn(axis, 4, j))]
    pallas_call x1, Pallas kernels: 9.89 us -> 6.39 us  [per_device(): call(first_kernel, (7,), [pl.BlockSpec((4, 256, 256), lambda t, s: (lax.m...]
  transfers between devices with their start and end apart: 30 -> 30, of which waited for: 17 -> 12; matrix products, arithmetic and copies ran while one was open for 2% -> 2% of each run, Pallas kernels for 25% -> 26%
where the time goes in v6:
time: 287 us; the launch traced here: 284 us
  Pallas kernels  119 us (41%)
  starting transfers between devices  81.6 us (28%)
  waiting for transfers between devices  65.9 us (23%)
  local copies, waits for them, and re-layouts  16.2 us (6%)
    all_to_all x1, waiting for transfers between devices, per_device(): lax.all_to_all(first_local, PLANE, split_axis=0, concat_axis=0, tiled=True)  34.8 us
    ppermute x9, starting transfers between devices, send_each(): lax.ppermute(parts[j], axis, turn(axis, 4, j))  23.9 us
    pallas_call x1, Pallas kernels, per_device(): call(mlp_kernel, (4,), [turned_rows(DB), whole(1, DB), whole(DB, 768), wh...  19.4 us
    pallas_call x1, Pallas kernels, per_device(): call(weight_grad_kernel, (2,), [rows(DB, 1024), rows(1536, 1024), rows(76...  11.1 us
    ppermute x6, starting transfers between devices, around(): lax.ppermute(value, axis, turn(axis, 4, -j))  11 us
    unnamed x68, local copies, waits for them, and re-layouts  9.78 us
    all_to_all x1, waiting for transfers between devices, per_device(): lax.all_to_all(second_cols, PLANE, split_axis=0, concat_axis=0, tiled=True)  8.06 us
    all_to_all x1, starting transfers between devices, per_device(): lax.all_to_all(first_local, PLANE, split_axis=0, concat_axis=0, tiled=True)  7.66 us
  transfers between devices with their start and end apart: 30, of which 12 were waited for; matrix products, arithmetic and copies ran while one was open for 2% of the time, Pallas kernels for 26%

profile of v6, /device:TPU:2, one launch (start us, length us, event | category | flops | bytes accessed | tf_op | source)
XLA Modules:
  0.0 284.5 jit_solution(11333331486933162580)
XLA Ops:
  1.4 2.8 gather_kernel.1
  4.2 3.9 %collective-permute-start.1 = (bf16[192,2048]{1,0:T(8,128)(2,1)}, bf16[192,2048]{1,0:T(8,128)(2,1)S(1)}, u32[]{:S(2)}, u32[]{:S(2)}) collective-permute-start(bf16[192,2048]{1,0:T(8,128)(2,1)} %gather_kernel.1), channel_id=1, source_target_pairs={{0,1},{1,0},{2,3},{3,2},{4,5},{5,4},{6,7},{7,6},{8,9},{9,8},{10,11... | collective-permute-start | bytes 2359304 | tf_op jit(solution)/shard_map/ppermute | solution.py:496
  12.0 7.5 %collective-permute-done.payload_ref = bf16[2,6,8,384]{3,2,1,0:T(8,128)(2,1)S(1)} collective-permute-done((bf16[2,6,8,384]{3,2,1,0:T(8,128)(2,1)}, bf16[2,6,8,384]{3,2,1,0:T(8,128)(2,1)S(1)}, u32[]{:S(2)}, u32[]{:S(2)}) %collective-permute-start) | collective-permute-done | bytes 73760 | tf_op jit(solution)/shard_map/ppermute | solution.py:504
  20.2 6.4 %first_kernel.1 = bf16[32,14,8,384]{3,2,1,0:T(8,128)(2,1)} custom-call(s32[5]{0:T(128)} %stack.23._.s_ref, bf16[16,256,256]{2,1,0:T(8,128)(2,1)} %f1_ref.1, bf16[192,4096]{1,0:T(8,128)(2,1)} %bitcast.26, bf16[2,6,8,384]{3,2,1,0:T(8,128)(2,1)} %copy-done.22), custom_call_target="tpu_custom_call" | custom-call | flops 1 | bytes 1 | tf_op jit(solution)/shard_map/first_kernel/pallas_call | solution.py:505
  28.3 7.7 %all-to-all-start = ((bf16[32,14,8,384]{3,2,1,0:T(8,128)(2,1)}), bf16[32,14,8,384]{3,2,1,0:T(8,128)(2,1)}, u32[]{:S(2)}, u32[]{:S(2)}) async-start(bf16[32,14,8,384]{3,2,1,0:T(8,128)(2,1)} %first_kernel.1), calls=%async_computation | async-start | bytes 5505024 | tf_op jit(solution)/shard_map/all_to_all | solution.py:516
  37.0 34.8 %all-to-all-done.piece_ref = bf16[32,14,8,384]{3,2,1,0:T(8,128)(2,1)} async-done(((bf16[32,14,8,384]{3,2,1,0:T(8,128)(2,1)}), bf16[32,14,8,384]{3,2,1,0:T(8,128)(2,1)}, u32[]{:S(2)}, u32[]{:S(2)}) %all-to-all-start) | async-done | bytes 2752544 | tf_op jit(solution)/shard_map/all_to_all | solution.py:516
  71.8 5.7 %second_kernel.1 = (bf16[32,8,8,384]{3,2,1,0:T(8,128)(2,1)}, bf16[8,256,384]{2,1,0:T(8,128)(2,1)}) custom-call(s32[5]{0:T(128)} %stack.23._.s_ref, bf16[32,14,8,384]{3,2,1,0:T(8,128)(2,1)} %all-to-all-done.piece_ref, bf16[8,256,256]{2,1,0:T(8,128)(2,1)} %constant_dynamic-slice_fusion.f2_ref), custom_call_target="tpu_custom_call" | custom-call | flops 400000000 | bytes 6000000 | tf_op jit(solution)/shard_map/second_kernel/pallas_call | solution.py:529
  77.6 6.3 %all-to-all-start.1 = ((bf16[32,8,8,384]{3,2,1,0:T(8,128)(2,1)}), bf16[32,8,8,384]{3,2,1,0:T(8,128)(2,1)S(1)}, u32[]{:S(2)}, u32[]{:S(2)}) async-start(bf16[32,8,8,384]{3,2,1,0:T(8,128)(2,1)} %get-tuple-element.104), calls=%async_computation.1 | async-start | bytes 3145728 | tf_op jit(solution)/shard_map/all_to_all | solution.py:537
  85.6 3.0 %copy_three_kernel.1 = (bf16[512,384]{1,0:T(8,128)(2,1)}, bf16[512,384]{1,0:T(8,128)(2,1)}, bf16[512,384]{1,0:T(8,128)(2,1)}) custom-call(s32[5]{0:T(128)} %stack.23._.s_ref, bf16[512,1536]{1,0:T(8,128)(2,1)} %refs_4_, bf16[512,1536]{1,0:T(8,128)(2,1)} %refs_4_, bf16[512,1536]{1,0:T(8,128)(2,1)} %refs_4_), custom_call_target="tpu_custom_call" | custom-call | flops 1 | bytes 1 | tf_op jit(solution)/shard_map/copy_three_kernel/pallas_call | solution.py:519
  94.5 4.5 %weights_kernel.1 = (bf16[384,768]{1,0:T(8,128)(2,1)}, bf16[384,768]{1,0:T(8,128)(2,1)}, bf16[384,384]{1,0:T(8,128)(2,1)}, bf16[768,384]{1,0:T(8,128)(2,1)}) custom-call(s32[5]{0:T(128)} %stack.23._.s_ref, bf16[32,6,8,384]{3,2,1,0:T(8,128)(2,1)} %copy-done.5, bf16[32,6,8,384]{3,2,1,0:T(8,128)(2,1)} %copy-done.7), custom_call_target="tpu_custom_call" | custom-call | flops 1 | bytes 1 | tf_op jit(solution)/shard_map/weights_kernel/pallas_call | solution.py:542
  99.1 8.1 %all-to-all-done.1.second_ref = bf16[32,8,8,384]{3,2,1,0:T(8,128)(2,1)S(1)} async-done(((bf16[32,8,8,384]{3,2,1,0:T(8,128)(2,1)}), bf16[32,8,8,384]{3,2,1,0:T(8,128)(2,1)S(1)}, u32[]{:S(2)}, u32[]{:S(2)}) %all-to-all-start.1) | async-done | bytes 1572896 | tf_op jit(solution)/shard_map/all_to_all | solution.py:537
  108.3 6.6 %gating_kernel.1 = (bf16[2048,384]{1,0:T(8,128)(2,1)}, bf16[2048,384]{1,0:T(8,128)(2,1)}, bf16[2048,384]{1,0:T(8,128)(2,1)}, f32[8,512]{1,0:T(8,128)}) custom-call(s32[5]{0:T(128)} %stack.23._.s_ref, bf16[192,4096]{1,0:T(8,128)(2,1)} %bitcast.27, bf16[192,2048]{1,0:T(8,128)(2,1)} %copy-done.8, bf16[32,8,8,384]{3,2,1,0:T(8,128)(2,1)} %copy-done.3, ...), custom_call_target="tpu_custom_call" | custom-call | flops 600000000 | bytes 10000000 | tf_op jit(solution)/shard_map/gating_kernel/pallas_call | solution.py:548
  122.6 19.4 %mlp_kernel.1 = (bf16[2048,384]{1,0:T(8,128)(2,1)}, bf16[2048,384]{1,0:T(8,128)(2,1)}, bf16[2048,768]{1,0:T(8,128)(2,1)}, bf16[2048,1536]{1,0:T(8,128)(2,1)}, f3...) custom-call(s32[5]{0:T(128)} %stack.23._.s_ref, ...), custom_call_target="tpu_custom_call" | custom-call | flops 7299999744 | bytes 24000000 | tf_op jit(solution)/shard_map/mlp_kernel/pallas_call | solution.py:558
  150.5 7.5 %resid_grad_kernel.1 = (bf16[2048,384]{1,0:T(8,128)(2,1)}, bf16[32,8,8,384]{3,2,1,0:T(8,128)(2,1)}) custom-call(s32[5]{0:T(128)} %stack.23._.s_ref, bf16[2048,384]{1,0:T(8,128)(2,1)} %get-tuple-element.107.resid_ref, bf16[2048,384]{1,0:T(8,128)(2,1)} %get-tuple-element.133.cot_ref, f32[1,384]{1,0:T(1,128)} %reshape.51.gain_ref, ...), custom_call_target="tpu_custom_call" | custom-call | flops 50000000 | bytes 12000000 | tf_op jit(solution)/shard_map/resid_grad_kernel/pallas_call | solution.py:569
  158.0 4.1 %all-to-all-start.2 = ((bf16[32,8,8,384]{3,2,1,0:T(8,128)(2,1)}), bf16[32,8,8,384]{3,2,1,0:T(8,128)(2,1)S(1)}, u32[]{:S(2)}, u32[]{:S(2)}) async-start(bf16[32,8,8,384]{3,2,1,0:T(8,128)(2,1)} %get-tuple-element.129), calls=%async_computation.2 | async-start | bytes 3145728 | tf_op jit(solution)/shard_map/all_to_all | solution.py:579
  162.1 7.1 %direct_kernel.1 = (bf16[384,2048]{1,0:T(8,128)(2,1)}, f32[384,384]{1,0:T(8,128)}) custom-call(s32[5]{0:T(128)} %stack.23._.s_ref, bf16[2048,384]{1,0:T(8,128)(2,1)} %get-tuple-element.134.g_resid_ref, bf16[2048,384]{1,0:T(8,128)(2,1)} %get-tuple-element.118.in_ref, bf16[32,8,8,384]{3,2,1,0:T(8,128)(2,1)} %copy-done.3, ...), custom_call_target="tpu_custom_call" | custom-call | flops 1 | bytes 1 | tf_op jit(solution)/shard_map/direct_kernel/pallas_call | solution.py:586
  169.1 11.1 %weight_grad_kernel.1 = (bf16[32,6,8,384]{3,2,1,0:T(8,128)(2,1)}, bf16[32,6,8,384]{3,2,1,0:T(8,128)(2,1)}) custom-call(s32[5]{0:T(128)} %stack.23._.s_ref, bf16[2048,384]{1,0:T(8,128)(2,1)} %get-tuple-element.130.normed_ref, bf16[2048,1536]{1,0:T(8,128)(2,1)} %get-tuple-element.131.grads_ref, bf16[2048,768]{1,0:T(8,128)(2,1)} %get-tuple-element.132.hidden_ref, ...), custom_call_target="tpu_custom_call" | custom-call | flops 1 | bytes 1 | tf_op jit(solution)/shard_map/weight_grad_kernel/pallas_call | solution.py:595
  180.5 2.8 collective-permute-done.12.got_ref
  186.5 6.6 %first_grad_kernel.1 = (bf16[32,14,8,384]{3,2,1,0:T(8,128)(2,1)}, bf16[8,256,384]{2,1,0:T(8,128)(2,1)}) custom-call(s32[5]{0:T(128)} %stack.23._.s_ref, bf16[32,8,8,384]{3,2,1,0:T(8,128)(2,1)} %copy-done.4, bf16[8,256,256]{2,1,0:T(8,128)(2,1)} %constant_dynamic-slice_fusion.f2_ref, bf16[32,6,8,384]{3,2,1,0:T(8,128)(2,1)} %get-tuple-element.140.keep_ref, ...), custom_call_target="tpu_custom_call" | custom-call | flops 400000000 | bytes 6000000 | tf_op jit(solution)/shard_map/first_grad_kernel/pallas_call | solution.py:603
  193.1 5.8 %all-to-all-start.3 = ((bf16[32,14,8,384]{3,2,1,0:T(8,128)(2,1)}), bf16[32,14,8,384]{3,2,1,0:T(8,128)(2,1)S(1)}, u32[]{:S(2)}, u32[]{:S(2)}) async-start(bf16[32,14,8,384]{3,2,1,0:T(8,128)(2,1)} %get-tuple-element.142), calls=%async_computation.3 | async-start | bytes 5505024 | tf_op jit(solution)/shard_map/all_to_all | solution.py:614
  203.8 5.2 %term_two_kernel.1 = (bf16[8,64,256]{2,1,0:T(8,128)(2,1)}, bf16[8,64,256]{2,1,0:T(8,128)(2,1)}, bf16[8,64,256]{2,1,0:T(8,128)(2,1)}, bf16[8,64,256]{2,1,0:T(8,128)(2,1)}) custom-call(s32[5]{0:T(128)} %stack.23._.s_ref, bf16[8,256,384]{2,1,0:T(8,128)(2,1)} %get-tuple-element.143.grad_ref, bf16[8,256,384]{2,1,0:T(8,128)(2,1)} %get-tuple-element.144.first_ref), custom_call_target="tpu_custom_call" | custom-call | flops 1 | bytes 1 | tf_op jit(solution)/shard_map/term_two_kernel/pallas_call | solution.py:630
  212.5 10.2 %collective-permute-start.15 = (bf16[8,64,256]{2,1,0:T(8,128)(2,1)}, bf16[8,64,256]{2,1,0:T(8,128)(2,1)S(1)}, u32[]{:S(2)}, u32[]{:S(2)}) collective-permute-start(bf16[8,64,256]{2,1,0:T(8,128)(2,1)} %get-tuple-element.148), channel_id=1, source_target_pairs={{0,6},{2,0},{4,2},{6,4},{1,7},{3,1},{5,3},{7,5},{8,14},{10,8},{12,... | collective-permute-start | bytes 786440 | tf_op jit(solution)/shard_map/ppermute | solution.py:471
  224.2 3.3 %mixed_join_kernel.1 = bf16[512,1536]{1,0:T(8,128)(2,1)} custom-call(s32[5]{0:T(128)} %stack.23._.s_ref, bf16[512,384]{1,0:T(8,128)(2,1)} %get-tuple-element.151.refs_0_, bf16[512,384]{1,0:T(8,128)(2,1)} %copy-done.10, bf16[512,384]{1,0:T(8,128)(2,1)} %copy-done.11, bf16[512,384]{1,0:T(8,128)(2,1)} %copy-done.12), custom_call_target="tpu_custom_call" | custom-call | flops 1 | bytes 1 | tf_op jit(solution)/shard_map/mixed_join_kernel/pallas_call | solution.py:582
  228.2 4.6 %collective-permute-done.15.d_ref = bf16[8,64,256]{2,1,0:T(8,128)(2,1)S(1)} collective-permute-done((bf16[8,64,256]{2,1,0:T(8,128)(2,1)}, bf16[8,64,256]{2,1,0:T(8,128)(2,1)S(1)}, u32[]{:S(2)}, u32[]{:S(2)}) %collective-permute-start.15) | collective-permute-done | bytes 262176 | tf_op jit(solution)/shard_map/ppermute | solution.py:471
  233.4 2.8 factor_sum_kernel.2
  236.2 3.2 %collective-permute-start.19 = (bf16[8,32,256]{2,1,0:T(8,128)(2,1)}, bf16[8,32,256]{2,1,0:T(8,128)(2,1)S(1)}, u32[]{:S(2)}, u32[]{:S(2)}) collective-permute-start(bf16[8,32,256]{2,1,0:T(8,128)(2,1)} %get-tuple-element.160), channel_id=1, source_target_pairs={{0,1},{1,0},{2,3},{3,2},{4,5},{5,4},{6,7},{7,6},{8,9},{9,8},{10,11... | collective-permute-start | bytes 393224 | tf_op jit(solution)/shard_map/ppermute | solution.py:645
  239.4 5.3 %back_kernel.1 = (bf16[192,2048]{1,0:T(8,128)(2,1)}, bf16[192,2048]{1,0:T(8,128)(2,1)}) custom-call(s32[5]{0:T(128)} %stack.23._.s_ref, bf16[32,14,8,384]{3,2,1,0:T(8,128)(2,1)} %copy-done.2, bf16[8,2,256,256]{3,2,1,0:T(8,128)(2,1)} %bitcast.28, bf16[384,2048]{1,0:T(8,128)(2,1)} %get-tuple-element.157.direct_ref), custom_call_target="tpu_custom_call" | custom-call | flops 12000000000 | bytes 6000000 | tf_op jit(solution)/shard_map/back_kernel/pallas_call | solution.py:638
  246.6 5.1 %term_one_kernel.1 = (bf16[8,64,256]{2,1,0:T(8,128)(2,1)}, bf16[8,64,256]{2,1,0:T(8,128)(2,1)}, bf16[8,64,256]{2,1,0:T(8,128)(2,1)}, bf16[8,64,256]{2,1,0:T(8,128)(2,1)}) custom-call(s32[5]{0:T(128)} %stack.23._.s_ref, bf16[32,14,8,384]{3,2,1,0:T(8,128)(2,1)} %copy-done.2, bf16[2048,384]{1,0:T(8,128)(2,1)} %get-tuple-element.118.in_ref), custom_call_target="tpu_custom_call" | custom-call | flops 1 | bytes 1 | tf_op jit(solution)/shard_map/term_one_kernel/pallas_call | solution.py:647
  256.9 3.5 %weight_sum_kernel.1 = f32[2,6,8,384]{3,2,1,0:T(8,128)} custom-call(s32[5]{0:T(128)} %stack.23._.s_ref, bf16[32,14,8,384]{3,2,1,0:T(8,128)(2,1)} %copy-done.2), custom_call_target="tpu_custom_call" | custom-call | flops 1 | bytes 1 | tf_op jit(solution)/shard_map/weight_sum_kernel/pallas_call | solution.py:656
  260.4 4.4 %collective-permute-start.24 = (f32[2,6,8,384]{3,2,1,0:T(8,128)}, f32[2,6,8,384]{3,2,1,0:T(8,128)S(1)}, u32[]{:S(2)}, u32[]{:S(2)}) collective-permute-start(f32[2,6,8,384]{3,2,1,0:T(8,128)} %weight_sum_kernel.1), channel_id=1, source_target_pairs={{0,0},{1,1},{8,2},{9,3},{16,4},{17,5},{24,6},{25,7},{32,8},{33,9},... | collective-permute-start | bytes 442376 | tf_op jit(solution)/shard_map/ppermute | solution.py:662
  268.9 2.7 factor_sum_kernel.3
  274.3 3.1 %join_kernel.1 = bf16[192,4096]{1,0:T(8,128)(2,1)} custom-call(s32[5]{0:T(128)} %stack.23._.s_ref, bf16[192,2048]{1,0:T(8,128)(2,1)} %get-tuple-element.158.own_ref, bf16[192,2048]{1,0:T(8,128)(2,1)} %copy-done.9), custom_call_target="tpu_custom_call" | custom-call | flops 1 | bytes 1 | tf_op jit(solution)/shard_map/join_kernel/pallas_call | solution.py:677
  (131 shorter events, 68.8 us)
Async XLA Ops:
  0.6 35.3 %copy-start = (bf16[16,256,256]{2,1,0:T(8,128)(2,1)S(1)}, bf16[16,256,256]{2,1,0:T(8,128)(2,1)}, u32[]{:S(2)}) copy-start(bf16[16,256,256]{2,1,0:T(8,128)(2,1)} %param.11) | copy-start | bytes 6291460
  4.2 23.2 %collective-permute-start.1 = (bf16[192,2048]{1,0:T(8,128)(2,1)}, bf16[192,2048]{1,0:T(8,128)(2,1)S(1)}, u32[]{:S(2)}, u32[]{:S(2)}) collective-permute-start(bf16[192,2048]{1,0:T(8,128)(2,1)} %gather_kernel.1), channel_id=1, source_target_pairs={{0,1},{1,0},{2,3},{3,2},{4,5},{5,4},{6,7},{7,6},{8,9},{9,8},{10,11... | collective-permute-start | bytes 2359304 | tf_op jit(solution)/shard_map/ppermute | solution.py:496
  10.1 9.4 %collective-permute-start = (bf16[2,6,8,384]{3,2,1,0:T(8,128)(2,1)}, bf16[2,6,8,384]{3,2,1,0:T(8,128)(2,1)S(1)}, u32[]{:S(2)}, u32[]{:S(2)}) collective-permute-start(bf16[2,6,8,384]{3,2,1,0:T(8,128)(2,1)} %payload_kernel.1), channel_id=1, source_target_pairs={{0,0},{1,1},{2,8},{3,9},{4,16},{5,17},{6,24},{7,25},{8,32},{9,33},... | collective-permute-start | bytes 221192 | tf_op jit(solution)/shard_map/ppermute | solution.py:504
  28.3 43.6 %all-to-all-start = ((bf16[32,14,8,384]{3,2,1,0:T(8,128)(2,1)}), bf16[32,14,8,384]{3,2,1,0:T(8,128)(2,1)}, u32[]{:S(2)}, u32[]{:S(2)}) async-start(bf16[32,14,8,384]{3,2,1,0:T(8,128)(2,1)} %first_kernel.1), calls=%async_computation | async-start | bytes 5505024 | tf_op jit(solution)/shard_map/all_to_all | solution.py:516
  77.6 29.5 %all-to-all-start.1 = ((bf16[32,8,8,384]{3,2,1,0:T(8,128)(2,1)}), bf16[32,8,8,384]{3,2,1,0:T(8,128)(2,1)S(1)}, u32[]{:S(2)}, u32[]{:S(2)}) async-start(bf16[32,8,8,384]{3,2,1,0:T(8,128)(2,1)} %get-tuple-element.104), calls=%async_computation.1 | async-start | bytes 3145728 | tf_op jit(solution)/shard_map/all_to_all | solution.py:537
  85.3 8.2 %collective-permute-start.2 = (bf16[32,6,8,384]{3,2,1,0:T(8,128)(2,1)S(1)}, bf16[32,6,8,384]{3,2,1,0:T(8,128)(2,1)S(1)}, u32[]{:S(2)}, u32[]{:S(2)}) collective-permute-start(bf16[32,6,8,384]{3,2,1,0:T(8,128)(2,1)S(1)} %slice.39.own_ref), channel_id=1, source_target_pairs={{0,8},{8,0},{1,9},{9,1},{2,10},{10,2},{3,11},{11,3},{4,12},{12,4},... | collective-permute-start | bytes 3538952 | tf_op jit(solution)/shard_map/ppermute | solution.py:540
  88.6 29.0 %collective-permute-start.6 = (bf16[512,384]{1,0:T(8,128)(2,1)}, bf16[512,384]{1,0:T(8,128)(2,1)S(1)}, u32[]{:S(2)}, u32[]{:S(2)}) collective-permute-start(bf16[512,384]{1,0:T(8,128)(2,1)} %get-tuple-element.113), channel_id=1, source_target_pairs={{0,6},{2,0},{4,2},{6,4},{1,7},{3,1},{5,3},{7,5},{8,14},{10,8},{12,... | collective-permute-start | bytes 1179656 | tf_op jit(solution)/shard_map/ppermute | solution.py:524
  89.1 32.1 %collective-permute-start.7 = (bf16[512,384]{1,0:T(8,128)(2,1)}, bf16[512,384]{1,0:T(8,128)(2,1)S(1)}, u32[]{:S(2)}, u32[]{:S(2)}) collective-permute-start(bf16[512,384]{1,0:T(8,128)(2,1)} %get-tuple-element.114), channel_id=1, source_target_pairs={{0,4},{2,6},{4,0},{6,2},{1,5},{3,7},{5,1},{7,3},{8,12},{10,14},{12... | collective-permute-start | bytes 1179656 | tf_op jit(solution)/shard_map/ppermute | solution.py:524
  91.7 29.5 %collective-permute-start.8 = (bf16[512,384]{1,0:T(8,128)(2,1)}, bf16[512,384]{1,0:T(8,128)(2,1)S(1)}, u32[]{:S(2)}, u32[]{:S(2)}) collective-permute-start(bf16[512,384]{1,0:T(8,128)(2,1)} %get-tuple-element.115), channel_id=1, source_target_pairs={{0,2},{2,4},{4,6},{6,0},{1,3},{3,5},{5,7},{7,1},{8,10},{10,12},{12... | collective-permute-start | bytes 1179656 | tf_op jit(solution)/shard_map/ppermute | solution.py:524
  114.9 6.4 %collective-permute-start.5 = (f32[8,512]{1,0:T(8,128)}, f32[8,512]{1,0:T(8,128)S(1)}, u32[]{:S(2)}, u32[]{:S(2)}) collective-permute-start(f32[8,512]{1,0:T(8,128)} %get-tuple-element.111.refs_0_), channel_id=1, source_target_pairs={{0,2},{2,4},{4,6},{6,0},{1,3},{3,5},{5,7},{7,1},{8,10},{10,12},{12... | collective-permute-start | bytes 49160 | tf_op jit(solution)/shard_map/ppermute | solution.py:467
  116.6 5.5 %collective-permute-start.4 = (f32[8,512]{1,0:T(8,128)}, f32[8,512]{1,0:T(8,128)S(1)}, u32[]{:S(2)}, u32[]{:S(2)}) collective-permute-start(f32[8,512]{1,0:T(8,128)} %get-tuple-element.111.refs_0_), channel_id=1, source_target_pairs={{0,4},{2,6},{4,0},{6,2},{1,5},{3,7},{5,1},{7,3},{8,12},{10,14},{12... | collective-permute-start | bytes 49160 | tf_op jit(solution)/shard_map/ppermute | solution.py:467
  117.5 4.5 %collective-permute-start.3 = (f32[8,512]{1,0:T(8,128)}, f32[8,512]{1,0:T(8,128)S(1)}, u32[]{:S(2)}, u32[]{:S(2)}) collective-permute-start(f32[8,512]{1,0:T(8,128)} %get-tuple-element.111.refs_0_), channel_id=1, source_target_pairs={{0,6},{2,0},{4,2},{6,4},{1,7},{3,1},{5,3},{7,5},{8,14},{10,8},{12,... | collective-permute-start | bytes 49160 | tf_op jit(solution)/shard_map/ppermute | solution.py:467
  142.0 6.1 %collective-permute-start.11 = (f32[8,512]{1,0:T(8,128)}, f32[8,512]{1,0:T(8,128)S(1)}, u32[]{:S(2)}, u32[]{:S(2)}) collective-permute-start(f32[8,512]{1,0:T(8,128)} %get-tuple-element.136.refs_4_.refs_0_), channel_id=1, source_target_pairs={{0,2},{2,4},{4,6},{6,0},{1,3},{3,5},{5,7},{7,1},{8,10},{10,12},{12... | collective-permute-start | bytes 49160 | tf_op jit(solution)/shard_map/ppermute | solution.py:467
  143.4 5.5 %collective-permute-start.10 = (f32[8,512]{1,0:T(8,128)}, f32[8,512]{1,0:T(8,128)S(1)}, u32[]{:S(2)}, u32[]{:S(2)}) collective-permute-start(f32[8,512]{1,0:T(8,128)} %get-tuple-element.136.refs_4_.refs_0_), channel_id=1, source_target_pairs={{0,4},{2,6},{4,0},{6,2},{1,5},{3,7},{5,1},{7,3},{8,12},{10,14},{12... | collective-permute-start | bytes 49160 | tf_op jit(solution)/shard_map/ppermute | solution.py:467
  146.0 4.0 %collective-permute-start.9 = (f32[8,512]{1,0:T(8,128)}, f32[8,512]{1,0:T(8,128)S(1)}, u32[]{:S(2)}, u32[]{:S(2)}) collective-permute-start(f32[8,512]{1,0:T(8,128)} %get-tuple-element.136.refs_4_.refs_0_), channel_id=1, source_target_pairs={{0,6},{2,0},{4,2},{6,4},{1,7},{3,1},{5,3},{7,5},{8,14},{10,8},{12,... | collective-permute-start | bytes 49160 | tf_op jit(solution)/shard_map/ppermute | solution.py:467
  158.0 27.4 %all-to-all-start.2 = ((bf16[32,8,8,384]{3,2,1,0:T(8,128)(2,1)}), bf16[32,8,8,384]{3,2,1,0:T(8,128)(2,1)S(1)}, u32[]{:S(2)}, u32[]{:S(2)}) async-start(bf16[32,8,8,384]{3,2,1,0:T(8,128)(2,1)} %get-tuple-element.129), calls=%async_computation.2 | async-start | bytes 3145728 | tf_op jit(solution)/shard_map/all_to_all | solution.py:579
  180.2 3.1 %collective-permute-start.12 = (bf16[32,6,8,384]{3,2,1,0:T(8,128)(2,1)}, bf16[32,6,8,384]{3,2,1,0:T(8,128)(2,1)S(1)}, u32[]{:S(2)}, u32[]{:S(2)}) collective-permute-start(bf16[32,6,8,384]{3,2,1,0:T(8,128)(2,1)} %get-tuple-element.141), channel_id=1, source_target_pairs={{0,8},{8,0},{1,9},{9,1},{2,10},{10,2},{3,11},{11,3},{4,12},{12,4},... | collective-permute-start | bytes 3538952 | tf_op jit(solution)/shard_map/ppermute | solution.py:601
  193.1 43.1 %all-to-all-start.3 = ((bf16[32,14,8,384]{3,2,1,0:T(8,128)(2,1)}), bf16[32,14,8,384]{3,2,1,0:T(8,128)(2,1)S(1)}, u32[]{:S(2)}, u32[]{:S(2)}) async-start(bf16[32,14,8,384]{3,2,1,0:T(8,128)(2,1)} %get-tuple-element.142), calls=%async_computation.3 | async-start | bytes 5505024 | tf_op jit(solution)/shard_map/all_to_all | solution.py:614
  198.9 13.6 %collective-permute-start.16 = (bf16[512,384]{1,0:T(8,128)(2,1)}, bf16[512,384]{1,0:T(8,128)(2,1)S(1)}, u32[]{:S(2)}, u32[]{:S(2)}) collective-permute-start(bf16[512,384]{1,0:T(8,128)(2,1)} %get-tuple-element.152), channel_id=1, source_target_pairs={{0,2},{2,4},{4,6},{6,0},{1,3},{3,5},{5,7},{7,1},{8,10},{10,12},{12... | collective-permute-start | bytes 1179656 | tf_op jit(solution)/shard_map/ppermute | solution.py:471
  200.5 22.2 %collective-permute-start.17 = (bf16[512,384]{1,0:T(8,128)(2,1)S(1)}, bf16[512,384]{1,0:T(8,128)(2,1)S(1)}, u32[]{:S(2)}, u32[]{:S(2)}) collective-permute-start(bf16[512,384]{1,0:T(8,128)(2,1)S(1)} %copy-done.30), channel_id=1, source_target_pairs={{0,4},{2,6},{4,0},{6,2},{1,5},{3,7},{5,1},{7,3},{8,12},{10,14},{12... | collective-permute-start | bytes 1179656 | tf_op jit(solution)/shard_map/ppermute | solution.py:471
  203.2 19.6 %collective-permute-start.18 = (bf16[512,384]{1,0:T(8,128)(2,1)S(1)}, bf16[512,384]{1,0:T(8,128)(2,1)S(1)}, u32[]{:S(2)}, u32[]{:S(2)}) collective-permute-start(bf16[512,384]{1,0:T(8,128)(2,1)S(1)} %copy-done.29), channel_id=1, source_target_pairs={{0,6},{2,0},{4,2},{6,4},{1,7},{3,1},{5,3},{7,5},{8,14},{10,8},{12,... | collective-permute-start | bytes 1179656 | tf_op jit(solution)/shard_map/ppermute | solution.py:471
  209.0 18.5 %collective-permute-start.13 = (bf16[8,64,256]{2,1,0:T(8,128)(2,1)}, bf16[8,64,256]{2,1,0:T(8,128)(2,1)S(1)}, u32[]{:S(2)}, u32[]{:S(2)}) collective-permute-start(bf16[8,64,256]{2,1,0:T(8,128)(2,1)} %get-tuple-element.146), channel_id=1, source_target_pairs={{0,2},{2,4},{4,6},{6,0},{1,3},{3,5},{5,7},{7,1},{8,10},{10,12},{12... | collective-permute-start | bytes 786440 | tf_op jit(solution)/shard_map/ppermute | solution.py:471
  210.4 17.8 %collective-permute-start.14 = (bf16[8,64,256]{2,1,0:T(8,128)(2,1)}, bf16[8,64,256]{2,1,0:T(8,128)(2,1)S(1)}, u32[]{:S(2)}, u32[]{:S(2)}) collective-permute-start(bf16[8,64,256]{2,1,0:T(8,128)(2,1)} %get-tuple-element.147), channel_id=1, source_target_pairs={{0,4},{2,6},{4,0},{6,2},{1,5},{3,7},{5,1},{7,3},{8,12},{10,14},{12... | collective-permute-start | bytes 786440 | tf_op jit(solution)/shard_map/ppermute | solution.py:471
  212.5 20.2 %collective-permute-start.15 = (bf16[8,64,256]{2,1,0:T(8,128)(2,1)}, bf16[8,64,256]{2,1,0:T(8,128)(2,1)S(1)}, u32[]{:S(2)}, u32[]{:S(2)}) collective-permute-start(bf16[8,64,256]{2,1,0:T(8,128)(2,1)} %get-tuple-element.148), channel_id=1, source_target_pairs={{0,6},{2,0},{4,2},{6,4},{1,7},{3,1},{5,3},{7,5},{8,14},{10,8},{12,... | collective-permute-start | bytes 786440 | tf_op jit(solution)/shard_map/ppermute | solution.py:471
  236.2 8.5 %collective-permute-start.19 = (bf16[8,32,256]{2,1,0:T(8,128)(2,1)}, bf16[8,32,256]{2,1,0:T(8,128)(2,1)S(1)}, u32[]{:S(2)}, u32[]{:S(2)}) collective-permute-start(bf16[8,32,256]{2,1,0:T(8,128)(2,1)} %get-tuple-element.160), channel_id=1, source_target_pairs={{0,1},{1,0},{2,3},{3,2},{4,5},{5,4},{6,7},{7,6},{8,9},{9,8},{10,11... | collective-permute-start | bytes 393224 | tf_op jit(solution)/shard_map/ppermute | solution.py:645
  244.7 26.9 %collective-permute-start.23 = (bf16[192,2048]{1,0:T(8,128)(2,1)}, bf16[192,2048]{1,0:T(8,128)(2,1)S(1)}, u32[]{:S(2)}, u32[]{:S(2)}) collective-permute-start(bf16[192,2048]{1,0:T(8,128)(2,1)} %get-tuple-element.176), channel_id=1, source_target_pairs={{0,1},{1,0},{2,3},{3,2},{4,5},{5,4},{6,7},{7,6},{8,9},{9,8},{10,11... | collective-permute-start | bytes 2359304 | tf_op jit(solution)/shard_map/ppermute | solution.py:655
  251.7 15.6 %collective-permute-start.20 = (bf16[8,64,256]{2,1,0:T(8,128)(2,1)}, bf16[8,64,256]{2,1,0:T(8,128)(2,1)S(1)}, u32[]{:S(2)}, u32[]{:S(2)}) collective-permute-start(bf16[8,64,256]{2,1,0:T(8,128)(2,1)} %get-tuple-element.172), channel_id=1, source_target_pairs={{0,2},{2,4},{4,6},{6,0},{1,3},{3,5},{5,7},{7,1},{8,10},{10,12},{12... | collective-permute-start | bytes 786440 | tf_op jit(solution)/shard_map/ppermute | solution.py:471
  252.1 15.2 %collective-permute-start.21 = (bf16[8,64,256]{2,1,0:T(8,128)(2,1)}, bf16[8,64,256]{2,1,0:T(8,128)(2,1)S(1)}, u32[]{:S(2)}, u32[]{:S(2)}) collective-permute-start(bf16[8,64,256]{2,1,0:T(8,128)(2,1)} %get-tuple-element.173), channel_id=1, source_target_pairs={{0,4},{2,6},{4,0},{6,2},{1,5},{3,7},{5,1},{7,3},{8,12},{10,14},{12... | collective-permute-start | bytes 786440 | tf_op jit(solution)/shard_map/ppermute | solution.py:471
  254.7 12.6 %collective-permute-start.22 = (bf16[8,64,256]{2,1,0:T(8,128)(2,1)}, bf16[8,64,256]{2,1,0:T(8,128)(2,1)S(1)}, u32[]{:S(2)}, u32[]{:S(2)}) collective-permute-start(bf16[8,64,256]{2,1,0:T(8,128)(2,1)} %get-tuple-element.174), channel_id=1, source_target_pairs={{0,6},{2,0},{4,2},{6,4},{1,7},{3,1},{5,3},{7,5},{8,14},{10,8},{12,... | collective-permute-start | bytes 786440 | tf_op jit(solution)/shard_map/ppermute | solution.py:471
  260.4 13.3 %copy-start.13 = (f32[2,6,8,384]{3,2,1,0:T(8,128)S(1)}, f32[2,6,8,384]{3,2,1,0:T(8,128)}, u32[]{:S(2)}) copy-start(f32[2,6,8,384]{3,2,1,0:T(8,128)} %weight_sum_kernel.1) | copy-start | bytes 442372
  260.4 17.0 %collective-permute-start.24 = (f32[2,6,8,384]{3,2,1,0:T(8,128)}, f32[2,6,8,384]{3,2,1,0:T(8,128)S(1)}, u32[]{:S(2)}, u32[]{:S(2)}) collective-permute-start(f32[2,6,8,384]{3,2,1,0:T(8,128)} %weight_sum_kernel.1), channel_id=1, source_target_pairs={{0,0},{1,1},{8,2},{9,3},{16,4},{17,5},{24,6},{25,7},{32,8},{33,9},... | collective-permute-start | bytes 442376 | tf_op jit(solution)/shard_map/ppermute | solution.py:662
  271.6 7.9 %collective-permute-start.25 = (bf16[8,32,256]{2,1,0:T(8,128)(2,1)}, bf16[8,32,256]{2,1,0:T(8,128)(2,1)S(1)}, u32[]{:S(2)}, u32[]{:S(2)}) collective-permute-start(bf16[8,32,256]{2,1,0:T(8,128)(2,1)} %get-tuple-element.180), channel_id=1, source_target_pairs={{0,1},{1,0},{2,3},{3,2},{4,5},{5,4},{6,7},{7,6},{8,9},{9,8},{10,11... | collective-permute-start | bytes 393224 | tf_op jit(solution)/shard_map/ppermute | solution.py:668
  (32 other events, 89.7 us)

commit v7 on v6

--- a/solution.py
+++ b/solution.py
@@ -77,6 +77,7 @@
 
 
 PIECES = pl.BlockSpec((32, 2, 8, DB), lambda t, s: (0, t, 0, 0))
+PAIRS = pl.BlockSpec((32, 4, 8, DB), lambda t, s: (0, t, 0, 0))
 SUMS = [whole(8, 512)] * 4
 
 
@@ -285,20 +286,22 @@
     _, resid_ref, cot_ref, gain_ref, gnormed_ref, in_ref, pgate_ref, *refs
 ):
     squares, inners, (g_resid_ref, g_second_ref) = refs[:4], refs[4:8], refs[8:]
-    step = pl.program_id(0)
-    rstd_row = lax.rsqrt(row_of(squares, step) * (1.0 / D) + 1e-06)
-    rstd = as_column(rstd_row)
-    factor = as_column(rstd_row * rstd_row * rstd_row * (row_of(inners, step) * (1.0 / D)))
-    scaled = gnormed_ref[...] * gain_ref[...]
-    g_resid = (
-        cot_ref[...].astype(F32) + rstd * scaled - resid_ref[...].astype(F32) * factor
-    ).astype(BF)
-    g_resid_ref[...] = g_resid
-    value = in_ref[...].astype(F32)
-    silu_in = value * sigmoid(value)
-    g_second = (g_resid.astype(F32) * pgate_ref[...].astype(F32) * silu_in).astype(BF)
-    for r in range(2):
-        g_second_ref[:, r] = g_second[r * 256 : (r + 1) * 256].reshape(32, 8, DB)
+    for q in range(2):
+        chunk = 2 * pl.program_id(0) + q
+        here = slice(q * 512, (q + 1) * 512)
+        rstd_row = lax.rsqrt(row_of(squares, chunk) * (1.0 / D) + 1e-06)
+        rstd = as_column(rstd_row)
+        factor = as_column(rstd_row * rstd_row * rstd_row * (row_of(inners, chunk) * (1.0 / D)))
+        scaled = gnormed_ref[here] * gain_ref[...]
+        g_resid = (
+            cot_ref[here].astype(F32) + rstd * scaled - resid_ref[here].astype(F32) * factor
+        ).astype(BF)
+        g_resid_ref[here] = g_resid
+        value = in_ref[here].astype(F32)
+        silu_in = value * sigmoid(value)
+        g_second = (g_resid.astype(F32) * pgate_ref[here].astype(F32) * silu_in).astype(BF)
+        for r in range(2):
+            g_second_ref[:, 2 * q + r] = g_second[r * 256 : (r + 1) * 256].reshape(32, 8, DB)
 
 
 def direct_kernel(_, g_resid_ref, in_ref, second_ref, pgate_ref, win_ref, g_direct_ref, term_ref):
@@ -334,7 +337,7 @@
 
 
 def term_one_kernel(s_ref, g_first_ref, in_ref, *refs):
-    for r in range(2):
+    for r in range(4):
         g_first = g_first_ref[:, r].reshape(256, DB)
         term = dot_t(g_first, in_ref[r * 256 : (r + 1) * 256])
         put_terms(s_ref, term, refs[4], refs[:4], r)
@@ -360,9 +363,9 @@
 
 def back_kernel(s_ref, g_first_ref, f1_ref, direct_ref, own_ref, give_ref):
     zh = s_ref[0]
-    for r in range(2):
+    for r in range(4):
         here = slice(r * 256, (r + 1) * 256)
-        back = t_dot(g_first_ref[:, r].reshape(256, DB), f1_ref[0, r])
+        back = t_dot(g_first_ref[:, r].reshape(256, DB), f1_ref[r // 2, 0, r % 2])
         total = direct_ref[:, here].astype(F32) + back
         low, high = total[:192], total[192:]
         own_ref[:, here] = jnp.where(zh == 0, low, high).astype(BF)
@@ -567,9 +570,9 @@
     )(at, resid, gain, wg, wu, wd, *squares, grad_out, *cots)
     inners = around(inner, "x")
     g_resid, g_second = call(
-        resid_grad_kernel, (4,),
-        [rows(DB), rows(DB), whole(1, DB), rows(DB), rows(DB), rows(DB)] + SUMS + SUMS,
-        [rows(DB), PIECES],
+        resid_grad_kernel, (2,),
+        [rows(DB, 1024)] * 2 + [whole(1, DB)] + [rows(DB, 1024)] * 3 + SUMS + SUMS,
+        [rows(DB, 1024), PAIRS],
         [bf(2048, DB), bf(32, 8, 8, DB)],
         (50_000_000, 12_000_000),
     )(at, resid, cot, gain, g_normed, input_mlp, pgate, *squares, *inners)
@@ -636,17 +639,17 @@
 
     g_first, sums_two, mixed_out = lax.optimization_barrier((g_first, sums_two, mixed_out))
     own_grad, give_grad = call(
-        back_kernel, (4,),
-        [PIECES, pl.BlockSpec((1, 2, 256, 256), lambda t, s: (2 * t + s[0], 0, 0, 0)), columns(DB)],
-        [columns(192), columns(192)],
+        back_kernel, (2,),
+        [PAIRS, pl.BlockSpec((2, 1, 2, 256, 256), lambda t, s: (t, s[0], 0, 0, 0)), columns(DB, 1024)],
+        [columns(192, 1024), columns(192, 1024)],
         [bf(192, 2048), bf(192, 2048)],
         (12_000_000_000, 6_000_000),
-    )(at, g_first, factor_one.reshape(8, 2, 256, 256), g_direct)
+    )(at, g_first, factor_one.reshape(4, 2, 2, 256, 256), g_direct)
     got_two = lax.ppermute(sums_two[1], "zh", SWAP)
     g_first, give_grad, got_two = lax.optimization_barrier((g_first, give_grad, got_two))
     terms_one = call(
-        term_one_kernel, (4,), [PIECES, rows(DB)],
-        [term_out] * 4, [bf(8, 64, 256)] * 4, (1, 1), square_scratch,
+        term_one_kernel, (2,), [PAIRS, rows(DB, 1024)],
+        [pl.BlockSpec((4, 64, 256), lambda t, s: (t, 0, 0))] * 4, [bf(8, 64, 256)] * 4, (1, 1), square_scratch,
     )(at, g_first, input_mlp)
 
     got_two, terms_one = lax.optimization_barrier((got_two, terms_one))

time: 287 us -> 284 us (0.990)
  Pallas kernels: 119 us -> 116 us
    pallas_call x3, Pallas kernels: 17.9 us -> 14.9 us  [the longest x1 6.7 us: per_device(): call(resid_grad_kernel, (2,), [rows(DB, 1024)] * 2 + [whole(1, DB)] + [ro...]
  transfers between devices with their start and end apart: 30 -> 30, of which waited for: 12 -> 12; matrix products, arithmetic and copies ran while one was open for 2% -> 2% of each run, Pallas kernels for 26% -> 25%
where the time goes in v7:
time: 284 us; the launch traced here: 283 us
  Pallas kernels  116 us (41%)
  starting transfers between devices  81.6 us (29%)
  waiting for transfers between devices  67 us (24%)
  local copies, waits for them, and re-layouts  16.2 us (6%)
    all_to_all x1, waiting for transfers between devices, per_device(): lax.all_to_all(first_local, PLANE, split_axis=0, concat_axis=0, tiled=True)  34.8 us
    ppermute x9, starting transfers between devices, send_each(): lax.ppermute(parts[j], axis, turn(axis, 4, j))  23.9 us
    pallas_call x1, Pallas kernels, per_device(): call(mlp_kernel, (4,), [turned_rows(DB), whole(1, DB), whole(DB, 768), wh...  19.4 us
    pallas_call x1, Pallas kernels, per_device(): call(weight_grad_kernel, (2,), [rows(DB, 1024), rows(1536, 1024), rows(76...  11.1 us
    ppermute x6, starting transfers between devices, around(): lax.ppermute(value, axis, turn(axis, 4, -j))  11 us
    unnamed x68, local copies, waits for them, and re-layouts  9.78 us
    all_to_all x1, waiting for transfers between devices, per_device(): lax.all_to_all(second_cols, PLANE, split_axis=0, concat_axis=0, tiled=True)  8.06 us
    all_to_all x1, starting transfers between devices, per_device(): lax.all_to_all(first_local, PLANE, split_axis=0, concat_axis=0, tiled=True)  7.66 us
  transfers between devices with their start and end apart: 30, of which 12 were waited for; matrix products, arithmetic and copies ran while one was open for 2% of the time, Pallas kernels for 25%

profile of v7, /device:TPU:2, one launch (start us, length us, event | category | flops | bytes accessed | tf_op | source)
XLA Modules:
  0.0 282.6 jit_solution(11365308935889904990)
XLA Ops:
  1.4 2.8 gather_kernel.1
  4.2 3.9 %collective-permute-start.1 = (bf16[192,2048]{1,0:T(8,128)(2,1)}, bf16[192,2048]{1,0:T(8,128)(2,1)S(1)}, u32[]{:S(2)}, u32[]{:S(2)}) collective-permute-start(bf16[192,2048]{1,0:T(8,128)(2,1)} %gather_kernel.1), channel_id=1, source_target_pairs={{0,1},{1,0},{2,3},{3,2},{4,5},{5,4},{6,7},{7,6},{8,9},{9,8},{10,11... | collective-permute-start | bytes 2359304 | tf_op jit(solution)/shard_map/ppermute | solution.py:499
  12.0 7.5 %collective-permute-done.payload_ref = bf16[2,6,8,384]{3,2,1,0:T(8,128)(2,1)S(1)} collective-permute-done((bf16[2,6,8,384]{3,2,1,0:T(8,128)(2,1)}, bf16[2,6,8,384]{3,2,1,0:T(8,128)(2,1)S(1)}, u32[]{:S(2)}, u32[]{:S(2)}) %collective-permute-start) | collective-permute-done | bytes 73760 | tf_op jit(solution)/shard_map/ppermute | solution.py:507
  20.2 6.4 %first_kernel.1 = bf16[32,14,8,384]{3,2,1,0:T(8,128)(2,1)} custom-call(s32[5]{0:T(128)} %stack.23._.s_ref, bf16[16,256,256]{2,1,0:T(8,128)(2,1)} %f1_ref.1, bf16[192,4096]{1,0:T(8,128)(2,1)} %bitcast.26, bf16[2,6,8,384]{3,2,1,0:T(8,128)(2,1)} %copy-done.22), custom_call_target="tpu_custom_call" | custom-call | flops 1 | bytes 1 | tf_op jit(solution)/shard_map/first_kernel/pallas_call | solution.py:508
  28.3 7.7 %all-to-all-start = ((bf16[32,14,8,384]{3,2,1,0:T(8,128)(2,1)}), bf16[32,14,8,384]{3,2,1,0:T(8,128)(2,1)}, u32[]{:S(2)}, u32[]{:S(2)}) async-start(bf16[32,14,8,384]{3,2,1,0:T(8,128)(2,1)} %first_kernel.1), calls=%async_computation | async-start | bytes 5505024 | tf_op jit(solution)/shard_map/all_to_all | solution.py:519
  37.0 34.8 %all-to-all-done.piece_ref = bf16[32,14,8,384]{3,2,1,0:T(8,128)(2,1)} async-done(((bf16[32,14,8,384]{3,2,1,0:T(8,128)(2,1)}), bf16[32,14,8,384]{3,2,1,0:T(8,128)(2,1)}, u32[]{:S(2)}, u32[]{:S(2)}) %all-to-all-start) | async-done | bytes 2752544 | tf_op jit(solution)/shard_map/all_to_all | solution.py:519
  71.8 5.7 %second_kernel.1 = (bf16[32,8,8,384]{3,2,1,0:T(8,128)(2,1)}, bf16[8,256,384]{2,1,0:T(8,128)(2,1)}) custom-call(s32[5]{0:T(128)} %stack.23._.s_ref, bf16[32,14,8,384]{3,2,1,0:T(8,128)(2,1)} %all-to-all-done.piece_ref, bf16[8,256,256]{2,1,0:T(8,128)(2,1)} %constant_dynamic-slice_fusion.f2_ref), custom_call_target="tpu_custom_call" | custom-call | flops 400000000 | bytes 6000000 | tf_op jit(solution)/shard_map/second_kernel/pallas_call | solution.py:532
  77.6 6.3 %all-to-all-start.1 = ((bf16[32,8,8,384]{3,2,1,0:T(8,128)(2,1)}), bf16[32,8,8,384]{3,2,1,0:T(8,128)(2,1)S(1)}, u32[]{:S(2)}, u32[]{:S(2)}) async-start(bf16[32,8,8,384]{3,2,1,0:T(8,128)(2,1)} %get-tuple-element.104), calls=%async_computation.1 | async-start | bytes 3145728 | tf_op jit(solution)/shard_map/all_to_all | solution.py:540
  85.6 3.0 %copy_three_kernel.1 = (bf16[512,384]{1,0:T(8,128)(2,1)}, bf16[512,384]{1,0:T(8,128)(2,1)}, bf16[512,384]{1,0:T(8,128)(2,1)}) custom-call(s32[5]{0:T(128)} %stack.23._.s_ref, bf16[512,1536]{1,0:T(8,128)(2,1)} %refs_4_, bf16[512,1536]{1,0:T(8,128)(2,1)} %refs_4_, bf16[512,1536]{1,0:T(8,128)(2,1)} %refs_4_), custom_call_target="tpu_custom_call" | custom-call | flops 1 | bytes 1 | tf_op jit(solution)/shard_map/copy_three_kernel/pallas_call | solution.py:522
  94.5 4.5 %weights_kernel.1 = (bf16[384,768]{1,0:T(8,128)(2,1)}, bf16[384,768]{1,0:T(8,128)(2,1)}, bf16[384,384]{1,0:T(8,128)(2,1)}, bf16[768,384]{1,0:T(8,128)(2,1)}) custom-call(s32[5]{0:T(128)} %stack.23._.s_ref, bf16[32,6,8,384]{3,2,1,0:T(8,128)(2,1)} %copy-done.5, bf16[32,6,8,384]{3,2,1,0:T(8,128)(2,1)} %copy-done.7), custom_call_target="tpu_custom_call" | custom-call | flops 1 | bytes 1 | tf_op jit(solution)/shard_map/weights_kernel/pallas_call | solution.py:545
  99.1 8.1 %all-to-all-done.1.second_ref = bf16[32,8,8,384]{3,2,1,0:T(8,128)(2,1)S(1)} async-done(((bf16[32,8,8,384]{3,2,1,0:T(8,128)(2,1)}), bf16[32,8,8,384]{3,2,1,0:T(8,128)(2,1)S(1)}, u32[]{:S(2)}, u32[]{:S(2)}) %all-to-all-start.1) | async-done | bytes 1572896 | tf_op jit(solution)/shard_map/all_to_all | solution.py:540
  108.3 6.6 %gating_kernel.1 = (bf16[2048,384]{1,0:T(8,128)(2,1)}, bf16[2048,384]{1,0:T(8,128)(2,1)}, bf16[2048,384]{1,0:T(8,128)(2,1)}, f32[8,512]{1,0:T(8,128)}) custom-call(s32[5]{0:T(128)} %stack.23._.s_ref, bf16[192,4096]{1,0:T(8,128)(2,1)} %bitcast.27, bf16[192,2048]{1,0:T(8,128)(2,1)} %copy-done.8, bf16[32,8,8,384]{3,2,1,0:T(8,128)(2,1)} %copy-done.3, ...), custom_call_target="tpu_custom_call" | custom-call | flops 600000000 | bytes 10000000 | tf_op jit(solution)/shard_map/gating_kernel/pallas_call | solution.py:551
  122.6 19.4 %mlp_kernel.1 = (bf16[2048,384]{1,0:T(8,128)(2,1)}, bf16[2048,384]{1,0:T(8,128)(2,1)}, bf16[2048,768]{1,0:T(8,128)(2,1)}, bf16[2048,1536]{1,0:T(8,128)(2,1)}, f3...) custom-call(s32[5]{0:T(128)} %stack.23._.s_ref, ...), custom_call_target="tpu_custom_call" | custom-call | flops 7299999744 | bytes 24000000 | tf_op jit(solution)/shard_map/mlp_kernel/pallas_call | solution.py:561
  150.5 6.7 %resid_grad_kernel.1 = (bf16[2048,384]{1,0:T(8,128)(2,1)}, bf16[32,8,8,384]{3,2,1,0:T(8,128)(2,1)}) custom-call(s32[5]{0:T(128)} %stack.23._.s_ref, bf16[2048,384]{1,0:T(8,128)(2,1)} %get-tuple-element.107.resid_ref, bf16[2048,384]{1,0:T(8,128)(2,1)} %get-tuple-element.133.cot_ref, f32[1,384]{1,0:T(1,128)} %reshape.51.gain_ref, ...), custom_call_target="tpu_custom_call" | custom-call | flops 50000000 | bytes 12000000 | tf_op jit(solution)/shard_map/resid_grad_kernel/pallas_call | solution.py:572
  157.2 4.1 %all-to-all-start.2 = ((bf16[32,8,8,384]{3,2,1,0:T(8,128)(2,1)}), bf16[32,8,8,384]{3,2,1,0:T(8,128)(2,1)S(1)}, u32[]{:S(2)}, u32[]{:S(2)}) async-start(bf16[32,8,8,384]{3,2,1,0:T(8,128)(2,1)} %get-tuple-element.129), calls=%async_computation.2 | async-start | bytes 3145728 | tf_op jit(solution)/shard_map/all_to_all | solution.py:582
  161.3 7.0 %direct_kernel.1 = (bf16[384,2048]{1,0:T(8,128)(2,1)}, f32[384,384]{1,0:T(8,128)}) custom-call(s32[5]{0:T(128)} %stack.23._.s_ref, bf16[2048,384]{1,0:T(8,128)(2,1)} %get-tuple-element.134.g_resid_ref, bf16[2048,384]{1,0:T(8,128)(2,1)} %get-tuple-element.118.in_ref, bf16[32,8,8,384]{3,2,1,0:T(8,128)(2,1)} %copy-done.3, ...), custom_call_target="tpu_custom_call" | custom-call | flops 1 | bytes 1 | tf_op jit(solution)/shard_map/direct_kernel/pallas_call | solution.py:589
  168.4 11.1 %weight_grad_kernel.1 = (bf16[32,6,8,384]{3,2,1,0:T(8,128)(2,1)}, bf16[32,6,8,384]{3,2,1,0:T(8,128)(2,1)}) custom-call(s32[5]{0:T(128)} %stack.23._.s_ref, bf16[2048,384]{1,0:T(8,128)(2,1)} %get-tuple-element.130.normed_ref, bf16[2048,1536]{1,0:T(8,128)(2,1)} %get-tuple-element.131.grads_ref, bf16[2048,768]{1,0:T(8,128)(2,1)} %get-tuple-element.132.hidden_ref, ...), custom_call_target="tpu_custom_call" | custom-call | flops 1 | bytes 1 | tf_op jit(solution)/shard_map/weight_grad_kernel/pallas_call | solution.py:598
  179.7 2.8 collective-permute-done.12.got_ref
  185.7 6.6 %first_grad_kernel.1 = (bf16[32,14,8,384]{3,2,1,0:T(8,128)(2,1)}, bf16[8,256,384]{2,1,0:T(8,128)(2,1)}) custom-call(s32[5]{0:T(128)} %stack.23._.s_ref, bf16[32,8,8,384]{3,2,1,0:T(8,128)(2,1)} %copy-done.4, bf16[8,256,256]{2,1,0:T(8,128)(2,1)} %constant_dynamic-slice_fusion.f2_ref, bf16[32,6,8,384]{3,2,1,0:T(8,128)(2,1)} %get-tuple-element.140.keep_ref, ...), custom_call_target="tpu_custom_call" | custom-call | flops 400000000 | bytes 6000000 | tf_op jit(solution)/shard_map/first_grad_kernel/pallas_call | solution.py:606
  192.3 5.8 %all-to-all-start.3 = ((bf16[32,14,8,384]{3,2,1,0:T(8,128)(2,1)}), bf16[32,14,8,384]{3,2,1,0:T(8,128)(2,1)S(1)}, u32[]{:S(2)}, u32[]{:S(2)}) async-start(bf16[32,14,8,384]{3,2,1,0:T(8,128)(2,1)} %get-tuple-element.142), calls=%async_computation.3 | async-start | bytes 5505024 | tf_op jit(solution)/shard_map/all_to_all | solution.py:617
  203.1 5.2 %term_two_kernel.1 = (bf16[8,64,256]{2,1,0:T(8,128)(2,1)}, bf16[8,64,256]{2,1,0:T(8,128)(2,1)}, bf16[8,64,256]{2,1,0:T(8,128)(2,1)}, bf16[8,64,256]{2,1,0:T(8,128)(2,1)}) custom-call(s32[5]{0:T(128)} %stack.23._.s_ref, bf16[8,256,384]{2,1,0:T(8,128)(2,1)} %get-tuple-element.143.grad_ref, bf16[8,256,384]{2,1,0:T(8,128)(2,1)} %get-tuple-element.144.first_ref), custom_call_target="tpu_custom_call" | custom-call | flops 1 | bytes 1 | tf_op jit(solution)/shard_map/term_two_kernel/pallas_call | solution.py:633
  211.8 10.2 %collective-permute-start.15 = (bf16[8,64,256]{2,1,0:T(8,128)(2,1)}, bf16[8,64,256]{2,1,0:T(8,128)(2,1)S(1)}, u32[]{:S(2)}, u32[]{:S(2)}) collective-permute-start(bf16[8,64,256]{2,1,0:T(8,128)(2,1)} %get-tuple-element.148), channel_id=1, source_target_pairs={{0,6},{2,0},{4,2},{6,4},{1,7},{3,1},{5,3},{7,5},{8,14},{10,8},{12,... | collective-permute-start | bytes 786440 | tf_op jit(solution)/shard_map/ppermute | solution.py:474
  223.5 3.3 %mixed_join_kernel.1 = bf16[512,1536]{1,0:T(8,128)(2,1)} custom-call(s32[5]{0:T(128)} %stack.23._.s_ref, bf16[512,384]{1,0:T(8,128)(2,1)} %get-tuple-element.151.refs_0_, bf16[512,384]{1,0:T(8,128)(2,1)} %copy-done.10, bf16[512,384]{1,0:T(8,128)(2,1)} %copy-done.11, bf16[512,384]{1,0:T(8,128)(2,1)} %copy-done.12), custom_call_target="tpu_custom_call" | custom-call | flops 1 | bytes 1 | tf_op jit(solution)/shard_map/mixed_join_kernel/pallas_call | solution.py:585
  227.4 4.6 %collective-permute-done.15.d_ref = bf16[8,64,256]{2,1,0:T(8,128)(2,1)S(1)} collective-permute-done((bf16[8,64,256]{2,1,0:T(8,128)(2,1)}, bf16[8,64,256]{2,1,0:T(8,128)(2,1)S(1)}, u32[]{:S(2)}, u32[]{:S(2)}) %collective-permute-start.15) | collective-permute-done | bytes 262176 | tf_op jit(solution)/shard_map/ppermute | solution.py:474
  235.4 3.2 %collective-permute-start.19 = (bf16[8,32,256]{2,1,0:T(8,128)(2,1)}, bf16[8,32,256]{2,1,0:T(8,128)(2,1)S(1)}, u32[]{:S(2)}, u32[]{:S(2)}) collective-permute-start(bf16[8,32,256]{2,1,0:T(8,128)(2,1)} %get-tuple-element.160), channel_id=1, source_target_pairs={{0,1},{1,0},{2,3},{3,2},{4,5},{5,4},{6,7},{7,6},{8,9},{9,8},{10,11... | collective-permute-start | bytes 393224 | tf_op jit(solution)/shard_map/ppermute | solution.py:648
  238.7 4.2 %back_kernel.1 = (bf16[192,2048]{1,0:T(8,128)(2,1)}, bf16[192,2048]{1,0:T(8,128)(2,1)}) custom-call(s32[5]{0:T(128)} %stack.23._.s_ref, bf16[32,14,8,384]{3,2,1,0:T(8,128)(2,1)} %copy-done.2, bf16[4,2,2,256,256]{4,3,2,1,0:T(8,128)(2,1)} %bitcast.28, bf16[384,2048]{1,0:T(8,128)(2,1)} %get-tuple-element.157.direct_ref), custom_call_target="tpu_custom_call" | custom-call | flops 12000000000 | bytes 6000000 | tf_op jit(solution)/shard_map/back_kernel/pallas_call | solution.py:641
  242.9 2.9 %collective-permute-start.23 = (bf16[192,2048]{1,0:T(8,128)(2,1)}, bf16[192,2048]{1,0:T(8,128)(2,1)S(1)}, u32[]{:S(2)}, u32[]{:S(2)}) collective-permute-start(bf16[192,2048]{1,0:T(8,128)(2,1)} %get-tuple-element.176), channel_id=1, source_target_pairs={{0,1},{1,0},{2,3},{3,2},{4,5},{5,4},{6,7},{7,6},{8,9},{9,8},{10,11... | collective-permute-start | bytes 2359304 | tf_op jit(solution)/shard_map/ppermute | solution.py:658
  245.8 4.0 %term_one_kernel.1 = (bf16[8,64,256]{2,1,0:T(8,128)(2,1)}, bf16[8,64,256]{2,1,0:T(8,128)(2,1)}, bf16[8,64,256]{2,1,0:T(8,128)(2,1)}, bf16[8,64,256]{2,1,0:T(8,128)(2,1)}) custom-call(s32[5]{0:T(128)} %stack.23._.s_ref, bf16[32,14,8,384]{3,2,1,0:T(8,128)(2,1)} %copy-done.2, bf16[2048,384]{1,0:T(8,128)(2,1)} %get-tuple-element.118.in_ref), custom_call_target="tpu_custom_call" | custom-call | flops 1 | bytes 1 | tf_op jit(solution)/shard_map/term_one_kernel/pallas_call | solution.py:650
  255.0 3.5 %weight_sum_kernel.1 = f32[2,6,8,384]{3,2,1,0:T(8,128)} custom-call(s32[5]{0:T(128)} %stack.23._.s_ref, bf16[32,14,8,384]{3,2,1,0:T(8,128)(2,1)} %copy-done.2), custom_call_target="tpu_custom_call" | custom-call | flops 1 | bytes 1 | tf_op jit(solution)/shard_map/weight_sum_kernel/pallas_call | solution.py:659
  258.5 4.4 %collective-permute-start.24 = (f32[2,6,8,384]{3,2,1,0:T(8,128)}, f32[2,6,8,384]{3,2,1,0:T(8,128)S(1)}, u32[]{:S(2)}, u32[]{:S(2)}) collective-permute-start(f32[2,6,8,384]{3,2,1,0:T(8,128)} %weight_sum_kernel.1), channel_id=1, source_target_pairs={{0,0},{1,1},{8,2},{9,3},{16,4},{17,5},{24,6},{25,7},{32,8},{33,9},... | collective-permute-start | bytes 442376 | tf_op jit(solution)/shard_map/ppermute | solution.py:665
  271.3 3.1 %join_kernel.1 = bf16[192,4096]{1,0:T(8,128)(2,1)} custom-call(s32[5]{0:T(128)} %stack.23._.s_ref, bf16[192,2048]{1,0:T(8,128)(2,1)} %get-tuple-element.158.own_ref, bf16[192,2048]{1,0:T(8,128)(2,1)} %copy-done.9), custom_call_target="tpu_custom_call" | custom-call | flops 1 | bytes 1 | tf_op jit(solution)/shard_map/join_kernel/pallas_call | solution.py:680
  274.4 3.1 %collective-permute-done.25 = bf16[8,32,256]{2,1,0:T(8,128)(2,1)S(1)} collective-permute-done((bf16[8,32,256]{2,1,0:T(8,128)(2,1)}, bf16[8,32,256]{2,1,0:T(8,128)(2,1)S(1)}, u32[]{:S(2)}, u32[]{:S(2)}) %collective-permute-start.25) | collective-permute-done | bytes 131104 | tf_op jit(solution)/shard_map/ppermute | solution.py:671
  (131 shorter events, 69.3 us)
Async XLA Ops:
  0.6 35.3 %copy-start = (bf16[16,256,256]{2,1,0:T(8,128)(2,1)S(1)}, bf16[16,256,256]{2,1,0:T(8,128)(2,1)}, u32[]{:S(2)}) copy-start(bf16[16,256,256]{2,1,0:T(8,128)(2,1)} %param.11) | copy-start | bytes 6291460
  4.2 23.2 %collective-permute-start.1 = (bf16[192,2048]{1,0:T(8,128)(2,1)}, bf16[192,2048]{1,0:T(8,128)(2,1)S(1)}, u32[]{:S(2)}, u32[]{:S(2)}) collective-permute-start(bf16[192,2048]{1,0:T(8,128)(2,1)} %gather_kernel.1), channel_id=1, source_target_pairs={{0,1},{1,0},{2,3},{3,2},{4,5},{5,4},{6,7},{7,6},{8,9},{9,8},{10,11... | collective-permute-start | bytes 2359304 | tf_op jit(solution)/shard_map/ppermute | solution.py:499
  10.1 9.4 %collective-permute-start = (bf16[2,6,8,384]{3,2,1,0:T(8,128)(2,1)}, bf16[2,6,8,384]{3,2,1,0:T(8,128)(2,1)S(1)}, u32[]{:S(2)}, u32[]{:S(2)}) collective-permute-start(bf16[2,6,8,384]{3,2,1,0:T(8,128)(2,1)} %payload_kernel.1), channel_id=1, source_target_pairs={{0,0},{1,1},{2,8},{3,9},{4,16},{5,17},{6,24},{7,25},{8,32},{9,33},... | collective-permute-start | bytes 221192 | tf_op jit(solution)/shard_map/ppermute | solution.py:507
  28.3 43.6 %all-to-all-start = ((bf16[32,14,8,384]{3,2,1,0:T(8,128)(2,1)}), bf16[32,14,8,384]{3,2,1,0:T(8,128)(2,1)}, u32[]{:S(2)}, u32[]{:S(2)}) async-start(bf16[32,14,8,384]{3,2,1,0:T(8,128)(2,1)} %first_kernel.1), calls=%async_computation | async-start | bytes 5505024 | tf_op jit(solution)/shard_map/all_to_all | solution.py:519
  77.6 29.5 %all-to-all-start.1 = ((bf16[32,8,8,384]{3,2,1,0:T(8,128)(2,1)}), bf16[32,8,8,384]{3,2,1,0:T(8,128)(2,1)S(1)}, u32[]{:S(2)}, u32[]{:S(2)}) async-start(bf16[32,8,8,384]{3,2,1,0:T(8,128)(2,1)} %get-tuple-element.104), calls=%async_computation.1 | async-start | bytes 3145728 | tf_op jit(solution)/shard_map/all_to_all | solution.py:540
  85.3 8.2 %collective-permute-start.2 = (bf16[32,6,8,384]{3,2,1,0:T(8,128)(2,1)S(1)}, bf16[32,6,8,384]{3,2,1,0:T(8,128)(2,1)S(1)}, u32[]{:S(2)}, u32[]{:S(2)}) collective-permute-start(bf16[32,6,8,384]{3,2,1,0:T(8,128)(2,1)S(1)} %slice.39.own_ref), channel_id=1, source_target_pairs={{0,8},{8,0},{1,9},{9,1},{2,10},{10,2},{3,11},{11,3},{4,12},{12,4},... | collective-permute-start | bytes 3538952 | tf_op jit(solution)/shard_map/ppermute | solution.py:543
  88.6 29.0 %collective-permute-start.6 = (bf16[512,384]{1,0:T(8,128)(2,1)}, bf16[512,384]{1,0:T(8,128)(2,1)S(1)}, u32[]{:S(2)}, u32[]{:S(2)}) collective-permute-start(bf16[512,384]{1,0:T(8,128)(2,1)} %get-tuple-element.113), channel_id=1, source_target_pairs={{0,6},{2,0},{4,2},{6,4},{1,7},{3,1},{5,3},{7,5},{8,14},{10,8},{12,... | collective-permute-start | bytes 1179656 | tf_op jit(solution)/shard_map/ppermute | solution.py:527
  89.1 32.1 %collective-permute-start.7 = (bf16[512,384]{1,0:T(8,128)(2,1)}, bf16[512,384]{1,0:T(8,128)(2,1)S(1)}, u32[]{:S(2)}, u32[]{:S(2)}) collective-permute-start(bf16[512,384]{1,0:T(8,128)(2,1)} %get-tuple-element.114), channel_id=1, source_target_pairs={{0,4},{2,6},{4,0},{6,2},{1,5},{3,7},{5,1},{7,3},{8,12},{10,14},{12... | collective-permute-start | bytes 1179656 | tf_op jit(solution)/shard_map/ppermute | solution.py:527
  91.7 29.5 %collective-permute-start.8 = (bf16[512,384]{1,0:T(8,128)(2,1)}, bf16[512,384]{1,0:T(8,128)(2,1)S(1)}, u32[]{:S(2)}, u32[]{:S(2)}) collective-permute-start(bf16[512,384]{1,0:T(8,128)(2,1)} %get-tuple-element.115), channel_id=1, source_target_pairs={{0,2},{2,4},{4,6},{6,0},{1,3},{3,5},{5,7},{7,1},{8,10},{10,12},{12... | collective-permute-start | bytes 1179656 | tf_op jit(solution)/shard_map/ppermute | solution.py:527
  114.9 6.4 %collective-permute-start.5 = (f32[8,512]{1,0:T(8,128)}, f32[8,512]{1,0:T(8,128)S(1)}, u32[]{:S(2)}, u32[]{:S(2)}) collective-permute-start(f32[8,512]{1,0:T(8,128)} %get-tuple-element.111.refs_0_), channel_id=1, source_target_pairs={{0,2},{2,4},{4,6},{6,0},{1,3},{3,5},{5,7},{7,1},{8,10},{10,12},{12... | collective-permute-start | bytes 49160 | tf_op jit(solution)/shard_map/ppermute | solution.py:470
  116.6 5.5 %collective-permute-start.4 = (f32[8,512]{1,0:T(8,128)}, f32[8,512]{1,0:T(8,128)S(1)}, u32[]{:S(2)}, u32[]{:S(2)}) collective-permute-start(f32[8,512]{1,0:T(8,128)} %get-tuple-element.111.refs_0_), channel_id=1, source_target_pairs={{0,4},{2,6},{4,0},{6,2},{1,5},{3,7},{5,1},{7,3},{8,12},{10,14},{12... | collective-permute-start | bytes 49160 | tf_op jit(solution)/shard_map/ppermute | solution.py:470
  117.5 4.5 %collective-permute-start.3 = (f32[8,512]{1,0:T(8,128)}, f32[8,512]{1,0:T(8,128)S(1)}, u32[]{:S(2)}, u32[]{:S(2)}) collective-permute-start(f32[8,512]{1,0:T(8,128)} %get-tuple-element.111.refs_0_), channel_id=1, source_target_pairs={{0,6},{2,0},{4,2},{6,4},{1,7},{3,1},{5,3},{7,5},{8,14},{10,8},{12,... | collective-permute-start | bytes 49160 | tf_op jit(solution)/shard_map/ppermute | solution.py:470
  142.0 6.1 %collective-permute-start.11 = (f32[8,512]{1,0:T(8,128)}, f32[8,512]{1,0:T(8,128)S(1)}, u32[]{:S(2)}, u32[]{:S(2)}) collective-permute-start(f32[8,512]{1,0:T(8,128)} %get-tuple-element.136.refs_4_.refs_0_), channel_id=1, source_target_pairs={{0,2},{2,4},{4,6},{6,0},{1,3},{3,5},{5,7},{7,1},{8,10},{10,12},{12... | collective-permute-start | bytes 49160 | tf_op jit(solution)/shard_map/ppermute | solution.py:470
  143.4 5.5 %collective-permute-start.10 = (f32[8,512]{1,0:T(8,128)}, f32[8,512]{1,0:T(8,128)S(1)}, u32[]{:S(2)}, u32[]{:S(2)}) collective-permute-start(f32[8,512]{1,0:T(8,128)} %get-tuple-element.136.refs_4_.refs_0_), channel_id=1, source_target_pairs={{0,4},{2,6},{4,0},{6,2},{1,5},{3,7},{5,1},{7,3},{8,12},{10,14},{12... | collective-permute-start | bytes 49160 | tf_op jit(solution)/shard_map/ppermute | solution.py:470
  146.0 4.0 %collective-permute-start.9 = (f32[8,512]{1,0:T(8,128)}, f32[8,512]{1,0:T(8,128)S(1)}, u32[]{:S(2)}, u32[]{:S(2)}) collective-permute-start(f32[8,512]{1,0:T(8,128)} %get-tuple-element.136.refs_4_.refs_0_), channel_id=1, source_target_pairs={{0,6},{2,0},{4,2},{6,4},{1,7},{3,1},{5,3},{7,5},{8,14},{10,8},{12,... | collective-permute-start | bytes 49160 | tf_op jit(solution)/shard_map/ppermute | solution.py:470
  157.2 27.4 %all-to-all-start.2 = ((bf16[32,8,8,384]{3,2,1,0:T(8,128)(2,1)}), bf16[32,8,8,384]{3,2,1,0:T(8,128)(2,1)S(1)}, u32[]{:S(2)}, u32[]{:S(2)}) async-start(bf16[32,8,8,384]{3,2,1,0:T(8,128)(2,1)} %get-tuple-element.129), calls=%async_computation.2 | async-start | bytes 3145728 | tf_op jit(solution)/shard_map/all_to_all | solution.py:582
  179.4 3.1 %collective-permute-start.12 = (bf16[32,6,8,384]{3,2,1,0:T(8,128)(2,1)}, bf16[32,6,8,384]{3,2,1,0:T(8,128)(2,1)S(1)}, u32[]{:S(2)}, u32[]{:S(2)}) collective-permute-start(bf16[32,6,8,384]{3,2,1,0:T(8,128)(2,1)} %get-tuple-element.141), channel_id=1, source_target_pairs={{0,8},{8,0},{1,9},{9,1},{2,10},{10,2},{3,11},{11,3},{4,12},{12,4},... | collective-permute-start | bytes 3538952 | tf_op jit(solution)/shard_map/ppermute | solution.py:604
  192.3 43.1 %all-to-all-start.3 = ((bf16[32,14,8,384]{3,2,1,0:T(8,128)(2,1)}), bf16[32,14,8,384]{3,2,1,0:T(8,128)(2,1)S(1)}, u32[]{:S(2)}, u32[]{:S(2)}) async-start(bf16[32,14,8,384]{3,2,1,0:T(8,128)(2,1)} %get-tuple-element.142), calls=%async_computation.3 | async-start | bytes 5505024 | tf_op jit(solution)/shard_map/all_to_all | solution.py:617
  198.1 13.6 %collective-permute-start.16 = (bf16[512,384]{1,0:T(8,128)(2,1)}, bf16[512,384]{1,0:T(8,128)(2,1)S(1)}, u32[]{:S(2)}, u32[]{:S(2)}) collective-permute-start(bf16[512,384]{1,0:T(8,128)(2,1)} %get-tuple-element.152), channel_id=1, source_target_pairs={{0,2},{2,4},{4,6},{6,0},{1,3},{3,5},{5,7},{7,1},{8,10},{10,12},{12... | collective-permute-start | bytes 1179656 | tf_op jit(solution)/shard_map/ppermute | solution.py:474
  199.8 22.2 %collective-permute-start.17 = (bf16[512,384]{1,0:T(8,128)(2,1)S(1)}, bf16[512,384]{1,0:T(8,128)(2,1)S(1)}, u32[]{:S(2)}, u32[]{:S(2)}) collective-permute-start(bf16[512,384]{1,0:T(8,128)(2,1)S(1)} %copy-done.30), channel_id=1, source_target_pairs={{0,4},{2,6},{4,0},{6,2},{1,5},{3,7},{5,1},{7,3},{8,12},{10,14},{12... | collective-permute-start | bytes 1179656 | tf_op jit(solution)/shard_map/ppermute | solution.py:474
  202.4 19.6 %collective-permute-start.18 = (bf16[512,384]{1,0:T(8,128)(2,1)S(1)}, bf16[512,384]{1,0:T(8,128)(2,1)S(1)}, u32[]{:S(2)}, u32[]{:S(2)}) collective-permute-start(bf16[512,384]{1,0:T(8,128)(2,1)S(1)} %copy-done.29), channel_id=1, source_target_pairs={{0,6},{2,0},{4,2},{6,4},{1,7},{3,1},{5,3},{7,5},{8,14},{10,8},{12,... | collective-permute-start | bytes 1179656 | tf_op jit(solution)/shard_map/ppermute | solution.py:474
  208.2 18.5 %collective-permute-start.13 = (bf16[8,64,256]{2,1,0:T(8,128)(2,1)}, bf16[8,64,256]{2,1,0:T(8,128)(2,1)S(1)}, u32[]{:S(2)}, u32[]{:S(2)}) collective-permute-start(bf16[8,64,256]{2,1,0:T(8,128)(2,1)} %get-tuple-element.146), channel_id=1, source_target_pairs={{0,2},{2,4},{4,6},{6,0},{1,3},{3,5},{5,7},{7,1},{8,10},{10,12},{12... | collective-permute-start | bytes 786440 | tf_op jit(solution)/shard_map/ppermute | solution.py:474
  209.6 17.8 %collective-permute-start.14 = (bf16[8,64,256]{2,1,0:T(8,128)(2,1)}, bf16[8,64,256]{2,1,0:T(8,128)(2,1)S(1)}, u32[]{:S(2)}, u32[]{:S(2)}) collective-permute-start(bf16[8,64,256]{2,1,0:T(8,128)(2,1)} %get-tuple-element.147), channel_id=1, source_target_pairs={{0,4},{2,6},{4,0},{6,2},{1,5},{3,7},{5,1},{7,3},{8,12},{10,14},{12... | collective-permute-start | bytes 786440 | tf_op jit(solution)/shard_map/ppermute | solution.py:474
  211.8 20.2 %collective-permute-start.15 = (bf16[8,64,256]{2,1,0:T(8,128)(2,1)}, bf16[8,64,256]{2,1,0:T(8,128)(2,1)S(1)}, u32[]{:S(2)}, u32[]{:S(2)}) collective-permute-start(bf16[8,64,256]{2,1,0:T(8,128)(2,1)} %get-tuple-element.148), channel_id=1, source_target_pairs={{0,6},{2,0},{4,2},{6,4},{1,7},{3,1},{5,3},{7,5},{8,14},{10,8},{12,... | collective-permute-start | bytes 786440 | tf_op jit(solution)/shard_map/ppermute | solution.py:474
  235.4 7.5 %collective-permute-start.19 = (bf16[8,32,256]{2,1,0:T(8,128)(2,1)}, bf16[8,32,256]{2,1,0:T(8,128)(2,1)S(1)}, u32[]{:S(2)}, u32[]{:S(2)}) collective-permute-start(bf16[8,32,256]{2,1,0:T(8,128)(2,1)} %get-tuple-element.160), channel_id=1, source_target_pairs={{0,1},{1,0},{2,3},{3,2},{4,5},{5,4},{6,7},{7,6},{8,9},{9,8},{10,11... | collective-permute-start | bytes 393224 | tf_op jit(solution)/shard_map/ppermute | solution.py:648
  242.9 26.8 %collective-permute-start.23 = (bf16[192,2048]{1,0:T(8,128)(2,1)}, bf16[192,2048]{1,0:T(8,128)(2,1)S(1)}, u32[]{:S(2)}, u32[]{:S(2)}) collective-permute-start(bf16[192,2048]{1,0:T(8,128)(2,1)} %get-tuple-element.176), channel_id=1, source_target_pairs={{0,1},{1,0},{2,3},{3,2},{4,5},{5,4},{6,7},{7,6},{8,9},{9,8},{10,11... | collective-permute-start | bytes 2359304 | tf_op jit(solution)/shard_map/ppermute | solution.py:658
  249.8 15.6 %collective-permute-start.20 = (bf16[8,64,256]{2,1,0:T(8,128)(2,1)}, bf16[8,64,256]{2,1,0:T(8,128)(2,1)S(1)}, u32[]{:S(2)}, u32[]{:S(2)}) collective-permute-start(bf16[8,64,256]{2,1,0:T(8,128)(2,1)} %get-tuple-element.172), channel_id=1, source_target_pairs={{0,2},{2,4},{4,6},{6,0},{1,3},{3,5},{5,7},{7,1},{8,10},{10,12},{12... | collective-permute-start | bytes 786440 | tf_op jit(solution)/shard_map/ppermute | solution.py:474
  250.1 15.4 %collective-permute-start.21 = (bf16[8,64,256]{2,1,0:T(8,128)(2,1)}, bf16[8,64,256]{2,1,0:T(8,128)(2,1)S(1)}, u32[]{:S(2)}, u32[]{:S(2)}) collective-permute-start(bf16[8,64,256]{2,1,0:T(8,128)(2,1)} %get-tuple-element.173), channel_id=1, source_target_pairs={{0,4},{2,6},{4,0},{6,2},{1,5},{3,7},{5,1},{7,3},{8,12},{10,14},{12... | collective-permute-start | bytes 786440 | tf_op jit(solution)/shard_map/ppermute | solution.py:474
  252.7 12.8 %collective-permute-start.22 = (bf16[8,64,256]{2,1,0:T(8,128)(2,1)}, bf16[8,64,256]{2,1,0:T(8,128)(2,1)S(1)}, u32[]{:S(2)}, u32[]{:S(2)}) collective-permute-start(bf16[8,64,256]{2,1,0:T(8,128)(2,1)} %get-tuple-element.174), channel_id=1, source_target_pairs={{0,6},{2,0},{4,2},{6,4},{1,7},{3,1},{5,3},{7,5},{8,14},{10,8},{12,... | collective-permute-start | bytes 786440 | tf_op jit(solution)/shard_map/ppermute | solution.py:474
  258.5 12.2 %copy-start.13 = (f32[2,6,8,384]{3,2,1,0:T(8,128)S(1)}, f32[2,6,8,384]{3,2,1,0:T(8,128)}, u32[]{:S(2)}) copy-start(f32[2,6,8,384]{3,2,1,0:T(8,128)} %weight_sum_kernel.1) | copy-start | bytes 442372
  258.5 15.9 %collective-permute-start.24 = (f32[2,6,8,384]{3,2,1,0:T(8,128)}, f32[2,6,8,384]{3,2,1,0:T(8,128)S(1)}, u32[]{:S(2)}, u32[]{:S(2)}) collective-permute-start(f32[2,6,8,384]{3,2,1,0:T(8,128)} %weight_sum_kernel.1), channel_id=1, source_target_pairs={{0,0},{1,1},{8,2},{9,3},{16,4},{17,5},{24,6},{25,7},{32,8},{33,9},... | collective-permute-start | bytes 442376 | tf_op jit(solution)/shard_map/ppermute | solution.py:665
  269.7 7.9 %collective-permute-start.25 = (bf16[8,32,256]{2,1,0:T(8,128)(2,1)}, bf16[8,32,256]{2,1,0:T(8,128)(2,1)S(1)}, u32[]{:S(2)}, u32[]{:S(2)}) collective-permute-start(bf16[8,32,256]{2,1,0:T(8,128)(2,1)} %get-tuple-element.180), channel_id=1, source_target_pairs={{0,1},{1,0},{2,3},{3,2},{4,5},{5,4},{6,7},{7,6},{8,9},{9,8},{10,11... | collective-permute-start | bytes 393224 | tf_op jit(solution)/shard_map/ppermute | solution.py:671
  (32 other events, 89.7 us)
